TPU v7x, 256 devices: a whole 4x4x8 slice. The times are simulated.
256 devices in a mesh: dp: 32 (over z, y), fsdp: 8 (over x, core).
Axes of the slice: x: 4, y: 4, z: 8, core: 2. Of those that a mesh axis runs over, the one named last changes fastest.
Arguments:
- tokens: bfloat16 [32768, 8192], P('dp', 'fsdp'), may hold values from -6 to 6
- basis: bfloat16 [8192, 512], P('fsdp'), may hold values from -0.0625 to 0.0625
- cotangent: bfloat16 [32768, 29568], P('dp', 'fsdp'), may hold values from -6 to 6
- exp_avg: float32 [512, 29568], P('dp', 'fsdp'), may hold values from -0.0078125 to 0.0078125
- exp_avg_sq: float32 [512, 29568], P('dp', 'fsdp'), may hold values from 1e-09 to 1e-07
Outputs:
- update: bfloat16 [8192, 29568], P('fsdp', 'dp')
- first: float32 [512, 29568], P('dp', 'fsdp')
- second: float32 [512, 29568], P('dp', 'fsdp')
All inputs are finite; a program needn't handle non-finite values.
Results may differ from a plain program's by a relative error of at most 0.0074.
Values may be sent and summed in bfloat16 or wider, within the bound.
No kernel may reach another device: no remote copies, remote signals or barrier semaphores. Data moves between devices by JAX's collectives and lax.ppermute only.
A program may use at most 64 MiB of HBM per device.

v0:
```python
import jax
import jax.numpy as jnp
from jax import lax
from jax.sharding import PartitionSpec as P

bias_first = 1.0 - 0.9**10
bias_second = 1.0 - 0.999**10


def shards(tokens, basis, cotangent, exp_avg, exp_avg_sq):
    partial_proj = jnp.dot(tokens, basis, preferred_element_type=jnp.float32)
    proj = lax.psum(partial_proj, "fsdp").astype(jnp.bfloat16)
    total_tokens = cotangent.shape[0] * lax.axis_size("dp")
    grad_low = lax.psum_scatter(
        lax.dot_general(
            proj, cotangent, (((0,), (0,)), ((), ())), preferred_element_type=jnp.float32
        ),
        "dp",
        scatter_dimension=0,
        tiled=True,
    ) * (1.0 / total_tokens)
    first = 0.9 * exp_avg + 0.1 * grad_low
    second = 0.999 * exp_avg_sq + 0.001 * grad_low * grad_low
    normed = (first / bias_first / (jnp.sqrt(second / bias_second) + 1e-08)).astype(jnp.bfloat16)
    wide_rows = lax.all_gather(normed, "fsdp", axis=1, tiled=True)
    all_rows = lax.all_to_all(wide_rows, "dp", split_axis=1, concat_axis=0, tiled=True)
    update = jnp.dot(basis, all_rows, preferred_element_type=jnp.float32).astype(jnp.bfloat16)
    return (update, first, second)


def solution(mesh):
    in_specs = (P("dp", "fsdp"), P("fsdp", None), P("dp", "fsdp"), P("dp", "fsdp"), P("dp", "fsdp"))
    out_specs = (P("fsdp", "dp"), P("dp", "fsdp"), P("dp", "fsdp"))
    return jax.shard_map(shards, mesh=mesh, in_specs=in_specs, out_specs=out_specs, check_vma=False)
```

profile of v0, /device:TPU:1, one launch (start us, length us, event | category | flops | bytes accessed | tf_op | source)
XLA Modules:
  0.0 371.0 jit_solution(16525423945772439121)
XLA Ops:
  7.2 0.0 copy-start
  7.2 0.0 reduce-scatter.2.cloned.1.call-start
  7.2 1.5 copy-done
  8.8 3.8 %fusion.3 = f32[1024,512]{1,0:T(8,128)} fusion(bf16[1024,1024]{1,0:T(8,128)(2,1)S(1)} %copy-done, bf16[1024,512]{1,0:T(8,128)(2,1)} %param.6), kind=kOutput, calls=%fused_computation.7 | convolution fusion | flops 1073741824 | bytes 5242880 | tf_op jit(solution)/shard_map/dot_general | solution.py:11
  12.6 54.7 %all-reduce.1 = bf16[1024,512]{1,0:T(8,128)(2,1)S(1)} all-reduce(f32[1024,512]{1,0:T(8,128)} %fusion.3), channel_id=1, replica_groups=mesh['dp'=32,'fsdp'=8] {'fsdp'}, use_global_device_ids=true, to_apply=%region_0.0 | all-reduce | flops 524288 | bytes 3145728 | tf_op jit(solution)/shard_map/psum | solution.py:12
  67.3 9.7 %fusion.4 = f32[512,3696]{1,0:T(8,128)} fusion(bf16[1024,512]{1,0:T(8,128)(2,1)S(1)} %all-reduce.1, bf16[1024,3696]{0,1:T(8,128)(2,1)} %param.7), kind=kOutput, calls=%fused_computation.8 | convolution fusion | flops 3875536896 | bytes 16187392 | tf_op jit(solution)/shard_map/dot_general | solution.py:15
  77.0 0.0 copy-start.1
  77.0 0.0 copy-start.2
  77.0 0.0 reduce-scatter.2.cloned.1.call-update
  77.0 225.3 %reduce-scatter.2.cloned.1.call-done = f32[16,3696]{1,0:T(8,128)} async-done(((f32[512,3696]{1,0:T(8,128)}), f32[16,3696]{1,0:T(8,128)}) %reduce-scatter.2.cloned.1.call-update) | async-done | bytes 236560 | tf_op jit(solution)/shard_map/reduce_scatter | solution.py:14
  302.4 0.0 copy-done.1
  302.4 0.0 copy-done.2
  302.4 1.9 fusion.2
  304.2 18.1 %all-gather = bf16[8,3696,16]{1,2,0:T(8,128)(2,1)S(1)} all-gather(bf16[1,3696,16]{1,2,0:T(8,128)(2,1)S(1)} %get-tuple-element.3), channel_id=1, replica_groups=mesh['dp'=32,'fsdp'=8] {'fsdp'}, dimensions={0}, use_global_device_ids=true | all-gather | bytes 1064448 | tf_op jit(solution)/shard_map/all_gather | solution.py:25
  322.3 0.2 copy.10
  322.5 1.8 reshape.10
  324.3 3.2 all_to_all.14
  327.5 0.0 copy-start.3
  327.5 0.6 copy.11
  328.1 33.5 %all_to_all.19 = bf16[16,32,924]{2,0,1:T(8,128)(2,1)S(1)} all-to-all(bf16[16,32,924]{2,0,1:T(8,128)(2,1)S(1)} %copy.11), channel_id=1, replica_groups=mesh['dp'=32,'fsdp'=8] {'dp'}, dimensions={1} | all-to-all | bytes 1892352 | tf_op jit(solution)/shard_map/all_to_all | solution.py:26
  361.6 0.0 copy-done.3
  361.6 2.6 convert_bitcast_fusion
Async XLA Ops:
  7.2 1.6 copy-start
  7.2 295.2 %reduce-scatter.2.cloned.1.call-start = ((), (), s32[]{:S(2)}) async-start(), calls=%async_computation.2 | async-start | bytes 7839744 | tf_op jit(solution)/shard_map/reduce_scatter | solution.py:14
  77.0 225.4 %copy-start.1 = (f32[16,3696]{1,0:T(8,128)S(1)}, f32[16,3696]{1,0:T(8,128)}, u32[]{:S(2)}) copy-start(f32[16,3696]{1,0:T(8,128)} %param.8) | copy-start | bytes 709636
  77.0 225.4 %copy-start.2 = (f32[16,3696]{1,0:T(8,128)S(1)}, f32[16,3696]{1,0:T(8,128)}, u32[]{:S(2)}) copy-start(f32[16,3696]{1,0:T(8,128)} %param.9) | copy-start | bytes 709636
  327.5 34.1 %copy-start.3 = (bf16[1024,512]{1,0:T(8,128)(2,1)S(1)}, bf16[1024,512]{1,0:T(8,128)(2,1)}, u32[]{:S(2)}) copy-start(bf16[1024,512]{1,0:T(8,128)(2,1)} %param.6) | copy-start | bytes 3145732
Sparse Core Ops, SparseCore 0:
  77.2 225.1 reduce-scatter.1
where the time goes:
time: 372 us; the launch traced here: 371 us
  waiting for transfers between devices  225 us (60%)
  blocking collectives  106 us (28%)
  matrix products  16.1 us (4%)
  between operations  14.1 us (4%)
  local copies, waits for them, and re-layouts  7.29 us (2%)
    reduce_scatter x1, waiting for transfers between devices, shards(): lax.psum_scatter(lax.dot_general(proj, cotangent, (((0,), (0,)), ((), ())...  225 us
    psum x1, blocking collectives, shards(): proj = lax.psum(partial_proj, 'fsdp').astype(jnp.bfloat16)  54.7 us
    all_to_all x1, blocking collectives, shards(): lax.all_to_all(wide_rows, 'dp', split_axis=1, concat_axis=0, tiled=True)  33.5 us
    all_gather x1, blocking collectives, shards(): wide_rows = lax.all_gather(normed, 'fsdp', axis=1, tiled=True)  18.1 us
    dot_general x1, matrix products, shards(): lax.dot_general(proj, cotangent, (((0,), (0,)), ((), ())), preferred_elem...  9.7 us
  transfers between devices with their start and end apart: 1, of which 1 were waited for; matrix products, arithmetic and copies ran while one was open for 0% of the time, Pallas kernels for 0%

commit v1 on v0

v1 whole, which is shorter than its diff:
```python
import numpy as np
import jax
import jax.numpy as jnp
from jax import lax
from jax.experimental import pallas as pl
from jax.experimental.pallas import tpu as pltpu
from jax.sharding import Mesh, PartitionSpec as P

bias_first = 1.0 - 0.9**10
bias_second = 1.0 - 0.999**10
Z, Y, X, C = 8, 4, 4, 2
f32, bf16 = jnp.float32, jnp.bfloat16


def moved(value, axis, by):
    n = {"z": Z, "y": Y, "x": X, "c": C}[axis]
    return lax.ppermute(value, axis, [(i, (i + by) % n) for i in range(n)])


def owner_rows(device, slot, block, lib):
    z, y, _, c = device
    dy, high = ((2, 0), (2, 1), (1, 1), (3, 0), (1, 0), (3, 1), (0, 1), (0, 0))[slot]
    dz = (4, 5, 3, 6, 2, 7, 1, 0)[slot]
    first = c == 0
    owner_z = lax.rem(z + lib.where(first, 4 * high + block, dz), Z)
    owner_y = lax.rem(y + lib.where(first, dy, block), Y)
    return owner_z, owner_y


def grad_kernel(here, mine_ref, other_ref, cot_ref, *rest):
    outs, held = rest[:-1], rest[-1]
    rows = held.shape[0] // (Z * Y)

    @pl.when(pl.program_id(0) == 0)
    def _():
        device = [here[i] for i in range(4)]
        _, _, x, c = device
        for slot in range(8):
            for block in range(4):
                oz, oy = owner_rows(device, slot, block, jnp)
                at = pl.multiple_of(lax.rem(x + X - lax.rem(oz, X), X) * (Y * rows) + oy * rows, rows)
                mine = lax.div(oz, X) == c
                to = (slot * 4 + block) * rows

                @pl.when(mine)
                def _():
                    held[pl.ds(to, rows), :] = mine_ref[pl.ds(at, rows), :]

                @pl.when(jnp.logical_not(mine))
                def _():
                    held[pl.ds(to, rows), :] = other_ref[pl.ds(at, rows), :]

    g = lax.dot_general(held[...], cot_ref[...], (((1,), (1,)), ((), ())), preferred_element_type=f32)
    unit = held.shape[0] // 8
    for slot, out in enumerate(outs):
        out[...] = g[slot * unit : (slot + 1) * unit].astype(out.dtype)


def gradient(mine, other, cotangent, here):
    half, tokens = mine.shape
    ff = cotangent.shape[1]
    unit, tile = half // 4, min(768, ff)
    whole = lambda i: (0, 0)
    return pl.pallas_call(
        grad_kernel,
        grid=(pl.cdiv(ff, tile),),
        in_specs=[
            pl.BlockSpec(memory_space=pltpu.SMEM),
            pl.BlockSpec((half, tokens), whole),
            pl.BlockSpec((half, tokens), whole),
            pl.BlockSpec((tile, tokens), lambda i: (i, 0)),
        ],
        out_specs=[pl.BlockSpec((unit, tile), lambda i: (0, i))] * 8,
        out_shape=[jax.ShapeDtypeStruct((unit, ff), bf16)] * 2 + [jax.ShapeDtypeStruct((unit, ff), f32)] * 6,
        scratch_shapes=[pltpu.VMEM((2 * half, tokens), bf16)],
        compiler_params=pltpu.CompilerParams(vmem_limit_bytes=40 * 2**20),
        cost_estimate=pl.CostEstimate(
            flops=4 * half * tokens * ff, bytes_accessed=2 * tokens * ff + 14 * half * ff // 2, transcendentals=0
        ),
    )(here, mine, other, cotangent.T)


def near_order(rank):
    c, x = lax.axis_index("c"), lax.axis_index("x")
    part = rank // (X * C)
    n = lax.broadcasted_iota(jnp.int32, (rank, rank), 0)
    r = lax.broadcasted_iota(jnp.int32, (rank, rank), 1)
    chunk = ((c + n // (part * X)) % C) * X + (x + (n // part) % X) % X
    return (r == chunk * part + n % part).astype(bf16)


def project(tokens, basis):
    rank = basis.shape[1]
    half, part = rank // C, rank // (X * C)
    lanes = (((1,), (1,)), ((), ()))
    ordered = lax.dot_general(near_order(rank), basis, lanes, preferred_element_type=f32).astype(bf16)
    away = lax.dot_general(ordered[half:], tokens, lanes, preferred_element_type=f32)
    sent = moved(away, "c", 1)
    both = lax.dot_general(ordered[:half], tokens, lanes, preferred_element_type=f32) + sent
    total = both[:part]
    for got in [moved(both[d * part : (d + 1) * part].astype(bf16), "x", d) for d in (1, 3, 2)]:
        total = total + got.astype(f32)
    mine = total.astype(bf16)
    got = {d: moved(mine, "x", d) for d in (1, 3, 2)}
    mine = jnp.concatenate([mine, got[1], got[2], got[3]], 0)
    return mine, moved(mine, "c", 1)


def crossed(value, by_y, by_z):
    pairs = []
    for z in range(Z):
        for y in range(Y):
            for x in range(X):
                at = lambda z, y, c: (((z % Z) * Y + y % Y) * X + x) * C + c
                if by_y is not None:
                    pairs.append((at(z, y, 0), at(z + by_y[1], y + by_y[0], 0)))
                if by_z is not None:
                    pairs.append((at(z, y, 1), at(z + by_z[1], y + by_z[0], 1)))
    return lax.ppermute(value, ("z", "y", "x", "c"), pairs)


def scatter(p1, m1, p2, m2, p3, m3, p4, own):
    first = lax.axis_index("c") == 0
    up, down = ((1, 0), (0, 1)), ((-1, 0), (0, -1))
    r_p1 = crossed(p1, *up)
    r_m1 = crossed(m1, *down)
    r_p2 = crossed((p2 + jnp.where(first, 0.0, r_p1.astype(f32))).astype(bf16), *up)
    r_m2 = crossed((m2 + jnp.where(first, 0.0, r_m1.astype(f32))).astype(bf16), *down)
    r_p3 = crossed((p3 + jnp.where(first, r_p1, r_p2).astype(f32)).astype(bf16), *up)
    r_m3 = crossed((m3 + jnp.where(first, r_m1, r_m2).astype(f32)).astype(bf16), *down)
    r_p4 = crossed((p4 + r_p3.astype(f32)).astype(bf16), None, (0, 1))
    low = own + jnp.where(first, r_p3.astype(f32) + r_m2.astype(f32), r_p4.astype(f32) + r_m3.astype(f32))
    high = p4 + r_p2.astype(f32) + r_m3.astype(f32)
    rows = own.shape[0] // 4
    total = low[:rows]
    low, high = low.astype(bf16), high.astype(bf16)
    got = [crossed(high[k * rows : (k + 1) * rows], (0, 4 + k), None) for k in (0, 1, 3, 2)]
    got += [crossed(low[k * rows : (k + 1) * rows], (0, k), (k, 0)) for k in (3, 2, 1)]
    for one in got:
        total = total + one.astype(f32)
    return total


def spread(normed):
    c, x = lax.axis_index("c"), lax.axis_index("x")
    _, rows, ff = normed.shape
    cut = normed.reshape(C, rows, Y, ff // Y).transpose(0, 2, 1, 3)
    keep = lax.dynamic_index_in_dim(cut, c, 0, keepdims=False)
    give = lax.dynamic_index_in_dim(cut, 1 - c, 0, keepdims=False)
    swap = moved(give, "c", 1)
    pair = jnp.stack([jnp.where(c == 0, keep, swap), jnp.where(c == 0, swap, keep)])
    wide = jnp.zeros((X,) + pair.shape, bf16)
    wide = lax.dynamic_update_index_in_dim(wide, pair, x, 0)
    for d in (1, 3, 2):
        wide = lax.dynamic_update_index_in_dim(wide, moved(pair, "x", d), (x - d) % X, 0)
    wide = wide.reshape(X * C * Y, rows, ff // Y)
    mine = lax.all_to_all(wide, ("z", "y"), 0, 0, tiled=True)
    other = moved(mine, "c", 1)
    return jnp.stack([jnp.where(c == 0, mine, other), jnp.where(c == 0, other, mine)])


def shards(tokens, basis, cotangent, exp_avg, exp_avg_sq):
    rank, ff = basis.shape[1], cotangent.shape[1]
    rows = rank // (2 * Z * Y)
    here = jnp.stack([lax.axis_index(axis) for axis in ("z", "y", "x", "c")]).astype(jnp.int32)
    mine, other = project(tokens, basis)
    total = scatter(*gradient(mine, other, cotangent, here))
    total_tokens = cotangent.shape[0] * Z * Y
    grad_low = total * (1.0 / total_tokens)
    first = 0.9 * exp_avg + 0.1 * grad_low
    second = 0.999 * exp_avg_sq + 0.001 * grad_low * grad_low
    normed = (first / bias_first / (jnp.sqrt(second / bias_second) + 1e-08)).astype(bf16)
    all_rows = spread(normed.reshape(2, rows, ff)).reshape(rank, ff // Y)
    by_half = basis.reshape(-1, Z * Y, 2, rows).transpose(0, 2, 1, 3).reshape(-1, rank)
    update = jnp.dot(by_half, all_rows, preferred_element_type=f32).astype(bf16)
    return (update, first, second)


def solution(mesh):
    fine = Mesh(np.asarray(mesh.devices).reshape(Z, Y, X, C), ("z", "y", "x", "c"))
    dp, fsdp = ("z", "y"), ("x", "c")
    in_specs = (P(dp, fsdp), P(fsdp, None), P(dp, fsdp), P(dp, fsdp), P(dp, fsdp))
    out_specs = (P(fsdp, dp), P(dp, fsdp), P(dp, fsdp))
    return jax.shard_map(shards, mesh=fine, in_specs=in_specs, out_specs=out_specs, check_vma=False)
```

time: 372 us -> 165 us (0.44)
  waiting for transfers between devices: 225 us -> 48.9 us
  blocking collectives: 106 us -> 22.8 us
  starting transfers between devices: 0.04 us -> 55.1 us
  between operations: 14.1 us -> 0.95 us
  Pallas kernels: 0 us -> 9.64 us
  matrix products: 16.1 us -> 7.19 us
  local copies, waits for them, and re-layouts: 7.29 us -> 14.5 us
  other arithmetic: 1.86 us -> 5.64 us
    reduce_scatter x1 -> x0, waiting for transfers between devices: 225 us -> none  [shards(): lax.psum_scatter(lax.dot_general(proj, cotangent, (((0,), (0,)), ((), ())...]
    ppermute x0 -> x27, starting transfers between devices: none -> 55.1 us  [the longest x13 35.8 us: moved(): return lax.ppermute(value, axis, [(i, (i + by) % n) for i in range(n)])]
    psum x1 -> x0, blocking collectives: 54.7 us -> none  [shards(): proj = lax.psum(partial_proj, 'fsdp').astype(jnp.bfloat16)]
    ppermute x0 -> x27, waiting for transfers between devices: none -> 48.9 us  [the longest x14 28.7 us: crossed(): return lax.ppermute(value, ('z', 'y', 'x', 'c'), pairs)]
    all_gather x1 -> x0, blocking collectives: 18.1 us -> none  [shards(): wide_rows = lax.all_gather(normed, 'fsdp', axis=1, tiled=True)]
    all_to_all x1, blocking collectives: 33.5 us -> 22.8 us  [spread(): mine = lax.all_to_all(wide, ('z', 'y'), 0, 0, tiled=True)]
    pallas_call x0 -> x1, Pallas kernels: none -> 9.64 us  [gradient(): pl.pallas_call(grad_kernel, grid=(pl.cdiv(ff, tile),), in_specs=[pl.Block...]
    dot_general x3 -> x4, matrix products: 16.1 us -> 7.19 us  [the longest x1 3.02 us: project(): lax.dot_general(near_order(rank), basis, lanes, preferred_element_type=f32)]
  transfers between devices with their start and end apart: 1 -> 27, of which waited for: 1 -> 18; matrix products, arithmetic and copies ran while one was open for 0% -> 4% of each run, Pallas kernels for 0% -> 0%
where the time goes in v1:
time: 165 us
  starting transfers between devices  55.1 us (33%)
  waiting for transfers between devices  48.9 us (30%)
  blocking collectives  22.8 us (14%)
  local copies, waits for them, and re-layouts  14.5 us (9%)
  Pallas kernels  9.64 us (6%)
  matrix products  7.19 us (4%)
  other arithmetic  5.64 us (3%)
    ppermute x13, starting transfers between devices, moved(): return lax.ppermute(value, axis, [(i, (i + by) % n) for i in range(n)])  35.8 us
    ppermute x14, waiting for transfers between devices, crossed(): return lax.ppermute(value, ('z', 'y', 'x', 'c'), pairs)  28.7 us
    all_to_all x1, blocking collectives, spread(): mine = lax.all_to_all(wide, ('z', 'y'), 0, 0, tiled=True)  22.8 us
    ppermute x13, waiting for transfers between devices, moved(): return lax.ppermute(value, axis, [(i, (i + by) % n) for i in range(n)])  20.2 us
    ppermute x14, starting transfers between devices, crossed(): return lax.ppermute(value, ('z', 'y', 'x', 'c'), pairs)  19.3 us
    unnamed x35, local copies, waits for them, and re-layouts  11.4 us
    pallas_call x1, Pallas kernels, gradient(): pl.pallas_call(grad_kernel, grid=(pl.cdiv(ff, tile),), in_specs=[pl.Block...  9.64 us
  transfers between devices with their start and end apart: 27, of which 18 were waited for; matrix products, arithmetic and copies ran while one was open for 4% of the time, Pallas kernels for 0%

profile of v1, /device:TPU:1, one launch (start us, length us, event | category | flops | bytes accessed | tf_op | source)
XLA Modules:
  0.0 164.7 jit_solution(63700489525023485)
XLA Ops:
  0.7 3.0 %convolution_convert_fusion = bf16[512,1024]{1,0:T(8,128)(2,1)S(1)} fusion(bf16[1024,512]{1,0:T(8,128)(2,1)} %param.6, s32[512]{0:T(512)S(1)} %get-tuple-element.48, s32[512]{0:T(512)S(1)} %get-tuple-element.49, s32[512]{0:T(512)S(1)} %get-tuple-element.47, s32[512]{0:T(512)S(1)} %get-tuple-element.50, s32[]{:T(128)} %axis_index.35, ...), kind=kOutput, calls=%fused_computation.13 | convolution fusion | flops 548667392 | bytes 2110984 | tf_op jit(solution)/shard_map/dot_general | solution.py:96
  4.5 3.3 %collective-permute-start = (f32[256,1024]{1,0:T(8,128)S(1)}, f32[256,1024]{1,0:T(8,128)S(1)}, u32[]{:S(2)}, u32[]{:S(2)}) collective-permute-start(f32[256,1024]{1,0:T(8,128)S(1)} %fusion.28), channel_id=1, source_target_pairs={{0,1},{1,0},{2,3},{3,2},{4,5},{5,4},{6,7},{7,6},{8,9},{9,8},{10,11... | collective-permute-start | bytes 3145736 | tf_op jit(solution)/shard_map/ppermute | solution.py:17
  7.8 2.3 %collective-permute-done = f32[256,1024]{1,0:T(8,128)S(1)} collective-permute-done((f32[256,1024]{1,0:T(8,128)S(1)}, f32[256,1024]{1,0:T(8,128)S(1)}, u32[]{:S(2)}, u32[]{:S(2)}) %collective-permute-start) | collective-permute-done | bytes 1048608 | tf_op jit(solution)/shard_map/ppermute | solution.py:17
  11.0 2.7 %collective-permute-start.2 = (bf16[64,1024]{1,0:T(8,128)(2,1)S(1)}, bf16[64,1024]{1,0:T(8,128)(2,1)S(1)}, u32[]{:S(2)}, u32[]{:S(2)}) collective-permute-start(bf16[64,1024]{1,0:T(8,128)(2,1)S(1)} %get-tuple-element.30), channel_id=1, source_target_pairs={{0,6},{2,0},{4,2},{6,4},{1,7},{3,1},{5,3},{7,5},{8,14},{10,8},{12,... | collective-permute-start | bytes 393224 | tf_op jit(solution)/shard_map/ppermute | solution.py:17
  13.7 3.2 %collective-permute-done.1 = bf16[64,1024]{1,0:T(8,128)(2,1)S(1)} collective-permute-done((bf16[64,1024]{1,0:T(8,128)(2,1)S(1)}, bf16[64,1024]{1,0:T(8,128)(2,1)S(1)}, u32[]{:S(2)}, u32[]{:S(2)}) %collective-permute-start.1) | collective-permute-done | bytes 131104 | tf_op jit(solution)/shard_map/ppermute | solution.py:17
  16.9 1.9 %collective-permute-done.2 = bf16[64,1024]{1,0:T(8,128)(2,1)S(1)} collective-permute-done((bf16[64,1024]{1,0:T(8,128)(2,1)S(1)}, bf16[64,1024]{1,0:T(8,128)(2,1)S(1)}, u32[]{:S(2)}, u32[]{:S(2)}) %collective-permute-start.2) | collective-permute-done | bytes 131104 | tf_op jit(solution)/shard_map/ppermute | solution.py:17
  19.1 1.4 collective-permute-start.4
  20.5 3.2 %collective-permute-start.5 = (bf16[64,1024]{1,0:T(8,128)(2,1)S(1)}, bf16[64,1024]{1,0:T(8,128)(2,1)S(1)}, u32[]{:S(2)}, u32[]{:S(2)}) collective-permute-start(bf16[64,1024]{1,0:T(8,128)(2,1)S(1)} %fusion.50), channel_id=1, source_target_pairs={{0,4},{2,6},{4,0},{6,2},{1,5},{3,7},{5,1},{7,3},{8,12},{10,14},{12... | collective-permute-start | bytes 393224 | tf_op jit(solution)/shard_map/ppermute | solution.py:17
  23.7 1.2 collective-permute-done.4
  24.9 3.6 %collective-permute-done.5 = bf16[64,1024]{1,0:T(8,128)(2,1)S(1)} collective-permute-done((bf16[64,1024]{1,0:T(8,128)(2,1)S(1)}, bf16[64,1024]{1,0:T(8,128)(2,1)S(1)}, u32[]{:S(2)}, u32[]{:S(2)}) %collective-permute-start.5) | collective-permute-done | bytes 131104 | tf_op jit(solution)/shard_map/ppermute | solution.py:17
  28.8 2.3 %collective-permute-start.7 = (bf16[256,1024]{1,0:T(8,128)(2,1)S(1)}, bf16[256,1024]{1,0:T(8,128)(2,1)S(1)}, u32[]{:S(2)}, u32[]{:S(2)}) collective-permute-start(bf16[256,1024]{1,0:T(8,128)(2,1)S(1)} %pad_maximum_fusion.mine_ref), channel_id=1, source_target_pairs={{0,1},{1,0},{2,3},{3,2},{4,5},{5,4},{6,7},{7,6},{8,9},{9,8},{10,11... | collective-permute-start | bytes 1572872 | tf_op jit(solution)/shard_map/ppermute | solution.py:17
  31.1 0.8 copy-done.10
  32.7 0.8 copy-done.12
  33.5 1.0 copy-done.11
  34.5 1.0 copy-done.13
  35.5 9.6 %shard_map.76 = (bf16[64,3696]{1,0:T(8,128)(2,1)}, bf16[64,3696]{1,0:T(8,128)(2,1)S(1)}, f32[64,3696]{1,0:T(8,128)S(1)}, f32[64,3696]{1,0:T(8,128)S(1)}, f32[64,...) custom-call(s32[4]{0:T(128)S(1)} %pad_add_fusion.here, ...), custom_call_target="tpu_custom_call" | custom-call | flops 3875536896 | bytes 14192640 | tf_op jit(solution)/shard_map/pallas_call | solution.py:64
  45.2 1.0 copy-done.1
  46.2 0.9 copy-done.3
  47.1 0.9 copy-done.5
  48.1 1.0 copy-done.7
  49.0 0.9 copy-done.8
  50.2 3.9 %collective-permute-start.11 = (bf16[64,3696]{1,0:T(8,128)(2,1)S(1)}, bf16[64,3696]{1,0:T(8,128)(2,1)S(1)}, u32[]{:S(2)}, u32[]{:S(2)}) collective-permute-start(bf16[64,3696]{1,0:T(8,128)(2,1)S(1)} %get-tuple-element.16), channel_id=1, source_target_pairs={{0,24},{1,225},{2,26},{3,227},{4,28},{5,229},{6,30},{7,231},{8,0},... | collective-permute-start | bytes 1419272 | tf_op jit(solution)/shard_map/ppermute | solution.py:119
  54.1 6.3 %collective-permute-done.8 = bf16[64,3696]{1,0:T(8,128)(2,1)} collective-permute-done((bf16[64,3696]{1,0:T(8,128)(2,1)}, bf16[64,3696]{1,0:T(8,128)(2,1)}, u32[]{:S(2)}, u32[]{:S(2)}) %collective-permute-start.8) | collective-permute-done | bytes 473120 | tf_op jit(solution)/shard_map/ppermute | solution.py:119
  60.5 1.4 add_convert_fusion.3
  62.3 2.7 %collective-permute-start.12 = (bf16[64,3696]{1,0:T(8,128)(2,1)S(1)}, bf16[64,3696]{1,0:T(8,128)(2,1)S(1)}, u32[]{:S(2)}, u32[]{:S(2)}) collective-permute-start(bf16[64,3696]{1,0:T(8,128)(2,1)S(1)} %add_convert_fusion.1), channel_id=1, source_target_pairs={{0,24},{1,225},{2,26},{3,227},{4,28},{5,229},{6,30},{7,231},{8,0},... | collective-permute-start | bytes 1419272 | tf_op jit(solution)/shard_map/ppermute | solution.py:119
  65.1 6.1 %collective-permute-done.9 = bf16[64,3696]{1,0:T(8,128)(2,1)S(1)} collective-permute-done((bf16[64,3696]{1,0:T(8,128)(2,1)S(1)}, bf16[64,3696]{1,0:T(8,128)(2,1)S(1)}, u32[]{:S(2)}, u32[]{:S(2)}) %collective-permute-start.9) | collective-permute-done | bytes 473120 | tf_op jit(solution)/shard_map/ppermute | solution.py:119
  71.6 2.7 %collective-permute-start.14 = (bf16[64,3696]{1,0:T(8,128)(2,1)S(1)}, bf16[64,3696]{1,0:T(8,128)(2,1)S(1)}, u32[]{:S(2)}, u32[]{:S(2)}) collective-permute-start(bf16[64,3696]{1,0:T(8,128)(2,1)S(1)} %add_convert_fusion), channel_id=1, source_target_pairs={{0,24},{1,225},{2,26},{3,227},{4,28},{5,229},{6,30},{7,231},{8,0},... | collective-permute-start | bytes 1419272 | tf_op jit(solution)/shard_map/ppermute | solution.py:119
  74.4 6.1 %collective-permute-done.10 = bf16[64,3696]{1,0:T(8,128)(2,1)S(1)} collective-permute-done((bf16[64,3696]{1,0:T(8,128)(2,1)S(1)}, bf16[64,3696]{1,0:T(8,128)(2,1)S(1)}, u32[]{:S(2)}, u32[]{:S(2)}) %collective-permute-start.10) | collective-permute-done | bytes 473120 | tf_op jit(solution)/shard_map/ppermute | solution.py:119
  80.7 2.1 %collective-permute-start.13 = (bf16[64,3696]{1,0:T(8,128)(2,1)S(1)}, bf16[64,3696]{1,0:T(8,128)(2,1)S(1)}, u32[]{:S(2)}, u32[]{:S(2)}) collective-permute-start(bf16[64,3696]{1,0:T(8,128)(2,1)S(1)} %get-tuple-element.27), channel_id=1, source_target_pairs={{1,33},{3,35},{5,37},{7,39},{9,41},{11,43},{13,45},{15,47},{17,49}... | collective-permute-start | bytes 1419272 | tf_op jit(solution)/shard_map/ppermute | solution.py:119
  84.2 1.3 collective-permute-start.16
  86.2 1.3 collective-permute-start.18
  87.5 4.2 %collective-permute-done.13 = bf16[64,3696]{1,0:T(8,128)(2,1)S(1)} collective-permute-done((bf16[64,3696]{1,0:T(8,128)(2,1)S(1)}, bf16[64,3696]{1,0:T(8,128)(2,1)S(1)}, u32[]{:S(2)}, u32[]{:S(2)}) %collective-permute-start.13) | collective-permute-done | bytes 473120 | tf_op jit(solution)/shard_map/ppermute | solution.py:119
  92.7 2.7 %collective-permute-start.19 = (bf16[16,3696]{1,0:T(8,128)(2,1)}, bf16[16,3696]{1,0:T(8,128)(2,1)}, u32[]{:S(2)}, u32[]{:S(2)}) collective-permute-start(bf16[16,3696]{1,0:T(8,128)(2,1)} %get-tuple-element.35), channel_id=1, source_target_pairs={{0,96},{1,25},{2,98},{3,27},{4,100},{5,29},{6,102},{7,31},{8,104},... | collective-permute-start | bytes 354824 | tf_op jit(solution)/shard_map/ppermute | solution.py:119
  96.1 2.8 %collective-permute-done.19 = bf16[16,3696]{1,0:T(8,128)(2,1)} collective-permute-done((bf16[16,3696]{1,0:T(8,128)(2,1)}, bf16[16,3696]{1,0:T(8,128)(2,1)}, u32[]{:S(2)}, u32[]{:S(2)}) %collective-permute-start.19) | collective-permute-done | bytes 118304 | tf_op jit(solution)/shard_map/ppermute | solution.py:119
  98.8 2.2 %collective-permute-done.20 = bf16[16,3696]{1,0:T(8,128)(2,1)} collective-permute-done((bf16[16,3696]{1,0:T(8,128)(2,1)}, bf16[16,3696]{1,0:T(8,128)(2,1)}, u32[]{:S(2)}, u32[]{:S(2)}) %collective-permute-start.20) | collective-permute-done | bytes 118304 | tf_op jit(solution)/shard_map/ppermute | solution.py:119
  101.1 1.0 collective-permute-done.21
  102.0 2.3 %divide_convert_fusion = (bf16[16,3696]{1,0:T(8,128)(2,1)S(1)}, f32[16,3696]{1,0:T(8,128)}, f32[16,3696]{1,0:T(8,128)}) fusion(f32[16,3696]{1,0:T(8,128)S(1)} %copy-done.15, f32[16,3696]{1,0:T(8,128)} %param.9, bf16[16,3696]{1,0:T(8,128)(2,1)} %collective-permute-done.21, bf16[16,3696]{1,0:T(8,128)(2,1)} %collective-permute-done.20, ...), kind=kLoop, calls=%fused_computation.83 | loop fusion | flops 1596672 | bytes 2128896 | tf_op jit(solution)/shard_map/convert_element_type | solution.py:172
  104.6 15.7 %collective-permute-start.22 = (bf16[4,8,924]{2,0,1:T(4,128)(2,1)S(1)}, bf16[4,8,924]{2,0,1:T(4,128)(2,1)S(1)}, u32[]{:S(2)}, u32[]{:S(2)}) collective-permute-start(bf16[4,8,924]{2,0,1:T(4,128)(2,1)S(1)} %dynamic-slice_bitcast_fusion), channel_id=1, source_target_pairs={{0,1},{1,0},{2,3},{3,2},{4,5},{5,4},{6,7},{7,6},{8,9},{9,8},{10,11... | collective-permute-start | bytes 177416 | tf_op jit(solution)/shard_map/ppermute | solution.py:17
  120.3 0.9 collective-permute-done.22
  121.9 2.3 %collective-permute-start.24 = (bf16[2,4,8,924]{3,1,2,0:T(4,128)(2,1)S(1)}, bf16[2,4,8,924]{3,1,2,0:T(4,128)(2,1)S(1)}, u32[]{:S(2)}, u32[]{:S(2)}) collective-permute-start(bf16[2,4,8,924]{3,1,2,0:T(4,128)(2,1)S(1)} %get-tuple-element.40), channel_id=1, source_target_pairs={{0,6},{2,0},{4,2},{6,4},{1,7},{3,1},{5,3},{7,5},{8,14},{10,8},{12,... | collective-permute-start | bytes 354824 | tf_op jit(solution)/shard_map/ppermute | solution.py:17
  124.2 0.9 collective-permute-start.25
  125.2 2.2 %collective-permute-done.23 = bf16[2,4,8,924]{3,1,2,0:T(4,128)(2,1)S(1)} collective-permute-done((bf16[2,4,8,924]{3,1,2,0:T(4,128)(2,1)S(1)}, bf16[2,4,8,924]{3,1,2,0:T(4,128)(2,1)S(1)}, u32[]{:S(2)}, u32[]{:S(2)}) %collective-permute-start.23) | collective-permute-done | bytes 118304 | tf_op jit(solution)/shard_map/ppermute | solution.py:17
  127.5 3.7 %collective-permute-done.25 = bf16[2,4,8,924]{3,1,2,0:T(4,128)(2,1)S(1)} collective-permute-done((bf16[2,4,8,924]{3,1,2,0:T(4,128)(2,1)S(1)}, bf16[2,4,8,924]{3,1,2,0:T(4,128)(2,1)S(1)}, u32[]{:S(2)}, u32[]{:S(2)}) %collective-permute-start.25) | collective-permute-done | bytes 118304 | tf_op jit(solution)/shard_map/ppermute | solution.py:17
  131.3 22.8 %all_to_all.5 = bf16[32,8,924]{2,1,0:T(8,128)(2,1)S(1)} all-to-all(bf16[32,8,924]{2,1,0:T(8,128)(2,1)S(1)} %bitcast.46), channel_id=1, replica_groups=mesh['z'=8,'y'=4,'x'=4,'c'=2] {'z','y'}, dimensions={0} | all-to-all | bytes 946176 | tf_op jit(solution)/shard_map/all_to_all | solution.py:157
  154.1 1.1 copy.24
  155.2 3.4 %collective-permute-start.26 = (bf16[32,8,924]{2,0,1:T(8,128)(2,1)}, bf16[32,8,924]{2,0,1:T(8,128)(2,1)S(1)}, u32[]{:S(2)}, u32[]{:S(2)}) collective-permute-start(bf16[32,8,924]{2,0,1:T(8,128)(2,1)} %copy.24), channel_id=1, source_target_pairs={{0,1},{1,0},{2,3},{3,2},{4,5},{5,4},{6,7},{7,6},{8,9},{9,8},{10,11... | collective-permute-start | bytes 1419272 | tf_op jit(solution)/shard_map/ppermute | solution.py:17
  158.6 2.3 %copy.26 = bf16[1024,512]{0,1:T(8,128)(2,1)} copy(bf16[1024,512]{1,0:T(8,128)(2,1)} %param.6) | data formatting | bytes 2097152 | tf_op args[1]
  162.1 2.7 %fusion = bf16[1024,924]{0,1:T(8,128)(2,1)} fusion(bf16[1,32,8,924]{3,1,2,0:T(8,128)(2,1)S(1)} %get-tuple-element.25, bf16[1,32,8,924]{3,1,2,0:T(8,128)(2,1)S(1)} %get-tuple-element.24, bf16[1024,2,32,8]{0,3,1,2:T(8,128)(2,1)S(1)} %bitcast.47), kind=kOutput, calls=%fused_computation.4 | convolution fusion | flops 970303488 | bytes 3887104 | tf_op jit(solution)/shard_map/dot_general | solution.py:175
  (76 shorter events, 10.4 us)
Async XLA Ops:
  0.6 3.1 %copy-start = (bf16[1024,1024]{1,0:T(8,128)(2,1)S(1)}, bf16[1024,1024]{1,0:T(8,128)(2,1)}, u32[]{:S(2)}) copy-start(bf16[1024,1024]{1,0:T(8,128)(2,1)} %param.5) | copy-start | bytes 6291460
  4.5 5.6 %collective-permute-start = (f32[256,1024]{1,0:T(8,128)S(1)}, f32[256,1024]{1,0:T(8,128)S(1)}, u32[]{:S(2)}, u32[]{:S(2)}) collective-permute-start(f32[256,1024]{1,0:T(8,128)S(1)} %fusion.28), channel_id=1, source_target_pairs={{0,1},{1,0},{2,3},{3,2},{4,5},{5,4},{6,7},{7,6},{8,9},{9,8},{10,11... | collective-permute-start | bytes 3145736 | tf_op jit(solution)/shard_map/ppermute | solution.py:17
  10.9 6.0 %collective-permute-start.1 = (bf16[64,1024]{1,0:T(8,128)(2,1)S(1)}, bf16[64,1024]{1,0:T(8,128)(2,1)S(1)}, u32[]{:S(2)}, u32[]{:S(2)}) collective-permute-start(bf16[64,1024]{1,0:T(8,128)(2,1)S(1)} %get-tuple-element.28), channel_id=1, source_target_pairs={{0,2},{2,4},{4,6},{6,0},{1,3},{3,5},{5,7},{7,1},{8,10},{10,12},{12... | collective-permute-start | bytes 393224 | tf_op jit(solution)/shard_map/ppermute | solution.py:17
  11.0 7.8 %collective-permute-start.2 = (bf16[64,1024]{1,0:T(8,128)(2,1)S(1)}, bf16[64,1024]{1,0:T(8,128)(2,1)S(1)}, u32[]{:S(2)}, u32[]{:S(2)}) collective-permute-start(bf16[64,1024]{1,0:T(8,128)(2,1)S(1)} %get-tuple-element.30), channel_id=1, source_target_pairs={{0,6},{2,0},{4,2},{6,4},{1,7},{3,1},{5,3},{7,5},{8,14},{10,8},{12,... | collective-permute-start | bytes 393224 | tf_op jit(solution)/shard_map/ppermute | solution.py:17
  13.7 5.3 %collective-permute-start.3 = (bf16[64,1024]{1,0:T(8,128)(2,1)S(1)}, bf16[64,1024]{1,0:T(8,128)(2,1)S(1)}, u32[]{:S(2)}, u32[]{:S(2)}) collective-permute-start(bf16[64,1024]{1,0:T(8,128)(2,1)S(1)} %get-tuple-element.29), channel_id=1, source_target_pairs={{0,4},{2,6},{4,0},{6,2},{1,5},{3,7},{5,1},{7,3},{8,12},{10,14},{12... | collective-permute-start | bytes 393224 | tf_op jit(solution)/shard_map/ppermute | solution.py:17
  19.1 5.8 %collective-permute-start.4 = (bf16[64,1024]{1,0:T(8,128)(2,1)S(1)}, bf16[64,1024]{1,0:T(8,128)(2,1)S(1)}, u32[]{:S(2)}, u32[]{:S(2)}) collective-permute-start(bf16[64,1024]{1,0:T(8,128)(2,1)S(1)} %fusion.50), channel_id=1, source_target_pairs={{0,2},{2,4},{4,6},{6,0},{1,3},{3,5},{5,7},{7,1},{8,10},{10,12},{12... | collective-permute-start | bytes 393224 | tf_op jit(solution)/shard_map/ppermute | solution.py:17
  20.5 8.0 %collective-permute-start.5 = (bf16[64,1024]{1,0:T(8,128)(2,1)S(1)}, bf16[64,1024]{1,0:T(8,128)(2,1)S(1)}, u32[]{:S(2)}, u32[]{:S(2)}) collective-permute-start(bf16[64,1024]{1,0:T(8,128)(2,1)S(1)} %fusion.50), channel_id=1, source_target_pairs={{0,4},{2,6},{4,0},{6,2},{1,5},{3,7},{5,1},{7,3},{8,12},{10,14},{12... | collective-permute-start | bytes 393224 | tf_op jit(solution)/shard_map/ppermute | solution.py:17
  23.7 5.1 %collective-permute-start.6 = (bf16[64,1024]{1,0:T(8,128)(2,1)S(1)}, bf16[64,1024]{1,0:T(8,128)(2,1)S(1)}, u32[]{:S(2)}, u32[]{:S(2)}) collective-permute-start(bf16[64,1024]{1,0:T(8,128)(2,1)S(1)} %fusion.50), channel_id=1, source_target_pairs={{0,6},{2,0},{4,2},{6,4},{1,7},{3,1},{5,3},{7,5},{8,14},{10,8},{12,... | collective-permute-start | bytes 393224 | tf_op jit(solution)/shard_map/ppermute | solution.py:17
  28.8 3.8 %collective-permute-start.7 = (bf16[256,1024]{1,0:T(8,128)(2,1)S(1)}, bf16[256,1024]{1,0:T(8,128)(2,1)S(1)}, u32[]{:S(2)}, u32[]{:S(2)}) collective-permute-start(bf16[256,1024]{1,0:T(8,128)(2,1)S(1)} %pad_maximum_fusion.mine_ref), channel_id=1, source_target_pairs={{0,1},{1,0},{2,3},{3,2},{4,5},{5,4},{6,7},{7,6},{8,9},{9,8},{10,11... | collective-permute-start | bytes 1572872 | tf_op jit(solution)/shard_map/ppermute | solution.py:17
  31.1 0.8 copy-start.10
  32.7 0.8 copy-start.12
  33.5 1.0 copy-start.11
  34.5 1.0 copy-start.13
  45.2 1.0 copy-start.1
  46.2 0.9 copy-start.3
  47.1 0.9 copy-start.5
  48.1 1.0 copy-start.7
  49.0 0.9 copy-start.8
  49.9 10.6 %collective-permute-start.8 = (bf16[64,3696]{1,0:T(8,128)(2,1)}, bf16[64,3696]{1,0:T(8,128)(2,1)}, u32[]{:S(2)}, u32[]{:S(2)}) collective-permute-start(bf16[64,3696]{1,0:T(8,128)(2,1)} %get-tuple-element.13), channel_id=1, source_target_pairs={{0,8},{1,33},{2,10},{3,35},{4,12},{5,37},{6,14},{7,39},{8,16},{9,4... | collective-permute-start | bytes 1419272 | tf_op jit(solution)/shard_map/ppermute | solution.py:119
  50.2 12.0 %copy-start.6 = (f32[64,3696]{1,0:T(8,128)S(1)}, f32[64,3696]{1,0:T(8,128)}, u32[]{:S(2)}) copy-start(f32[64,3696]{1,0:T(8,128)} %copy-done.5) | copy-start | bytes 2838532
  50.2 21.0 %copy-start.4 = (f32[64,3696]{1,0:T(8,128)S(1)}, f32[64,3696]{1,0:T(8,128)}, u32[]{:S(2)}) copy-start(f32[64,3696]{1,0:T(8,128)} %copy-done.3) | copy-start | bytes 2838532
  50.2 12.0 %collective-permute-start.11 = (bf16[64,3696]{1,0:T(8,128)(2,1)S(1)}, bf16[64,3696]{1,0:T(8,128)(2,1)S(1)}, u32[]{:S(2)}, u32[]{:S(2)}) collective-permute-start(bf16[64,3696]{1,0:T(8,128)(2,1)S(1)} %get-tuple-element.16), channel_id=1, source_target_pairs={{0,24},{1,225},{2,26},{3,227},{4,28},{5,229},{6,30},{7,231},{8,0},... | collective-permute-start | bytes 1419272 | tf_op jit(solution)/shard_map/ppermute | solution.py:119
  61.9 9.3 %collective-permute-start.9 = (bf16[64,3696]{1,0:T(8,128)(2,1)S(1)}, bf16[64,3696]{1,0:T(8,128)(2,1)S(1)}, u32[]{:S(2)}, u32[]{:S(2)}) collective-permute-start(bf16[64,3696]{1,0:T(8,128)(2,1)S(1)} %add_convert_fusion.3), channel_id=1, source_target_pairs={{0,8},{1,33},{2,10},{3,35},{4,12},{5,37},{6,14},{7,39},{8,16},{9,4... | collective-permute-start | bytes 1419272 | tf_op jit(solution)/shard_map/ppermute | solution.py:119
  62.2 9.3 %copy-start.2 = (f32[64,3696]{1,0:T(8,128)S(1)}, f32[64,3696]{1,0:T(8,128)}, u32[]{:S(2)}) copy-start(f32[64,3696]{1,0:T(8,128)} %copy-done.1) | copy-start | bytes 2838532
  62.3 9.1 %collective-permute-start.12 = (bf16[64,3696]{1,0:T(8,128)(2,1)S(1)}, bf16[64,3696]{1,0:T(8,128)(2,1)S(1)}, u32[]{:S(2)}, u32[]{:S(2)}) collective-permute-start(bf16[64,3696]{1,0:T(8,128)(2,1)S(1)} %add_convert_fusion.1), channel_id=1, source_target_pairs={{0,24},{1,225},{2,26},{3,227},{4,28},{5,229},{6,30},{7,231},{8,0},... | collective-permute-start | bytes 1419272 | tf_op jit(solution)/shard_map/ppermute | solution.py:119
  71.4 9.1 %collective-permute-start.10 = (bf16[64,3696]{1,0:T(8,128)(2,1)S(1)}, bf16[64,3696]{1,0:T(8,128)(2,1)S(1)}, u32[]{:S(2)}, u32[]{:S(2)}) collective-permute-start(bf16[64,3696]{1,0:T(8,128)(2,1)S(1)} %add_convert_fusion.2), channel_id=1, source_target_pairs={{0,8},{1,33},{2,10},{3,35},{4,12},{5,37},{6,14},{7,39},{8,16},{9,4... | collective-permute-start | bytes 1419272 | tf_op jit(solution)/shard_map/ppermute | solution.py:119
  71.6 8.8 %collective-permute-start.14 = (bf16[64,3696]{1,0:T(8,128)(2,1)S(1)}, bf16[64,3696]{1,0:T(8,128)(2,1)S(1)}, u32[]{:S(2)}, u32[]{:S(2)}) collective-permute-start(bf16[64,3696]{1,0:T(8,128)(2,1)S(1)} %add_convert_fusion), channel_id=1, source_target_pairs={{0,24},{1,225},{2,26},{3,227},{4,28},{5,229},{6,30},{7,231},{8,0},... | collective-permute-start | bytes 1419272 | tf_op jit(solution)/shard_map/ppermute | solution.py:119
  80.5 11.2 %copy-start.9 = (f32[64,3696]{1,0:T(8,128)S(1)}, f32[64,3696]{1,0:T(8,128)}, u32[]{:S(2)}) copy-start(f32[64,3696]{1,0:T(8,128)} %copy-done.8) | copy-start | bytes 2838532
  80.7 11.0 %collective-permute-start.13 = (bf16[64,3696]{1,0:T(8,128)(2,1)S(1)}, bf16[64,3696]{1,0:T(8,128)(2,1)S(1)}, u32[]{:S(2)}, u32[]{:S(2)}) collective-permute-start(bf16[64,3696]{1,0:T(8,128)(2,1)S(1)} %get-tuple-element.27), channel_id=1, source_target_pairs={{1,33},{3,35},{5,37},{7,39},{9,41},{11,43},{13,45},{15,47},{17,49}... | collective-permute-start | bytes 1419272 | tf_op jit(solution)/shard_map/ppermute | solution.py:119
  83.5 11.9 %collective-permute-start.15 = (bf16[16,3696]{1,0:T(8,128)(2,1)S(1)}, bf16[16,3696]{1,0:T(8,128)(2,1)S(1)}, u32[]{:S(2)}, u32[]{:S(2)}) collective-permute-start(bf16[16,3696]{1,0:T(8,128)(2,1)S(1)} %get-tuple-element.31), channel_id=1, source_target_pairs={{0,128},{2,130},{4,132},{6,134},{8,136},{10,138},{12,140},{14,142}... | collective-permute-start | bytes 354824 | tf_op jit(solution)/shard_map/ppermute | solution.py:119
  84.2 11.3 %collective-permute-start.16 = (bf16[16,3696]{1,0:T(8,128)(2,1)S(1)}, bf16[16,3696]{1,0:T(8,128)(2,1)}, u32[]{:S(2)}, u32[]{:S(2)}) collective-permute-start(bf16[16,3696]{1,0:T(8,128)(2,1)S(1)} %get-tuple-element.34), channel_id=1, source_target_pairs={{0,160},{2,162},{4,164},{6,166},{8,168},{10,170},{12,172},{14,174}... | collective-permute-start | bytes 354824 | tf_op jit(solution)/shard_map/ppermute | solution.py:119
  85.5 10.6 %collective-permute-start.17 = (bf16[16,3696]{1,0:T(8,128)(2,1)}, bf16[16,3696]{1,0:T(8,128)(2,1)S(1)}, u32[]{:S(2)}, u32[]{:S(2)}) collective-permute-start(bf16[16,3696]{1,0:T(8,128)(2,1)} %get-tuple-element.33), channel_id=1, source_target_pairs={{0,224},{2,226},{4,228},{6,230},{8,232},{10,234},{12,236},{14,238}... | collective-permute-start | bytes 354824 | tf_op jit(solution)/shard_map/ppermute | solution.py:119
  86.2 9.9 %collective-permute-start.18 = (bf16[16,3696]{1,0:T(8,128)(2,1)}, bf16[16,3696]{1,0:T(8,128)(2,1)}, u32[]{:S(2)}, u32[]{:S(2)}) collective-permute-start(bf16[16,3696]{1,0:T(8,128)(2,1)} %get-tuple-element.32), channel_id=1, source_target_pairs={{0,192},{2,194},{4,196},{6,198},{8,200},{10,202},{12,204},{14,206}... | collective-permute-start | bytes 354824 | tf_op jit(solution)/shard_map/ppermute | solution.py:119
  91.7 10.3 %copy-start.15 = (f32[16,3696]{1,0:T(8,128)S(1)}, f32[16,3696]{1,0:T(8,128)}, u32[]{:S(2)}) copy-start(f32[16,3696]{1,0:T(8,128)} %param.8) | copy-start | bytes 709636
  92.7 6.1 %collective-permute-start.19 = (bf16[16,3696]{1,0:T(8,128)(2,1)}, bf16[16,3696]{1,0:T(8,128)(2,1)}, u32[]{:S(2)}, u32[]{:S(2)}) collective-permute-start(bf16[16,3696]{1,0:T(8,128)(2,1)} %get-tuple-element.35), channel_id=1, source_target_pairs={{0,96},{1,25},{2,98},{3,27},{4,100},{5,29},{6,102},{7,31},{8,104},... | collective-permute-start | bytes 354824 | tf_op jit(solution)/shard_map/ppermute | solution.py:119
  95.4 5.6 %collective-permute-start.20 = (bf16[16,3696]{1,0:T(8,128)(2,1)}, bf16[16,3696]{1,0:T(8,128)(2,1)}, u32[]{:S(2)}, u32[]{:S(2)}) collective-permute-start(bf16[16,3696]{1,0:T(8,128)(2,1)} %get-tuple-element.37), channel_id=1, source_target_pairs={{0,64},{1,17},{2,66},{3,19},{4,68},{5,21},{6,70},{7,23},{8,72},{9,... | collective-permute-start | bytes 354824 | tf_op jit(solution)/shard_map/ppermute | solution.py:119
  95.5 6.6 %collective-permute-start.21 = (bf16[16,3696]{1,0:T(8,128)(2,1)}, bf16[16,3696]{1,0:T(8,128)(2,1)}, u32[]{:S(2)}, u32[]{:S(2)}) collective-permute-start(bf16[16,3696]{1,0:T(8,128)(2,1)} %get-tuple-element.36), channel_id=1, source_target_pairs={{0,32},{1,9},{2,34},{3,11},{4,36},{5,13},{6,38},{7,15},{8,40},{9,1... | collective-permute-start | bytes 354824 | tf_op jit(solution)/shard_map/ppermute | solution.py:119
  96.1 5.9 %copy-start.16 = (bf16[16,3696]{1,0:T(8,128)(2,1)}, bf16[16,3696]{1,0:T(8,128)(2,1)S(1)}, u32[]{:S(2)}) copy-start(bf16[16,3696]{1,0:T(8,128)(2,1)S(1)} %collective-permute-done.17) | copy-start | bytes 354820
  104.6 16.6 %collective-permute-start.22 = (bf16[4,8,924]{2,0,1:T(4,128)(2,1)S(1)}, bf16[4,8,924]{2,0,1:T(4,128)(2,1)S(1)}, u32[]{:S(2)}, u32[]{:S(2)}) collective-permute-start(bf16[4,8,924]{2,0,1:T(4,128)(2,1)S(1)} %dynamic-slice_bitcast_fusion), channel_id=1, source_target_pairs={{0,1},{1,0},{2,3},{3,2},{4,5},{5,4},{6,7},{7,6},{8,9},{9,8},{10,11... | collective-permute-start | bytes 177416 | tf_op jit(solution)/shard_map/ppermute | solution.py:17
  121.4 6.0 %collective-permute-start.23 = (bf16[2,4,8,924]{3,1,2,0:T(4,128)(2,1)S(1)}, bf16[2,4,8,924]{3,1,2,0:T(4,128)(2,1)S(1)}, u32[]{:S(2)}, u32[]{:S(2)}) collective-permute-start(bf16[2,4,8,924]{3,1,2,0:T(4,128)(2,1)S(1)} %get-tuple-element.40), channel_id=1, source_target_pairs={{0,2},{2,4},{4,6},{6,0},{1,3},{3,5},{5,7},{7,1},{8,10},{10,12},{12... | collective-permute-start | bytes 354824 | tf_op jit(solution)/shard_map/ppermute | solution.py:17
  121.9 5.6 %collective-permute-start.24 = (bf16[2,4,8,924]{3,1,2,0:T(4,128)(2,1)S(1)}, bf16[2,4,8,924]{3,1,2,0:T(4,128)(2,1)S(1)}, u32[]{:S(2)}, u32[]{:S(2)}) collective-permute-start(bf16[2,4,8,924]{3,1,2,0:T(4,128)(2,1)S(1)} %get-tuple-element.40), channel_id=1, source_target_pairs={{0,6},{2,0},{4,2},{6,4},{1,7},{3,1},{5,3},{7,5},{8,14},{10,8},{12,... | collective-permute-start | bytes 354824 | tf_op jit(solution)/shard_map/ppermute | solution.py:17
  124.2 7.0 %collective-permute-start.25 = (bf16[2,4,8,924]{3,1,2,0:T(4,128)(2,1)S(1)}, bf16[2,4,8,924]{3,1,2,0:T(4,128)(2,1)S(1)}, u32[]{:S(2)}, u32[]{:S(2)}) collective-permute-start(bf16[2,4,8,924]{3,1,2,0:T(4,128)(2,1)S(1)} %get-tuple-element.40), channel_id=1, source_target_pairs={{0,4},{2,6},{4,0},{6,2},{1,5},{3,7},{5,1},{7,3},{8,12},{10,14},{12... | collective-permute-start | bytes 354824 | tf_op jit(solution)/shard_map/ppermute | solution.py:17
  155.2 5.7 %collective-permute-start.26 = (bf16[32,8,924]{2,0,1:T(8,128)(2,1)}, bf16[32,8,924]{2,0,1:T(8,128)(2,1)S(1)}, u32[]{:S(2)}, u32[]{:S(2)}) collective-permute-start(bf16[32,8,924]{2,0,1:T(8,128)(2,1)} %copy.24), channel_id=1, source_target_pairs={{0,1},{1,0},{2,3},{3,2},{4,5},{5,4},{6,7},{7,6},{8,9},{9,8},{10,11... | collective-permute-start | bytes 1419272 | tf_op jit(solution)/shard_map/ppermute | solution.py:17
  160.8 1.2 copy-start.14

commit v2 on v1

--- a/solution.py
+++ b/solution.py
@@ -22,7 +22,8 @@
     dy, high = ((2, 0), (2, 1), (1, 1), (3, 0), (1, 0), (3, 1), (0, 1), (0, 0))[slot]
     dz = (4, 5, 3, 6, 2, 7, 1, 0)[slot]
     first = c == 0
-    owner_z = lax.rem(z + lib.where(first, 4 * high + block, dz), Z)
+    pair = z + 1 - 2 * lax.rem(z, 2)
+    owner_z = lax.rem(lib.where(first, (pair if high else z) + 2 * block, z + dz), Z)
     owner_y = lax.rem(y + lib.where(first, dy, block), Y)
     return owner_z, owner_y
 
@@ -42,13 +43,8 @@
                 mine = lax.div(oz, X) == c
                 to = (slot * 4 + block) * rows
 
-                @pl.when(mine)
-                def _():
-                    held[pl.ds(to, rows), :] = mine_ref[pl.ds(at, rows), :]
-
-                @pl.when(jnp.logical_not(mine))
-                def _():
-                    held[pl.ds(to, rows), :] = other_ref[pl.ds(at, rows), :]
+                block_here, block_there = mine_ref[pl.ds(at, rows), :], other_ref[pl.ds(at, rows), :]
+                held[pl.ds(to, rows), :] = jnp.where(mine, block_here, block_there)
 
     g = lax.dot_general(held[...], cot_ref[...], (((1,), (1,)), ((), ())), preferred_element_type=f32)
     unit = held.shape[0] // 8
@@ -59,7 +55,7 @@
 def gradient(mine, other, cotangent, here):
     half, tokens = mine.shape
     ff = cotangent.shape[1]
-    unit, tile = half // 4, min(768, ff)
+    unit, tile = half // 4, min(1280, ff)
     whole = lambda i: (0, 0)
     return pl.pallas_call(
         grad_kernel,
@@ -73,7 +69,7 @@
         out_specs=[pl.BlockSpec((unit, tile), lambda i: (0, i))] * 8,
         out_shape=[jax.ShapeDtypeStruct((unit, ff), bf16)] * 2 + [jax.ShapeDtypeStruct((unit, ff), f32)] * 6,
         scratch_shapes=[pltpu.VMEM((2 * half, tokens), bf16)],
-        compiler_params=pltpu.CompilerParams(vmem_limit_bytes=40 * 2**20),
+        compiler_params=pltpu.CompilerParams(vmem_limit_bytes=20 * 2**20),
         cost_estimate=pl.CostEstimate(
             flops=4 * half * tokens * ff, bytes_accessed=2 * tokens * ff + 14 * half * ff // 2, transcendentals=0
         ),
@@ -130,38 +126,67 @@
     r_m3 = crossed((m3 + jnp.where(first, r_m1, r_m2).astype(f32)).astype(bf16), *down)
     r_p4 = crossed((p4 + r_p3.astype(f32)).astype(bf16), None, (0, 1))
     low = own + jnp.where(first, r_p3.astype(f32) + r_m2.astype(f32), r_p4.astype(f32) + r_m3.astype(f32))
-    high = p4 + r_p2.astype(f32) + r_m3.astype(f32)
+    high = (p4 + r_p2.astype(f32) + r_m3.astype(f32)).astype(bf16)
+    low = low + paired(high).astype(f32)
     rows = own.shape[0] // 4
-    total = low[:rows]
-    low, high = low.astype(bf16), high.astype(bf16)
-    got = [crossed(high[k * rows : (k + 1) * rows], (0, 4 + k), None) for k in (0, 1, 3, 2)]
-    got += [crossed(low[k * rows : (k + 1) * rows], (0, k), (k, 0)) for k in (3, 2, 1)]
-    for one in got:
-        total = total + one.astype(f32)
+    total, low = low[:rows], low.astype(bf16)
+    for k in (2, 1, 3):
+        total = total + crossed(low[k * rows : (k + 1) * rows], (0, 2 * k), (k, 0)).astype(f32)
     return total
 
 
+def paired(value):
+    at = lambda z, rest: (z * Y * X + rest) * C
+    return lax.ppermute(value, ("z", "y", "x", "c"), [(at(z, r), at(z ^ 1, r)) for z in range(Z) for r in range(Y * X)])
+
+
+def picked(choices, index):
+    out = choices[0]
+    for k in range(1, len(choices)):
+        out = jnp.where(index == k, choices[k], out)
+    return out
+
+
 def spread(normed):
-    c, x = lax.axis_index("c"), lax.axis_index("x")
-    _, rows, ff = normed.shape
-    cut = normed.reshape(C, rows, Y, ff // Y).transpose(0, 2, 1, 3)
-    keep = lax.dynamic_index_in_dim(cut, c, 0, keepdims=False)
-    give = lax.dynamic_index_in_dim(cut, 1 - c, 0, keepdims=False)
-    swap = moved(give, "c", 1)
-    pair = jnp.stack([jnp.where(c == 0, keep, swap), jnp.where(c == 0, swap, keep)])
-    wide = jnp.zeros((X,) + pair.shape, bf16)
-    wide = lax.dynamic_update_index_in_dim(wide, pair, x, 0)
-    for d in (1, 3, 2):
-        wide = lax.dynamic_update_index_in_dim(wide, moved(pair, "x", d), (x - d) % X, 0)
-    wide = wide.reshape(X * C * Y, rows, ff // Y)
-    mine = lax.all_to_all(wide, ("z", "y"), 0, 0, tiled=True)
-    other = moved(mine, "c", 1)
-    return jnp.stack([jnp.where(c == 0, mine, other), jnp.where(c == 0, other, mine)])
+    z, y, x, c = (lax.axis_index(axis) for axis in ("z", "y", "x", "c"))
+    rows, ff = normed.shape
+    cut = normed.reshape(rows, Y, ff // Y).transpose(1, 0, 2)
+    piece = lambda k: lax.dynamic_index_in_dim(cut, (y + k) % Y, 0, keepdims=False)
+    got = {d: moved(piece(d), "y", d) for d in (1, 3, 2)}
+    tall = jnp.stack([piece(0), got[1], got[2], got[3]])
+    got = {d: moved(tall, "x", d) for d in (1, 3, 2)}
+    wide = [tall, got[1], got[2], got[3]]
+    odd = (z + c) % 2
+    half = []
+    for k in (0, 1, 2, 3):
+        to = (z + 2 * k + odd) % Z
+        sent = picked(wide, (x - to // 2) % X)
+        pairs = []
+        for pz in range(Z):
+            for pc in range(C):
+                po = (pz + pc) % 2
+                for r in range(Y * X):
+                    if k or po:
+                        pairs.append(((pz * Y * X + r) * C + pc, (((pz + 2 * k + po) % Z) * Y * X + r) * C + (pc ^ po)))
+        moved_in = lax.ppermute(sent, ("z", "y", "x", "c"), pairs)
+        half.append(moved_in if k else jnp.where(odd == 0, sent, moved_in))
+    half = jnp.stack(half)
+    return half, moved(half, "c", 1)
+
+
+def spread_order(rank):
+    z, y, c = (lax.axis_index(axis) for axis in ("z", "y", "c"))
+    rows = rank // (Z * Y)
+    n = lax.broadcasted_iota(jnp.int32, (rank, rank), 1)
+    r = lax.broadcasted_iota(jnp.int32, (rank, rank), 0)
+    h, k, j = n // (rank // 2), (n // (rows * Y)) % (Z // 2), (n // rows) % Y
+    owner_z = (z + 2 * Z - 2 * k - (z + c + h) % 2) % Z
+    want = (owner_z * Y + (y + Y - j) % Y) * rows + n % rows
+    return (r == want).astype(bf16)
 
 
 def shards(tokens, basis, cotangent, exp_avg, exp_avg_sq):
     rank, ff = basis.shape[1], cotangent.shape[1]
-    rows = rank // (2 * Z * Y)
     here = jnp.stack([lax.axis_index(axis) for axis in ("z", "y", "x", "c")]).astype(jnp.int32)
     mine, other = project(tokens, basis)
     total = scatter(*gradient(mine, other, cotangent, here))
@@ -170,9 +195,9 @@
     first = 0.9 * exp_avg + 0.1 * grad_low
     second = 0.999 * exp_avg_sq + 0.001 * grad_low * grad_low
     normed = (first / bias_first / (jnp.sqrt(second / bias_second) + 1e-08)).astype(bf16)
-    all_rows = spread(normed.reshape(2, rows, ff)).reshape(rank, ff // Y)
-    by_half = basis.reshape(-1, Z * Y, 2, rows).transpose(0, 2, 1, 3).reshape(-1, rank)
-    update = jnp.dot(by_half, all_rows, preferred_element_type=f32).astype(bf16)
+    all_rows = jnp.stack(spread(normed)).reshape(rank, ff // Y)
+    ordered = jnp.dot(basis, spread_order(rank), preferred_element_type=f32).astype(bf16)
+    update = jnp.dot(ordered, all_rows, preferred_element_type=f32).astype(bf16)
     return (update, first, second)
 
 

time: 165 us -> 163 us (0.988)
  blocking collectives: 22.8 us -> 0 us
  waiting for transfers between devices: 48.9 us -> 70.7 us
  Pallas kernels: 9.64 us -> 7.15 us
  other arithmetic: 5.64 us -> 7.91 us
  local copies, waits for them, and re-layouts: 14.5 us -> 12.3 us
  matrix products: 7.19 us -> 9.08 us
    ppermute x0 -> x5, starting transfers between devices: none -> 23.6 us  [the longest x4 22.9 us: spread(): moved_in = lax.ppermute(sent, ('z', 'y', 'x', 'c'), pairs)]
    ppermute x13 -> x15, starting transfers between devices: 35.8 us -> 12.9 us  [moved(): return lax.ppermute(value, axis, [(i, (i + by) % n) for i in range(n)])]
    all_to_all x1 -> x0, blocking collectives: 22.8 us -> none  [spread(): mine = lax.all_to_all(wide, ('z', 'y'), 0, 0, tiled=True)]
    ppermute x13 -> x15, waiting for transfers between devices: 20.2 us -> 29.6 us  [moved(): return lax.ppermute(value, axis, [(i, (i + by) % n) for i in range(n)])]
    ppermute x0 -> x5, waiting for transfers between devices: none -> 8.84 us  [the longest x4 8.83 us: spread(): moved_in = lax.ppermute(sent, ('z', 'y', 'x', 'c'), pairs)]
    ppermute x14 -> x10, waiting for transfers between devices: 28.7 us -> 32.2 us  [crossed(): return lax.ppermute(value, ('z', 'y', 'x', 'c'), pairs)]
    pallas_call x1, Pallas kernels: 9.64 us -> 7.15 us  [gradient(): pl.pallas_call(grad_kernel, grid=(pl.cdiv(ff, tile),), in_specs=[pl.Block...]
    dot_general x1, matrix products: 2.66 us -> 4.56 us  [shards(): update = jnp.dot(ordered, all_rows, preferred_element_type=f32).astype(bf16)]
  transfers between devices with their start and end apart: 27 -> 30, of which waited for: 18 -> 24; matrix products, arithmetic and copies ran while one was open for 4% -> 1% of each run, Pallas kernels for 0% -> 0%
where the time goes in v2:
time: 163 us; the launch traced here: 162 us
  waiting for transfers between devices  70.7 us (43%)
  starting transfers between devices  54 us (33%)
  local copies, waits for them, and re-layouts  12.3 us (8%)
  matrix products  9.08 us (6%)
  other arithmetic  7.91 us (5%)
  Pallas kernels  7.15 us (4%)
    ppermute x10, waiting for transfers between devices, crossed(): return lax.ppermute(value, ('z', 'y', 'x', 'c'), pairs)  32.2 us
    ppermute x15, waiting for transfers between devices, moved(): return lax.ppermute(value, axis, [(i, (i + by) % n) for i in range(n)])  29.6 us
    ppermute x4, starting transfers between devices, spread(): moved_in = lax.ppermute(sent, ('z', 'y', 'x', 'c'), pairs)  22.9 us
    ppermute x10, starting transfers between devices, crossed(): return lax.ppermute(value, ('z', 'y', 'x', 'c'), pairs)  17.6 us
    ppermute x15, starting transfers between devices, moved(): return lax.ppermute(value, axis, [(i, (i + by) % n) for i in range(n)])  12.9 us
    unnamed x38, local copies, waits for them, and re-layouts  11.7 us
    ppermute x4, waiting for transfers between devices, spread(): moved_in = lax.ppermute(sent, ('z', 'y', 'x', 'c'), pairs)  8.83 us
    pallas_call x1, Pallas kernels, gradient(): pl.pallas_call(grad_kernel, grid=(pl.cdiv(ff, tile),), in_specs=[pl.Block...  7.15 us
  transfers between devices with their start and end apart: 30, of which 24 were waited for; matrix products, arithmetic and copies ran while one was open for 1% of the time, Pallas kernels for 0%

profile of v2, /device:TPU:1, one launch (start us, length us, event | category | flops | bytes accessed | tf_op | source)
XLA Modules:
  0.0 162.1 jit_solution(11572905150535161708)
XLA Ops:
  0.7 3.0 %convolution_convert_fusion.1 = bf16[512,1024]{1,0:T(8,128)(2,1)S(1)} fusion(bf16[1024,512]{1,0:T(8,128)(2,1)} %param.6, s32[512]{0:T(512)S(1)} %get-tuple-element.45, s32[512]{0:T(512)S(1)} %get-tuple-element.47, s32[512]{0:T(512)S(1)} %get-tuple-element.44, s32[512]{0:T(512)S(1)} %get-tuple-element.51, s32[]{:T(128)} %axis_index.35, ...), kind=kOutput, calls=%fused_computation.31 | convolution fusion | flops 548667392 | bytes 2110984 | tf_op jit(solution)/shard_map/dot_general | solution.py:92
  4.5 3.3 %collective-permute-start = (f32[256,1024]{1,0:T(8,128)S(1)}, f32[256,1024]{1,0:T(8,128)S(1)}, u32[]{:S(2)}, u32[]{:S(2)}) collective-permute-start(f32[256,1024]{1,0:T(8,128)S(1)} %fusion.41), channel_id=1, source_target_pairs={{0,1},{1,0},{2,3},{3,2},{4,5},{5,4},{6,7},{7,6},{8,9},{9,8},{10,11... | collective-permute-start | bytes 3145736 | tf_op jit(solution)/shard_map/ppermute | solution.py:17
  7.8 2.3 %collective-permute-done = f32[256,1024]{1,0:T(8,128)S(1)} collective-permute-done((f32[256,1024]{1,0:T(8,128)S(1)}, f32[256,1024]{1,0:T(8,128)S(1)}, u32[]{:S(2)}, u32[]{:S(2)}) %collective-permute-start) | collective-permute-done | bytes 1048608 | tf_op jit(solution)/shard_map/ppermute | solution.py:17
  10.9 1.1 collective-permute-start.3
  13.5 3.7 %collective-permute-done.3 = bf16[64,1024]{1,0:T(8,128)(2,1)S(1)} collective-permute-done((bf16[64,1024]{1,0:T(8,128)(2,1)S(1)}, bf16[64,1024]{1,0:T(8,128)(2,1)S(1)}, u32[]{:S(2)}, u32[]{:S(2)}) %collective-permute-start.3) | collective-permute-done | bytes 131104 | tf_op jit(solution)/shard_map/ppermute | solution.py:17
  17.2 1.2 collective-permute-done.2
  18.4 1.9 %collective-permute-done.1 = bf16[64,1024]{1,0:T(8,128)(2,1)S(1)} collective-permute-done((bf16[64,1024]{1,0:T(8,128)(2,1)S(1)}, bf16[64,1024]{1,0:T(8,128)(2,1)S(1)}, u32[]{:S(2)}, u32[]{:S(2)}) %collective-permute-start.1) | collective-permute-done | bytes 131104 | tf_op jit(solution)/shard_map/ppermute | solution.py:17
  20.4 1.3 collective-permute-start.6
  22.8 1.5 collective-permute-done.6
  24.3 3.1 %collective-permute-done.5 = bf16[64,1024]{1,0:T(8,128)(2,1)S(1)} collective-permute-done((bf16[64,1024]{1,0:T(8,128)(2,1)S(1)}, bf16[64,1024]{1,0:T(8,128)(2,1)S(1)}, u32[]{:S(2)}, u32[]{:S(2)}) %collective-permute-start.5) | collective-permute-done | bytes 131104 | tf_op jit(solution)/shard_map/ppermute | solution.py:17
  27.4 4.0 %collective-permute-done.4 = bf16[64,1024]{1,0:T(8,128)(2,1)S(1)} collective-permute-done((bf16[64,1024]{1,0:T(8,128)(2,1)S(1)}, bf16[64,1024]{1,0:T(8,128)(2,1)S(1)}, u32[]{:S(2)}, u32[]{:S(2)}) %collective-permute-start.4) | collective-permute-done | bytes 131104 | tf_op jit(solution)/shard_map/ppermute | solution.py:17
  34.3 1.0 copy-done.11
  35.4 3.1 %copy-done.12 = bf16[1024,3696]{0,1:T(8,128)(2,1)S(1)} copy-done((bf16[1024,3696]{0,1:T(8,128)(2,1)S(1)}, bf16[1024,3696]{0,1:T(8,128)(2,1)}, u32[]{:S(2)}) %copy-start.12) | copy-done | bytes 7569432
  38.5 1.0 copy-done.14
  39.6 7.2 %shard_map.76 = (bf16[64,3696]{1,0:T(8,128)(2,1)}, bf16[64,3696]{1,0:T(8,128)(2,1)S(1)}, f32[64,3696]{1,0:T(8,128)S(1)}, f32[64,3696]{1,0:T(8,128)S(1)}, f32[64,...) custom-call(s32[4]{0:T(128)S(1)} %pad_add_fusion.here, ...), custom_call_target="tpu_custom_call" | custom-call | flops 3875536896 | bytes 14192640 | tf_op jit(solution)/shard_map/pallas_call | solution.py:60
  47.7 1.0 copy-done.3
  48.7 1.0 copy-done.5
  50.6 1.0 copy-done.9
  51.5 1.6 %collective-permute-start.8 = (bf16[64,3696]{1,0:T(8,128)(2,1)}, bf16[64,3696]{1,0:T(8,128)(2,1)}, u32[]{:S(2)}, u32[]{:S(2)}) collective-permute-start(bf16[64,3696]{1,0:T(8,128)(2,1)} %get-tuple-element.13), channel_id=1, source_target_pairs={{0,8},{1,33},{2,10},{3,35},{4,12},{5,37},{6,14},{7,39},{8,16},{9,4... | collective-permute-start | bytes 1419272 | tf_op jit(solution)/shard_map/ppermute | solution.py:115
  53.2 3.9 %collective-permute-start.11 = (bf16[64,3696]{1,0:T(8,128)(2,1)S(1)}, bf16[64,3696]{1,0:T(8,128)(2,1)S(1)}, u32[]{:S(2)}, u32[]{:S(2)}) collective-permute-start(bf16[64,3696]{1,0:T(8,128)(2,1)S(1)} %get-tuple-element.16), channel_id=1, source_target_pairs={{0,24},{1,225},{2,26},{3,227},{4,28},{5,229},{6,30},{7,231},{8,0},... | collective-permute-start | bytes 1419272 | tf_op jit(solution)/shard_map/ppermute | solution.py:115
  57.1 6.3 %collective-permute-done.8 = bf16[64,3696]{1,0:T(8,128)(2,1)} collective-permute-done((bf16[64,3696]{1,0:T(8,128)(2,1)}, bf16[64,3696]{1,0:T(8,128)(2,1)}, u32[]{:S(2)}, u32[]{:S(2)}) %collective-permute-start.8) | collective-permute-done | bytes 473120 | tf_op jit(solution)/shard_map/ppermute | solution.py:115
  63.4 1.4 add_convert_fusion.3
  65.3 2.7 %collective-permute-start.12 = (bf16[64,3696]{1,0:T(8,128)(2,1)S(1)}, bf16[64,3696]{1,0:T(8,128)(2,1)S(1)}, u32[]{:S(2)}, u32[]{:S(2)}) collective-permute-start(bf16[64,3696]{1,0:T(8,128)(2,1)S(1)} %add_convert_fusion.1), channel_id=1, source_target_pairs={{0,24},{1,225},{2,26},{3,227},{4,28},{5,229},{6,30},{7,231},{8,0},... | collective-permute-start | bytes 1419272 | tf_op jit(solution)/shard_map/ppermute | solution.py:115
  68.0 5.8 %collective-permute-done.9 = bf16[64,3696]{1,0:T(8,128)(2,1)S(1)} collective-permute-done((bf16[64,3696]{1,0:T(8,128)(2,1)S(1)}, bf16[64,3696]{1,0:T(8,128)(2,1)S(1)}, u32[]{:S(2)}, u32[]{:S(2)}) %collective-permute-start.9) | collective-permute-done | bytes 473120 | tf_op jit(solution)/shard_map/ppermute | solution.py:115
  74.3 3.0 %collective-permute-start.14 = (bf16[64,3696]{1,0:T(8,128)(2,1)S(1)}, bf16[64,3696]{1,0:T(8,128)(2,1)S(1)}, u32[]{:S(2)}, u32[]{:S(2)}) collective-permute-start(bf16[64,3696]{1,0:T(8,128)(2,1)S(1)} %add_convert_fusion), channel_id=1, source_target_pairs={{0,24},{1,225},{2,26},{3,227},{4,28},{5,229},{6,30},{7,231},{8,0},... | collective-permute-start | bytes 1419272 | tf_op jit(solution)/shard_map/ppermute | solution.py:115
  77.3 5.9 %collective-permute-done.10 = bf16[64,3696]{1,0:T(8,128)(2,1)S(1)} collective-permute-done((bf16[64,3696]{1,0:T(8,128)(2,1)S(1)}, bf16[64,3696]{1,0:T(8,128)(2,1)S(1)}, u32[]{:S(2)}, u32[]{:S(2)}) %collective-permute-start.10) | collective-permute-done | bytes 473120 | tf_op jit(solution)/shard_map/ppermute | solution.py:115
  84.0 1.9 %collective-permute-start.13 = (bf16[64,3696]{1,0:T(8,128)(2,1)S(1)}, bf16[64,3696]{1,0:T(8,128)(2,1)S(1)}, u32[]{:S(2)}, u32[]{:S(2)}) collective-permute-start(bf16[64,3696]{1,0:T(8,128)(2,1)S(1)} %get-tuple-element.24), channel_id=1, source_target_pairs={{1,33},{3,35},{5,37},{7,39},{9,41},{11,43},{13,45},{15,47},{17,49}... | collective-permute-start | bytes 1419272 | tf_op jit(solution)/shard_map/ppermute | solution.py:115
  86.0 9.1 %collective-permute-done.13 = bf16[64,3696]{1,0:T(8,128)(2,1)S(1)} collective-permute-done((bf16[64,3696]{1,0:T(8,128)(2,1)S(1)}, bf16[64,3696]{1,0:T(8,128)(2,1)S(1)}, u32[]{:S(2)}, u32[]{:S(2)}) %collective-permute-start.13) | collective-permute-done | bytes 473120 | tf_op jit(solution)/shard_map/ppermute | solution.py:115
  95.1 1.3 fusion.148
  96.4 2.8 %collective-permute-start.18 = (bf16[16,3696]{1,0:T(8,128)(2,1)S(1)}, bf16[16,3696]{1,0:T(8,128)(2,1)S(1)}, u32[]{:S(2)}, u32[]{:S(2)}) collective-permute-start(bf16[16,3696]{1,0:T(8,128)(2,1)S(1)} %get-tuple-element.36), channel_id=1, source_target_pairs={{0,192},{1,25},{2,194},{3,27},{4,196},{5,29},{6,198},{7,31},{8,200... | collective-permute-start | bytes 354824 | tf_op jit(solution)/shard_map/ppermute | solution.py:115
  99.3 1.3 collective-permute-start.16
  101.1 4.5 %collective-permute-done.17 = bf16[16,3696]{1,0:T(8,128)(2,1)S(1)} collective-permute-done((bf16[16,3696]{1,0:T(8,128)(2,1)S(1)}, bf16[16,3696]{1,0:T(8,128)(2,1)S(1)}, u32[]{:S(2)}, u32[]{:S(2)}) %collective-permute-start.17) | collective-permute-done | bytes 118304 | tf_op jit(solution)/shard_map/ppermute | solution.py:115
  105.6 1.9 %divide_convert_fusion = (bf16[16,3696]{1,0:T(8,128)(2,1)S(1)}, f32[16,3696]{1,0:T(8,128)}, f32[16,3696]{1,0:T(8,128)}) fusion(bf16[16,3696]{1,0:T(8,128)(2,1)S(1)} %collective-permute-done.18, bf16[16,3696]{1,0:T(8,128)(2,1)S(1)} %collective-permute-done.17, bf16[16,3696]{1,0:T(8,128)(2,1)S(1)} %collective-permute-done.16, ...), kind=kLoop, calls=%fused_computation.133 | loop fusion | flops 1123584 | bytes 1655808 | tf_op jit(solution)/shard_map/convert_element_type | solution.py:197
  108.0 1.6 %collective-permute-start.21 = (bf16[16,924]{1,0:T(8,128)(2,1)S(1)}, bf16[16,924]{1,0:T(8,128)(2,1)S(1)}, u32[]{:S(2)}, u32[]{:S(2)}) collective-permute-start(bf16[16,924]{1,0:T(8,128)(2,1)S(1)} %bitcast.51), channel_id=1, source_target_pairs={{0,24},{8,0},{16,8},{24,16},{1,25},{9,1},{17,9},{25,17},{2,26},{10... | collective-permute-start | bytes 88712 | tf_op jit(solution)/shard_map/ppermute | solution.py:17
  111.2 3.0 %collective-permute-done.20 = bf16[16,924]{1,0:T(8,128)(2,1)S(1)} collective-permute-done((bf16[16,924]{1,0:T(8,128)(2,1)S(1)}, bf16[16,924]{1,0:T(8,128)(2,1)S(1)}, u32[]{:S(2)}, u32[]{:S(2)}) %collective-permute-start.20) | collective-permute-done | bytes 29600 | tf_op jit(solution)/shard_map/ppermute | solution.py:17
  115.8 2.3 %collective-permute-done.22 = bf16[4,16,924]{2,1,0:T(8,128)(2,1)S(1)} collective-permute-done((bf16[4,16,924]{2,1,0:T(8,128)(2,1)S(1)}, bf16[4,16,924]{2,1,0:T(8,128)(2,1)S(1)}, u32[]{:S(2)}, u32[]{:S(2)}) %collective-permute-start.22) | collective-permute-done | bytes 118304 | tf_op jit(solution)/shard_map/ppermute | solution.py:17
  118.1 1.9 %collective-permute-done.23 = bf16[4,16,924]{2,1,0:T(8,128)(2,1)S(1)} collective-permute-done((bf16[4,16,924]{2,1,0:T(8,128)(2,1)S(1)}, bf16[4,16,924]{2,1,0:T(8,128)(2,1)S(1)}, u32[]{:S(2)}, u32[]{:S(2)}) %collective-permute-start.23) | collective-permute-done | bytes 118304 | tf_op jit(solution)/shard_map/ppermute | solution.py:17
  120.0 1.3 collective-permute-done.24
  121.4 16.3 %collective-permute-start.28 = (bf16[4,16,924]{2,1,0:T(8,128)(2,1)S(1)}, bf16[4,16,924]{2,1,0:T(8,128)(2,1)S(1)}, u32[]{:S(2)}, u32[]{:S(2)}) collective-permute-start(bf16[4,16,924]{2,1,0:T(8,128)(2,1)S(1)} %get-tuple-element.29), channel_id=1, source_target_pairs={{0,192},{2,194},{4,196},{6,198},{8,200},{10,202},{12,204},{14,206}... | collective-permute-start | bytes 354824 | tf_op jit(solution)/shard_map/ppermute | solution.py:171
  137.7 1.9 %collective-permute-start.25 = (bf16[4,16,924]{2,1,0:T(8,128)(2,1)S(1)}, bf16[4,16,924]{2,1,0:T(8,128)(2,1)S(1)}, u32[]{:S(2)}, u32[]{:S(2)}) collective-permute-start(bf16[4,16,924]{2,1,0:T(8,128)(2,1)S(1)} %get-tuple-element.28), channel_id=1, source_target_pairs={{1,32},{3,34},{5,36},{7,38},{9,40},{11,42},{13,44},{15,46},{17,48}... | collective-permute-start | bytes 354824 | tf_op jit(solution)/shard_map/ppermute | solution.py:171
  139.7 3.0 %collective-permute-start.27 = (bf16[4,16,924]{2,1,0:T(8,128)(2,1)S(1)}, bf16[4,16,924]{2,1,0:T(8,128)(2,1)S(1)}, u32[]{:S(2)}, u32[]{:S(2)}) collective-permute-start(bf16[4,16,924]{2,1,0:T(8,128)(2,1)S(1)} %get-tuple-element.31), channel_id=1, source_target_pairs={{0,128},{2,130},{4,132},{6,134},{8,136},{10,138},{12,140},{14,142}... | collective-permute-start | bytes 354824 | tf_op jit(solution)/shard_map/ppermute | solution.py:171
  142.7 1.6 collective-permute-start.26
  144.3 1.5 collective-permute-done.25
  145.8 2.9 %collective-permute-done.27 = bf16[4,16,924]{2,1,0:T(8,128)(2,1)S(1)} collective-permute-done((bf16[4,16,924]{2,1,0:T(8,128)(2,1)S(1)}, bf16[4,16,924]{2,1,0:T(8,128)(2,1)S(1)}, u32[]{:S(2)}, u32[]{:S(2)}) %collective-permute-start.27) | collective-permute-done | bytes 118304 | tf_op jit(solution)/shard_map/ppermute | solution.py:171
  148.7 4.5 %collective-permute-done.26 = bf16[4,16,924]{2,1,0:T(8,128)(2,1)S(1)} collective-permute-done((bf16[4,16,924]{2,1,0:T(8,128)(2,1)S(1)}, bf16[4,16,924]{2,1,0:T(8,128)(2,1)S(1)}, u32[]{:S(2)}, u32[]{:S(2)}) %collective-permute-start.26) | collective-permute-done | bytes 118304 | tf_op jit(solution)/shard_map/ppermute | solution.py:171
  153.4 2.0 %collective-permute-done.29 = bf16[4,4,16,924]{3,2,1,0:T(8,128)(2,1)} collective-permute-done((bf16[4,4,16,924]{3,2,1,0:T(8,128)(2,1)S(1)}, bf16[4,4,16,924]{3,2,1,0:T(8,128)(2,1)}, u32[]{:S(2)}, u32[]{:S(2)}) %collective-permute-start.29) | collective-permute-done | bytes 473120 | tf_op jit(solution)/shard_map/ppermute | solution.py:17
  155.4 2.2 %pad_maximum_fusion = bf16[2,4,4,16,924]{4,3,2,1,0:T(8,128)(2,1)} fusion(bf16[1,4,4,16,924]{4,3,2,1,0:T(8,128)(2,1)} %bitcast.17, bf16[1,4,4,16,924]{4,3,2,1,0:T(8,128)(2,1)S(1)} %get-tuple-element.26), kind=kLoop, calls=%fused_computation.61 | loop fusion | flops 473088 | bytes 1892352 | tf_op jit(solution)/shard_map/stack | solution.py:198
  157.6 4.6 %convolution_convert_fusion = bf16[1024,924]{0,1:T(8,128)(2,1)} fusion(bf16[512,924]{1,0:T(8,128)(2,1)} %bitcast.35, bf16[1024,512]{1,0:T(8,128)(2,1)} %param.6, s32[512]{0:T(512)S(1)} %get-tuple-element.53, s32[512]{0:T(512)S(1)} %get-tuple-element.54, s32[512]{0:T(512)S(1)} %get-tuple-element.52, s32[512]{0:T(512)S(1)} %get-tuple-element.55, ...), kind=kOutput, calls=%fused_computation.9 | convolution fusion | flops 1525575680 | bytes 3905548 | tf_op jit(solution)/shard_map/dot_general | solution.py:200
  (83 shorter events, 15.3 us)
Async XLA Ops:
  0.6 3.1 %copy-start = (bf16[1024,1024]{1,0:T(8,128)(2,1)S(1)}, bf16[1024,1024]{1,0:T(8,128)(2,1)}, u32[]{:S(2)}) copy-start(bf16[1024,1024]{1,0:T(8,128)(2,1)} %param.5) | copy-start | bytes 6291460
  4.5 5.6 %collective-permute-start = (f32[256,1024]{1,0:T(8,128)S(1)}, f32[256,1024]{1,0:T(8,128)S(1)}, u32[]{:S(2)}, u32[]{:S(2)}) collective-permute-start(f32[256,1024]{1,0:T(8,128)S(1)} %fusion.41), channel_id=1, source_target_pairs={{0,1},{1,0},{2,3},{3,2},{4,5},{5,4},{6,7},{7,6},{8,9},{9,8},{10,11... | collective-permute-start | bytes 3145736 | tf_op jit(solution)/shard_map/ppermute | solution.py:17
  10.9 6.3 %collective-permute-start.3 = (bf16[64,1024]{1,0:T(8,128)(2,1)S(1)}, bf16[64,1024]{1,0:T(8,128)(2,1)S(1)}, u32[]{:S(2)}, u32[]{:S(2)}) collective-permute-start(bf16[64,1024]{1,0:T(8,128)(2,1)S(1)} %get-tuple-element.33), channel_id=1, source_target_pairs={{0,4},{2,6},{4,0},{6,2},{1,5},{3,7},{5,1},{7,3},{8,12},{10,14},{12... | collective-permute-start | bytes 393224 | tf_op jit(solution)/shard_map/ppermute | solution.py:17
  12.0 6.4 %collective-permute-start.2 = (bf16[64,1024]{1,0:T(8,128)(2,1)S(1)}, bf16[64,1024]{1,0:T(8,128)(2,1)S(1)}, u32[]{:S(2)}, u32[]{:S(2)}) collective-permute-start(bf16[64,1024]{1,0:T(8,128)(2,1)S(1)} %get-tuple-element.34), channel_id=1, source_target_pairs={{0,6},{2,0},{4,2},{6,4},{1,7},{3,1},{5,3},{7,5},{8,14},{10,8},{12,... | collective-permute-start | bytes 393224 | tf_op jit(solution)/shard_map/ppermute | solution.py:17
  12.9 7.4 %collective-permute-start.1 = (bf16[64,1024]{1,0:T(8,128)(2,1)S(1)}, bf16[64,1024]{1,0:T(8,128)(2,1)S(1)}, u32[]{:S(2)}, u32[]{:S(2)}) collective-permute-start(bf16[64,1024]{1,0:T(8,128)(2,1)S(1)} %get-tuple-element.32), channel_id=1, source_target_pairs={{0,2},{2,4},{4,6},{6,0},{1,3},{3,5},{5,7},{7,1},{8,10},{10,12},{12... | collective-permute-start | bytes 393224 | tf_op jit(solution)/shard_map/ppermute | solution.py:17
  20.4 3.9 %collective-permute-start.6 = (bf16[64,1024]{1,0:T(8,128)(2,1)S(1)}, bf16[64,1024]{1,0:T(8,128)(2,1)S(1)}, u32[]{:S(2)}, u32[]{:S(2)}) collective-permute-start(bf16[64,1024]{1,0:T(8,128)(2,1)S(1)} %fusion.109), channel_id=1, source_target_pairs={{0,6},{2,0},{4,2},{6,4},{1,7},{3,1},{5,3},{7,5},{8,14},{10,8},{12,... | collective-permute-start | bytes 393224 | tf_op jit(solution)/shard_map/ppermute | solution.py:17
  21.6 5.8 %collective-permute-start.5 = (bf16[64,1024]{1,0:T(8,128)(2,1)S(1)}, bf16[64,1024]{1,0:T(8,128)(2,1)S(1)}, u32[]{:S(2)}, u32[]{:S(2)}) collective-permute-start(bf16[64,1024]{1,0:T(8,128)(2,1)S(1)} %fusion.109), channel_id=1, source_target_pairs={{0,4},{2,6},{4,0},{6,2},{1,5},{3,7},{5,1},{7,3},{8,12},{10,14},{12... | collective-permute-start | bytes 393224 | tf_op jit(solution)/shard_map/ppermute | solution.py:17
  22.2 9.2 %collective-permute-start.4 = (bf16[64,1024]{1,0:T(8,128)(2,1)S(1)}, bf16[64,1024]{1,0:T(8,128)(2,1)S(1)}, u32[]{:S(2)}, u32[]{:S(2)}) collective-permute-start(bf16[64,1024]{1,0:T(8,128)(2,1)S(1)} %fusion.109), channel_id=1, source_target_pairs={{0,2},{2,4},{4,6},{6,0},{1,3},{3,5},{5,7},{7,1},{8,10},{10,12},{12... | collective-permute-start | bytes 393224 | tf_op jit(solution)/shard_map/ppermute | solution.py:17
  31.4 2.1 %collective-permute-start.7 = (bf16[256,1024]{1,0:T(8,128)(2,1)S(1)}, bf16[256,1024]{1,0:T(8,128)(2,1)S(1)}, u32[]{:S(2)}, u32[]{:S(2)}) collective-permute-start(bf16[256,1024]{1,0:T(8,128)(2,1)S(1)} %pad_maximum_fusion.1.mine_ref), channel_id=1, source_target_pairs={{0,1},{1,0},{2,3},{3,2},{4,5},{5,4},{6,7},{7,6},{8,9},{9,8},{10,11... | collective-permute-start | bytes 1572872 | tf_op jit(solution)/shard_map/ppermute | solution.py:17
  32.0 0.8 copy-start.10
  33.5 0.8 copy-start.13
  34.3 1.0 copy-start.11
  35.4 3.1 %copy-start.12 = (bf16[1024,3696]{0,1:T(8,128)(2,1)S(1)}, bf16[1024,3696]{0,1:T(8,128)(2,1)}, u32[]{:S(2)}) copy-start(bf16[1024,3696]{0,1:T(8,128)(2,1)} %param.7) | copy-start | bytes 22708228
  38.5 1.0 copy-start.14
  46.7 0.9 copy-start.1
  47.7 1.0 copy-start.3
  48.7 1.0 copy-start.5
  49.6 0.9 copy-start.7
  50.6 1.0 copy-start.9
  51.5 11.9 %collective-permute-start.8 = (bf16[64,3696]{1,0:T(8,128)(2,1)}, bf16[64,3696]{1,0:T(8,128)(2,1)}, u32[]{:S(2)}, u32[]{:S(2)}) collective-permute-start(bf16[64,3696]{1,0:T(8,128)(2,1)} %get-tuple-element.13), channel_id=1, source_target_pairs={{0,8},{1,33},{2,10},{3,35},{4,12},{5,37},{6,14},{7,39},{8,16},{9,4... | collective-permute-start | bytes 1419272 | tf_op jit(solution)/shard_map/ppermute | solution.py:115
  53.2 12.0 %copy-start.8 = (f32[64,3696]{1,0:T(8,128)S(1)}, f32[64,3696]{1,0:T(8,128)}, u32[]{:S(2)}) copy-start(f32[64,3696]{1,0:T(8,128)} %copy-done.7) | copy-start | bytes 2838532
  53.2 20.7 %copy-start.6 = (f32[64,3696]{1,0:T(8,128)S(1)}, f32[64,3696]{1,0:T(8,128)}, u32[]{:S(2)}) copy-start(f32[64,3696]{1,0:T(8,128)} %copy-done.5) | copy-start | bytes 2838532
  53.2 12.0 %collective-permute-start.11 = (bf16[64,3696]{1,0:T(8,128)(2,1)S(1)}, bf16[64,3696]{1,0:T(8,128)(2,1)S(1)}, u32[]{:S(2)}, u32[]{:S(2)}) collective-permute-start(bf16[64,3696]{1,0:T(8,128)(2,1)S(1)} %get-tuple-element.16), channel_id=1, source_target_pairs={{0,24},{1,225},{2,26},{3,227},{4,28},{5,229},{6,30},{7,231},{8,0},... | collective-permute-start | bytes 1419272 | tf_op jit(solution)/shard_map/ppermute | solution.py:115
  64.9 9.0 %collective-permute-start.9 = (bf16[64,3696]{1,0:T(8,128)(2,1)S(1)}, bf16[64,3696]{1,0:T(8,128)(2,1)S(1)}, u32[]{:S(2)}, u32[]{:S(2)}) collective-permute-start(bf16[64,3696]{1,0:T(8,128)(2,1)S(1)} %add_convert_fusion.3), channel_id=1, source_target_pairs={{0,8},{1,33},{2,10},{3,35},{4,12},{5,37},{6,14},{7,39},{8,16},{9,4... | collective-permute-start | bytes 1419272 | tf_op jit(solution)/shard_map/ppermute | solution.py:115
  65.2 9.0 %copy-start.4 = (f32[64,3696]{1,0:T(8,128)S(1)}, f32[64,3696]{1,0:T(8,128)}, u32[]{:S(2)}) copy-start(f32[64,3696]{1,0:T(8,128)} %copy-done.3) | copy-start | bytes 2838532
  65.3 8.8 %collective-permute-start.12 = (bf16[64,3696]{1,0:T(8,128)(2,1)S(1)}, bf16[64,3696]{1,0:T(8,128)(2,1)S(1)}, u32[]{:S(2)}, u32[]{:S(2)}) collective-permute-start(bf16[64,3696]{1,0:T(8,128)(2,1)S(1)} %add_convert_fusion.1), channel_id=1, source_target_pairs={{0,24},{1,225},{2,26},{3,227},{4,28},{5,229},{6,30},{7,231},{8,0},... | collective-permute-start | bytes 1419272 | tf_op jit(solution)/shard_map/ppermute | solution.py:115
  73.8 9.3 %copy-start.2 = (f32[64,3696]{1,0:T(8,128)S(1)}, f32[64,3696]{1,0:T(8,128)}, u32[]{:S(2)}) copy-start(f32[64,3696]{1,0:T(8,128)} %copy-done.1) | copy-start | bytes 2838532
  74.0 9.1 %collective-permute-start.10 = (bf16[64,3696]{1,0:T(8,128)(2,1)S(1)}, bf16[64,3696]{1,0:T(8,128)(2,1)S(1)}, u32[]{:S(2)}, u32[]{:S(2)}) collective-permute-start(bf16[64,3696]{1,0:T(8,128)(2,1)S(1)} %add_convert_fusion.2), channel_id=1, source_target_pairs={{0,8},{1,33},{2,10},{3,35},{4,12},{5,37},{6,14},{7,39},{8,16},{9,4... | collective-permute-start | bytes 1419272 | tf_op jit(solution)/shard_map/ppermute | solution.py:115
  74.3 8.8 %collective-permute-start.14 = (bf16[64,3696]{1,0:T(8,128)(2,1)S(1)}, bf16[64,3696]{1,0:T(8,128)(2,1)S(1)}, u32[]{:S(2)}, u32[]{:S(2)}) collective-permute-start(bf16[64,3696]{1,0:T(8,128)(2,1)S(1)} %add_convert_fusion), channel_id=1, source_target_pairs={{0,24},{1,225},{2,26},{3,227},{4,28},{5,229},{6,30},{7,231},{8,0},... | collective-permute-start | bytes 1419272 | tf_op jit(solution)/shard_map/ppermute | solution.py:115
  83.3 2.6 %collective-permute-start.15 = (bf16[64,3696]{1,0:T(8,128)(2,1)S(1)}, bf16[64,3696]{1,0:T(8,128)(2,1)S(1)}, u32[]{:S(2)}, u32[]{:S(2)}) collective-permute-start(bf16[64,3696]{1,0:T(8,128)(2,1)S(1)} %get-tuple-element.25), channel_id=1, source_target_pairs={{0,32},{2,34},{4,36},{6,38},{8,40},{10,42},{12,44},{14,46},{16,48}... | collective-permute-start | bytes 1419272 | tf_op jit(solution)/shard_map/ppermute | solution.py:140
  84.0 11.1 %collective-permute-start.13 = (bf16[64,3696]{1,0:T(8,128)(2,1)S(1)}, bf16[64,3696]{1,0:T(8,128)(2,1)S(1)}, u32[]{:S(2)}, u32[]{:S(2)}) collective-permute-start(bf16[64,3696]{1,0:T(8,128)(2,1)S(1)} %get-tuple-element.24), channel_id=1, source_target_pairs={{1,33},{3,35},{5,37},{7,39},{9,41},{11,43},{13,45},{15,47},{17,49}... | collective-permute-start | bytes 1419272 | tf_op jit(solution)/shard_map/ppermute | solution.py:115
  95.1 10.4 %copy-start.15 = (f32[16,3696]{1,0:T(8,128)S(1)}, f32[16,3696]{1,0:T(8,128)}, u32[]{:S(2)}) copy-start(f32[16,3696]{1,0:T(8,128)} %param.8) | copy-start | bytes 709636
  95.1 10.4 %copy-start.16 = (f32[16,3696]{1,0:T(8,128)S(1)}, f32[16,3696]{1,0:T(8,128)}, u32[]{:S(2)}) copy-start(f32[16,3696]{1,0:T(8,128)} %param.9) | copy-start | bytes 709636
  96.4 4.6 %collective-permute-start.18 = (bf16[16,3696]{1,0:T(8,128)(2,1)S(1)}, bf16[16,3696]{1,0:T(8,128)(2,1)S(1)}, u32[]{:S(2)}, u32[]{:S(2)}) collective-permute-start(bf16[16,3696]{1,0:T(8,128)(2,1)S(1)} %get-tuple-element.36), channel_id=1, source_target_pairs={{0,192},{1,25},{2,194},{3,27},{4,196},{5,29},{6,198},{7,31},{8,200... | collective-permute-start | bytes 354824 | tf_op jit(solution)/shard_map/ppermute | solution.py:115
  99.3 6.3 %collective-permute-start.17 = (bf16[16,3696]{1,0:T(8,128)(2,1)S(1)}, bf16[16,3696]{1,0:T(8,128)(2,1)S(1)}, u32[]{:S(2)}, u32[]{:S(2)}) collective-permute-start(bf16[16,3696]{1,0:T(8,128)(2,1)S(1)} %get-tuple-element.37), channel_id=1, source_target_pairs={{0,64},{1,9},{2,66},{3,11},{4,68},{5,13},{6,70},{7,15},{8,72},{9,1... | collective-permute-start | bytes 354824 | tf_op jit(solution)/shard_map/ppermute | solution.py:115
  99.3 6.3 %collective-permute-start.16 = (bf16[16,3696]{1,0:T(8,128)(2,1)S(1)}, bf16[16,3696]{1,0:T(8,128)(2,1)S(1)}, u32[]{:S(2)}, u32[]{:S(2)}) collective-permute-start(bf16[16,3696]{1,0:T(8,128)(2,1)S(1)} %get-tuple-element.35), channel_id=1, source_target_pairs={{0,128},{1,17},{2,130},{3,19},{4,132},{5,21},{6,134},{7,23},{8,136... | collective-permute-start | bytes 354824 | tf_op jit(solution)/shard_map/ppermute | solution.py:115
  108.0 3.1 %collective-permute-start.21 = (bf16[16,924]{1,0:T(8,128)(2,1)S(1)}, bf16[16,924]{1,0:T(8,128)(2,1)S(1)}, u32[]{:S(2)}, u32[]{:S(2)}) collective-permute-start(bf16[16,924]{1,0:T(8,128)(2,1)S(1)} %bitcast.51), channel_id=1, source_target_pairs={{0,24},{8,0},{16,8},{24,16},{1,25},{9,1},{17,9},{25,17},{2,26},{10... | collective-permute-start | bytes 88712 | tf_op jit(solution)/shard_map/ppermute | solution.py:17
  109.7 4.5 %collective-permute-start.20 = (bf16[16,924]{1,0:T(8,128)(2,1)S(1)}, bf16[16,924]{1,0:T(8,128)(2,1)S(1)}, u32[]{:S(2)}, u32[]{:S(2)}) collective-permute-start(bf16[16,924]{1,0:T(8,128)(2,1)S(1)} %bitcast.52), channel_id=1, source_target_pairs={{0,16},{8,24},{16,0},{24,8},{1,17},{9,25},{17,1},{25,9},{2,18},{10... | collective-permute-start | bytes 88712 | tf_op jit(solution)/shard_map/ppermute | solution.py:17
  109.8 4.4 %collective-permute-start.19 = (bf16[16,924]{1,0:T(8,128)(2,1)S(1)}, bf16[16,924]{1,0:T(8,128)(2,1)S(1)}, u32[]{:S(2)}, u32[]{:S(2)}) collective-permute-start(bf16[16,924]{1,0:T(8,128)(2,1)S(1)} %bitcast.53), channel_id=1, source_target_pairs={{0,8},{8,16},{16,24},{24,0},{1,9},{9,17},{17,25},{25,1},{2,10},{10... | collective-permute-start | bytes 88712 | tf_op jit(solution)/shard_map/ppermute | solution.py:17
  114.2 3.9 %collective-permute-start.22 = (bf16[4,16,924]{2,1,0:T(8,128)(2,1)S(1)}, bf16[4,16,924]{2,1,0:T(8,128)(2,1)S(1)}, u32[]{:S(2)}, u32[]{:S(2)}) collective-permute-start(bf16[4,16,924]{2,1,0:T(8,128)(2,1)S(1)} %pad_maximum_fusion.3), channel_id=1, source_target_pairs={{0,6},{2,0},{4,2},{6,4},{1,7},{3,1},{5,3},{7,5},{8,14},{10,8},{12,... | collective-permute-start | bytes 354824 | tf_op jit(solution)/shard_map/ppermute | solution.py:17
  114.6 5.4 %collective-permute-start.23 = (bf16[4,16,924]{2,1,0:T(8,128)(2,1)S(1)}, bf16[4,16,924]{2,1,0:T(8,128)(2,1)S(1)}, u32[]{:S(2)}, u32[]{:S(2)}) collective-permute-start(bf16[4,16,924]{2,1,0:T(8,128)(2,1)S(1)} %pad_maximum_fusion.3), channel_id=1, source_target_pairs={{0,4},{2,6},{4,0},{6,2},{1,5},{3,7},{5,1},{7,3},{8,12},{10,14},{12... | collective-permute-start | bytes 354824 | tf_op jit(solution)/shard_map/ppermute | solution.py:17
  115.1 6.2 %collective-permute-start.24 = (bf16[4,16,924]{2,1,0:T(8,128)(2,1)S(1)}, bf16[4,16,924]{2,1,0:T(8,128)(2,1)S(1)}, u32[]{:S(2)}, u32[]{:S(2)}) collective-permute-start(bf16[4,16,924]{2,1,0:T(8,128)(2,1)S(1)} %pad_maximum_fusion.3), channel_id=1, source_target_pairs={{0,2},{2,4},{4,6},{6,0},{1,3},{3,5},{5,7},{7,1},{8,10},{10,12},{12... | collective-permute-start | bytes 354824 | tf_op jit(solution)/shard_map/ppermute | solution.py:17
  121.4 24.5 %collective-permute-start.28 = (bf16[4,16,924]{2,1,0:T(8,128)(2,1)S(1)}, bf16[4,16,924]{2,1,0:T(8,128)(2,1)S(1)}, u32[]{:S(2)}, u32[]{:S(2)}) collective-permute-start(bf16[4,16,924]{2,1,0:T(8,128)(2,1)S(1)} %get-tuple-element.29), channel_id=1, source_target_pairs={{0,192},{2,194},{4,196},{6,198},{8,200},{10,202},{12,204},{14,206}... | collective-permute-start | bytes 354824 | tf_op jit(solution)/shard_map/ppermute | solution.py:171
  137.7 8.1 %collective-permute-start.25 = (bf16[4,16,924]{2,1,0:T(8,128)(2,1)S(1)}, bf16[4,16,924]{2,1,0:T(8,128)(2,1)S(1)}, u32[]{:S(2)}, u32[]{:S(2)}) collective-permute-start(bf16[4,16,924]{2,1,0:T(8,128)(2,1)S(1)} %get-tuple-element.28), channel_id=1, source_target_pairs={{1,32},{3,34},{5,36},{7,38},{9,40},{11,42},{13,44},{15,46},{17,48}... | collective-permute-start | bytes 354824 | tf_op jit(solution)/shard_map/ppermute | solution.py:171
  139.7 9.0 %collective-permute-start.27 = (bf16[4,16,924]{2,1,0:T(8,128)(2,1)S(1)}, bf16[4,16,924]{2,1,0:T(8,128)(2,1)S(1)}, u32[]{:S(2)}, u32[]{:S(2)}) collective-permute-start(bf16[4,16,924]{2,1,0:T(8,128)(2,1)S(1)} %get-tuple-element.31), channel_id=1, source_target_pairs={{0,128},{2,130},{4,132},{6,134},{8,136},{10,138},{12,140},{14,142}... | collective-permute-start | bytes 354824 | tf_op jit(solution)/shard_map/ppermute | solution.py:171
  142.7 10.5 %collective-permute-start.26 = (bf16[4,16,924]{2,1,0:T(8,128)(2,1)S(1)}, bf16[4,16,924]{2,1,0:T(8,128)(2,1)S(1)}, u32[]{:S(2)}, u32[]{:S(2)}) collective-permute-start(bf16[4,16,924]{2,1,0:T(8,128)(2,1)S(1)} %get-tuple-element.30), channel_id=1, source_target_pairs={{0,64},{2,66},{4,68},{6,70},{8,72},{10,74},{12,76},{14,78},{16,80}... | collective-permute-start | bytes 354824 | tf_op jit(solution)/shard_map/ppermute | solution.py:171
  153.3 2.1 %collective-permute-start.29 = (bf16[4,4,16,924]{3,2,1,0:T(8,128)(2,1)S(1)}, bf16[4,4,16,924]{3,2,1,0:T(8,128)(2,1)}, u32[]{:S(2)}, u32[]{:S(2)}) collective-permute-start(bf16[4,4,16,924]{3,2,1,0:T(8,128)(2,1)S(1)} %get-tuple-element.27), channel_id=1, source_target_pairs={{0,1},{1,0},{2,3},{3,2},{4,5},{5,4},{6,7},{7,6},{8,9},{9,8},{10,11... | collective-permute-start | bytes 1419272 | tf_op jit(solution)/shard_map/ppermute | solution.py:17

commit v3 on v2

--- a/solution.py
+++ b/solution.py
@@ -17,46 +17,47 @@
     return lax.ppermute(value, axis, [(i, (i + by) % n) for i in range(n)])
 
 
-def owner_rows(device, slot, block, lib):
-    z, y, _, c = device
-    dy, high = ((2, 0), (2, 1), (1, 1), (3, 0), (1, 0), (3, 1), (0, 1), (0, 0))[slot]
-    dz = (4, 5, 3, 6, 2, 7, 1, 0)[slot]
-    first = c == 0
-    pair = z + 1 - 2 * lax.rem(z, 2)
-    owner_z = lax.rem(lib.where(first, (pair if high else z) + 2 * block, z + dz), Z)
-    owner_y = lax.rem(y + lib.where(first, dy, block), Y)
-    return owner_z, owner_y
-
-
 def grad_kernel(here, mine_ref, other_ref, cot_ref, *rest):
     outs, held = rest[:-1], rest[-1]
     rows = held.shape[0] // (Z * Y)
 
     @pl.when(pl.program_id(0) == 0)
     def _():
-        device = [here[i] for i in range(4)]
-        _, _, x, c = device
-        for slot in range(8):
-            for block in range(4):
-                oz, oy = owner_rows(device, slot, block, jnp)
+        z, y, x, c = (here[i] for i in range(4))
+        for dy in range(Y):
+            for dz in range(Z):
+                oz, oy = lax.rem(z + dz, Z), lax.rem(y + dy, Y)
                 at = pl.multiple_of(lax.rem(x + X - lax.rem(oz, X), X) * (Y * rows) + oy * rows, rows)
-                mine = lax.div(oz, X) == c
-                to = (slot * 4 + block) * rows
-
                 block_here, block_there = mine_ref[pl.ds(at, rows), :], other_ref[pl.ds(at, rows), :]
-                held[pl.ds(to, rows), :] = jnp.where(mine, block_here, block_there)
+                held[pl.ds((dy * Z + dz) * rows, rows), :] = jnp.where(lax.div(oz, X) == c, block_here, block_there)
 
     g = lax.dot_general(held[...], cot_ref[...], (((1,), (1,)), ((), ())), preferred_element_type=f32)
-    unit = held.shape[0] // 8
-    for slot, out in enumerate(outs):
-        out[...] = g[slot * unit : (slot + 1) * unit].astype(out.dtype)
+    part = rows // 2
+    for out, places in zip(outs, UNITS):
+        pieces = [g[(dy * Z + dz) * rows + s * part :][:part] for dy, dz, s in places]
+        if out.dtype == f32:
+            for i, piece in enumerate(pieces):
+                out[i * part : (i + 1) * part, :] = piece
+        else:
+            out[...] = jnp.concatenate(pieces, 0).astype(out.dtype)
+
+
+EVEN, ODD = (0, 2, 4, 6), (1, 3, 5, 7)
+UNITS = [[(2, dz, 0) for dz in EVEN], [(2, dz, 0) for dz in ODD]]
+UNITS += [[(dy, dz, 0) for dz in EVEN + ODD] for dy in (1, 3, 0)]
+UNITS += [[(dy, dz, 1) for dy in range(Y)] for dz in (4, 5, 3, 6, 2, 7, 1, 0)]
+ROUNDED = (0, 1, 5, 6)
 
 
 def gradient(mine, other, cotangent, here):
     half, tokens = mine.shape
     ff = cotangent.shape[1]
-    unit, tile = half // 4, min(1280, ff)
+    part, tile = half // (Z * Y), min(1280, ff)
     whole = lambda i: (0, 0)
+    shapes = [(len(places) * part, bf16 if k in ROUNDED else f32) for k, places in enumerate(UNITS)]
+    cot = pltpu.with_memory_space_constraint(cotangent.T, pltpu.HBM)
+    mine = pltpu.with_memory_space_constraint(mine, pltpu.HBM)
+    other = pltpu.with_memory_space_constraint(other, pltpu.HBM)
     return pl.pallas_call(
         grad_kernel,
         grid=(pl.cdiv(ff, tile),),
@@ -66,14 +67,14 @@
             pl.BlockSpec((half, tokens), whole),
             pl.BlockSpec((tile, tokens), lambda i: (i, 0)),
         ],
-        out_specs=[pl.BlockSpec((unit, tile), lambda i: (0, i))] * 8,
-        out_shape=[jax.ShapeDtypeStruct((unit, ff), bf16)] * 2 + [jax.ShapeDtypeStruct((unit, ff), f32)] * 6,
+        out_specs=[pl.BlockSpec((n, tile), lambda i: (0, i)) for n, _ in shapes],
+        out_shape=[pltpu.HBM((n, ff), t) for n, t in shapes],
         scratch_shapes=[pltpu.VMEM((2 * half, tokens), bf16)],
-        compiler_params=pltpu.CompilerParams(vmem_limit_bytes=20 * 2**20),
+        compiler_params=pltpu.CompilerParams(vmem_limit_bytes=24 * 2**20),
         cost_estimate=pl.CostEstimate(
             flops=4 * half * tokens * ff, bytes_accessed=2 * tokens * ff + 14 * half * ff // 2, transcendentals=0
         ),
-    )(here, mine, other, cotangent.T)
+    )(here, mine, other, cot)
 
 
 def near_order(rank):
@@ -102,42 +103,35 @@
     return mine, moved(mine, "c", 1)
 
 
-def crossed(value, by_y, by_z):
-    pairs = []
-    for z in range(Z):
-        for y in range(Y):
-            for x in range(X):
-                at = lambda z, y, c: (((z % Z) * Y + y % Y) * X + x) * C + c
-                if by_y is not None:
-                    pairs.append((at(z, y, 0), at(z + by_y[1], y + by_y[0], 0)))
-                if by_z is not None:
-                    pairs.append((at(z, y, 1), at(z + by_z[1], y + by_z[0], 1)))
-    return lax.ppermute(value, ("z", "y", "x", "c"), pairs)
-
-
-def scatter(p1, m1, p2, m2, p3, m3, p4, own):
-    first = lax.axis_index("c") == 0
-    up, down = ((1, 0), (0, 1)), ((-1, 0), (0, -1))
-    r_p1 = crossed(p1, *up)
-    r_m1 = crossed(m1, *down)
-    r_p2 = crossed((p2 + jnp.where(first, 0.0, r_p1.astype(f32))).astype(bf16), *up)
-    r_m2 = crossed((m2 + jnp.where(first, 0.0, r_m1.astype(f32))).astype(bf16), *down)
-    r_p3 = crossed((p3 + jnp.where(first, r_p1, r_p2).astype(f32)).astype(bf16), *up)
-    r_m3 = crossed((m3 + jnp.where(first, r_m1, r_m2).astype(f32)).astype(bf16), *down)
-    r_p4 = crossed((p4 + r_p3.astype(f32)).astype(bf16), None, (0, 1))
-    low = own + jnp.where(first, r_p3.astype(f32) + r_m2.astype(f32), r_p4.astype(f32) + r_m3.astype(f32))
-    high = (p4 + r_p2.astype(f32) + r_m3.astype(f32)).astype(bf16)
-    low = low + paired(high).astype(f32)
-    rows = own.shape[0] // 4
+def scatter_y_first(two_low, two_high, one, three, zero):
+    h = two_low.shape[0]
+    up, down = moved(two_low, "y", 1).astype(f32), moved(two_high, "y", -1).astype(f32)
+    up = moved(jnp.concatenate([one[:h] + up, one[h:]], 0).astype(bf16), "y", 1)
+    down = moved(jnp.concatenate([three[:h], three[h:] + down], 0).astype(bf16), "y", -1)
+    low = zero[:h] + up[:h].astype(f32) + down[:h].astype(f32)
+    high = zero[h:] + up[h:].astype(f32) + down[h:].astype(f32)
+    rows = h // 4
+    got = lax.ppermute(high.astype(bf16), "z", [(z, z ^ 1) for z in range(Z)]).astype(f32)
+    turned = jnp.concatenate([got[-rows:], got[:-rows]], 0)
+    low = low + jnp.where(lax.axis_index("z") % 2 == 0, turned, got)
     total, low = low[:rows], low.astype(bf16)
     for k in (2, 1, 3):
-        total = total + crossed(low[k * rows : (k + 1) * rows], (0, 2 * k), (k, 0)).astype(f32)
+        total = total + moved(low[k * rows : (k + 1) * rows], "z", 2 * k).astype(f32)
     return total
 
 
-def paired(value):
-    at = lambda z, rest: (z * Y * X + rest) * C
-    return lax.ppermute(value, ("z", "y", "x", "c"), [(at(z, r), at(z ^ 1, r)) for z in range(Z) for r in range(Y * X)])
+def scatter_z_first(four, five, three, six, two, seven, one, zero):
+    up, down = moved(four, "z", 1), moved(five, "z", -1)
+    for k, m in ((three, six), (two, seven)):
+        up = moved((k + up.astype(f32)).astype(bf16), "z", 1)
+        down = moved((m + down.astype(f32)).astype(bf16), "z", -1)
+    up = moved((one + up.astype(f32)).astype(bf16), "z", 1)
+    total = zero + up.astype(f32) + down.astype(f32)
+    rows = zero.shape[0] // Y
+    total, rounded = total[:rows], total.astype(bf16)
+    for k in (2, 1, 3):
+        total = total + moved(rounded[k * rows : (k + 1) * rows], "y", k).astype(f32)
+    return total
 
 
 def picked(choices, index):
@@ -189,7 +183,8 @@
     rank, ff = basis.shape[1], cotangent.shape[1]
     here = jnp.stack([lax.axis_index(axis) for axis in ("z", "y", "x", "c")]).astype(jnp.int32)
     mine, other = project(tokens, basis)
-    total = scatter(*gradient(mine, other, cotangent, here))
+    units = gradient(mine, other, cotangent, here)
+    total = jnp.concatenate([scatter_y_first(*units[:5]), scatter_z_first(*units[5:])], 0)
     total_tokens = cotangent.shape[0] * Z * Y
     grad_low = total * (1.0 / total_tokens)
     first = 0.9 * exp_avg + 0.1 * grad_low

time: 163 us -> 145 us (0.89)
  waiting for transfers between devices: 70.7 us -> 54.1 us
  local copies, waits for them, and re-layouts: 12.3 us -> 3.69 us
  starting transfers between devices: 54 us -> 62.4 us
  other arithmetic: 7.91 us -> 5.39 us
  Pallas kernels: 7.15 us -> 9.11 us
    ppermute x11 -> x1, waiting for transfers between devices: 32.2 us -> 3.35 us  [scatter_y_first(): lax.ppermute(high.astype(bf16), 'z', [(z, z ^ 1) for z in range(Z)])]
    ppermute x15 -> x32, starting transfers between devices: 12.9 us -> 40.9 us  [moved(): return lax.ppermute(value, axis, [(i, (i + by) % n) for i in range(n)])]
    ppermute x11 -> x1, starting transfers between devices: 18.3 us -> 0.09 us  [scatter_y_first(): lax.ppermute(high.astype(bf16), 'z', [(z, z ^ 1) for z in range(Z)])]
    ppermute x15 -> x32, waiting for transfers between devices: 29.6 us -> 43 us  [moved(): return lax.ppermute(value, axis, [(i, (i + by) % n) for i in range(n)])]
    unnamed x38 -> x30, local copies, waits for them, and re-layouts: 11.7 us -> 0.92 us
    slice x1 -> x6, local copies, waits for them, and re-layouts: 0.03 us -> 2.25 us  [the longest x1 1.13 us: scatter_y_first(): up = moved(jnp.concatenate([one[:h] + up, one[h:]], 0).astype(bf16), 'y', 1)]
    pallas_call x1, Pallas kernels: 7.15 us -> 9.11 us  [gradient(): pl.pallas_call(grad_kernel, grid=(pl.cdiv(ff, tile),), in_specs=[pl.Block...]
    convert_element_type x6 -> x8, other arithmetic: 3.37 us -> 1.61 us  [the longest x2 1.17 us: scatter_z_first(): down = moved((m + down.astype(f32)).astype(bf16), 'z', -1)]
  transfers between devices with their start and end apart: 30 -> 37, of which waited for: 24 -> 26; matrix products, arithmetic and copies ran while one was open for 1% -> 3% of each run, Pallas kernels for 0% -> 0%
where the time goes in v3:
time: 145 us
  starting transfers between devices  62.4 us (43%)
  waiting for transfers between devices  54.1 us (37%)
  Pallas kernels  9.11 us (6%)
  matrix products  9.08 us (6%)
  other arithmetic  5.39 us (4%)
  local copies, waits for them, and re-layouts  3.69 us (3%)
    ppermute x32, waiting for transfers between devices, moved(): return lax.ppermute(value, axis, [(i, (i + by) % n) for i in range(n)])  43 us
    ppermute x32, starting transfers between devices, moved(): return lax.ppermute(value, axis, [(i, (i + by) % n) for i in range(n)])  40.9 us
    ppermute x4, starting transfers between devices, spread(): moved_in = lax.ppermute(sent, ('z', 'y', 'x', 'c'), pairs)  21.4 us
    pallas_call x1, Pallas kernels, gradient(): pl.pallas_call(grad_kernel, grid=(pl.cdiv(ff, tile),), in_specs=[pl.Block...  9.11 us
    ppermute x4, waiting for transfers between devices, spread(): moved_in = lax.ppermute(sent, ('z', 'y', 'x', 'c'), pairs)  7.74 us
    dot_general x1, matrix products, shards(): update = jnp.dot(ordered, all_rows, preferred_element_type=f32).astype(bf16)  4.56 us
    ppermute x1, waiting for transfers between devices, scatter_y_first(): lax.ppermute(high.astype(bf16), 'z', [(z, z ^ 1) for z in range(Z)])  3.35 us
    dot_general x1, matrix products, project(): lax.dot_general(near_order(rank), basis, lanes, preferred_element_type=f32)  3.02 us
  transfers between devices with their start and end apart: 37, of which 26 were waited for; matrix products, arithmetic and copies ran while one was open for 3% of the time, Pallas kernels for 0%

profile of v3, /device:TPU:1, one launch (start us, length us, event | category | flops | bytes accessed | tf_op | source)
XLA Modules:
  0.0 144.9 jit_solution(14802369331566657901)
XLA Ops:
  0.7 3.0 %convolution_convert_fusion.1 = bf16[512,1024]{1,0:T(8,128)(2,1)S(1)} fusion(bf16[1024,512]{1,0:T(8,128)(2,1)} %param.6, s32[512]{0:T(512)S(1)} %get-tuple-element.58, s32[512]{0:T(512)S(1)} %get-tuple-element.60, s32[512]{0:T(512)S(1)} %get-tuple-element.57, s32[512]{0:T(512)S(1)} %get-tuple-element.64, s32[]{:T(128)} %axis_index.35, ...), kind=kOutput, calls=%fused_computation.31 | convolution fusion | flops 548667392 | bytes 2110984 | tf_op jit(solution)/shard_map/dot_general | solution.py:93
  4.5 3.3 %collective-permute-start = (f32[256,1024]{1,0:T(8,128)S(1)}, f32[256,1024]{1,0:T(8,128)S(1)}, u32[]{:S(2)}, u32[]{:S(2)}) collective-permute-start(f32[256,1024]{1,0:T(8,128)S(1)} %fusion.36), channel_id=1, source_target_pairs={{0,1},{1,0},{2,3},{3,2},{4,5},{5,4},{6,7},{7,6},{8,9},{9,8},{10,11... | collective-permute-start | bytes 3145736 | tf_op jit(solution)/shard_map/ppermute | solution.py:17
  7.8 2.3 %collective-permute-done = f32[256,1024]{1,0:T(8,128)S(1)} collective-permute-done((f32[256,1024]{1,0:T(8,128)S(1)}, f32[256,1024]{1,0:T(8,128)S(1)}, u32[]{:S(2)}, u32[]{:S(2)}) %collective-permute-start) | collective-permute-done | bytes 1048608 | tf_op jit(solution)/shard_map/ppermute | solution.py:17
  10.9 1.1 collective-permute-start.3
  13.5 3.7 %collective-permute-done.3 = bf16[64,1024]{1,0:T(8,128)(2,1)S(1)} collective-permute-done((bf16[64,1024]{1,0:T(8,128)(2,1)S(1)}, bf16[64,1024]{1,0:T(8,128)(2,1)S(1)}, u32[]{:S(2)}, u32[]{:S(2)}) %collective-permute-start.3) | collective-permute-done | bytes 131104 | tf_op jit(solution)/shard_map/ppermute | solution.py:17
  17.2 1.2 collective-permute-done.2
  18.4 1.9 %collective-permute-done.1 = bf16[64,1024]{1,0:T(8,128)(2,1)S(1)} collective-permute-done((bf16[64,1024]{1,0:T(8,128)(2,1)S(1)}, bf16[64,1024]{1,0:T(8,128)(2,1)S(1)}, u32[]{:S(2)}, u32[]{:S(2)}) %collective-permute-start.1) | collective-permute-done | bytes 131104 | tf_op jit(solution)/shard_map/ppermute | solution.py:17
  20.4 1.3 collective-permute-start.6
  22.8 1.5 %collective-permute-done.6 = bf16[64,1024]{1,0:T(8,128)(2,1)S(1)} collective-permute-done((bf16[64,1024]{1,0:T(8,128)(2,1)S(1)}, bf16[64,1024]{1,0:T(8,128)(2,1)S(1)}, u32[]{:S(2)}, u32[]{:S(2)}) %collective-permute-start.6) | collective-permute-done | bytes 131104 | tf_op jit(solution)/shard_map/ppermute | solution.py:17
  24.3 3.1 %collective-permute-done.5 = bf16[64,1024]{1,0:T(8,128)(2,1)S(1)} collective-permute-done((bf16[64,1024]{1,0:T(8,128)(2,1)S(1)}, bf16[64,1024]{1,0:T(8,128)(2,1)S(1)}, u32[]{:S(2)}, u32[]{:S(2)}) %collective-permute-start.5) | collective-permute-done | bytes 131104 | tf_op jit(solution)/shard_map/ppermute | solution.py:17
  27.4 4.0 %collective-permute-done.4 = bf16[64,1024]{1,0:T(8,128)(2,1)S(1)} collective-permute-done((bf16[64,1024]{1,0:T(8,128)(2,1)S(1)}, bf16[64,1024]{1,0:T(8,128)(2,1)S(1)}, u32[]{:S(2)}, u32[]{:S(2)}) %collective-permute-start.4) | collective-permute-done | bytes 131104 | tf_op jit(solution)/shard_map/ppermute | solution.py:17
  32.1 1.5 %collective-permute-done.7.other_ref = bf16[256,1024]{1,0:T(8,128)(2,1)S(1)} collective-permute-done((bf16[256,1024]{1,0:T(8,128)(2,1)S(1)}, bf16[256,1024]{1,0:T(8,128)(2,1)S(1)}, u32[]{:S(2)}, u32[]{:S(2)}) %collective-permute-start.7) | collective-permute-done | bytes 524320 | tf_op jit(solution)/shard_map/ppermute | solution.py:17
  34.3 9.1 %shard_map.76 = (bf16[32,3696]{1,0:T(8,128)(2,1)}, bf16[32,3696]{1,0:T(8,128)(2,1)}, f32[64,3696]{1,0:T(8,128)}, f32[64,3696]{1,0:T(8,128)}, f32[64,3696]{1,0:T(...) custom-call(s32[4]{0:T(128)S(1)} %pad_add_fusion.here, ...), custom_call_target="tpu_custom_call" | custom-call | flops 3875536896 | bytes 14192640 | tf_op jit(solution)/shard_map/pallas_call | solution.py:61
  43.5 5.6 %collective-permute-start.20 = (bf16[32,3696]{1,0:T(8,128)(2,1)}, bf16[32,3696]{1,0:T(8,128)(2,1)}, u32[]{:S(2)}, u32[]{:S(2)}) collective-permute-start(bf16[32,3696]{1,0:T(8,128)(2,1)} %get-tuple-element.28), channel_id=1, source_target_pairs={{0,224},{32,0},{64,32},{96,64},{128,96},{160,128},{192,160},{224,1... | collective-permute-start | bytes 709640 | tf_op jit(solution)/shard_map/ppermute | solution.py:17
  49.1 2.7 %collective-permute-start.10 = (bf16[32,3696]{1,0:T(8,128)(2,1)}, bf16[32,3696]{1,0:T(8,128)(2,1)S(1)}, u32[]{:S(2)}, u32[]{:S(2)}) collective-permute-start(bf16[32,3696]{1,0:T(8,128)(2,1)} %get-tuple-element.20), channel_id=1, source_target_pairs={{0,24},{8,0},{16,8},{24,16},{1,25},{9,1},{17,9},{25,17},{2,26},{10... | collective-permute-start | bytes 709640 | tf_op jit(solution)/shard_map/ppermute | solution.py:17
  51.8 1.0 slice.162
  52.9 1.1 slice.163
  54.3 1.1 add_convert_fusion.1
  55.5 3.4 %collective-permute-start.21 = (bf16[32,3696]{1,0:T(8,128)(2,1)S(1)}, bf16[32,3696]{1,0:T(8,128)(2,1)S(1)}, u32[]{:S(2)}, u32[]{:S(2)}) collective-permute-start(bf16[32,3696]{1,0:T(8,128)(2,1)S(1)} %add_convert_fusion.1), channel_id=1, source_target_pairs={{0,224},{32,0},{64,32},{96,64},{128,96},{160,128},{192,160},{224,1... | collective-permute-start | bytes 709640 | tf_op jit(solution)/shard_map/ppermute | solution.py:17
  59.1 2.8 %collective-permute-start.11 = (bf16[64,3696]{1,0:T(8,128)(2,1)S(1)}, bf16[64,3696]{1,0:T(8,128)(2,1)S(1)}, u32[]{:S(2)}, u32[]{:S(2)}) collective-permute-start(bf16[64,3696]{1,0:T(8,128)(2,1)S(1)} %pad_maximum_fusion.4), channel_id=1, source_target_pairs={{0,24},{8,0},{16,8},{24,16},{1,25},{9,1},{17,9},{25,17},{2,26},{10... | collective-permute-start | bytes 1419272 | tf_op jit(solution)/shard_map/ppermute | solution.py:17
  62.7 3.5 %collective-permute-start.22 = (bf16[32,3696]{1,0:T(8,128)(2,1)S(1)}, bf16[32,3696]{1,0:T(8,128)(2,1)S(1)}, u32[]{:S(2)}, u32[]{:S(2)}) collective-permute-start(bf16[32,3696]{1,0:T(8,128)(2,1)S(1)} %add_convert_fusion), channel_id=1, source_target_pairs={{0,224},{32,0},{64,32},{96,64},{128,96},{160,128},{192,160},{224,1... | collective-permute-start | bytes 709640 | tf_op jit(solution)/shard_map/ppermute | solution.py:17
  66.4 4.3 %collective-permute-done.11 = bf16[64,3696]{1,0:T(8,128)(2,1)S(1)} collective-permute-done((bf16[64,3696]{1,0:T(8,128)(2,1)S(1)}, bf16[64,3696]{1,0:T(8,128)(2,1)S(1)}, u32[]{:S(2)}, u32[]{:S(2)}) %collective-permute-start.11) | collective-permute-done | bytes 473120 | tf_op jit(solution)/shard_map/ppermute | solution.py:17
  70.6 3.4 %collective-permute-done.9 = bf16[64,3696]{1,0:T(8,128)(2,1)S(1)} collective-permute-done((bf16[64,3696]{1,0:T(8,128)(2,1)S(1)}, bf16[64,3696]{1,0:T(8,128)(2,1)S(1)}, u32[]{:S(2)}, u32[]{:S(2)}) %collective-permute-start.9) | collective-permute-done | bytes 473120 | tf_op jit(solution)/shard_map/ppermute | solution.py:17
  74.3 1.5 %collective-permute-start.19 = (bf16[32,3696]{1,0:T(8,128)(2,1)S(1)}, bf16[32,3696]{1,0:T(8,128)(2,1)S(1)}, u32[]{:S(2)}, u32[]{:S(2)}) collective-permute-start(bf16[32,3696]{1,0:T(8,128)(2,1)S(1)} %add_convert_fusion.2), channel_id=1, source_target_pairs={{0,32},{32,64},{64,96},{96,128},{128,160},{160,192},{192,224},{224... | collective-permute-start | bytes 709640 | tf_op jit(solution)/shard_map/ppermute | solution.py:17
  75.8 3.4 %collective-permute-done.12 = bf16[32,3696]{1,0:T(8,128)(2,1)S(1)} collective-permute-done((bf16[32,3696]{1,0:T(8,128)(2,1)S(1)}, bf16[32,3696]{1,0:T(8,128)(2,1)S(1)}, u32[]{:S(2)}, u32[]{:S(2)}) %collective-permute-start.12) | collective-permute-done | bytes 236576 | tf_op jit(solution)/shard_map/ppermute | solution.py:114
  79.4 2.1 %collective-permute-start.15 = (bf16[8,3696]{1,0:T(8,128)(2,1)S(1)}, bf16[8,3696]{1,0:T(8,128)(2,1)S(1)}, u32[]{:S(2)}, u32[]{:S(2)}) collective-permute-start(bf16[8,3696]{1,0:T(8,128)(2,1)S(1)} %get-tuple-element.46), channel_id=1, source_target_pairs={{0,192},{32,224},{64,0},{96,32},{128,64},{160,96},{192,128},{224,1... | collective-permute-start | bytes 177416 | tf_op jit(solution)/shard_map/ppermute | solution.py:17
  81.8 2.3 %collective-permute-start.13 = (bf16[8,3696]{1,0:T(8,128)(2,1)S(1)}, bf16[8,3696]{1,0:T(8,128)(2,1)S(1)}, u32[]{:S(2)}, u32[]{:S(2)}) collective-permute-start(bf16[8,3696]{1,0:T(8,128)(2,1)S(1)} %get-tuple-element.45), channel_id=1, source_target_pairs={{0,128},{32,160},{64,192},{96,224},{128,0},{160,32},{192,64},{224,... | collective-permute-start | bytes 177416 | tf_op jit(solution)/shard_map/ppermute | solution.py:17
  84.3 1.5 %collective-permute-start.24 = (bf16[8,3696]{1,0:T(8,128)(2,1)S(1)}, bf16[8,3696]{1,0:T(8,128)(2,1)S(1)}, u32[]{:S(2)}, u32[]{:S(2)}) collective-permute-start(bf16[8,3696]{1,0:T(8,128)(2,1)S(1)} %get-tuple-element.50), channel_id=1, source_target_pairs={{0,8},{8,16},{16,24},{24,0},{1,9},{9,17},{17,25},{25,1},{2,10},{10... | collective-permute-start | bytes 177416 | tf_op jit(solution)/shard_map/ppermute | solution.py:17
  85.7 1.9 %collective-permute-done.14 = bf16[8,3696]{1,0:T(8,128)(2,1)S(1)} collective-permute-done((bf16[8,3696]{1,0:T(8,128)(2,1)S(1)}, bf16[8,3696]{1,0:T(8,128)(2,1)S(1)}, u32[]{:S(2)}, u32[]{:S(2)}) %collective-permute-start.14) | collective-permute-done | bytes 59168 | tf_op jit(solution)/shard_map/ppermute | solution.py:17
  87.7 2.3 %collective-permute-done.13 = bf16[8,3696]{1,0:T(8,128)(2,1)S(1)} collective-permute-done((bf16[8,3696]{1,0:T(8,128)(2,1)S(1)}, bf16[8,3696]{1,0:T(8,128)(2,1)S(1)}, u32[]{:S(2)}, u32[]{:S(2)}) %collective-permute-start.13) | collective-permute-done | bytes 59168 | tf_op jit(solution)/shard_map/ppermute | solution.py:17
  90.3 0.9 divide_convert_fusion
  91.8 1.6 %collective-permute-start.28 = (bf16[16,924]{1,0:T(8,128)(2,1)S(1)}, bf16[16,924]{1,0:T(8,128)(2,1)S(1)}, u32[]{:S(2)}, u32[]{:S(2)}) collective-permute-start(bf16[16,924]{1,0:T(8,128)(2,1)S(1)} %bitcast.50), channel_id=1, source_target_pairs={{0,24},{8,0},{16,8},{24,16},{1,25},{9,1},{17,9},{25,17},{2,26},{10... | collective-permute-start | bytes 88712 | tf_op jit(solution)/shard_map/ppermute | solution.py:17
  94.2 0.9 collective-permute-done.28
  95.2 2.8 %collective-permute-done.27 = bf16[16,924]{1,0:T(8,128)(2,1)S(1)} collective-permute-done((bf16[16,924]{1,0:T(8,128)(2,1)S(1)}, bf16[16,924]{1,0:T(8,128)(2,1)S(1)}, u32[]{:S(2)}, u32[]{:S(2)}) %collective-permute-start.27) | collective-permute-done | bytes 29600 | tf_op jit(solution)/shard_map/ppermute | solution.py:17
  99.8 2.3 %collective-permute-done.29 = bf16[4,16,924]{2,1,0:T(8,128)(2,1)S(1)} collective-permute-done((bf16[4,16,924]{2,1,0:T(8,128)(2,1)S(1)}, bf16[4,16,924]{2,1,0:T(8,128)(2,1)S(1)}, u32[]{:S(2)}, u32[]{:S(2)}) %collective-permute-start.29) | collective-permute-done | bytes 118304 | tf_op jit(solution)/shard_map/ppermute | solution.py:17
  102.1 1.8 %collective-permute-done.30 = bf16[4,16,924]{2,1,0:T(8,128)(2,1)S(1)} collective-permute-done((bf16[4,16,924]{2,1,0:T(8,128)(2,1)S(1)}, bf16[4,16,924]{2,1,0:T(8,128)(2,1)S(1)}, u32[]{:S(2)}, u32[]{:S(2)}) %collective-permute-start.30) | collective-permute-done | bytes 118304 | tf_op jit(solution)/shard_map/ppermute | solution.py:17
  104.0 1.3 collective-permute-done.31
  105.3 15.0 %collective-permute-start.35 = (bf16[4,16,924]{2,1,0:T(8,128)(2,1)S(1)}, bf16[4,16,924]{2,1,0:T(8,128)(2,1)S(1)}, u32[]{:S(2)}, u32[]{:S(2)}) collective-permute-start(bf16[4,16,924]{2,1,0:T(8,128)(2,1)S(1)} %get-tuple-element.39), channel_id=1, source_target_pairs={{0,192},{2,194},{4,196},{6,198},{8,200},{10,202},{12,204},{14,206}... | collective-permute-start | bytes 354824 | tf_op jit(solution)/shard_map/ppermute | solution.py:165
  120.4 1.9 %collective-permute-start.32 = (bf16[4,16,924]{2,1,0:T(8,128)(2,1)S(1)}, bf16[4,16,924]{2,1,0:T(8,128)(2,1)S(1)}, u32[]{:S(2)}, u32[]{:S(2)}) collective-permute-start(bf16[4,16,924]{2,1,0:T(8,128)(2,1)S(1)} %get-tuple-element.38), channel_id=1, source_target_pairs={{1,32},{3,34},{5,36},{7,38},{9,40},{11,42},{13,44},{15,46},{17,48}... | collective-permute-start | bytes 354824 | tf_op jit(solution)/shard_map/ppermute | solution.py:165
  122.3 1.8 %collective-permute-start.34 = (bf16[4,16,924]{2,1,0:T(8,128)(2,1)S(1)}, bf16[4,16,924]{2,1,0:T(8,128)(2,1)S(1)}, u32[]{:S(2)}, u32[]{:S(2)}) collective-permute-start(bf16[4,16,924]{2,1,0:T(8,128)(2,1)S(1)} %get-tuple-element.41), channel_id=1, source_target_pairs={{0,128},{2,130},{4,132},{6,134},{8,136},{10,138},{12,140},{14,142}... | collective-permute-start | bytes 354824 | tf_op jit(solution)/shard_map/ppermute | solution.py:165
  124.1 2.7 %collective-permute-start.33 = (bf16[4,16,924]{2,1,0:T(8,128)(2,1)S(1)}, bf16[4,16,924]{2,1,0:T(8,128)(2,1)S(1)}, u32[]{:S(2)}, u32[]{:S(2)}) collective-permute-start(bf16[4,16,924]{2,1,0:T(8,128)(2,1)S(1)} %get-tuple-element.40), channel_id=1, source_target_pairs={{0,64},{2,66},{4,68},{6,70},{8,72},{10,74},{12,76},{14,78},{16,80}... | collective-permute-start | bytes 354824 | tf_op jit(solution)/shard_map/ppermute | solution.py:165
  126.8 2.9 %collective-permute-done.32 = bf16[4,16,924]{2,1,0:T(8,128)(2,1)S(1)} collective-permute-done((bf16[4,16,924]{2,1,0:T(8,128)(2,1)S(1)}, bf16[4,16,924]{2,1,0:T(8,128)(2,1)S(1)}, u32[]{:S(2)}, u32[]{:S(2)}) %collective-permute-start.32) | collective-permute-done | bytes 118304 | tf_op jit(solution)/shard_map/ppermute | solution.py:165
  129.7 2.4 %collective-permute-done.34 = bf16[4,16,924]{2,1,0:T(8,128)(2,1)S(1)} collective-permute-done((bf16[4,16,924]{2,1,0:T(8,128)(2,1)S(1)}, bf16[4,16,924]{2,1,0:T(8,128)(2,1)S(1)}, u32[]{:S(2)}, u32[]{:S(2)}) %collective-permute-start.34) | collective-permute-done | bytes 118304 | tf_op jit(solution)/shard_map/ppermute | solution.py:165
  132.1 2.5 %collective-permute-done.33 = bf16[4,16,924]{2,1,0:T(8,128)(2,1)S(1)} collective-permute-done((bf16[4,16,924]{2,1,0:T(8,128)(2,1)S(1)}, bf16[4,16,924]{2,1,0:T(8,128)(2,1)S(1)}, u32[]{:S(2)}, u32[]{:S(2)}) %collective-permute-start.33) | collective-permute-done | bytes 118304 | tf_op jit(solution)/shard_map/ppermute | solution.py:165
  134.7 1.8 %collective-permute-start.36 = (bf16[4,4,16,924]{3,2,1,0:T(8,128)(2,1)S(1)}, bf16[4,4,16,924]{3,2,1,0:T(8,128)(2,1)}, u32[]{:S(2)}, u32[]{:S(2)}) collective-permute-start(bf16[4,4,16,924]{3,2,1,0:T(8,128)(2,1)S(1)} %get-tuple-element.37), channel_id=1, source_target_pairs={{0,1},{1,0},{2,3},{3,2},{4,5},{5,4},{6,7},{7,6},{8,9},{9,8},{10,11... | collective-permute-start | bytes 1419272 | tf_op jit(solution)/shard_map/ppermute | solution.py:17
  136.5 1.6 %collective-permute-done.36 = bf16[4,4,16,924]{3,2,1,0:T(8,128)(2,1)} collective-permute-done((bf16[4,4,16,924]{3,2,1,0:T(8,128)(2,1)S(1)}, bf16[4,4,16,924]{3,2,1,0:T(8,128)(2,1)}, u32[]{:S(2)}, u32[]{:S(2)}) %collective-permute-start.36) | collective-permute-done | bytes 473120 | tf_op jit(solution)/shard_map/ppermute | solution.py:17
  138.2 2.1 %pad_maximum_fusion = bf16[2,4,4,16,924]{4,3,2,1,0:T(8,128)(2,1)} fusion(bf16[1,4,4,16,924]{4,3,2,1,0:T(8,128)(2,1)} %bitcast.17, bf16[1,4,4,16,924]{4,3,2,1,0:T(8,128)(2,1)S(1)} %get-tuple-element.36), kind=kLoop, calls=%fused_computation.57 | loop fusion | flops 473088 | bytes 1892352 | tf_op jit(solution)/shard_map/stack | solution.py:193
  140.3 4.6 %convolution_convert_fusion = bf16[1024,924]{0,1:T(8,128)(2,1)} fusion(bf16[512,924]{1,0:T(8,128)(2,1)} %bitcast.34, bf16[1024,512]{1,0:T(8,128)(2,1)} %param.6, s32[512]{0:T(512)S(1)} %get-tuple-element.66, s32[512]{0:T(512)S(1)} %get-tuple-element.67, s32[512]{0:T(512)S(1)} %get-tuple-element.65, s32[512]{0:T(512)S(1)} %get-tuple-element.68, ...), kind=kOutput, calls=%fused_computation.9 | convolution fusion | flops 1525575680 | bytes 3905548 | tf_op jit(solution)/shard_map/dot_general | solution.py:195
  (102 shorter events, 11.8 us)
Async XLA Ops:
  0.6 3.1 %copy-start = (bf16[1024,1024]{1,0:T(8,128)(2,1)S(1)}, bf16[1024,1024]{1,0:T(8,128)(2,1)}, u32[]{:S(2)}) copy-start(bf16[1024,1024]{1,0:T(8,128)(2,1)} %param.5) | copy-start | bytes 6291460
  4.5 5.6 %collective-permute-start = (f32[256,1024]{1,0:T(8,128)S(1)}, f32[256,1024]{1,0:T(8,128)S(1)}, u32[]{:S(2)}, u32[]{:S(2)}) collective-permute-start(f32[256,1024]{1,0:T(8,128)S(1)} %fusion.36), channel_id=1, source_target_pairs={{0,1},{1,0},{2,3},{3,2},{4,5},{5,4},{6,7},{7,6},{8,9},{9,8},{10,11... | collective-permute-start | bytes 3145736 | tf_op jit(solution)/shard_map/ppermute | solution.py:17
  10.9 6.3 %collective-permute-start.3 = (bf16[64,1024]{1,0:T(8,128)(2,1)S(1)}, bf16[64,1024]{1,0:T(8,128)(2,1)S(1)}, u32[]{:S(2)}, u32[]{:S(2)}) collective-permute-start(bf16[64,1024]{1,0:T(8,128)(2,1)S(1)} %get-tuple-element.43), channel_id=1, source_target_pairs={{0,4},{2,6},{4,0},{6,2},{1,5},{3,7},{5,1},{7,3},{8,12},{10,14},{12... | collective-permute-start | bytes 393224 | tf_op jit(solution)/shard_map/ppermute | solution.py:17
  12.0 6.4 %collective-permute-start.2 = (bf16[64,1024]{1,0:T(8,128)(2,1)S(1)}, bf16[64,1024]{1,0:T(8,128)(2,1)S(1)}, u32[]{:S(2)}, u32[]{:S(2)}) collective-permute-start(bf16[64,1024]{1,0:T(8,128)(2,1)S(1)} %get-tuple-element.44), channel_id=1, source_target_pairs={{0,6},{2,0},{4,2},{6,4},{1,7},{3,1},{5,3},{7,5},{8,14},{10,8},{12,... | collective-permute-start | bytes 393224 | tf_op jit(solution)/shard_map/ppermute | solution.py:17
  12.9 7.4 %collective-permute-start.1 = (bf16[64,1024]{1,0:T(8,128)(2,1)S(1)}, bf16[64,1024]{1,0:T(8,128)(2,1)S(1)}, u32[]{:S(2)}, u32[]{:S(2)}) collective-permute-start(bf16[64,1024]{1,0:T(8,128)(2,1)S(1)} %get-tuple-element.42), channel_id=1, source_target_pairs={{0,2},{2,4},{4,6},{6,0},{1,3},{3,5},{5,7},{7,1},{8,10},{10,12},{12... | collective-permute-start | bytes 393224 | tf_op jit(solution)/shard_map/ppermute | solution.py:17
  20.4 3.9 %collective-permute-start.6 = (bf16[64,1024]{1,0:T(8,128)(2,1)S(1)}, bf16[64,1024]{1,0:T(8,128)(2,1)S(1)}, u32[]{:S(2)}, u32[]{:S(2)}) collective-permute-start(bf16[64,1024]{1,0:T(8,128)(2,1)S(1)} %fusion.105), channel_id=1, source_target_pairs={{0,6},{2,0},{4,2},{6,4},{1,7},{3,1},{5,3},{7,5},{8,14},{10,8},{12,... | collective-permute-start | bytes 393224 | tf_op jit(solution)/shard_map/ppermute | solution.py:17
  21.6 5.8 %collective-permute-start.5 = (bf16[64,1024]{1,0:T(8,128)(2,1)S(1)}, bf16[64,1024]{1,0:T(8,128)(2,1)S(1)}, u32[]{:S(2)}, u32[]{:S(2)}) collective-permute-start(bf16[64,1024]{1,0:T(8,128)(2,1)S(1)} %fusion.105), channel_id=1, source_target_pairs={{0,4},{2,6},{4,0},{6,2},{1,5},{3,7},{5,1},{7,3},{8,12},{10,14},{12... | collective-permute-start | bytes 393224 | tf_op jit(solution)/shard_map/ppermute | solution.py:17
  22.2 9.2 %collective-permute-start.4 = (bf16[64,1024]{1,0:T(8,128)(2,1)S(1)}, bf16[64,1024]{1,0:T(8,128)(2,1)S(1)}, u32[]{:S(2)}, u32[]{:S(2)}) collective-permute-start(bf16[64,1024]{1,0:T(8,128)(2,1)S(1)} %fusion.105), channel_id=1, source_target_pairs={{0,2},{2,4},{4,6},{6,0},{1,3},{3,5},{5,7},{7,1},{8,10},{10,12},{12... | collective-permute-start | bytes 393224 | tf_op jit(solution)/shard_map/ppermute | solution.py:17
  31.4 2.1 %collective-permute-start.7 = (bf16[256,1024]{1,0:T(8,128)(2,1)S(1)}, bf16[256,1024]{1,0:T(8,128)(2,1)S(1)}, u32[]{:S(2)}, u32[]{:S(2)}) collective-permute-start(bf16[256,1024]{1,0:T(8,128)(2,1)S(1)} %pad_maximum_fusion.1.mine_ref), channel_id=1, source_target_pairs={{0,1},{1,0},{2,3},{3,2},{4,5},{5,4},{6,7},{7,6},{8,9},{9,8},{10,11... | collective-permute-start | bytes 1572872 | tf_op jit(solution)/shard_map/ppermute | solution.py:17
  43.4 15.4 %copy-start.9 = (f32[32,3696]{1,0:T(8,128)S(1)}, f32[32,3696]{1,0:T(8,128)}, u32[]{:S(2)}) copy-start(f32[32,3696]{1,0:T(8,128)} %get-tuple-element.24) | copy-start | bytes 1419268
  43.5 15.5 %copy-start.3 = (f32[64,3696]{1,0:T(8,128)S(1)}, f32[64,3696]{1,0:T(8,128)}, u32[]{:S(2)}) copy-start(f32[64,3696]{1,0:T(8,128)} %get-tuple-element.19) | copy-start | bytes 2838532
  43.5 10.8 %collective-permute-start.20 = (bf16[32,3696]{1,0:T(8,128)(2,1)}, bf16[32,3696]{1,0:T(8,128)(2,1)}, u32[]{:S(2)}, u32[]{:S(2)}) collective-permute-start(bf16[32,3696]{1,0:T(8,128)(2,1)} %get-tuple-element.28), channel_id=1, source_target_pairs={{0,224},{32,0},{64,32},{96,64},{128,96},{160,128},{192,160},{224,1... | collective-permute-start | bytes 709640 | tf_op jit(solution)/shard_map/ppermute | solution.py:17
  49.1 9.7 %collective-permute-start.16 = (bf16[32,3696]{1,0:T(8,128)(2,1)}, bf16[32,3696]{1,0:T(8,128)(2,1)S(1)}, u32[]{:S(2)}, u32[]{:S(2)}) collective-permute-start(bf16[32,3696]{1,0:T(8,128)(2,1)} %get-tuple-element.25), channel_id=1, source_target_pairs={{0,32},{32,64},{64,96},{96,128},{128,160},{160,192},{192,224},{224... | collective-permute-start | bytes 709640 | tf_op jit(solution)/shard_map/ppermute | solution.py:17
  49.1 9.9 %collective-permute-start.10 = (bf16[32,3696]{1,0:T(8,128)(2,1)}, bf16[32,3696]{1,0:T(8,128)(2,1)S(1)}, u32[]{:S(2)}, u32[]{:S(2)}) collective-permute-start(bf16[32,3696]{1,0:T(8,128)(2,1)} %get-tuple-element.20), channel_id=1, source_target_pairs={{0,24},{8,0},{16,8},{24,16},{1,25},{9,1},{17,9},{25,17},{2,26},{10... | collective-permute-start | bytes 709640 | tf_op jit(solution)/shard_map/ppermute | solution.py:17
  52.9 9.2 %copy-start.2 = (f32[64,3696]{1,0:T(8,128)S(1)}, f32[64,3696]{1,0:T(8,128)}, u32[]{:S(2)}) copy-start(f32[64,3696]{1,0:T(8,128)} %get-tuple-element.17) | copy-start | bytes 2838532
  54.0 8.0 %collective-permute-start.8 = (bf16[32,3696]{1,0:T(8,128)(2,1)}, bf16[32,3696]{1,0:T(8,128)(2,1)S(1)}, u32[]{:S(2)}, u32[]{:S(2)}) collective-permute-start(bf16[32,3696]{1,0:T(8,128)(2,1)} %get-tuple-element.18), channel_id=1, source_target_pairs={{0,8},{8,16},{16,24},{24,0},{1,9},{9,17},{17,25},{25,1},{2,10},{10... | collective-permute-start | bytes 709640 | tf_op jit(solution)/shard_map/ppermute | solution.py:17
  55.5 7.2 %collective-permute-start.21 = (bf16[32,3696]{1,0:T(8,128)(2,1)S(1)}, bf16[32,3696]{1,0:T(8,128)(2,1)S(1)}, u32[]{:S(2)}, u32[]{:S(2)}) collective-permute-start(bf16[32,3696]{1,0:T(8,128)(2,1)S(1)} %add_convert_fusion.1), channel_id=1, source_target_pairs={{0,224},{32,0},{64,32},{96,64},{128,96},{160,128},{192,160},{224,1... | collective-permute-start | bytes 709640 | tf_op jit(solution)/shard_map/ppermute | solution.py:17
  58.9 3.8 %copy-start.8 = (f32[32,3696]{1,0:T(8,128)S(1)}, f32[32,3696]{1,0:T(8,128)}, u32[]{:S(2)}) copy-start(f32[32,3696]{1,0:T(8,128)} %get-tuple-element.26) | copy-start | bytes 1419268
  58.9 7.3 %collective-permute-start.17 = (bf16[32,3696]{1,0:T(8,128)(2,1)S(1)}, bf16[32,3696]{1,0:T(8,128)(2,1)S(1)}, u32[]{:S(2)}, u32[]{:S(2)}) collective-permute-start(bf16[32,3696]{1,0:T(8,128)(2,1)S(1)} %add_convert_fusion.4), channel_id=1, source_target_pairs={{0,32},{32,64},{64,96},{96,128},{128,160},{160,192},{192,224},{224... | collective-permute-start | bytes 709640 | tf_op jit(solution)/shard_map/ppermute | solution.py:17
  59.1 7.2 %copy-start.7 = (f32[32,3696]{1,0:T(8,128)S(1)}, f32[32,3696]{1,0:T(8,128)}, u32[]{:S(2)}) copy-start(f32[32,3696]{1,0:T(8,128)} %get-tuple-element.23) | copy-start | bytes 1419268
  59.1 14.9 %copy-start.1 = (f32[64,3696]{1,0:T(8,128)S(1)}, f32[64,3696]{1,0:T(8,128)}, u32[]{:S(2)}) copy-start(f32[64,3696]{1,0:T(8,128)} %get-tuple-element.16) | copy-start | bytes 2838532
  59.1 11.5 %collective-permute-start.11 = (bf16[64,3696]{1,0:T(8,128)(2,1)S(1)}, bf16[64,3696]{1,0:T(8,128)(2,1)S(1)}, u32[]{:S(2)}, u32[]{:S(2)}) collective-permute-start(bf16[64,3696]{1,0:T(8,128)(2,1)S(1)} %pad_maximum_fusion.4), channel_id=1, source_target_pairs={{0,24},{8,0},{16,8},{24,16},{1,25},{9,1},{17,9},{25,17},{2,26},{10... | collective-permute-start | bytes 1419272 | tf_op jit(solution)/shard_map/ppermute | solution.py:17
  62.1 12.1 %copy-start.6 = (f32[32,3696]{1,0:T(8,128)S(1)}, f32[32,3696]{1,0:T(8,128)}, u32[]{:S(2)}) copy-start(f32[32,3696]{1,0:T(8,128)} %get-tuple-element.22) | copy-start | bytes 1419268
  62.2 11.8 %collective-permute-start.9 = (bf16[64,3696]{1,0:T(8,128)(2,1)S(1)}, bf16[64,3696]{1,0:T(8,128)(2,1)S(1)}, u32[]{:S(2)}, u32[]{:S(2)}) collective-permute-start(bf16[64,3696]{1,0:T(8,128)(2,1)S(1)} %pad_maximum_fusion.3), channel_id=1, source_target_pairs={{0,8},{8,16},{16,24},{24,0},{1,9},{9,17},{17,25},{25,1},{2,10},{10... | collective-permute-start | bytes 1419272 | tf_op jit(solution)/shard_map/ppermute | solution.py:17
  62.7 21.3 %collective-permute-start.22 = (bf16[32,3696]{1,0:T(8,128)(2,1)S(1)}, bf16[32,3696]{1,0:T(8,128)(2,1)S(1)}, u32[]{:S(2)}, u32[]{:S(2)}) collective-permute-start(bf16[32,3696]{1,0:T(8,128)(2,1)S(1)} %add_convert_fusion), channel_id=1, source_target_pairs={{0,224},{32,0},{64,32},{96,64},{128,96},{160,128},{192,160},{224,1... | collective-permute-start | bytes 709640 | tf_op jit(solution)/shard_map/ppermute | solution.py:17
  66.3 7.9 %collective-permute-start.18 = (bf16[32,3696]{1,0:T(8,128)(2,1)S(1)}, bf16[32,3696]{1,0:T(8,128)(2,1)S(1)}, u32[]{:S(2)}, u32[]{:S(2)}) collective-permute-start(bf16[32,3696]{1,0:T(8,128)(2,1)S(1)} %add_convert_fusion.3), channel_id=1, source_target_pairs={{0,32},{32,64},{64,96},{96,128},{128,160},{160,192},{192,224},{224... | collective-permute-start | bytes 709640 | tf_op jit(solution)/shard_map/ppermute | solution.py:17
  74.1 5.0 %collective-permute-start.12 = (bf16[32,3696]{1,0:T(8,128)(2,1)S(1)}, bf16[32,3696]{1,0:T(8,128)(2,1)S(1)}, u32[]{:S(2)}, u32[]{:S(2)}) collective-permute-start(bf16[32,3696]{1,0:T(8,128)(2,1)S(1)} %add_convert_fusion.5), channel_id=1, source_target_pairs={{0,32},{32,0},{64,96},{96,64},{128,160},{160,128},{192,224},{224,1... | collective-permute-start | bytes 709640 | tf_op jit(solution)/shard_map/ppermute | solution.py:114
  74.2 9.9 %copy-start.5 = (f32[32,3696]{1,0:T(8,128)S(1)}, f32[32,3696]{1,0:T(8,128)}, u32[]{:S(2)}) copy-start(f32[32,3696]{1,0:T(8,128)} %get-tuple-element.21) | copy-start | bytes 1419268
  74.3 9.8 %collective-permute-start.19 = (bf16[32,3696]{1,0:T(8,128)(2,1)S(1)}, bf16[32,3696]{1,0:T(8,128)(2,1)S(1)}, u32[]{:S(2)}, u32[]{:S(2)}) collective-permute-start(bf16[32,3696]{1,0:T(8,128)(2,1)S(1)} %add_convert_fusion.2), channel_id=1, source_target_pairs={{0,32},{32,64},{64,96},{96,128},{128,160},{160,192},{192,224},{224... | collective-permute-start | bytes 709640 | tf_op jit(solution)/shard_map/ppermute | solution.py:17
  79.3 11.0 %copy-start.10 = (f32[16,3696]{1,0:T(8,128)S(1)}, f32[16,3696]{1,0:T(8,128)}, u32[]{:S(2)}) copy-start(f32[16,3696]{1,0:T(8,128)} %param.8) | copy-start | bytes 709636
  79.3 11.0 %copy-start.11 = (f32[16,3696]{1,0:T(8,128)S(1)}, f32[16,3696]{1,0:T(8,128)}, u32[]{:S(2)}) copy-start(f32[16,3696]{1,0:T(8,128)} %param.9) | copy-start | bytes 709636
  79.4 6.4 %collective-permute-start.15 = (bf16[8,3696]{1,0:T(8,128)(2,1)S(1)}, bf16[8,3696]{1,0:T(8,128)(2,1)S(1)}, u32[]{:S(2)}, u32[]{:S(2)}) collective-permute-start(bf16[8,3696]{1,0:T(8,128)(2,1)S(1)} %get-tuple-element.46), channel_id=1, source_target_pairs={{0,192},{32,224},{64,0},{96,32},{128,64},{160,96},{192,128},{224,1... | collective-permute-start | bytes 177416 | tf_op jit(solution)/shard_map/ppermute | solution.py:17
  81.5 6.2 %collective-permute-start.14 = (bf16[8,3696]{1,0:T(8,128)(2,1)S(1)}, bf16[8,3696]{1,0:T(8,128)(2,1)S(1)}, u32[]{:S(2)}, u32[]{:S(2)}) collective-permute-start(bf16[8,3696]{1,0:T(8,128)(2,1)S(1)} %get-tuple-element.47), channel_id=1, source_target_pairs={{0,64},{32,96},{64,128},{96,160},{128,192},{160,224},{192,0},{224,... | collective-permute-start | bytes 177416 | tf_op jit(solution)/shard_map/ppermute | solution.py:17
  81.8 8.2 %collective-permute-start.13 = (bf16[8,3696]{1,0:T(8,128)(2,1)S(1)}, bf16[8,3696]{1,0:T(8,128)(2,1)S(1)}, u32[]{:S(2)}, u32[]{:S(2)}) collective-permute-start(bf16[8,3696]{1,0:T(8,128)(2,1)S(1)} %get-tuple-element.45), channel_id=1, source_target_pairs={{0,128},{32,160},{64,192},{96,224},{128,0},{160,32},{192,64},{224,... | collective-permute-start | bytes 177416 | tf_op jit(solution)/shard_map/ppermute | solution.py:17
  84.2 5.8 %collective-permute-start.25 = (bf16[8,3696]{1,0:T(8,128)(2,1)S(1)}, bf16[8,3696]{1,0:T(8,128)(2,1)S(1)}, u32[]{:S(2)}, u32[]{:S(2)}) collective-permute-start(bf16[8,3696]{1,0:T(8,128)(2,1)S(1)} %get-tuple-element.49), channel_id=1, source_target_pairs={{0,24},{8,0},{16,8},{24,16},{1,25},{9,1},{17,9},{25,17},{2,26},{10... | collective-permute-start | bytes 177416 | tf_op jit(solution)/shard_map/ppermute | solution.py:17
  84.3 5.8 %collective-permute-start.24 = (bf16[8,3696]{1,0:T(8,128)(2,1)S(1)}, bf16[8,3696]{1,0:T(8,128)(2,1)S(1)}, u32[]{:S(2)}, u32[]{:S(2)}) collective-permute-start(bf16[8,3696]{1,0:T(8,128)(2,1)S(1)} %get-tuple-element.50), channel_id=1, source_target_pairs={{0,8},{8,16},{16,24},{24,0},{1,9},{9,17},{17,25},{25,1},{2,10},{10... | collective-permute-start | bytes 177416 | tf_op jit(solution)/shard_map/ppermute | solution.py:17
  85.7 4.6 %collective-permute-start.23 = (bf16[8,3696]{1,0:T(8,128)(2,1)S(1)}, bf16[8,3696]{1,0:T(8,128)(2,1)S(1)}, u32[]{:S(2)}, u32[]{:S(2)}) collective-permute-start(bf16[8,3696]{1,0:T(8,128)(2,1)S(1)} %get-tuple-element.48), channel_id=1, source_target_pairs={{0,16},{8,24},{16,0},{24,8},{1,17},{9,25},{17,1},{25,9},{2,18},{10... | collective-permute-start | bytes 177416 | tf_op jit(solution)/shard_map/ppermute | solution.py:17
  91.8 3.4 %collective-permute-start.28 = (bf16[16,924]{1,0:T(8,128)(2,1)S(1)}, bf16[16,924]{1,0:T(8,128)(2,1)S(1)}, u32[]{:S(2)}, u32[]{:S(2)}) collective-permute-start(bf16[16,924]{1,0:T(8,128)(2,1)S(1)} %bitcast.50), channel_id=1, source_target_pairs={{0,24},{8,0},{16,8},{24,16},{1,25},{9,1},{17,9},{25,17},{2,26},{10... | collective-permute-start | bytes 88712 | tf_op jit(solution)/shard_map/ppermute | solution.py:17
  93.4 4.5 %collective-permute-start.27 = (bf16[16,924]{1,0:T(8,128)(2,1)S(1)}, bf16[16,924]{1,0:T(8,128)(2,1)S(1)}, u32[]{:S(2)}, u32[]{:S(2)}) collective-permute-start(bf16[16,924]{1,0:T(8,128)(2,1)S(1)} %bitcast.51), channel_id=1, source_target_pairs={{0,16},{8,24},{16,0},{24,8},{1,17},{9,25},{17,1},{25,9},{2,18},{10... | collective-permute-start | bytes 88712 | tf_op jit(solution)/shard_map/ppermute | solution.py:17
  94.0 4.2 %collective-permute-start.26 = (bf16[16,924]{1,0:T(8,128)(2,1)S(1)}, bf16[16,924]{1,0:T(8,128)(2,1)S(1)}, u32[]{:S(2)}, u32[]{:S(2)}) collective-permute-start(bf16[16,924]{1,0:T(8,128)(2,1)S(1)} %bitcast.52), channel_id=1, source_target_pairs={{0,8},{8,16},{16,24},{24,0},{1,9},{9,17},{17,25},{25,1},{2,10},{10... | collective-permute-start | bytes 88712 | tf_op jit(solution)/shard_map/ppermute | solution.py:17
  98.2 3.9 %collective-permute-start.29 = (bf16[4,16,924]{2,1,0:T(8,128)(2,1)S(1)}, bf16[4,16,924]{2,1,0:T(8,128)(2,1)S(1)}, u32[]{:S(2)}, u32[]{:S(2)}) collective-permute-start(bf16[4,16,924]{2,1,0:T(8,128)(2,1)S(1)} %pad_maximum_fusion.6), channel_id=1, source_target_pairs={{0,6},{2,0},{4,2},{6,4},{1,7},{3,1},{5,3},{7,5},{8,14},{10,8},{12,... | collective-permute-start | bytes 354824 | tf_op jit(solution)/shard_map/ppermute | solution.py:17
  98.5 5.4 %collective-permute-start.30 = (bf16[4,16,924]{2,1,0:T(8,128)(2,1)S(1)}, bf16[4,16,924]{2,1,0:T(8,128)(2,1)S(1)}, u32[]{:S(2)}, u32[]{:S(2)}) collective-permute-start(bf16[4,16,924]{2,1,0:T(8,128)(2,1)S(1)} %pad_maximum_fusion.6), channel_id=1, source_target_pairs={{0,4},{2,6},{4,0},{6,2},{1,5},{3,7},{5,1},{7,3},{8,12},{10,14},{12... | collective-permute-start | bytes 354824 | tf_op jit(solution)/shard_map/ppermute | solution.py:17
  99.1 6.2 %collective-permute-start.31 = (bf16[4,16,924]{2,1,0:T(8,128)(2,1)S(1)}, bf16[4,16,924]{2,1,0:T(8,128)(2,1)S(1)}, u32[]{:S(2)}, u32[]{:S(2)}) collective-permute-start(bf16[4,16,924]{2,1,0:T(8,128)(2,1)S(1)} %pad_maximum_fusion.6), channel_id=1, source_target_pairs={{0,2},{2,4},{4,6},{6,0},{1,3},{3,5},{5,7},{7,1},{8,10},{10,12},{12... | collective-permute-start | bytes 354824 | tf_op jit(solution)/shard_map/ppermute | solution.py:17
  105.3 24.4 %collective-permute-start.35 = (bf16[4,16,924]{2,1,0:T(8,128)(2,1)S(1)}, bf16[4,16,924]{2,1,0:T(8,128)(2,1)S(1)}, u32[]{:S(2)}, u32[]{:S(2)}) collective-permute-start(bf16[4,16,924]{2,1,0:T(8,128)(2,1)S(1)} %get-tuple-element.39), channel_id=1, source_target_pairs={{0,192},{2,194},{4,196},{6,198},{8,200},{10,202},{12,204},{14,206}... | collective-permute-start | bytes 354824 | tf_op jit(solution)/shard_map/ppermute | solution.py:165
  120.4 9.3 %collective-permute-start.32 = (bf16[4,16,924]{2,1,0:T(8,128)(2,1)S(1)}, bf16[4,16,924]{2,1,0:T(8,128)(2,1)S(1)}, u32[]{:S(2)}, u32[]{:S(2)}) collective-permute-start(bf16[4,16,924]{2,1,0:T(8,128)(2,1)S(1)} %get-tuple-element.38), channel_id=1, source_target_pairs={{1,32},{3,34},{5,36},{7,38},{9,40},{11,42},{13,44},{15,46},{17,48}... | collective-permute-start | bytes 354824 | tf_op jit(solution)/shard_map/ppermute | solution.py:165
  122.3 9.8 %collective-permute-start.34 = (bf16[4,16,924]{2,1,0:T(8,128)(2,1)S(1)}, bf16[4,16,924]{2,1,0:T(8,128)(2,1)S(1)}, u32[]{:S(2)}, u32[]{:S(2)}) collective-permute-start(bf16[4,16,924]{2,1,0:T(8,128)(2,1)S(1)} %get-tuple-element.41), channel_id=1, source_target_pairs={{0,128},{2,130},{4,132},{6,134},{8,136},{10,138},{12,140},{14,142}... | collective-permute-start | bytes 354824 | tf_op jit(solution)/shard_map/ppermute | solution.py:165
  124.1 10.5 %collective-permute-start.33 = (bf16[4,16,924]{2,1,0:T(8,128)(2,1)S(1)}, bf16[4,16,924]{2,1,0:T(8,128)(2,1)S(1)}, u32[]{:S(2)}, u32[]{:S(2)}) collective-permute-start(bf16[4,16,924]{2,1,0:T(8,128)(2,1)S(1)} %get-tuple-element.40), channel_id=1, source_target_pairs={{0,64},{2,66},{4,68},{6,70},{8,72},{10,74},{12,76},{14,78},{16,80}... | collective-permute-start | bytes 354824 | tf_op jit(solution)/shard_map/ppermute | solution.py:165
  134.7 3.5 %collective-permute-start.36 = (bf16[4,4,16,924]{3,2,1,0:T(8,128)(2,1)S(1)}, bf16[4,4,16,924]{3,2,1,0:T(8,128)(2,1)}, u32[]{:S(2)}, u32[]{:S(2)}) collective-permute-start(bf16[4,4,16,924]{3,2,1,0:T(8,128)(2,1)S(1)} %get-tuple-element.37), channel_id=1, source_target_pairs={{0,1},{1,0},{2,3},{3,2},{4,5},{5,4},{6,7},{7,6},{8,9},{9,8},{10,11... | collective-permute-start | bytes 1419272 | tf_op jit(solution)/shard_map/ppermute | solution.py:17
  (2 other events, 2.9 us)

commit v4 on v3

--- a/solution.py
+++ b/solution.py
@@ -33,8 +33,14 @@
 
     g = lax.dot_general(held[...], cot_ref[...], (((1,), (1,)), ((), ())), preferred_element_type=f32)
     part = rows // 2
+    z_odd = lax.rem(here[0], 2) == 1
+
+    def at_place(dy, dz, s):
+        place = lambda dz: g[(dy * Z + dz) * rows + s * part :][:part]
+        return place(dz) if s or dz in EVEN else jnp.where(z_odd, place((dz + Z - 2) % Z), place(dz))
+
     for out, places in zip(outs, UNITS):
-        pieces = [g[(dy * Z + dz) * rows + s * part :][:part] for dy, dz, s in places]
+        pieces = [at_place(*place) for place in places]
         if out.dtype == f32:
             for i, piece in enumerate(pieces):
                 out[i * part : (i + 1) * part, :] = piece
@@ -43,10 +49,9 @@
 
 
 EVEN, ODD = (0, 2, 4, 6), (1, 3, 5, 7)
-UNITS = [[(2, dz, 0) for dz in EVEN], [(2, dz, 0) for dz in ODD]]
-UNITS += [[(dy, dz, 0) for dz in EVEN + ODD] for dy in (1, 3, 0)]
-UNITS += [[(dy, dz, 1) for dy in range(Y)] for dz in (4, 5, 3, 6, 2, 7, 1, 0)]
-ROUNDED = (0, 1, 5, 6)
+UNITS = [[(dy, dz, 0) for dz in EVEN + ODD] for dy in (1, 3, 2)] + [[(dy, dz, 1) for dy in range(Y)] for dz in (4, 5)]
+ROUNDED = len(UNITS)
+UNITS += [[(0, dz, 0) for dz in EVEN + ODD]] + [[(dy, dz, 1) for dy in range(Y)] for dz in (3, 6, 2, 7, 1, 0)]
 
 
 def gradient(mine, other, cotangent, here):
@@ -54,7 +59,7 @@
     ff = cotangent.shape[1]
     part, tile = half // (Z * Y), min(1280, ff)
     whole = lambda i: (0, 0)
-    shapes = [(len(places) * part, bf16 if k in ROUNDED else f32) for k, places in enumerate(UNITS)]
+    shapes = [(len(places) * part, bf16 if k < ROUNDED else f32) for k, places in enumerate(UNITS)]
     cot = pltpu.with_memory_space_constraint(cotangent.T, pltpu.HBM)
     mine = pltpu.with_memory_space_constraint(mine, pltpu.HBM)
     other = pltpu.with_memory_space_constraint(other, pltpu.HBM)
@@ -77,25 +82,18 @@
     )(here, mine, other, cot)
 
 
-def near_order(rank):
+def project(tokens, basis):
     c, x = lax.axis_index("c"), lax.axis_index("x")
-    part = rank // (X * C)
-    n = lax.broadcasted_iota(jnp.int32, (rank, rank), 0)
-    r = lax.broadcasted_iota(jnp.int32, (rank, rank), 1)
-    chunk = ((c + n // (part * X)) % C) * X + (x + (n // part) % X) % X
-    return (r == chunk * part + n % part).astype(bf16)
-
-
-def project(tokens, basis):
     rank = basis.shape[1]
     half, part = rank // C, rank // (X * C)
-    lanes = (((1,), (1,)), ((), ()))
-    ordered = lax.dot_general(near_order(rank), basis, lanes, preferred_element_type=f32).astype(bf16)
-    away = lax.dot_general(ordered[half:], tokens, lanes, preferred_element_type=f32)
-    sent = moved(away, "c", 1)
-    both = lax.dot_general(ordered[:half], tokens, lanes, preferred_element_type=f32) + sent
-    total = both[:part]
-    for got in [moved(both[d * part : (d + 1) * part].astype(bf16), "x", d) for d in (1, 3, 2)]:
+    share = lambda k: lax.dot_general(
+        lax.dynamic_slice_in_dim(basis, k * half, half, 1), tokens, (((0,), (1,)), ((), ())), preferred_element_type=f32
+    )
+    sent = moved(share(1 - c), "c", 1)
+    both = share(c) + sent
+    chunk = lambda d: lax.dynamic_slice_in_dim(both, (x + d) % X * part, part, 0)
+    total = chunk(0)
+    for got in [moved(chunk(d).astype(bf16), "x", d) for d in (1, 3, 2)]:
         total = total + got.astype(f32)
     mine = total.astype(bf16)
     got = {d: moved(mine, "x", d) for d in (1, 3, 2)}
@@ -103,35 +101,33 @@
     return mine, moved(mine, "c", 1)
 
 
-def scatter_y_first(two_low, two_high, one, three, zero):
-    h = two_low.shape[0]
-    up, down = moved(two_low, "y", 1).astype(f32), moved(two_high, "y", -1).astype(f32)
-    up = moved(jnp.concatenate([one[:h] + up, one[h:]], 0).astype(bf16), "y", 1)
-    down = moved(jnp.concatenate([three[:h], three[h:] + down], 0).astype(bf16), "y", -1)
-    low = zero[:h] + up[:h].astype(f32) + down[:h].astype(f32)
-    high = zero[h:] + up[h:].astype(f32) + down[h:].astype(f32)
+def scatter(one, three, two, four, five, zero, *rest):
+    k3, k6, k2, k7, k1, k0 = rest
+    up, down = moved(four, "z", 1), moved(five, "z", -1)
+    across = [moved(one, "y", 1), moved(three, "y", 3), moved(two, "y", 2)]
+    up = moved((k3 + up.astype(f32)).astype(bf16), "z", 1)
+    down = moved((k6 + down.astype(f32)).astype(bf16), "z", -1)
+    up, down = (k2 + up.astype(f32)).astype(bf16), (k7 + down.astype(f32)).astype(bf16)
+    zero, up, down = lax.optimization_barrier((zero, up, down))
+    up, down = moved(up, "z", 1), moved(down, "z", -1)
+    h = zero.shape[0] // 2
     rows = h // 4
-    got = lax.ppermute(high.astype(bf16), "z", [(z, z ^ 1) for z in range(Z)]).astype(f32)
-    turned = jnp.concatenate([got[-rows:], got[:-rows]], 0)
-    low = low + jnp.where(lax.axis_index("z") % 2 == 0, turned, got)
-    total, low = low[:rows], low.astype(bf16)
+    high = zero[h:]
+    for got in across:
+        high = high + got[h:].astype(f32)
+    pair = lax.ppermute(high.astype(bf16), "z", [(z, z ^ 1) for z in range(Z)])
+    up = moved((k1 + up.astype(f32)).astype(bf16), "z", 1)
+    low = zero[:h] + pair.astype(f32)
+    for got in across:
+        low = low + got[:h].astype(f32)
+    first, low = low[:rows], low.astype(bf16)
     for k in (2, 1, 3):
-        total = total + moved(low[k * rows : (k + 1) * rows], "z", 2 * k).astype(f32)
-    return total
-
-
-def scatter_z_first(four, five, three, six, two, seven, one, zero):
-    up, down = moved(four, "z", 1), moved(five, "z", -1)
-    for k, m in ((three, six), (two, seven)):
-        up = moved((k + up.astype(f32)).astype(bf16), "z", 1)
-        down = moved((m + down.astype(f32)).astype(bf16), "z", -1)
-    up = moved((one + up.astype(f32)).astype(bf16), "z", 1)
-    total = zero + up.astype(f32) + down.astype(f32)
-    rows = zero.shape[0] // Y
-    total, rounded = total[:rows], total.astype(bf16)
+        first = first + moved(low[k * rows : (k + 1) * rows], "z", 2 * k).astype(f32)
+    second = k0 + up.astype(f32) + down.astype(f32)
+    second, rounded = second[:rows], second.astype(bf16)
     for k in (2, 1, 3):
-        total = total + moved(rounded[k * rows : (k + 1) * rows], "y", k).astype(f32)
-    return total
+        second = second + moved(rounded[k * rows : (k + 1) * rows], "y", k).astype(f32)
+    return jnp.concatenate([first, second], 0)
 
 
 def picked(choices, index):
@@ -141,7 +137,7 @@
     return out
 
 
-def spread(normed):
+def spread(normed, beside):
     z, y, x, c = (lax.axis_index(axis) for axis in ("z", "y", "x", "c"))
     rows, ff = normed.shape
     cut = normed.reshape(rows, Y, ff // Y).transpose(1, 0, 2)
@@ -164,8 +160,8 @@
                         pairs.append(((pz * Y * X + r) * C + pc, (((pz + 2 * k + po) % Z) * Y * X + r) * C + (pc ^ po)))
         moved_in = lax.ppermute(sent, ("z", "y", "x", "c"), pairs)
         half.append(moved_in if k else jnp.where(odd == 0, sent, moved_in))
-    half = jnp.stack(half)
-    return half, moved(half, "c", 1)
+    half, beside = lax.optimization_barrier((jnp.stack(half), beside))
+    return beside, half, moved(half, "c", 1)
 
 
 def spread_order(rank):
@@ -184,15 +180,17 @@
     here = jnp.stack([lax.axis_index(axis) for axis in ("z", "y", "x", "c")]).astype(jnp.int32)
     mine, other = project(tokens, basis)
     units = gradient(mine, other, cotangent, here)
-    total = jnp.concatenate([scatter_y_first(*units[:5]), scatter_z_first(*units[5:])], 0)
+    total = scatter(*units)
     total_tokens = cotangent.shape[0] * Z * Y
     grad_low = total * (1.0 / total_tokens)
     first = 0.9 * exp_avg + 0.1 * grad_low
     second = 0.999 * exp_avg_sq + 0.001 * grad_low * grad_low
     normed = (first / bias_first / (jnp.sqrt(second / bias_second) + 1e-08)).astype(bf16)
-    all_rows = jnp.stack(spread(normed)).reshape(rank, ff // Y)
     ordered = jnp.dot(basis, spread_order(rank), preferred_element_type=f32).astype(bf16)
-    update = jnp.dot(ordered, all_rows, preferred_element_type=f32).astype(bf16)
+    ordered, *parts = spread(normed, ordered)
+    mine, other = (part.reshape(rank // 2, ff // Y) for part in parts)
+    update = jnp.dot(ordered[:, : rank // 2], mine, preferred_element_type=f32)
+    update = (update + jnp.dot(ordered[:, rank // 2 :], other, preferred_element_type=f32)).astype(bf16)
     return (update, first, second)
 
 

time: 145 us -> 144 us (level)
  other arithmetic: 5.39 us -> 9.9 us
  waiting for transfers between devices: 54.1 us -> 50.7 us
  starting transfers between devices: 62.4 us -> 60.4 us
    ppermute x32 -> x31, waiting for transfers between devices: 43 us -> 39.8 us  [moved(): return lax.ppermute(value, axis, [(i, (i + by) % n) for i in range(n)])]
    ppermute x4, starting transfers between devices: 21.4 us -> 18.3 us  [spread(): moved_in = lax.ppermute(sent, ('z', 'y', 'x', 'c'), pairs)]
    another operation x5 -> x2, other arithmetic: 2.36 us -> 0.09 us  [spread(): half, beside = lax.optimization_barrier((jnp.stack(half), beside))]
    slice x7 -> x2, local copies, waits for them, and re-layouts: 2.28 us -> 0.03 us  [the longest x1 0.01 us: scatter(): rounded[k * rows:(k + 1) * rows]]
    select_n x2, other arithmetic: 0.1 us -> 1.91 us  [picked(): out = jnp.where(index == k, choices[k], out)]
    unnamed x30 -> x24, local copies, waits for them, and re-layouts: 0.92 us -> 2.48 us
    ppermute x32 -> x31, starting transfers between devices: 40.9 us -> 42.1 us  [moved(): return lax.ppermute(value, axis, [(i, (i + by) % n) for i in range(n)])]
    dot_general x4 -> x5, matrix products: 9.08 us -> 8.68 us  [the longest x2 3.93 us: project(): lax.dot_general(lax.dynamic_slice_in_dim(basis, k * half, half, 1), token...]
  transfers between devices with their start and end apart: 37 -> 36, of which waited for: 26 -> 24; matrix products, arithmetic and copies ran while one was open for 3% -> 6% of each run, Pallas kernels for 0% -> 0%
where the time goes in v4:
time: 144 us
  starting transfers between devices  60.4 us (42%)
  waiting for transfers between devices  50.7 us (35%)
  other arithmetic  9.9 us (7%)
  Pallas kernels  8.91 us (6%)
  matrix products  8.68 us (6%)
  local copies, waits for them, and re-layouts  3.73 us (3%)
    ppermute x31, starting transfers between devices, moved(): return lax.ppermute(value, axis, [(i, (i + by) % n) for i in range(n)])  42.1 us
    ppermute x31, waiting for transfers between devices, moved(): return lax.ppermute(value, axis, [(i, (i + by) % n) for i in range(n)])  39.8 us
    ppermute x4, starting transfers between devices, spread(): moved_in = lax.ppermute(sent, ('z', 'y', 'x', 'c'), pairs)  18.3 us
    pallas_call x1, Pallas kernels, gradient(): pl.pallas_call(grad_kernel, grid=(pl.cdiv(ff, tile),), in_specs=[pl.Block...  8.91 us
    ppermute x4, waiting for transfers between devices, spread(): moved_in = lax.ppermute(sent, ('z', 'y', 'x', 'c'), pairs)  7.73 us
    dot_general x2, matrix products, project(): lax.dot_general(lax.dynamic_slice_in_dim(basis, k * half, half, 1), token...  3.93 us
    ppermute x1, waiting for transfers between devices, scatter(): pair = lax.ppermute(high.astype(bf16), 'z', [(z, z ^ 1) for z in range(Z)])  3.14 us
  transfers between devices with their start and end apart: 36, of which 24 were waited for; matrix products, arithmetic and copies ran while one was open for 6% of the time, Pallas kernels for 0%

profile of v4, /device:TPU:1, one launch (start us, length us, event | category | flops | bytes accessed | tf_op | source)
XLA Modules:
  0.0 143.5 jit_solution(17569378267398655818)
XLA Ops:
  0.7 1.6 %copy-done = bf16[1024,1024]{1,0:T(8,128)(2,1)S(1)} copy-done((bf16[1024,1024]{1,0:T(8,128)(2,1)S(1)}, bf16[1024,1024]{1,0:T(8,128)(2,1)}, u32[]{:S(2)}) %copy-start) | copy-done | bytes 2097176
  2.2 1.8 %fusion.39 = f32[256,1024]{1,0:T(8,128)S(1)} fusion(bf16[1024,1024]{1,0:T(8,128)(2,1)S(1)} %copy-done, bf16[1024,512]{1,0:T(8,128)(2,1)} %param.6, s32[]{:T(128)S(6)} %select_n.239), kind=kOutput, calls=%fused_computation.62 | convolution fusion | flops 536870912 | bytes 3670020 | tf_op jit(solution)/shard_map/dot_general | solution.py:89
  4.0 3.3 %collective-permute-start = (f32[256,1024]{1,0:T(8,128)S(1)}, f32[256,1024]{1,0:T(8,128)}, u32[]{:S(2)}, u32[]{:S(2)}) collective-permute-start(f32[256,1024]{1,0:T(8,128)S(1)} %fusion.39), channel_id=1, source_target_pairs={{0,1},{1,0},{2,3},{3,2},{4,5},{5,4},{6,7},{7,6},{8,9},{9,8},{10,11... | collective-permute-start | bytes 3145736 | tf_op jit(solution)/shard_map/ppermute | solution.py:17
  7.4 2.4 %collective-permute-done = f32[256,1024]{1,0:T(8,128)} collective-permute-done((f32[256,1024]{1,0:T(8,128)S(1)}, f32[256,1024]{1,0:T(8,128)}, u32[]{:S(2)}, u32[]{:S(2)}) %collective-permute-start) | collective-permute-done | bytes 1048608 | tf_op jit(solution)/shard_map/ppermute | solution.py:17
  9.8 2.1 %convolution_add_fusion = f32[256,1024]{1,0:T(8,128)S(1)} fusion(f32[256,1024]{1,0:T(8,128)} %collective-permute-done, bf16[1024,1024]{1,0:T(8,128)(2,1)S(1)} %copy-done, bf16[1024,512]{1,0:T(8,128)(2,1)} %param.6, s32[]{:T(128)S(6)} %select_n.238), kind=kOutput, calls=%fused_computation.22 | convolution fusion | flops 537133056 | bytes 4718596 | tf_op jit(solution)/shard_map/dot_general | solution.py:89
  12.6 2.7 %collective-permute-start.2 = (bf16[64,1024]{1,0:T(8,128)(2,1)S(1)}, bf16[64,1024]{1,0:T(8,128)(2,1)}, u32[]{:S(2)}, u32[]{:S(2)}) collective-permute-start(bf16[64,1024]{1,0:T(8,128)(2,1)S(1)} %get-tuple-element.46), channel_id=1, source_target_pairs={{0,6},{2,0},{4,2},{6,4},{1,7},{3,1},{5,3},{7,5},{8,14},{10,8},{12,... | collective-permute-start | bytes 393224 | tf_op jit(solution)/shard_map/ppermute | solution.py:17
  15.3 3.5 %collective-permute-done.1 = bf16[64,1024]{1,0:T(8,128)(2,1)S(1)} collective-permute-done((bf16[64,1024]{1,0:T(8,128)(2,1)}, bf16[64,1024]{1,0:T(8,128)(2,1)S(1)}, u32[]{:S(2)}, u32[]{:S(2)}) %collective-permute-start.1) | collective-permute-done | bytes 131104 | tf_op jit(solution)/shard_map/ppermute | solution.py:17
  18.8 1.7 %collective-permute-done.2 = bf16[64,1024]{1,0:T(8,128)(2,1)} collective-permute-done((bf16[64,1024]{1,0:T(8,128)(2,1)S(1)}, bf16[64,1024]{1,0:T(8,128)(2,1)}, u32[]{:S(2)}, u32[]{:S(2)}) %collective-permute-start.2) | collective-permute-done | bytes 131104 | tf_op jit(solution)/shard_map/ppermute | solution.py:17
  20.8 1.0 add_convert_fusion.7
  21.8 1.3 collective-permute-start.4
  23.2 3.3 %collective-permute-start.5 = (bf16[64,1024]{1,0:T(8,128)(2,1)S(1)}, bf16[64,1024]{1,0:T(8,128)(2,1)S(1)}, u32[]{:S(2)}, u32[]{:S(2)}) collective-permute-start(bf16[64,1024]{1,0:T(8,128)(2,1)S(1)} %add_convert_fusion.7), channel_id=1, source_target_pairs={{0,4},{2,6},{4,0},{6,2},{1,5},{3,7},{5,1},{7,3},{8,12},{10,14},{12... | collective-permute-start | bytes 393224 | tf_op jit(solution)/shard_map/ppermute | solution.py:17
  26.4 1.2 collective-permute-done.4
  27.6 3.6 %collective-permute-done.5 = bf16[64,1024]{1,0:T(8,128)(2,1)S(1)} collective-permute-done((bf16[64,1024]{1,0:T(8,128)(2,1)S(1)}, bf16[64,1024]{1,0:T(8,128)(2,1)S(1)}, u32[]{:S(2)}, u32[]{:S(2)}) %collective-permute-start.5) | collective-permute-done | bytes 131104 | tf_op jit(solution)/shard_map/ppermute | solution.py:17
  31.6 2.3 %collective-permute-start.7 = (bf16[256,1024]{1,0:T(8,128)(2,1)S(1)}, bf16[256,1024]{1,0:T(8,128)(2,1)S(1)}, u32[]{:S(2)}, u32[]{:S(2)}) collective-permute-start(bf16[256,1024]{1,0:T(8,128)(2,1)S(1)} %pad_maximum_fusion.mine_ref), channel_id=1, source_target_pairs={{0,1},{1,0},{2,3},{3,2},{4,5},{5,4},{6,7},{7,6},{8,9},{9,8},{10,11... | collective-permute-start | bytes 1572872 | tf_op jit(solution)/shard_map/ppermute | solution.py:17
  34.0 1.5 %collective-permute-done.7.other_ref = bf16[256,1024]{1,0:T(8,128)(2,1)S(1)} collective-permute-done((bf16[256,1024]{1,0:T(8,128)(2,1)S(1)}, bf16[256,1024]{1,0:T(8,128)(2,1)S(1)}, u32[]{:S(2)}, u32[]{:S(2)}) %collective-permute-start.7) | collective-permute-done | bytes 524320 | tf_op jit(solution)/shard_map/ppermute | solution.py:17
  36.2 8.9 %shard_map.76 = (bf16[64,3696]{1,0:T(8,128)(2,1)}, bf16[64,3696]{1,0:T(8,128)(2,1)}, bf16[64,3696]{1,0:T(8,128)(2,1)}, bf16[32,3696]{1,0:T(8,128)(2,1)}, bf16[32...) custom-call(s32[4]{0:T(128)S(1)} %pad_add_fusion.here, ...), custom_call_target="tpu_custom_call" | custom-call | flops 3875536896 | bytes 14192640 | tf_op jit(solution)/shard_map/pallas_call | solution.py:66
  45.2 4.5 %collective-permute-start.10 = (bf16[32,3696]{1,0:T(8,128)(2,1)}, bf16[32,3696]{1,0:T(8,128)(2,1)}, u32[]{:S(2)}, u32[]{:S(2)}) collective-permute-start(bf16[32,3696]{1,0:T(8,128)(2,1)} %get-tuple-element.26), channel_id=1, source_target_pairs={{0,224},{32,0},{64,32},{96,64},{128,96},{160,128},{192,160},{224,1... | collective-permute-start | bytes 709640 | tf_op jit(solution)/shard_map/ppermute | solution.py:17
  51.4 1.3 collective-permute-start.12
  52.8 1.5 %collective-permute-start.13 = (bf16[64,3696]{1,0:T(8,128)(2,1)}, bf16[64,3696]{1,0:T(8,128)(2,1)S(1)}, u32[]{:S(2)}, u32[]{:S(2)}) collective-permute-start(bf16[64,3696]{1,0:T(8,128)(2,1)} %get-tuple-element.29), channel_id=1, source_target_pairs={{0,24},{8,0},{16,8},{24,16},{1,25},{9,1},{17,9},{25,17},{2,26},{10... | collective-permute-start | bytes 1419272 | tf_op jit(solution)/shard_map/ppermute | solution.py:17
  54.3 1.6 %collective-permute-start.14 = (bf16[64,3696]{1,0:T(8,128)(2,1)}, bf16[64,3696]{1,0:T(8,128)(2,1)S(1)}, u32[]{:S(2)}, u32[]{:S(2)}) collective-permute-start(bf16[64,3696]{1,0:T(8,128)(2,1)} %get-tuple-element.30), channel_id=1, source_target_pairs={{0,16},{8,24},{16,0},{24,8},{1,17},{9,25},{17,1},{25,9},{2,18},{10... | collective-permute-start | bytes 1419272 | tf_op jit(solution)/shard_map/ppermute | solution.py:17
  55.8 1.1 add_convert_fusion.4
  57.0 2.9 %collective-permute-start.11 = (bf16[32,3696]{1,0:T(8,128)(2,1)S(1)}, bf16[32,3696]{1,0:T(8,128)(2,1)S(1)}, u32[]{:S(2)}, u32[]{:S(2)}) collective-permute-start(bf16[32,3696]{1,0:T(8,128)(2,1)S(1)} %add_convert_fusion.4), channel_id=1, source_target_pairs={{0,224},{32,0},{64,32},{96,64},{128,96},{160,128},{192,160},{224,1... | collective-permute-start | bytes 709640 | tf_op jit(solution)/shard_map/ppermute | solution.py:17
  59.9 1.1 add_convert_fusion.6
  61.1 2.1 %collective-permute-done.11 = bf16[32,3696]{1,0:T(8,128)(2,1)S(1)} collective-permute-done((bf16[32,3696]{1,0:T(8,128)(2,1)S(1)}, bf16[32,3696]{1,0:T(8,128)(2,1)S(1)}, u32[]{:S(2)}, u32[]{:S(2)}) %collective-permute-start.11) | collective-permute-done | bytes 236576 | tf_op jit(solution)/shard_map/ppermute | solution.py:17
  63.2 4.0 %collective-permute-done.9 = bf16[32,3696]{1,0:T(8,128)(2,1)S(1)} collective-permute-done((bf16[32,3696]{1,0:T(8,128)(2,1)S(1)}, bf16[32,3696]{1,0:T(8,128)(2,1)S(1)}, u32[]{:S(2)}, u32[]{:S(2)}) %collective-permute-start.9) | collective-permute-done | bytes 236576 | tf_op jit(solution)/shard_map/ppermute | solution.py:17
  67.5 8.6 %collective-permute-done.14 = bf16[64,3696]{1,0:T(8,128)(2,1)S(1)} collective-permute-done((bf16[64,3696]{1,0:T(8,128)(2,1)}, bf16[64,3696]{1,0:T(8,128)(2,1)S(1)}, u32[]{:S(2)}, u32[]{:S(2)}) %collective-permute-start.14) | collective-permute-done | bytes 473120 | tf_op jit(solution)/shard_map/ppermute | solution.py:17
  76.3 2.4 %collective-permute-start.21 = (bf16[32,3696]{1,0:T(8,128)(2,1)S(1)}, bf16[32,3696]{1,0:T(8,128)(2,1)S(1)}, u32[]{:S(2)}, u32[]{:S(2)}) collective-permute-start(bf16[32,3696]{1,0:T(8,128)(2,1)S(1)} %add_convert_fusion.3), channel_id=1, source_target_pairs={{0,224},{32,0},{64,32},{96,64},{128,96},{160,128},{192,160},{224,1... | collective-permute-start | bytes 709640 | tf_op jit(solution)/shard_map/ppermute | solution.py:17
  78.8 3.1 %collective-permute-done.15 = bf16[32,3696]{1,0:T(8,128)(2,1)S(1)} collective-permute-done((bf16[32,3696]{1,0:T(8,128)(2,1)S(1)}, bf16[32,3696]{1,0:T(8,128)(2,1)S(1)}, u32[]{:S(2)}, u32[]{:S(2)}) %collective-permute-start.15) | collective-permute-done | bytes 236576 | tf_op jit(solution)/shard_map/ppermute | solution.py:118
  82.2 2.2 %collective-permute-start.16 = (bf16[8,3696]{1,0:T(8,128)(2,1)S(1)}, bf16[8,3696]{1,0:T(8,128)(2,1)S(1)}, u32[]{:S(2)}, u32[]{:S(2)}) collective-permute-start(bf16[8,3696]{1,0:T(8,128)(2,1)S(1)} %get-tuple-element.51), channel_id=1, source_target_pairs={{0,128},{32,160},{64,192},{96,224},{128,0},{160,32},{192,64},{224,... | collective-permute-start | bytes 177416 | tf_op jit(solution)/shard_map/ppermute | solution.py:17
  84.4 2.0 %collective-permute-start.17 = (bf16[8,3696]{1,0:T(8,128)(2,1)S(1)}, bf16[8,3696]{1,0:T(8,128)(2,1)S(1)}, u32[]{:S(2)}, u32[]{:S(2)}) collective-permute-start(bf16[8,3696]{1,0:T(8,128)(2,1)S(1)} %get-tuple-element.53), channel_id=1, source_target_pairs={{0,64},{32,96},{64,128},{96,160},{128,192},{160,224},{192,0},{224,... | collective-permute-start | bytes 177416 | tf_op jit(solution)/shard_map/ppermute | solution.py:17
  86.4 1.6 %collective-permute-start.18 = (bf16[8,3696]{1,0:T(8,128)(2,1)S(1)}, bf16[8,3696]{1,0:T(8,128)(2,1)S(1)}, u32[]{:S(2)}, u32[]{:S(2)}) collective-permute-start(bf16[8,3696]{1,0:T(8,128)(2,1)S(1)} %get-tuple-element.52), channel_id=1, source_target_pairs={{0,192},{32,224},{64,0},{96,32},{128,64},{160,96},{192,128},{224,1... | collective-permute-start | bytes 177416 | tf_op jit(solution)/shard_map/ppermute | solution.py:17
  90.0 1.2 collective-permute-start.24
  91.3 1.1 collective-permute-done.17
  95.2 2.2 %collective-permute-start.27 = (bf16[16,924]{1,0:T(8,128)(2,1)S(1)}, bf16[16,924]{1,0:T(8,128)(2,1)S(1)}, u32[]{:S(2)}, u32[]{:S(2)}) collective-permute-start(bf16[16,924]{1,0:T(8,128)(2,1)S(1)} %bitcast.51), channel_id=1, source_target_pairs={{0,24},{8,0},{16,8},{24,16},{1,25},{9,1},{17,9},{25,17},{2,26},{10... | collective-permute-start | bytes 88712 | tf_op jit(solution)/shard_map/ppermute | solution.py:17
  97.5 1.3 collective-permute-start.26
  99.4 2.1 %collective-permute-done.25 = bf16[16,924]{1,0:T(8,128)(2,1)S(1)} collective-permute-done((bf16[16,924]{1,0:T(8,128)(2,1)S(1)}, bf16[16,924]{1,0:T(8,128)(2,1)S(1)}, u32[]{:S(2)}, u32[]{:S(2)}) %collective-permute-start.25) | collective-permute-done | bytes 29600 | tf_op jit(solution)/shard_map/ppermute | solution.py:17
  102.6 2.2 %collective-permute-start.28 = (bf16[4,16,924]{2,1,0:T(8,128)(2,1)}, bf16[4,16,924]{2,1,0:T(8,128)(2,1)S(1)}, u32[]{:S(2)}, u32[]{:S(2)}) collective-permute-start(bf16[4,16,924]{2,1,0:T(8,128)(2,1)} %pad_maximum_fusion.3), channel_id=1, source_target_pairs={{0,6},{2,0},{4,2},{6,4},{1,7},{3,1},{5,3},{7,5},{8,14},{10,8},{12,... | collective-permute-start | bytes 354824 | tf_op jit(solution)/shard_map/ppermute | solution.py:17
  105.3 2.0 %fusion = bf16[1024,512]{0,1:T(8,128)(2,1)S(1)} fusion(bf16[1024,512]{1,0:T(8,128)(2,1)} %param.6, s32[512]{0:T(512)S(1)} %get-tuple-element.67, s32[512]{0:T(512)} %get-tuple-element.69, s32[512]{0:T(512)S(1)} %get-tuple-element.66, s32[512]{0:T(512)} %get-tuple-element.70, s32[]{:T(128)S(6)} %add.343, s32[512]{0:T(512)S(1)} %get-tuple-element.68, ...), kind=kOutput, calls=%fused_computation.21 | convolution fusion | flops 555745280 | bytes 2115596 | tf_op jit(solution)/shard_map/dot_general | solution.py:189
  108.4 2.0 %collective-permute-done.29 = bf16[4,16,924]{2,1,0:T(8,128)(2,1)S(1)} collective-permute-done((bf16[4,16,924]{2,1,0:T(8,128)(2,1)}, bf16[4,16,924]{2,1,0:T(8,128)(2,1)S(1)}, u32[]{:S(2)}, u32[]{:S(2)}) %collective-permute-start.29) | collective-permute-done | bytes 118304 | tf_op jit(solution)/shard_map/ppermute | solution.py:17
  110.4 1.1 collective-permute-done.30
  112.5 12.9 %collective-permute-start.31 = (bf16[4,16,924]{2,1,0:T(8,128)(2,1)S(1)}, bf16[4,16,924]{2,1,0:T(8,128)(2,1)S(1)}, u32[]{:S(2)}, u32[]{:S(2)}) collective-permute-start(bf16[4,16,924]{2,1,0:T(8,128)(2,1)S(1)} %get-tuple-element.47), channel_id=1, source_target_pairs={{1,32},{3,34},{5,36},{7,38},{9,40},{11,42},{13,44},{15,46},{17,48}... | collective-permute-start | bytes 354824 | tf_op jit(solution)/shard_map/ppermute | solution.py:161
  125.4 1.0 select_select_fusion.4
  126.4 1.7 %collective-permute-start.32 = (bf16[4,16,924]{2,1,0:T(8,128)(2,1)S(1)}, bf16[4,16,924]{2,1,0:T(8,128)(2,1)S(1)}, u32[]{:S(2)}, u32[]{:S(2)}) collective-permute-start(bf16[4,16,924]{2,1,0:T(8,128)(2,1)S(1)} %get-tuple-element.49), channel_id=1, source_target_pairs={{0,64},{2,66},{4,68},{6,70},{8,72},{10,74},{12,76},{14,78},{16,80}... | collective-permute-start | bytes 354824 | tf_op jit(solution)/shard_map/ppermute | solution.py:161
  128.1 3.1 %collective-permute-start.33 = (bf16[4,16,924]{2,1,0:T(8,128)(2,1)S(1)}, bf16[4,16,924]{2,1,0:T(8,128)(2,1)S(1)}, u32[]{:S(2)}, u32[]{:S(2)}) collective-permute-start(bf16[4,16,924]{2,1,0:T(8,128)(2,1)S(1)} %get-tuple-element.50), channel_id=1, source_target_pairs={{0,128},{2,130},{4,132},{6,134},{8,136},{10,138},{12,140},{14,142}... | collective-permute-start | bytes 354824 | tf_op jit(solution)/shard_map/ppermute | solution.py:161
  131.7 5.3 %collective-permute-done.32 = bf16[4,16,924]{2,1,0:T(8,128)(2,1)S(1)} collective-permute-done((bf16[4,16,924]{2,1,0:T(8,128)(2,1)S(1)}, bf16[4,16,924]{2,1,0:T(8,128)(2,1)S(1)}, u32[]{:S(2)}, u32[]{:S(2)}) %collective-permute-start.32) | collective-permute-done | bytes 118304 | tf_op jit(solution)/shard_map/ppermute | solution.py:161
  137.1 2.4 %collective-permute-done.34 = bf16[4,16,924]{2,1,0:T(8,128)(2,1)S(1)} collective-permute-done((bf16[4,16,924]{2,1,0:T(8,128)(2,1)S(1)}, bf16[4,16,924]{2,1,0:T(8,128)(2,1)S(1)}, u32[]{:S(2)}, u32[]{:S(2)}) %collective-permute-start.34) | collective-permute-done | bytes 118304 | tf_op jit(solution)/shard_map/ppermute | solution.py:161
  140.4 1.2 collective-permute-done.35
  141.5 2.0 %add_convert_fusion = bf16[1024,924]{0,1:T(8,128)(2,1)} fusion(f32[1024,924]{0,1:T(8,128)S(1)} %fusion.18, bf16[256,924]{1,0:T(8,128)(2,1)S(1)} %bitcast.35, bf16[1024,512]{0,1:T(8,128)(2,1)S(1)} %fusion), kind=kOutput, calls=%fused_computation | convolution fusion | flops 486334464 | bytes 6742016 | tf_op jit(solution)/shard_map/dot_general | solution.py:193
  (84 shorter events, 15.3 us)
Async XLA Ops:
  0.6 1.6 %copy-start = (bf16[1024,1024]{1,0:T(8,128)(2,1)S(1)}, bf16[1024,1024]{1,0:T(8,128)(2,1)}, u32[]{:S(2)}) copy-start(bf16[1024,1024]{1,0:T(8,128)(2,1)} %param.5) | copy-start | bytes 6291460
  4.0 5.7 %collective-permute-start = (f32[256,1024]{1,0:T(8,128)S(1)}, f32[256,1024]{1,0:T(8,128)}, u32[]{:S(2)}, u32[]{:S(2)}) collective-permute-start(f32[256,1024]{1,0:T(8,128)S(1)} %fusion.39), channel_id=1, source_target_pairs={{0,1},{1,0},{2,3},{3,2},{4,5},{5,4},{6,7},{7,6},{8,9},{9,8},{10,11... | collective-permute-start | bytes 3145736 | tf_op jit(solution)/shard_map/ppermute | solution.py:17
  12.6 6.1 %collective-permute-start.1 = (bf16[64,1024]{1,0:T(8,128)(2,1)}, bf16[64,1024]{1,0:T(8,128)(2,1)S(1)}, u32[]{:S(2)}, u32[]{:S(2)}) collective-permute-start(bf16[64,1024]{1,0:T(8,128)(2,1)} %get-tuple-element.44), channel_id=1, source_target_pairs={{0,2},{2,4},{4,6},{6,0},{1,3},{3,5},{5,7},{7,1},{8,10},{10,12},{12... | collective-permute-start | bytes 393224 | tf_op jit(solution)/shard_map/ppermute | solution.py:17
  12.6 7.8 %collective-permute-start.2 = (bf16[64,1024]{1,0:T(8,128)(2,1)S(1)}, bf16[64,1024]{1,0:T(8,128)(2,1)}, u32[]{:S(2)}, u32[]{:S(2)}) collective-permute-start(bf16[64,1024]{1,0:T(8,128)(2,1)S(1)} %get-tuple-element.46), channel_id=1, source_target_pairs={{0,6},{2,0},{4,2},{6,4},{1,7},{3,1},{5,3},{7,5},{8,14},{10,8},{12,... | collective-permute-start | bytes 393224 | tf_op jit(solution)/shard_map/ppermute | solution.py:17
  15.3 5.5 %collective-permute-start.3 = (bf16[64,1024]{1,0:T(8,128)(2,1)S(1)}, bf16[64,1024]{1,0:T(8,128)(2,1)}, u32[]{:S(2)}, u32[]{:S(2)}) collective-permute-start(bf16[64,1024]{1,0:T(8,128)(2,1)S(1)} %get-tuple-element.45), channel_id=1, source_target_pairs={{0,4},{2,6},{4,0},{6,2},{1,5},{3,7},{5,1},{7,3},{8,12},{10,14},{12... | collective-permute-start | bytes 393224 | tf_op jit(solution)/shard_map/ppermute | solution.py:17
  21.8 5.8 %collective-permute-start.4 = (bf16[64,1024]{1,0:T(8,128)(2,1)S(1)}, bf16[64,1024]{1,0:T(8,128)(2,1)S(1)}, u32[]{:S(2)}, u32[]{:S(2)}) collective-permute-start(bf16[64,1024]{1,0:T(8,128)(2,1)S(1)} %add_convert_fusion.7), channel_id=1, source_target_pairs={{0,2},{2,4},{4,6},{6,0},{1,3},{3,5},{5,7},{7,1},{8,10},{10,12},{12... | collective-permute-start | bytes 393224 | tf_op jit(solution)/shard_map/ppermute | solution.py:17
  23.2 8.1 %collective-permute-start.5 = (bf16[64,1024]{1,0:T(8,128)(2,1)S(1)}, bf16[64,1024]{1,0:T(8,128)(2,1)S(1)}, u32[]{:S(2)}, u32[]{:S(2)}) collective-permute-start(bf16[64,1024]{1,0:T(8,128)(2,1)S(1)} %add_convert_fusion.7), channel_id=1, source_target_pairs={{0,4},{2,6},{4,0},{6,2},{1,5},{3,7},{5,1},{7,3},{8,12},{10,14},{12... | collective-permute-start | bytes 393224 | tf_op jit(solution)/shard_map/ppermute | solution.py:17
  26.4 5.1 %collective-permute-start.6 = (bf16[64,1024]{1,0:T(8,128)(2,1)S(1)}, bf16[64,1024]{1,0:T(8,128)(2,1)S(1)}, u32[]{:S(2)}, u32[]{:S(2)}) collective-permute-start(bf16[64,1024]{1,0:T(8,128)(2,1)S(1)} %add_convert_fusion.7), channel_id=1, source_target_pairs={{0,6},{2,0},{4,2},{6,4},{1,7},{3,1},{5,3},{7,5},{8,14},{10,8},{12,... | collective-permute-start | bytes 393224 | tf_op jit(solution)/shard_map/ppermute | solution.py:17
  31.6 3.8 %copy-start.2 = (bf16[256,1024]{1,0:T(8,128)(2,1)}, bf16[256,1024]{1,0:T(8,128)(2,1)S(1)}, u32[]{:S(2)}) copy-start(bf16[256,1024]{1,0:T(8,128)(2,1)S(1)} %pad_maximum_fusion.mine_ref) | copy-start | bytes 1572868
  31.6 3.8 %collective-permute-start.7 = (bf16[256,1024]{1,0:T(8,128)(2,1)S(1)}, bf16[256,1024]{1,0:T(8,128)(2,1)S(1)}, u32[]{:S(2)}, u32[]{:S(2)}) collective-permute-start(bf16[256,1024]{1,0:T(8,128)(2,1)S(1)} %pad_maximum_fusion.mine_ref), channel_id=1, source_target_pairs={{0,1},{1,0},{2,3},{3,2},{4,5},{5,4},{6,7},{7,6},{8,9},{9,8},{10,11... | collective-permute-start | bytes 1572872 | tf_op jit(solution)/shard_map/ppermute | solution.py:17
  35.4 0.8 copy-start.9
  45.1 22.1 %copy-start.5 = (f32[32,3696]{1,0:T(8,128)S(1)}, f32[32,3696]{1,0:T(8,128)}, u32[]{:S(2)}) copy-start(f32[32,3696]{1,0:T(8,128)} %get-tuple-element.21) | copy-start | bytes 1419268
  45.2 30.9 %copy-start.1 = (f32[64,3696]{1,0:T(8,128)S(1)}, f32[64,3696]{1,0:T(8,128)}, u32[]{:S(2)}) copy-start(f32[64,3696]{1,0:T(8,128)} %get-tuple-element.27) | copy-start | bytes 2838532
  45.2 10.7 %collective-permute-start.10 = (bf16[32,3696]{1,0:T(8,128)(2,1)}, bf16[32,3696]{1,0:T(8,128)(2,1)}, u32[]{:S(2)}, u32[]{:S(2)}) collective-permute-start(bf16[32,3696]{1,0:T(8,128)(2,1)} %get-tuple-element.26), channel_id=1, source_target_pairs={{0,224},{32,0},{64,32},{96,64},{128,96},{160,128},{192,160},{224,1... | collective-permute-start | bytes 709640 | tf_op jit(solution)/shard_map/ppermute | solution.py:17
  50.2 12.9 %copy-start.6 = (f32[32,3696]{1,0:T(8,128)S(1)}, f32[32,3696]{1,0:T(8,128)}, u32[]{:S(2)}) copy-start(f32[32,3696]{1,0:T(8,128)} %get-tuple-element.24) | copy-start | bytes 1419268
  51.4 8.5 %collective-permute-start.8 = (bf16[32,3696]{1,0:T(8,128)(2,1)}, bf16[32,3696]{1,0:T(8,128)(2,1)S(1)}, u32[]{:S(2)}, u32[]{:S(2)}) collective-permute-start(bf16[32,3696]{1,0:T(8,128)(2,1)} %get-tuple-element.23), channel_id=1, source_target_pairs={{0,32},{32,64},{64,96},{96,128},{128,160},{160,192},{192,224},{224... | collective-permute-start | bytes 709640 | tf_op jit(solution)/shard_map/ppermute | solution.py:17
  51.4 16.0 %collective-permute-start.12 = (bf16[64,3696]{1,0:T(8,128)(2,1)}, bf16[64,3696]{1,0:T(8,128)(2,1)S(1)}, u32[]{:S(2)}, u32[]{:S(2)}) collective-permute-start(bf16[64,3696]{1,0:T(8,128)(2,1)} %get-tuple-element.28), channel_id=1, source_target_pairs={{0,8},{8,16},{16,24},{24,0},{1,9},{9,17},{17,25},{25,1},{2,10},{10... | collective-permute-start | bytes 1419272 | tf_op jit(solution)/shard_map/ppermute | solution.py:17
  52.8 14.7 %collective-permute-start.13 = (bf16[64,3696]{1,0:T(8,128)(2,1)}, bf16[64,3696]{1,0:T(8,128)(2,1)S(1)}, u32[]{:S(2)}, u32[]{:S(2)}) collective-permute-start(bf16[64,3696]{1,0:T(8,128)(2,1)} %get-tuple-element.29), channel_id=1, source_target_pairs={{0,24},{8,0},{16,8},{24,16},{1,25},{9,1},{17,9},{25,17},{2,26},{10... | collective-permute-start | bytes 1419272 | tf_op jit(solution)/shard_map/ppermute | solution.py:17
  54.3 21.8 %collective-permute-start.14 = (bf16[64,3696]{1,0:T(8,128)(2,1)}, bf16[64,3696]{1,0:T(8,128)(2,1)S(1)}, u32[]{:S(2)}, u32[]{:S(2)}) collective-permute-start(bf16[64,3696]{1,0:T(8,128)(2,1)} %get-tuple-element.30), channel_id=1, source_target_pairs={{0,16},{8,24},{16,0},{24,8},{1,17},{9,25},{17,1},{25,9},{2,18},{10... | collective-permute-start | bytes 1419272 | tf_op jit(solution)/shard_map/ppermute | solution.py:17
  57.0 6.2 %collective-permute-start.11 = (bf16[32,3696]{1,0:T(8,128)(2,1)S(1)}, bf16[32,3696]{1,0:T(8,128)(2,1)S(1)}, u32[]{:S(2)}, u32[]{:S(2)}) collective-permute-start(bf16[32,3696]{1,0:T(8,128)(2,1)S(1)} %add_convert_fusion.4), channel_id=1, source_target_pairs={{0,224},{32,0},{64,32},{96,64},{128,96},{160,128},{192,160},{224,1... | collective-permute-start | bytes 709640 | tf_op jit(solution)/shard_map/ppermute | solution.py:17
  59.9 18.8 %copy-start.4 = (f32[32,3696]{1,0:T(8,128)S(1)}, f32[32,3696]{1,0:T(8,128)}, u32[]{:S(2)}) copy-start(f32[32,3696]{1,0:T(8,128)} %get-tuple-element.32) | copy-start | bytes 1419268
  61.0 6.2 %collective-permute-start.9 = (bf16[32,3696]{1,0:T(8,128)(2,1)S(1)}, bf16[32,3696]{1,0:T(8,128)(2,1)S(1)}, u32[]{:S(2)}, u32[]{:S(2)}) collective-permute-start(bf16[32,3696]{1,0:T(8,128)(2,1)S(1)} %add_convert_fusion.6), channel_id=1, source_target_pairs={{0,32},{32,64},{64,96},{96,128},{128,160},{160,192},{192,224},{224... | collective-permute-start | bytes 709640 | tf_op jit(solution)/shard_map/ppermute | solution.py:17
  67.3 20.7 %copy-start.3 = (f32[32,3696]{1,0:T(8,128)S(1)}, f32[32,3696]{1,0:T(8,128)}, u32[]{:S(2)}) copy-start(f32[32,3696]{1,0:T(8,128)} %get-tuple-element.31) | copy-start | bytes 1419268
  67.3 11.4 %collective-permute-start.19 = (bf16[32,3696]{1,0:T(8,128)(2,1)S(1)}, bf16[32,3696]{1,0:T(8,128)(2,1)S(1)}, u32[]{:S(2)}, u32[]{:S(2)}) collective-permute-start(bf16[32,3696]{1,0:T(8,128)(2,1)S(1)} %add_convert_fusion.5), channel_id=1, source_target_pairs={{0,32},{32,64},{64,96},{96,128},{128,160},{160,192},{192,224},{224... | collective-permute-start | bytes 709640 | tf_op jit(solution)/shard_map/ppermute | solution.py:17
  76.2 5.8 %collective-permute-start.15 = (bf16[32,3696]{1,0:T(8,128)(2,1)S(1)}, bf16[32,3696]{1,0:T(8,128)(2,1)S(1)}, u32[]{:S(2)}, u32[]{:S(2)}) collective-permute-start(bf16[32,3696]{1,0:T(8,128)(2,1)S(1)} %add_convert_fusion.2), channel_id=1, source_target_pairs={{0,32},{32,0},{64,96},{96,64},{128,160},{160,128},{192,224},{224,1... | collective-permute-start | bytes 709640 | tf_op jit(solution)/shard_map/ppermute | solution.py:118
  76.3 11.7 %collective-permute-start.21 = (bf16[32,3696]{1,0:T(8,128)(2,1)S(1)}, bf16[32,3696]{1,0:T(8,128)(2,1)S(1)}, u32[]{:S(2)}, u32[]{:S(2)}) collective-permute-start(bf16[32,3696]{1,0:T(8,128)(2,1)S(1)} %add_convert_fusion.3), channel_id=1, source_target_pairs={{0,224},{32,0},{64,32},{96,64},{128,96},{160,128},{192,160},{224,1... | collective-permute-start | bytes 709640 | tf_op jit(solution)/shard_map/ppermute | solution.py:17
  78.8 9.2 %collective-permute-start.20 = (bf16[32,3696]{1,0:T(8,128)(2,1)S(1)}, bf16[32,3696]{1,0:T(8,128)(2,1)S(1)}, u32[]{:S(2)}, u32[]{:S(2)}) collective-permute-start(bf16[32,3696]{1,0:T(8,128)(2,1)S(1)} %add_convert_fusion.1), channel_id=1, source_target_pairs={{0,32},{32,64},{64,96},{96,128},{128,160},{160,192},{192,224},{224... | collective-permute-start | bytes 709640 | tf_op jit(solution)/shard_map/ppermute | solution.py:17
  82.1 11.6 %copy-start.7 = (f32[16,3696]{1,0:T(8,128)S(1)}, f32[16,3696]{1,0:T(8,128)}, u32[]{:S(2)}) copy-start(f32[16,3696]{1,0:T(8,128)} %param.8) | copy-start | bytes 709636
  82.2 11.6 %copy-start.8 = (f32[16,3696]{1,0:T(8,128)S(1)}, f32[16,3696]{1,0:T(8,128)}, u32[]{:S(2)}) copy-start(f32[16,3696]{1,0:T(8,128)} %param.9) | copy-start | bytes 709636
  82.2 7.8 %collective-permute-start.16 = (bf16[8,3696]{1,0:T(8,128)(2,1)S(1)}, bf16[8,3696]{1,0:T(8,128)(2,1)S(1)}, u32[]{:S(2)}, u32[]{:S(2)}) collective-permute-start(bf16[8,3696]{1,0:T(8,128)(2,1)S(1)} %get-tuple-element.51), channel_id=1, source_target_pairs={{0,128},{32,160},{64,192},{96,224},{128,0},{160,32},{192,64},{224,... | collective-permute-start | bytes 177416 | tf_op jit(solution)/shard_map/ppermute | solution.py:17
  84.4 7.9 %collective-permute-start.17 = (bf16[8,3696]{1,0:T(8,128)(2,1)S(1)}, bf16[8,3696]{1,0:T(8,128)(2,1)S(1)}, u32[]{:S(2)}, u32[]{:S(2)}) collective-permute-start(bf16[8,3696]{1,0:T(8,128)(2,1)S(1)} %get-tuple-element.53), channel_id=1, source_target_pairs={{0,64},{32,96},{64,128},{96,160},{128,192},{160,224},{192,0},{224,... | collective-permute-start | bytes 177416 | tf_op jit(solution)/shard_map/ppermute | solution.py:17
  86.4 6.0 %collective-permute-start.18 = (bf16[8,3696]{1,0:T(8,128)(2,1)S(1)}, bf16[8,3696]{1,0:T(8,128)(2,1)S(1)}, u32[]{:S(2)}, u32[]{:S(2)}) collective-permute-start(bf16[8,3696]{1,0:T(8,128)(2,1)S(1)} %get-tuple-element.52), channel_id=1, source_target_pairs={{0,192},{32,224},{64,0},{96,32},{128,64},{160,96},{192,128},{224,1... | collective-permute-start | bytes 177416 | tf_op jit(solution)/shard_map/ppermute | solution.py:17
  88.1 4.7 %collective-permute-start.22 = (bf16[8,3696]{1,0:T(8,128)(2,1)S(1)}, bf16[8,3696]{1,0:T(8,128)(2,1)S(1)}, u32[]{:S(2)}, u32[]{:S(2)}) collective-permute-start(bf16[8,3696]{1,0:T(8,128)(2,1)S(1)} %get-tuple-element.54), channel_id=1, source_target_pairs={{0,16},{8,24},{16,0},{24,8},{1,17},{9,25},{17,1},{25,9},{2,18},{10... | collective-permute-start | bytes 177416 | tf_op jit(solution)/shard_map/ppermute | solution.py:17
  88.6 5.1 %collective-permute-start.23 = (bf16[8,3696]{1,0:T(8,128)(2,1)S(1)}, bf16[8,3696]{1,0:T(8,128)(2,1)S(1)}, u32[]{:S(2)}, u32[]{:S(2)}) collective-permute-start(bf16[8,3696]{1,0:T(8,128)(2,1)S(1)} %get-tuple-element.56), channel_id=1, source_target_pairs={{0,8},{8,16},{16,24},{24,0},{1,9},{9,17},{17,25},{25,1},{2,10},{10... | collective-permute-start | bytes 177416 | tf_op jit(solution)/shard_map/ppermute | solution.py:17
  90.0 3.6 %collective-permute-start.24 = (bf16[8,3696]{1,0:T(8,128)(2,1)S(1)}, bf16[8,3696]{1,0:T(8,128)(2,1)S(1)}, u32[]{:S(2)}, u32[]{:S(2)}) collective-permute-start(bf16[8,3696]{1,0:T(8,128)(2,1)S(1)} %get-tuple-element.55), channel_id=1, source_target_pairs={{0,24},{8,0},{16,8},{24,16},{1,25},{9,1},{17,9},{25,17},{2,26},{10... | collective-permute-start | bytes 177416 | tf_op jit(solution)/shard_map/ppermute | solution.py:17
  95.2 4.2 %collective-permute-start.27 = (bf16[16,924]{1,0:T(8,128)(2,1)S(1)}, bf16[16,924]{1,0:T(8,128)(2,1)S(1)}, u32[]{:S(2)}, u32[]{:S(2)}) collective-permute-start(bf16[16,924]{1,0:T(8,128)(2,1)S(1)} %bitcast.51), channel_id=1, source_target_pairs={{0,24},{8,0},{16,8},{24,16},{1,25},{9,1},{17,9},{25,17},{2,26},{10... | collective-permute-start | bytes 88712 | tf_op jit(solution)/shard_map/ppermute | solution.py:17
  97.4 4.1 %collective-permute-start.25 = (bf16[16,924]{1,0:T(8,128)(2,1)S(1)}, bf16[16,924]{1,0:T(8,128)(2,1)S(1)}, u32[]{:S(2)}, u32[]{:S(2)}) collective-permute-start(bf16[16,924]{1,0:T(8,128)(2,1)S(1)} %bitcast.52), channel_id=1, source_target_pairs={{0,8},{8,16},{16,24},{24,0},{1,9},{9,17},{17,25},{25,1},{2,10},{10... | collective-permute-start | bytes 88712 | tf_op jit(solution)/shard_map/ppermute | solution.py:17
  97.5 4.4 %collective-permute-start.26 = (bf16[16,924]{1,0:T(8,128)(2,1)S(1)}, bf16[16,924]{1,0:T(8,128)(2,1)S(1)}, u32[]{:S(2)}, u32[]{:S(2)}) collective-permute-start(bf16[16,924]{1,0:T(8,128)(2,1)S(1)} %bitcast.53), channel_id=1, source_target_pairs={{0,16},{8,24},{16,0},{24,8},{1,17},{9,25},{17,1},{25,9},{2,18},{10... | collective-permute-start | bytes 88712 | tf_op jit(solution)/shard_map/ppermute | solution.py:17
  102.6 5.9 %collective-permute-start.28 = (bf16[4,16,924]{2,1,0:T(8,128)(2,1)}, bf16[4,16,924]{2,1,0:T(8,128)(2,1)S(1)}, u32[]{:S(2)}, u32[]{:S(2)}) collective-permute-start(bf16[4,16,924]{2,1,0:T(8,128)(2,1)} %pad_maximum_fusion.3), channel_id=1, source_target_pairs={{0,6},{2,0},{4,2},{6,4},{1,7},{3,1},{5,3},{7,5},{8,14},{10,8},{12,... | collective-permute-start | bytes 354824 | tf_op jit(solution)/shard_map/ppermute | solution.py:17
  104.8 5.7 %collective-permute-start.29 = (bf16[4,16,924]{2,1,0:T(8,128)(2,1)}, bf16[4,16,924]{2,1,0:T(8,128)(2,1)S(1)}, u32[]{:S(2)}, u32[]{:S(2)}) collective-permute-start(bf16[4,16,924]{2,1,0:T(8,128)(2,1)} %pad_maximum_fusion.3), channel_id=1, source_target_pairs={{0,4},{2,6},{4,0},{6,2},{1,5},{3,7},{5,1},{7,3},{8,12},{10,14},{12... | collective-permute-start | bytes 354824 | tf_op jit(solution)/shard_map/ppermute | solution.py:17
  104.8 6.7 %collective-permute-start.30 = (bf16[4,16,924]{2,1,0:T(8,128)(2,1)}, bf16[4,16,924]{2,1,0:T(8,128)(2,1)}, u32[]{:S(2)}, u32[]{:S(2)}) collective-permute-start(bf16[4,16,924]{2,1,0:T(8,128)(2,1)} %pad_maximum_fusion.3), channel_id=1, source_target_pairs={{0,2},{2,4},{4,6},{6,0},{1,3},{3,5},{5,7},{7,1},{8,10},{10,12},{12... | collective-permute-start | bytes 354824 | tf_op jit(solution)/shard_map/ppermute | solution.py:17
  112.5 19.2 %collective-permute-start.31 = (bf16[4,16,924]{2,1,0:T(8,128)(2,1)S(1)}, bf16[4,16,924]{2,1,0:T(8,128)(2,1)S(1)}, u32[]{:S(2)}, u32[]{:S(2)}) collective-permute-start(bf16[4,16,924]{2,1,0:T(8,128)(2,1)S(1)} %get-tuple-element.47), channel_id=1, source_target_pairs={{1,32},{3,34},{5,36},{7,38},{9,40},{11,42},{13,44},{15,46},{17,48}... | collective-permute-start | bytes 354824 | tf_op jit(solution)/shard_map/ppermute | solution.py:161
  126.4 10.7 %collective-permute-start.32 = (bf16[4,16,924]{2,1,0:T(8,128)(2,1)S(1)}, bf16[4,16,924]{2,1,0:T(8,128)(2,1)S(1)}, u32[]{:S(2)}, u32[]{:S(2)}) collective-permute-start(bf16[4,16,924]{2,1,0:T(8,128)(2,1)S(1)} %get-tuple-element.49), channel_id=1, source_target_pairs={{0,64},{2,66},{4,68},{6,70},{8,72},{10,74},{12,76},{14,78},{16,80}... | collective-permute-start | bytes 354824 | tf_op jit(solution)/shard_map/ppermute | solution.py:161
  128.1 9.0 %collective-permute-start.33 = (bf16[4,16,924]{2,1,0:T(8,128)(2,1)S(1)}, bf16[4,16,924]{2,1,0:T(8,128)(2,1)S(1)}, u32[]{:S(2)}, u32[]{:S(2)}) collective-permute-start(bf16[4,16,924]{2,1,0:T(8,128)(2,1)S(1)} %get-tuple-element.50), channel_id=1, source_target_pairs={{0,128},{2,130},{4,132},{6,134},{8,136},{10,138},{12,140},{14,142}... | collective-permute-start | bytes 354824 | tf_op jit(solution)/shard_map/ppermute | solution.py:161
  131.2 8.3 %collective-permute-start.34 = (bf16[4,16,924]{2,1,0:T(8,128)(2,1)S(1)}, bf16[4,16,924]{2,1,0:T(8,128)(2,1)S(1)}, u32[]{:S(2)}, u32[]{:S(2)}) collective-permute-start(bf16[4,16,924]{2,1,0:T(8,128)(2,1)S(1)} %get-tuple-element.48), channel_id=1, source_target_pairs={{0,192},{2,194},{4,196},{6,198},{8,200},{10,202},{12,204},{14,206}... | collective-permute-start | bytes 354824 | tf_op jit(solution)/shard_map/ppermute | solution.py:161
  139.5 2.0 %collective-permute-start.35 = (bf16[4,4,16,924]{3,2,1,0:T(8,128)(2,1)S(1)}, bf16[4,4,16,924]{3,2,1,0:T(8,128)(2,1)S(1)}, u32[]{:S(2)}, u32[]{:S(2)}) collective-permute-start(bf16[4,4,16,924]{3,2,1,0:T(8,128)(2,1)S(1)} %pad_maximum_fusion.1), channel_id=1, source_target_pairs={{0,1},{1,0},{2,3},{3,2},{4,5},{5,4},{6,7},{7,6},{8,9},{9,8},{10,11... | collective-permute-start | bytes 1419272 | tf_op jit(solution)/shard_map/ppermute | solution.py:17

commit v5 on v4

v5 whole, which is shorter than its diff:
```python
import functools

import numpy as np
import jax
import jax.numpy as jnp
from jax import lax
from jax.experimental import pallas as pl
from jax.experimental.pallas import tpu as pltpu
from jax.sharding import Mesh, PartitionSpec as P

bias_first = 1.0 - 0.9**10
bias_second = 1.0 - 0.999**10
Z, Y, X, C = 8, 4, 4, 2
f32, bf16 = jnp.float32, jnp.bfloat16


def moved(value, axis, by):
    n = {"z": Z, "y": Y, "x": X, "c": C}[axis]
    return lax.ppermute(value, axis, [(i, (i + by) % n) for i in range(n)])


EVEN, ODD = (0, 2, 4, 6), (1, 3, 5, 7)
Y_FIRST = [[(dy, dz) for dz in half] for dy in (2, 1, 3, 0) for half in (EVEN, ODD)]
Z_FIRST = [[(dy, dz) for dy in range(Y)] for dz in (4, 5, 3, 6, 2, 7, 1, 0)]


def grad_kernel(units, here, mine_ref, other_ref, cot_ref, *rest):
    outs, held = rest[:-1], rest[-1]
    rows = held.shape[0] // (Z * Y)
    z_odd = lax.rem(here[0], 2) == 1

    @pl.when(pl.program_id(0) == 0)
    def _():
        z, y, x, c = (here[i] for i in range(4))
        for dy in range(Y):
            for dz in range(Z):
                oz, oy = lax.rem(z + dz, Z), lax.rem(y + dy, Y)
                at = pl.multiple_of(lax.rem(x + X - lax.rem(oz, X), X) * (Y * rows) + oy * rows, rows)
                block_here, block_there = mine_ref[pl.ds(at, rows), :], other_ref[pl.ds(at, rows), :]
                held[pl.ds((dy * Z + dz) * rows, rows), :] = jnp.where(lax.div(oz, X) == c, block_here, block_there)

    g = lax.dot_general(held[...], cot_ref[...], (((1,), (1,)), ((), ())), preferred_element_type=f32)
    place = lambda dy, dz: g[(dy * Z + dz % Z) * rows :][:rows]
    for out, places in zip(outs, units):
        turn = units is Y_FIRST and places[0][1] in ODD
        for i, (dy, dz) in enumerate(places):
            piece = jnp.where(z_odd, place(dy, dz - 2), place(dy, dz)) if turn else place(dy, dz)
            out[i * rows : (i + 1) * rows, :] = piece.astype(out.dtype)


def gradient(units, mine, other, cotangent, here, tile, start, stop):
    half, tokens = mine.shape
    ff = min(stop * tile, cotangent.shape[1]) - start * tile
    rows = 2 * half // (Z * Y)
    whole = lambda i: (0, 0)
    shapes = [(len(places) * rows, f32 if k > 1 else bf16) for k, places in enumerate(units)]
    return pl.pallas_call(
        functools.partial(grad_kernel, units),
        grid=(stop - start,),
        in_specs=[
            pl.BlockSpec(memory_space=pltpu.SMEM),
            pl.BlockSpec((half, tokens), whole),
            pl.BlockSpec((half, tokens), whole),
            pl.BlockSpec((tile, tokens), lambda i: (start + i, 0)),
        ],
        out_specs=[pl.BlockSpec((n, tile), lambda i: (0, i)) for n, _ in shapes],
        out_shape=[pltpu.HBM((n, ff), t) for n, t in shapes],
        scratch_shapes=[pltpu.VMEM((2 * half, tokens), bf16)],
        compiler_params=pltpu.CompilerParams(vmem_limit_bytes=20 * 2**20),
        cost_estimate=pl.CostEstimate(
            flops=4 * half * tokens * ff, bytes_accessed=2 * tokens * ff + 14 * half * ff // 2, transcendentals=0
        ),
    )(here, *(pltpu.with_memory_space_constraint(v, pltpu.HBM) for v in (mine, other, cotangent.T)))


def near_order(rank):
    c, x = lax.axis_index("c"), lax.axis_index("x")
    part = rank // (X * C)
    n = lax.broadcasted_iota(jnp.int32, (rank, rank), 0)
    r = lax.broadcasted_iota(jnp.int32, (rank, rank), 1)
    chunk = ((c + n // (part * X)) % C) * X + (x + (n // part) % X) % X
    return (r == chunk * part + n % part).astype(bf16)


def project(tokens, basis, beside):
    rank = basis.shape[1]
    half, part = rank // C, rank // (X * C)
    lanes = (((1,), (1,)), ((), ()))
    ordered = lax.dot_general(near_order(rank), basis, lanes, preferred_element_type=f32).astype(bf16)
    away = lax.dot_general(ordered[half:], tokens, lanes, preferred_element_type=f32)
    sent = moved(away, "c", 1)
    both = lax.dot_general(ordered[:half], tokens, lanes, preferred_element_type=f32) + sent
    total = both[:part]
    for got in [moved(both[d * part : (d + 1) * part].astype(bf16), "x", d) for d in (1, 3, 2)]:
        total = total + got.astype(f32)
    mine = total.astype(bf16)
    got = {d: moved(mine, "x", d) for d in (1, 3, 2)}
    mine, beside = lax.optimization_barrier((jnp.concatenate([mine, got[1], got[2], got[3]], 0), beside))
    return mine, moved(mine, "c", 1), beside


def scatter(ring, relay):
    four, five, k3, k6, k2, k7, k1, k0 = ring()
    up, down = moved(four, "z", 1), moved(five, "z", -1)
    two_low, two_high, one_low, one_high, three_low, three_high, low, high = relay()
    high_y, low_y = moved(two_low, "y", 1), moved(two_high, "y", -1)
    up = moved((k3 + up.astype(f32)).astype(bf16), "z", 1)
    down = moved((k6 + down.astype(f32)).astype(bf16), "z", -1)
    one = jnp.concatenate([(one_low + high_y.astype(f32)).astype(bf16), one_high.astype(bf16)], 0)
    three = jnp.concatenate([three_low.astype(bf16), (three_high + low_y.astype(f32)).astype(bf16)], 0)
    across = [moved(one, "y", 1), moved(three, "y", -1)]
    up, down = (k2 + up.astype(f32)).astype(bf16), (k7 + down.astype(f32)).astype(bf16)
    up, down = moved(up, "z", 1), moved(down, "z", -1)
    h = low.shape[0]
    rows = h // 4
    for got in across:
        high = high + got[h:].astype(f32)
    pair = lax.ppermute(high.astype(bf16), "z", [(z, z ^ 1) for z in range(Z)])
    up = moved((k1 + up.astype(f32)).astype(bf16), "z", 1)
    low = low + pair.astype(f32)
    for got in across:
        low = low + got[:h].astype(f32)
    first, low = low[:rows], low.astype(bf16)
    for k in (2, 1, 3):
        first = first + moved(low[k * rows : (k + 1) * rows], "z", 2 * k).astype(f32)
    second = k0 + up.astype(f32) + down.astype(f32)
    second, rounded = second[:rows], second.astype(bf16)
    for k in (2, 1, 3):
        second = second + moved(rounded[k * rows : (k + 1) * rows], "y", k).astype(f32)
    return jnp.concatenate([first, second], 1)


def picked(choices, index):
    out = choices[0]
    for k in range(1, len(choices)):
        out = jnp.where(index == k, choices[k], out)
    return out


def spread(normed):
    z, y, x, c = (lax.axis_index(axis) for axis in ("z", "y", "x", "c"))
    rows, ff = normed.shape
    cut = normed.reshape(rows, Y, ff // Y).transpose(1, 0, 2)
    piece = lambda k: lax.dynamic_index_in_dim(cut, (y + k) % Y, 0, keepdims=False)
    got = {d: moved(piece(d), "y", d) for d in (1, 3, 2)}
    tall = jnp.stack([piece(0), got[1], got[2], got[3]])
    got = {d: moved(tall, "x", d) for d in (1, 3, 2)}
    wide = [tall, got[1], got[2], got[3]]
    odd = (z + c) % 2
    half = []
    for k in range(Z // 2):
        to = (z + 2 * k + odd) % Z
        sent = picked(wide, (x - to // 2) % X)
        pairs = []
        for pz in range(Z):
            for pc in range(C):
                po = (pz + pc) % 2
                for r in range(Y * X):
                    if k or po:
                        pairs.append(((pz * Y * X + r) * C + pc, (((pz + 2 * k + po) % Z) * Y * X + r) * C + (pc ^ po)))
        moved_in = lax.ppermute(sent, ("z", "y", "x", "c"), pairs)
        half.append(moved_in if k else jnp.where(odd == 0, sent, moved_in))
    half = jnp.stack(half)
    return half, moved(half, "c", 1)


def spread_order(rank):
    z, y, c = (lax.axis_index(axis) for axis in ("z", "y", "c"))
    rows = rank // (Z * Y)
    n = lax.broadcasted_iota(jnp.int32, (rank, rank), 1)
    r = lax.broadcasted_iota(jnp.int32, (rank, rank), 0)
    h, k, j = n // (rank // 2), (n // (rows * Y)) % (Z // 2), (n // rows) % Y
    owner_z = (z + 2 * Z - 2 * k - (z + c + h) % 2) % Z
    want = (owner_z * Y + (y + Y - j) % Y) * rows + n % rows
    return (r == want).astype(bf16)


def shards(tokens, basis, cotangent, exp_avg, exp_avg_sq):
    rank, ff = basis.shape[1], cotangent.shape[1]
    here = jnp.stack([lax.axis_index(axis) for axis in ("z", "y", "x", "c")]).astype(jnp.int32)
    ordered = jnp.dot(basis, spread_order(rank), preferred_element_type=f32).astype(bf16)
    mine, other, ordered = project(tokens, basis, ordered)
    lanes = 128
    tile = pl.cdiv(pl.cdiv(ff, lanes), 6) * lanes
    tiles = pl.cdiv(ff, tile)
    made = functools.partial(gradient, mine=mine, other=other, cotangent=cotangent, here=here, tile=tile)
    total = scatter(
        lambda: made(Z_FIRST, start=tiles // 2, stop=tiles), lambda: made(Y_FIRST, start=0, stop=tiles // 2)
    )
    total_tokens = cotangent.shape[0] * Z * Y
    grad_low = total * (1.0 / total_tokens)
    first = 0.9 * exp_avg + 0.1 * grad_low
    second = 0.999 * exp_avg_sq + 0.001 * grad_low * grad_low
    normed = (first / bias_first / (jnp.sqrt(second / bias_second) + 1e-08)).astype(bf16)
    mine, other = (part.reshape(rank // 2, ff // Y) for part in spread(normed))
    update = jnp.dot(ordered[:, : rank // 2], mine, preferred_element_type=f32)
    update = (update + jnp.dot(ordered[:, rank // 2 :], other, preferred_element_type=f32)).astype(bf16)
    return (update, first, second)


def solution(mesh):
    fine = Mesh(np.asarray(mesh.devices).reshape(Z, Y, X, C), ("z", "y", "x", "c"))
    dp, fsdp = ("z", "y"), ("x", "c")
    in_specs = (P(dp, fsdp), P(fsdp, None), P(dp, fsdp), P(dp, fsdp), P(dp, fsdp))
    out_specs = (P(fsdp, dp), P(dp, fsdp), P(dp, fsdp))
    return jax.shard_map(shards, mesh=fine, in_specs=in_specs, out_specs=out_specs, check_vma=False)
```

time: 144 us -> 142 us (0.986)
  Pallas kernels: 8.91 us -> 12.9 us
  waiting for transfers between devices: 50.7 us -> 48.3 us
  starting transfers between devices: 60.4 us -> 58.3 us
  local copies, waits for them, and re-layouts: 3.73 us -> 2.18 us
  matrix products: 8.68 us -> 10.2 us
    pallas_call x1 -> x2, Pallas kernels: 8.91 us -> 12.9 us  [gradient(): pl.pallas_call(functools.partial(grad_kernel, units), grid=(stop - start,...]
    ppermute x4, starting transfers between devices: 18.3 us -> 15.9 us  [spread(): moved_in = lax.ppermute(sent, ('z', 'y', 'x', 'c'), pairs)]
    convert_element_type x0 -> x4, other arithmetic: none -> 2.35 us  [the longest x1 1.14 us: scatter(): one_high.astype(bf16)]
    ppermute x1, waiting for transfers between devices: 3.14 us -> 0.97 us  [scatter(): pair = lax.ppermute(high.astype(bf16), 'z', [(z, z ^ 1) for z in range(Z)])]
    unnamed x24 -> x40, local copies, waits for them, and re-layouts: 2.48 us -> 0.93 us
    dot_general x2 -> x3, matrix products: 3.93 us -> 4.51 us  [the longest x1 3.02 us: project(): lax.dot_general(near_order(rank), basis, lanes, preferred_element_type=f32)]
    ppermute x31 -> x32, starting transfers between devices: 42.1 us -> 42.3 us  [moved(): return lax.ppermute(value, axis, [(i, (i + by) % n) for i in range(n)])]
    ppermute x31 -> x32, waiting for transfers between devices: 39.8 us -> 39.9 us  [moved(): return lax.ppermute(value, axis, [(i, (i + by) % n) for i in range(n)])]
  transfers between devices with their start and end apart: 36 -> 37, of which waited for: 24 -> 25; matrix products, arithmetic and copies ran while one was open for 6% -> 6% of each run, Pallas kernels for 0% -> 5%
where the time goes in v5:
time: 142 us
  starting transfers between devices  58.3 us (41%)
  waiting for transfers between devices  48.3 us (34%)
  Pallas kernels  12.9 us (9%)
  matrix products  10.2 us (7%)
  other arithmetic  8.85 us (6%)
  local copies, waits for them, and re-layouts  2.18 us (2%)
    ppermute x32, starting transfers between devices, moved(): return lax.ppermute(value, axis, [(i, (i + by) % n) for i in range(n)])  42.3 us
    ppermute x32, waiting for transfers between devices, moved(): return lax.ppermute(value, axis, [(i, (i + by) % n) for i in range(n)])  39.9 us
    ppermute x4, starting transfers between devices, spread(): moved_in = lax.ppermute(sent, ('z', 'y', 'x', 'c'), pairs)  15.9 us
    pallas_call x2, Pallas kernels, gradient(): pl.pallas_call(functools.partial(grad_kernel, units), grid=(stop - start,...  12.9 us
    ppermute x4, waiting for transfers between devices, spread(): moved_in = lax.ppermute(sent, ('z', 'y', 'x', 'c'), pairs)  7.51 us
    dot_general x1, matrix products, project(): lax.dot_general(near_order(rank), basis, lanes, preferred_element_type=f32)  3.02 us
    dot_general x1, matrix products, shards(): jnp.dot(basis, spread_order(rank), preferred_element_type=f32).astype(bf16)  3.01 us
  transfers between devices with their start and end apart: 37, of which 25 were waited for; matrix products, arithmetic and copies ran while one was open for 6% of the time, Pallas kernels for 5%

profile of v5, /device:TPU:1, one launch (start us, length us, event | category | flops | bytes accessed | tf_op | source)
XLA Modules:
  0.0 142.1 jit_solution(5308003221770678064)
XLA Ops:
  0.7 3.0 %convolution_convert_fusion = bf16[512,1024]{1,0:T(8,128)(2,1)S(1)} fusion(bf16[1024,512]{1,0:T(8,128)(2,1)} %param.6, s32[512]{0:T(512)S(1)} %get-tuple-element.67, s32[512]{0:T(512)S(1)} %get-tuple-element.68, s32[512]{0:T(512)S(1)} %get-tuple-element.66, s32[512]{0:T(512)S(1)} %get-tuple-element.71, s32[]{:T(128)} %axis_index.29, ...), kind=kOutput, calls=%fused_computation.31 | convolution fusion | flops 548667392 | bytes 2110984 | tf_op jit(solution)/shard_map/dot_general | solution.py:89
  4.5 3.3 %collective-permute-start = (f32[256,1024]{1,0:T(8,128)S(1)}, f32[256,1024]{1,0:T(8,128)S(1)}, u32[]{:S(2)}, u32[]{:S(2)}) collective-permute-start(f32[256,1024]{1,0:T(8,128)S(1)} %fusion.36), channel_id=1, source_target_pairs={{0,1},{1,0},{2,3},{3,2},{4,5},{5,4},{6,7},{7,6},{8,9},{9,8},{10,11... | collective-permute-start | bytes 3145736 | tf_op jit(solution)/shard_map/ppermute | solution.py:19
  8.5 1.7 %collective-permute-done = f32[256,1024]{1,0:T(8,128)S(1)} collective-permute-done((f32[256,1024]{1,0:T(8,128)S(1)}, f32[256,1024]{1,0:T(8,128)S(1)}, u32[]{:S(2)}, u32[]{:S(2)}) %collective-permute-start) | collective-permute-done | bytes 1048608 | tf_op jit(solution)/shard_map/ppermute | solution.py:19
  11.6 1.9 %collective-permute-start.3 = (bf16[64,1024]{1,0:T(8,128)(2,1)}, bf16[64,1024]{1,0:T(8,128)(2,1)S(1)}, u32[]{:S(2)}, u32[]{:S(2)}) collective-permute-start(bf16[64,1024]{1,0:T(8,128)(2,1)} %get-tuple-element.51), channel_id=1, source_target_pairs={{0,4},{2,6},{4,0},{6,2},{1,5},{3,7},{5,1},{7,3},{8,12},{10,14},{12... | collective-permute-start | bytes 393224 | tf_op jit(solution)/shard_map/ppermute | solution.py:19
  13.6 1.2 collective-permute-start.2
  15.3 3.2 %collective-permute-done.1 = bf16[64,1024]{1,0:T(8,128)(2,1)S(1)} collective-permute-done((bf16[64,1024]{1,0:T(8,128)(2,1)}, bf16[64,1024]{1,0:T(8,128)(2,1)S(1)}, u32[]{:S(2)}, u32[]{:S(2)}) %collective-permute-start.1) | collective-permute-done | bytes 131104 | tf_op jit(solution)/shard_map/ppermute | solution.py:19
  18.5 1.4 collective-permute-done.3
  19.9 1.2 collective-permute-done.2
  21.0 1.0 fusion.84
  22.0 3.2 %collective-permute-start.6 = (bf16[64,1024]{1,0:T(8,128)(2,1)S(1)}, bf16[64,1024]{1,0:T(8,128)(2,1)S(1)}, u32[]{:S(2)}, u32[]{:S(2)}) collective-permute-start(bf16[64,1024]{1,0:T(8,128)(2,1)S(1)} %fusion.84), channel_id=1, source_target_pairs={{0,6},{2,0},{4,2},{6,4},{1,7},{3,1},{5,3},{7,5},{8,14},{10,8},{12,... | collective-permute-start | bytes 393224 | tf_op jit(solution)/shard_map/ppermute | solution.py:19
  25.9 3.0 %fusion = bf16[1024,512]{0,1:T(8,128)(2,1)} fusion(bf16[1024,512]{1,0:T(8,128)(2,1)} %param.6, s32[512]{0:T(512)S(1)} %get-tuple-element.74, s32[512]{0:T(512)} %get-tuple-element.75, s32[512]{0:T(512)S(1)} %get-tuple-element.73, s32[512]{0:T(512)} %get-tuple-element.76, s32[]{:T(128)S(6)} %add.289, s32[512]{0:T(512)S(1)} %get-tuple-element.65, ...), kind=kOutput, calls=%fused_computation.33 | convolution fusion | flops 555745280 | bytes 2115596 | tf_op jit(solution)/shard_map/dot_general | solution.py:181
  28.9 1.6 %collective-permute-done.6 = bf16[64,1024]{1,0:T(8,128)(2,1)S(1)} collective-permute-done((bf16[64,1024]{1,0:T(8,128)(2,1)S(1)}, bf16[64,1024]{1,0:T(8,128)(2,1)S(1)}, u32[]{:S(2)}, u32[]{:S(2)}) %collective-permute-start.6) | collective-permute-done | bytes 131104 | tf_op jit(solution)/shard_map/ppermute | solution.py:19
  31.0 3.4 %collective-permute-done.4 = bf16[64,1024]{1,0:T(8,128)(2,1)S(1)} collective-permute-done((bf16[64,1024]{1,0:T(8,128)(2,1)S(1)}, bf16[64,1024]{1,0:T(8,128)(2,1)S(1)}, u32[]{:S(2)}, u32[]{:S(2)}) %collective-permute-start.4) | collective-permute-done | bytes 131104 | tf_op jit(solution)/shard_map/ppermute | solution.py:19
  35.4 1.5 %collective-permute-done.7.other_ref = bf16[256,1024]{1,0:T(8,128)(2,1)S(1)} collective-permute-done((bf16[256,1024]{1,0:T(8,128)(2,1)S(1)}, bf16[256,1024]{1,0:T(8,128)(2,1)S(1)}, u32[]{:S(2)}, u32[]{:S(2)}) %collective-permute-start.7) | collective-permute-done | bytes 524320 | tf_op jit(solution)/shard_map/ppermute | solution.py:19
  37.6 6.4 %shard_map.77 = (bf16[64,1776]{1,0:T(8,128)(2,1)}, bf16[64,1776]{1,0:T(8,128)(2,1)}, f32[64,1776]{1,0:T(8,128)}, f32[64,1776]{1,0:T(8,128)}, f32[64,1776]{1,0:T(...) custom-call(s32[4]{0:T(128)S(1)} %pad_add_fusion.here, bf16[256,1024]{1,0:T(8,128)(2,1)} %copy-done.1, ...), custom_call_target="tpu_custom_call" | custom-call | flops 1862270976 | bytes 6819840 | tf_op jit(solution)/shard_map/pallas_call | solution.py:57
  44.2 3.6 %collective-permute-start.20 = (bf16[64,1776]{1,0:T(8,128)(2,1)}, bf16[64,1776]{1,0:T(8,128)(2,1)S(1)}, u32[]{:S(2)}, u32[]{:S(2)}) collective-permute-start(bf16[64,1776]{1,0:T(8,128)(2,1)} %get-tuple-element.38), channel_id=1, source_target_pairs={{0,224},{32,0},{64,32},{96,64},{128,96},{160,128},{192,160},{224,1... | collective-permute-start | bytes 681992 | tf_op jit(solution)/shard_map/ppermute | solution.py:19
  47.8 6.5 %shard_map.76 = (bf16[64,1920]{1,0:T(8,128)(2,1)}, bf16[64,1920]{1,0:T(8,128)(2,1)}, f32[64,1920]{1,0:T(8,128)}, f32[64,1920]{1,0:T(8,128)}, f32[64,1920]{1,0:T(...) custom-call(s32[4]{0:T(128)S(1)} %pad_add_fusion.here, bf16[256,1024]{1,0:T(8,128)(2,1)} %copy-done.1, ...), custom_call_target="tpu_custom_call" | custom-call | flops 2013265920 | bytes 7372800 | tf_op jit(solution)/shard_map/pallas_call | solution.py:57
  54.3 1.1 convert_element_type.137
  55.4 1.1 convert_element_type.139
  56.5 1.5 %collective-permute-start.8 = (bf16[64,1920]{1,0:T(8,128)(2,1)}, bf16[64,1920]{1,0:T(8,128)(2,1)S(1)}, u32[]{:S(2)}, u32[]{:S(2)}) collective-permute-start(bf16[64,1920]{1,0:T(8,128)(2,1)} %get-tuple-element.26), channel_id=1, source_target_pairs={{0,8},{8,16},{16,24},{24,0},{1,9},{9,17},{17,25},{25,1},{2,10},{10... | collective-permute-start | bytes 737288 | tf_op jit(solution)/shard_map/ppermute | solution.py:19
  58.1 1.5 %collective-permute-start.10 = (bf16[64,1920]{1,0:T(8,128)(2,1)}, bf16[64,1920]{1,0:T(8,128)(2,1)S(1)}, u32[]{:S(2)}, u32[]{:S(2)}) collective-permute-start(bf16[64,1920]{1,0:T(8,128)(2,1)} %get-tuple-element.30), channel_id=1, source_target_pairs={{0,24},{8,0},{16,8},{24,16},{1,25},{9,1},{17,9},{25,17},{2,26},{10... | collective-permute-start | bytes 737288 | tf_op jit(solution)/shard_map/ppermute | solution.py:19
  59.8 2.7 %collective-permute-start.21 = (bf16[64,1776]{1,0:T(8,128)(2,1)S(1)}, bf16[64,1776]{1,0:T(8,128)(2,1)S(1)}, u32[]{:S(2)}, u32[]{:S(2)}) collective-permute-start(bf16[64,1776]{1,0:T(8,128)(2,1)S(1)} %add_convert_fusion.5), channel_id=1, source_target_pairs={{0,224},{32,0},{64,32},{96,64},{128,96},{160,128},{192,160},{224,1... | collective-permute-start | bytes 681992 | tf_op jit(solution)/shard_map/ppermute | solution.py:19
  62.6 2.2 %collective-permute-done.10 = bf16[64,1920]{1,0:T(8,128)(2,1)S(1)} collective-permute-done((bf16[64,1920]{1,0:T(8,128)(2,1)}, bf16[64,1920]{1,0:T(8,128)(2,1)S(1)}, u32[]{:S(2)}, u32[]{:S(2)}) %collective-permute-start.10) | collective-permute-done | bytes 245792 | tf_op jit(solution)/shard_map/ppermute | solution.py:19
  64.9 2.9 %collective-permute-start.11 = (bf16[128,1920]{1,0:T(8,128)(2,1)S(1)}, bf16[128,1920]{1,0:T(8,128)(2,1)S(1)}, u32[]{:S(2)}, u32[]{:S(2)}) collective-permute-start(bf16[128,1920]{1,0:T(8,128)(2,1)S(1)} %pad_maximum_fusion.3), channel_id=1, source_target_pairs={{0,24},{8,0},{16,8},{24,16},{1,25},{9,1},{17,9},{25,17},{2,26},{10... | collective-permute-start | bytes 1474568 | tf_op jit(solution)/shard_map/ppermute | solution.py:19
  68.3 2.7 %collective-permute-start.22 = (bf16[64,1776]{1,0:T(8,128)(2,1)S(1)}, bf16[64,1776]{1,0:T(8,128)(2,1)S(1)}, u32[]{:S(2)}, u32[]{:S(2)}) collective-permute-start(bf16[64,1776]{1,0:T(8,128)(2,1)S(1)} %add_convert_fusion.4), channel_id=1, source_target_pairs={{0,224},{32,0},{64,32},{96,64},{128,96},{160,128},{192,160},{224,1... | collective-permute-start | bytes 681992 | tf_op jit(solution)/shard_map/ppermute | solution.py:19
  71.1 3.6 %collective-permute-done.18 = bf16[64,1776]{1,0:T(8,128)(2,1)S(1)} collective-permute-done((bf16[64,1776]{1,0:T(8,128)(2,1)S(1)}, bf16[64,1776]{1,0:T(8,128)(2,1)S(1)}, u32[]{:S(2)}, u32[]{:S(2)}) %collective-permute-start.18) | collective-permute-done | bytes 227360 | tf_op jit(solution)/shard_map/ppermute | solution.py:19
  74.8 1.9 %collective-permute-done.11 = bf16[128,1920]{1,0:T(8,128)(2,1)S(1)} collective-permute-done((bf16[128,1920]{1,0:T(8,128)(2,1)S(1)}, bf16[128,1920]{1,0:T(8,128)(2,1)S(1)}, u32[]{:S(2)}, u32[]{:S(2)}) %collective-permute-start.11) | collective-permute-done | bytes 491552 | tf_op jit(solution)/shard_map/ppermute | solution.py:19
  76.7 3.3 %collective-permute-done.9 = bf16[128,1920]{1,0:T(8,128)(2,1)S(1)} collective-permute-done((bf16[128,1920]{1,0:T(8,128)(2,1)S(1)}, bf16[128,1920]{1,0:T(8,128)(2,1)S(1)}, u32[]{:S(2)}, u32[]{:S(2)}) %collective-permute-start.9) | collective-permute-done | bytes 491552 | tf_op jit(solution)/shard_map/ppermute | solution.py:19
  81.9 1.8 %collective-permute-start.25 = (bf16[16,1776]{1,0:T(8,128)(2,1)S(1)}, bf16[16,1776]{1,0:T(8,128)(2,1)S(1)}, u32[]{:S(2)}, u32[]{:S(2)}) collective-permute-start(bf16[16,1776]{1,0:T(8,128)(2,1)S(1)} %get-tuple-element.57), channel_id=1, source_target_pairs={{0,24},{8,0},{16,8},{24,16},{1,25},{9,1},{17,9},{25,17},{2,26},{10... | collective-permute-start | bytes 170504 | tf_op jit(solution)/shard_map/ppermute | solution.py:19
  84.3 1.0 collective-permute-done.12
  85.4 3.4 %collective-permute-start.13 = (bf16[16,1920]{1,0:T(8,128)(2,1)S(1)}, bf16[16,1920]{1,0:T(8,128)(2,1)S(1)}, u32[]{:S(2)}, u32[]{:S(2)}) collective-permute-start(bf16[16,1920]{1,0:T(8,128)(2,1)S(1)} %get-tuple-element.53), channel_id=1, source_target_pairs={{0,128},{32,160},{64,192},{96,224},{128,0},{160,32},{192,64},{224,... | collective-permute-start | bytes 184328 | tf_op jit(solution)/shard_map/ppermute | solution.py:19
  89.2 2.0 %collective-permute-start.14 = (bf16[16,1920]{1,0:T(8,128)(2,1)S(1)}, bf16[16,1920]{1,0:T(8,128)(2,1)S(1)}, u32[]{:S(2)}, u32[]{:S(2)}) collective-permute-start(bf16[16,1920]{1,0:T(8,128)(2,1)S(1)} %get-tuple-element.55), channel_id=1, source_target_pairs={{0,64},{32,96},{64,128},{96,160},{128,192},{160,224},{192,0},{224,... | collective-permute-start | bytes 184328 | tf_op jit(solution)/shard_map/ppermute | solution.py:19
  91.2 1.2 collective-permute-done.13
  92.4 1.4 collective-permute-done.15
  93.8 1.3 collective-permute-done.14
  96.7 2.8 %collective-permute-start.28 = (bf16[16,924]{1,0:T(8,128)(2,1)S(1)}, bf16[16,924]{1,0:T(8,128)(2,1)S(1)}, u32[]{:S(2)}, u32[]{:S(2)}) collective-permute-start(bf16[16,924]{1,0:T(8,128)(2,1)S(1)} %bitcast.56), channel_id=1, source_target_pairs={{0,24},{8,0},{16,8},{24,16},{1,25},{9,1},{17,9},{25,17},{2,26},{10... | collective-permute-start | bytes 88712 | tf_op jit(solution)/shard_map/ppermute | solution.py:19
  99.5 1.3 collective-permute-start.27
  100.8 2.7 %collective-permute-done.26 = bf16[16,924]{1,0:T(8,128)(2,1)S(1)} collective-permute-done((bf16[16,924]{1,0:T(8,128)(2,1)S(1)}, bf16[16,924]{1,0:T(8,128)(2,1)S(1)}, u32[]{:S(2)}, u32[]{:S(2)}) %collective-permute-start.26) | collective-permute-done | bytes 29600 | tf_op jit(solution)/shard_map/ppermute | solution.py:19
  104.5 1.7 %collective-permute-start.30 = (bf16[4,16,924]{2,1,0:T(8,128)(2,1)}, bf16[4,16,924]{2,1,0:T(8,128)(2,1)S(1)}, u32[]{:S(2)}, u32[]{:S(2)}) collective-permute-start(bf16[4,16,924]{2,1,0:T(8,128)(2,1)} %pad_maximum_fusion.5), channel_id=1, source_target_pairs={{0,4},{2,6},{4,0},{6,2},{1,5},{3,7},{5,1},{7,3},{8,12},{10,14},{12... | collective-permute-start | bytes 354824 | tf_op jit(solution)/shard_map/ppermute | solution.py:19
  107.2 4.0 %collective-permute-done.31 = bf16[4,16,924]{2,1,0:T(8,128)(2,1)S(1)} collective-permute-done((bf16[4,16,924]{2,1,0:T(8,128)(2,1)}, bf16[4,16,924]{2,1,0:T(8,128)(2,1)S(1)}, u32[]{:S(2)}, u32[]{:S(2)}) %collective-permute-start.31) | collective-permute-done | bytes 118304 | tf_op jit(solution)/shard_map/ppermute | solution.py:19
  111.9 1.0 select_select_fusion.6
  112.9 11.1 %collective-permute-start.32 = (bf16[4,16,924]{2,1,0:T(8,128)(2,1)S(1)}, bf16[4,16,924]{2,1,0:T(8,128)(2,1)S(1)}, u32[]{:S(2)}, u32[]{:S(2)}) collective-permute-start(bf16[4,16,924]{2,1,0:T(8,128)(2,1)S(1)} %get-tuple-element.46), channel_id=1, source_target_pairs={{1,32},{3,34},{5,36},{7,38},{9,40},{11,42},{13,44},{15,46},{17,48}... | collective-permute-start | bytes 354824 | tf_op jit(solution)/shard_map/ppermute | solution.py:161
  123.9 1.0 select_select_fusion.5
  125.0 4.7 %collective-permute-start.34 = (bf16[4,16,924]{2,1,0:T(8,128)(2,1)S(1)}, bf16[4,16,924]{2,1,0:T(8,128)(2,1)S(1)}, u32[]{:S(2)}, u32[]{:S(2)}) collective-permute-start(bf16[4,16,924]{2,1,0:T(8,128)(2,1)S(1)} %get-tuple-element.49), channel_id=1, source_target_pairs={{0,128},{2,130},{4,132},{6,134},{8,136},{10,138},{12,140},{14,142}... | collective-permute-start | bytes 354824 | tf_op jit(solution)/shard_map/ppermute | solution.py:161
  129.8 5.7 %collective-permute-done.33 = bf16[4,16,924]{2,1,0:T(8,128)(2,1)S(1)} collective-permute-done((bf16[4,16,924]{2,1,0:T(8,128)(2,1)S(1)}, bf16[4,16,924]{2,1,0:T(8,128)(2,1)S(1)}, u32[]{:S(2)}, u32[]{:S(2)}) %collective-permute-start.33) | collective-permute-done | bytes 118304 | tf_op jit(solution)/shard_map/ppermute | solution.py:161
  135.7 1.6 %collective-permute-done.35 = bf16[4,16,924]{2,1,0:T(8,128)(2,1)S(1)} collective-permute-done((bf16[4,16,924]{2,1,0:T(8,128)(2,1)S(1)}, bf16[4,16,924]{2,1,0:T(8,128)(2,1)S(1)}, u32[]{:S(2)}, u32[]{:S(2)}) %collective-permute-start.35) | collective-permute-done | bytes 118304 | tf_op jit(solution)/shard_map/ppermute | solution.py:161
  137.4 1.9 %collective-permute-done.36 = bf16[4,4,16,924]{3,2,1,0:T(8,128)(2,1)S(1)} collective-permute-done((bf16[4,4,16,924]{3,2,1,0:T(8,128)(2,1)S(1)}, bf16[4,4,16,924]{3,2,1,0:T(8,128)(2,1)S(1)}, u32[]{:S(2)}, u32[]{:S(2)}) %collective-permute-start.36) | collective-permute-done | bytes 473120 | tf_op jit(solution)/shard_map/ppermute | solution.py:19
  140.1 2.0 %add_convert_fusion = bf16[1024,924]{0,1:T(8,128)(2,1)} fusion(f32[1024,924]{0,1:T(8,128)S(1)} %fusion.39, bf16[256,924]{1,0:T(8,128)(2,1)S(1)} %bitcast.37, bf16[1024,512]{0,1:T(8,128)(2,1)S(1)} %copy-done.3), kind=kOutput, calls=%fused_computation | convolution fusion | flops 486334464 | bytes 6742016 | tf_op jit(solution)/shard_map/dot_general | solution.py:196
  (112 shorter events, 15.6 us)
Async XLA Ops:
  4.5 5.6 %collective-permute-start = (f32[256,1024]{1,0:T(8,128)S(1)}, f32[256,1024]{1,0:T(8,128)S(1)}, u32[]{:S(2)}, u32[]{:S(2)}) collective-permute-start(f32[256,1024]{1,0:T(8,128)S(1)} %fusion.36), channel_id=1, source_target_pairs={{0,1},{1,0},{2,3},{3,2},{4,5},{5,4},{6,7},{7,6},{8,9},{9,8},{10,11... | collective-permute-start | bytes 3145736 | tf_op jit(solution)/shard_map/ppermute | solution.py:19
  11.6 6.9 %collective-permute-start.1 = (bf16[64,1024]{1,0:T(8,128)(2,1)}, bf16[64,1024]{1,0:T(8,128)(2,1)S(1)}, u32[]{:S(2)}, u32[]{:S(2)}) collective-permute-start(bf16[64,1024]{1,0:T(8,128)(2,1)} %get-tuple-element.50), channel_id=1, source_target_pairs={{0,2},{2,4},{4,6},{6,0},{1,3},{3,5},{5,7},{7,1},{8,10},{10,12},{12... | collective-permute-start | bytes 393224 | tf_op jit(solution)/shard_map/ppermute | solution.py:19
  11.6 8.2 %collective-permute-start.3 = (bf16[64,1024]{1,0:T(8,128)(2,1)}, bf16[64,1024]{1,0:T(8,128)(2,1)S(1)}, u32[]{:S(2)}, u32[]{:S(2)}) collective-permute-start(bf16[64,1024]{1,0:T(8,128)(2,1)} %get-tuple-element.51), channel_id=1, source_target_pairs={{0,4},{2,6},{4,0},{6,2},{1,5},{3,7},{5,1},{7,3},{8,12},{10,14},{12... | collective-permute-start | bytes 393224 | tf_op jit(solution)/shard_map/ppermute | solution.py:19
  13.6 7.5 %collective-permute-start.2 = (bf16[64,1024]{1,0:T(8,128)(2,1)S(1)}, bf16[64,1024]{1,0:T(8,128)(2,1)}, u32[]{:S(2)}, u32[]{:S(2)}) collective-permute-start(bf16[64,1024]{1,0:T(8,128)(2,1)S(1)} %get-tuple-element.52), channel_id=1, source_target_pairs={{0,6},{2,0},{4,2},{6,4},{1,7},{3,1},{5,3},{7,5},{8,14},{10,8},{12,... | collective-permute-start | bytes 393224 | tf_op jit(solution)/shard_map/ppermute | solution.py:19
  22.0 8.5 %collective-permute-start.6 = (bf16[64,1024]{1,0:T(8,128)(2,1)S(1)}, bf16[64,1024]{1,0:T(8,128)(2,1)S(1)}, u32[]{:S(2)}, u32[]{:S(2)}) collective-permute-start(bf16[64,1024]{1,0:T(8,128)(2,1)S(1)} %fusion.84), channel_id=1, source_target_pairs={{0,6},{2,0},{4,2},{6,4},{1,7},{3,1},{5,3},{7,5},{8,14},{10,8},{12,... | collective-permute-start | bytes 393224 | tf_op jit(solution)/shard_map/ppermute | solution.py:19
  25.2 5.7 %collective-permute-start.5 = (bf16[64,1024]{1,0:T(8,128)(2,1)S(1)}, bf16[64,1024]{1,0:T(8,128)(2,1)S(1)}, u32[]{:S(2)}, u32[]{:S(2)}) collective-permute-start(bf16[64,1024]{1,0:T(8,128)(2,1)S(1)} %fusion.84), channel_id=1, source_target_pairs={{0,4},{2,6},{4,0},{6,2},{1,5},{3,7},{5,1},{7,3},{8,12},{10,14},{12... | collective-permute-start | bytes 393224 | tf_op jit(solution)/shard_map/ppermute | solution.py:19
  25.2 9.1 %collective-permute-start.4 = (bf16[64,1024]{1,0:T(8,128)(2,1)S(1)}, bf16[64,1024]{1,0:T(8,128)(2,1)S(1)}, u32[]{:S(2)}, u32[]{:S(2)}) collective-permute-start(bf16[64,1024]{1,0:T(8,128)(2,1)S(1)} %fusion.84), channel_id=1, source_target_pairs={{0,2},{2,4},{4,6},{6,0},{1,3},{3,5},{5,7},{7,1},{8,10},{10,12},{12... | collective-permute-start | bytes 393224 | tf_op jit(solution)/shard_map/ppermute | solution.py:19
  34.4 2.5 %collective-permute-start.7 = (bf16[256,1024]{1,0:T(8,128)(2,1)S(1)}, bf16[256,1024]{1,0:T(8,128)(2,1)S(1)}, u32[]{:S(2)}, u32[]{:S(2)}) collective-permute-start(bf16[256,1024]{1,0:T(8,128)(2,1)S(1)} %pad_maximum_fusion.mine_ref), channel_id=1, source_target_pairs={{0,1},{1,0},{2,3},{3,2},{4,5},{5,4},{6,7},{7,6},{8,9},{9,8},{10,11... | collective-permute-start | bytes 1572872 | tf_op jit(solution)/shard_map/ppermute | solution.py:19
  44.0 15.6 %collective-permute-start.16 = (bf16[64,1776]{1,0:T(8,128)(2,1)}, bf16[64,1776]{1,0:T(8,128)(2,1)S(1)}, u32[]{:S(2)}, u32[]{:S(2)}) collective-permute-start(bf16[64,1776]{1,0:T(8,128)(2,1)} %get-tuple-element.35), channel_id=1, source_target_pairs={{0,32},{32,64},{64,96},{96,128},{128,160},{160,192},{192,224},{224... | collective-permute-start | bytes 681992 | tf_op jit(solution)/shard_map/ppermute | solution.py:19
  44.2 15.5 %copy-start.12 = (f32[64,1776]{1,0:T(8,128)S(1)}, f32[64,1776]{1,0:T(8,128)}, u32[]{:S(2)}) copy-start(f32[64,1776]{1,0:T(8,128)} %get-tuple-element.34) | copy-start | bytes 1363972
  44.2 15.6 %collective-permute-start.20 = (bf16[64,1776]{1,0:T(8,128)(2,1)}, bf16[64,1776]{1,0:T(8,128)(2,1)S(1)}, u32[]{:S(2)}, u32[]{:S(2)}) collective-permute-start(bf16[64,1776]{1,0:T(8,128)(2,1)} %get-tuple-element.38), channel_id=1, source_target_pairs={{0,224},{32,0},{64,32},{96,64},{128,96},{160,128},{192,160},{224,1... | collective-permute-start | bytes 681992 | tf_op jit(solution)/shard_map/ppermute | solution.py:19
  54.3 10.6 %copy-start.6 = (f32[64,1920]{1,0:T(8,128)S(1)}, f32[64,1920]{1,0:T(8,128)}, u32[]{:S(2)}) copy-start(f32[64,1920]{1,0:T(8,128)} %get-tuple-element.29) | copy-start | bytes 1474564
  55.4 12.5 %copy-start.5 = (f32[64,1920]{1,0:T(8,128)S(1)}, f32[64,1920]{1,0:T(8,128)}, u32[]{:S(2)}) copy-start(f32[64,1920]{1,0:T(8,128)} %get-tuple-element.25) | copy-start | bytes 1474564
  56.5 11.3 %collective-permute-start.8 = (bf16[64,1920]{1,0:T(8,128)(2,1)}, bf16[64,1920]{1,0:T(8,128)(2,1)S(1)}, u32[]{:S(2)}, u32[]{:S(2)}) collective-permute-start(bf16[64,1920]{1,0:T(8,128)(2,1)} %get-tuple-element.26), channel_id=1, source_target_pairs={{0,8},{8,16},{16,24},{24,0},{1,9},{9,17},{17,25},{25,1},{2,10},{10... | collective-permute-start | bytes 737288 | tf_op jit(solution)/shard_map/ppermute | solution.py:19
  58.1 6.7 %collective-permute-start.10 = (bf16[64,1920]{1,0:T(8,128)(2,1)}, bf16[64,1920]{1,0:T(8,128)(2,1)S(1)}, u32[]{:S(2)}, u32[]{:S(2)}) collective-permute-start(bf16[64,1920]{1,0:T(8,128)(2,1)} %get-tuple-element.30), channel_id=1, source_target_pairs={{0,24},{8,0},{16,8},{24,16},{1,25},{9,1},{17,9},{25,17},{2,26},{10... | collective-permute-start | bytes 737288 | tf_op jit(solution)/shard_map/ppermute | solution.py:19
  59.7 8.4 %collective-permute-start.17 = (bf16[64,1776]{1,0:T(8,128)(2,1)S(1)}, bf16[64,1776]{1,0:T(8,128)(2,1)S(1)}, u32[]{:S(2)}, u32[]{:S(2)}) collective-permute-start(bf16[64,1776]{1,0:T(8,128)(2,1)S(1)} %add_convert_fusion.8), channel_id=1, source_target_pairs={{0,32},{32,64},{64,96},{96,128},{128,160},{160,192},{192,224},{224... | collective-permute-start | bytes 681992 | tf_op jit(solution)/shard_map/ppermute | solution.py:19
  59.8 8.3 %copy-start.10 = (f32[64,1776]{1,0:T(8,128)S(1)}, f32[64,1776]{1,0:T(8,128)}, u32[]{:S(2)}) copy-start(f32[64,1776]{1,0:T(8,128)} %get-tuple-element.33) | copy-start | bytes 1363972
  59.8 8.4 %collective-permute-start.21 = (bf16[64,1776]{1,0:T(8,128)(2,1)S(1)}, bf16[64,1776]{1,0:T(8,128)(2,1)S(1)}, u32[]{:S(2)}, u32[]{:S(2)}) collective-permute-start(bf16[64,1776]{1,0:T(8,128)(2,1)S(1)} %add_convert_fusion.5), channel_id=1, source_target_pairs={{0,224},{32,0},{64,32},{96,64},{128,96},{160,128},{192,160},{224,1... | collective-permute-start | bytes 681992 | tf_op jit(solution)/shard_map/ppermute | solution.py:19
  64.9 9.7 %copy-start.8 = (f32[64,1776]{1,0:T(8,128)S(1)}, f32[64,1776]{1,0:T(8,128)}, u32[]{:S(2)}) copy-start(f32[64,1776]{1,0:T(8,128)} %get-tuple-element.32) | copy-start | bytes 1363972
  64.9 11.7 %collective-permute-start.11 = (bf16[128,1920]{1,0:T(8,128)(2,1)S(1)}, bf16[128,1920]{1,0:T(8,128)(2,1)S(1)}, u32[]{:S(2)}, u32[]{:S(2)}) collective-permute-start(bf16[128,1920]{1,0:T(8,128)(2,1)S(1)} %pad_maximum_fusion.3), channel_id=1, source_target_pairs={{0,24},{8,0},{16,8},{24,16},{1,25},{9,1},{17,9},{25,17},{2,26},{10... | collective-permute-start | bytes 1474568 | tf_op jit(solution)/shard_map/ppermute | solution.py:19
  67.9 12.1 %copy-start.4 = (f32[64,1920]{1,0:T(8,128)S(1)}, f32[64,1920]{1,0:T(8,128)}, u32[]{:S(2)}) copy-start(f32[64,1920]{1,0:T(8,128)} %get-tuple-element.24) | copy-start | bytes 1474564
  68.0 13.1 %copy-start.13 = (f32[64,1776]{1,0:T(8,128)S(1)}, f32[64,1776]{1,0:T(8,128)}, u32[]{:S(2)}) copy-start(f32[64,1776]{1,0:T(8,128)} %get-tuple-element.31) | copy-start | bytes 1363972
  68.0 12.0 %collective-permute-start.9 = (bf16[128,1920]{1,0:T(8,128)(2,1)S(1)}, bf16[128,1920]{1,0:T(8,128)(2,1)S(1)}, u32[]{:S(2)}, u32[]{:S(2)}) collective-permute-start(bf16[128,1920]{1,0:T(8,128)(2,1)S(1)} %pad_maximum_fusion.2), channel_id=1, source_target_pairs={{0,8},{8,16},{16,24},{24,0},{1,9},{9,17},{17,25},{25,1},{2,10},{10... | collective-permute-start | bytes 1474568 | tf_op jit(solution)/shard_map/ppermute | solution.py:19
  68.2 6.5 %collective-permute-start.18 = (bf16[64,1776]{1,0:T(8,128)(2,1)S(1)}, bf16[64,1776]{1,0:T(8,128)(2,1)S(1)}, u32[]{:S(2)}, u32[]{:S(2)}) collective-permute-start(bf16[64,1776]{1,0:T(8,128)(2,1)S(1)} %add_convert_fusion.7), channel_id=1, source_target_pairs={{0,32},{32,64},{64,96},{96,128},{128,160},{160,192},{192,224},{224... | collective-permute-start | bytes 681992 | tf_op jit(solution)/shard_map/ppermute | solution.py:19
  68.3 16.9 %copy-start.7 = (f32[64,1920]{1,0:T(8,128)S(1)}, f32[64,1920]{1,0:T(8,128)}, u32[]{:S(2)}) copy-start(f32[64,1920]{1,0:T(8,128)} %get-tuple-element.23) | copy-start | bytes 1474564
  68.3 11.9 %collective-permute-start.22 = (bf16[64,1776]{1,0:T(8,128)(2,1)S(1)}, bf16[64,1776]{1,0:T(8,128)(2,1)S(1)}, u32[]{:S(2)}, u32[]{:S(2)}) collective-permute-start(bf16[64,1776]{1,0:T(8,128)(2,1)S(1)} %add_convert_fusion.4), channel_id=1, source_target_pairs={{0,224},{32,0},{64,32},{96,64},{128,96},{160,128},{192,160},{224,1... | collective-permute-start | bytes 681992 | tf_op jit(solution)/shard_map/ppermute | solution.py:19
  74.7 6.5 %collective-permute-start.19 = (bf16[64,1776]{1,0:T(8,128)(2,1)S(1)}, bf16[64,1776]{1,0:T(8,128)(2,1)S(1)}, u32[]{:S(2)}, u32[]{:S(2)}) collective-permute-start(bf16[64,1776]{1,0:T(8,128)(2,1)S(1)} %add_convert_fusion.6), channel_id=1, source_target_pairs={{0,32},{32,64},{64,96},{96,128},{128,160},{160,192},{192,224},{224... | collective-permute-start | bytes 681992 | tf_op jit(solution)/shard_map/ppermute | solution.py:19
  80.1 5.1 %collective-permute-start.12 = (bf16[64,1920]{1,0:T(8,128)(2,1)S(1)}, bf16[64,1920]{1,0:T(8,128)(2,1)S(1)}, u32[]{:S(2)}, u32[]{:S(2)}) collective-permute-start(bf16[64,1920]{1,0:T(8,128)(2,1)S(1)} %add_convert_fusion.1), channel_id=1, source_target_pairs={{0,32},{32,0},{64,96},{96,64},{128,160},{160,128},{192,224},{224,1... | collective-permute-start | bytes 737288 | tf_op jit(solution)/shard_map/ppermute | solution.py:118
  81.2 14.0 %copy-start.14 = (f32[16,3696]{1,0:T(8,128)S(1)}, f32[16,3696]{1,0:T(8,128)}, u32[]{:S(2)}) copy-start(f32[16,3696]{1,0:T(8,128)} %param.8) | copy-start | bytes 709636
  81.2 14.0 %copy-start.15 = (f32[16,3696]{1,0:T(8,128)S(1)}, f32[16,3696]{1,0:T(8,128)}, u32[]{:S(2)}) copy-start(f32[16,3696]{1,0:T(8,128)} %param.9) | copy-start | bytes 709636
  81.2 7.9 %collective-permute-start.23 = (bf16[16,1776]{1,0:T(8,128)(2,1)S(1)}, bf16[16,1776]{1,0:T(8,128)(2,1)S(1)}, u32[]{:S(2)}, u32[]{:S(2)}) collective-permute-start(bf16[16,1776]{1,0:T(8,128)(2,1)S(1)} %get-tuple-element.56), channel_id=1, source_target_pairs={{0,16},{8,24},{16,0},{24,8},{1,17},{9,25},{17,1},{25,9},{2,18},{10... | collective-permute-start | bytes 170504 | tf_op jit(solution)/shard_map/ppermute | solution.py:19
  81.9 9.2 %collective-permute-start.25 = (bf16[16,1776]{1,0:T(8,128)(2,1)S(1)}, bf16[16,1776]{1,0:T(8,128)(2,1)S(1)}, u32[]{:S(2)}, u32[]{:S(2)}) collective-permute-start(bf16[16,1776]{1,0:T(8,128)(2,1)S(1)} %get-tuple-element.57), channel_id=1, source_target_pairs={{0,24},{8,0},{16,8},{24,16},{1,25},{9,1},{17,9},{25,17},{2,26},{10... | collective-permute-start | bytes 170504 | tf_op jit(solution)/shard_map/ppermute | solution.py:19
  83.8 7.4 %collective-permute-start.24 = (bf16[16,1776]{1,0:T(8,128)(2,1)S(1)}, bf16[16,1776]{1,0:T(8,128)(2,1)S(1)}, u32[]{:S(2)}, u32[]{:S(2)}) collective-permute-start(bf16[16,1776]{1,0:T(8,128)(2,1)S(1)} %get-tuple-element.58), channel_id=1, source_target_pairs={{0,8},{8,16},{16,24},{24,0},{1,9},{9,17},{17,25},{25,1},{2,10},{10... | collective-permute-start | bytes 170504 | tf_op jit(solution)/shard_map/ppermute | solution.py:19
  85.4 7.1 %collective-permute-start.13 = (bf16[16,1920]{1,0:T(8,128)(2,1)S(1)}, bf16[16,1920]{1,0:T(8,128)(2,1)S(1)}, u32[]{:S(2)}, u32[]{:S(2)}) collective-permute-start(bf16[16,1920]{1,0:T(8,128)(2,1)S(1)} %get-tuple-element.53), channel_id=1, source_target_pairs={{0,128},{32,160},{64,192},{96,224},{128,0},{160,32},{192,64},{224,... | collective-permute-start | bytes 184328 | tf_op jit(solution)/shard_map/ppermute | solution.py:19
  88.8 5.1 %collective-permute-start.15 = (bf16[16,1920]{1,0:T(8,128)(2,1)S(1)}, bf16[16,1920]{1,0:T(8,128)(2,1)S(1)}, u32[]{:S(2)}, u32[]{:S(2)}) collective-permute-start(bf16[16,1920]{1,0:T(8,128)(2,1)S(1)} %get-tuple-element.54), channel_id=1, source_target_pairs={{0,192},{32,224},{64,0},{96,32},{128,64},{160,96},{192,128},{224,1... | collective-permute-start | bytes 184328 | tf_op jit(solution)/shard_map/ppermute | solution.py:19
  89.2 6.0 %collective-permute-start.14 = (bf16[16,1920]{1,0:T(8,128)(2,1)S(1)}, bf16[16,1920]{1,0:T(8,128)(2,1)S(1)}, u32[]{:S(2)}, u32[]{:S(2)}) collective-permute-start(bf16[16,1920]{1,0:T(8,128)(2,1)S(1)} %get-tuple-element.55), channel_id=1, source_target_pairs={{0,64},{32,96},{64,128},{96,160},{128,192},{160,224},{192,0},{224,... | collective-permute-start | bytes 184328 | tf_op jit(solution)/shard_map/ppermute | solution.py:19
  96.7 42.7 %copy-start.3 = (bf16[1024,512]{0,1:T(8,128)(2,1)S(1)}, bf16[1024,512]{0,1:T(8,128)(2,1)}, u32[]{:S(2)}) copy-start(bf16[1024,512]{0,1:T(8,128)(2,1)} %fusion) | copy-start | bytes 3145732
  96.7 4.1 %collective-permute-start.28 = (bf16[16,924]{1,0:T(8,128)(2,1)S(1)}, bf16[16,924]{1,0:T(8,128)(2,1)S(1)}, u32[]{:S(2)}, u32[]{:S(2)}) collective-permute-start(bf16[16,924]{1,0:T(8,128)(2,1)S(1)} %bitcast.56), channel_id=1, source_target_pairs={{0,24},{8,0},{16,8},{24,16},{1,25},{9,1},{17,9},{25,17},{2,26},{10... | collective-permute-start | bytes 88712 | tf_op jit(solution)/shard_map/ppermute | solution.py:19
  99.5 4.0 %collective-permute-start.26 = (bf16[16,924]{1,0:T(8,128)(2,1)S(1)}, bf16[16,924]{1,0:T(8,128)(2,1)S(1)}, u32[]{:S(2)}, u32[]{:S(2)}) collective-permute-start(bf16[16,924]{1,0:T(8,128)(2,1)S(1)} %bitcast.55), channel_id=1, source_target_pairs={{0,8},{8,16},{16,24},{24,0},{1,9},{9,17},{17,25},{25,1},{2,10},{10... | collective-permute-start | bytes 88712 | tf_op jit(solution)/shard_map/ppermute | solution.py:19
  99.5 4.3 %collective-permute-start.27 = (bf16[16,924]{1,0:T(8,128)(2,1)S(1)}, bf16[16,924]{1,0:T(8,128)(2,1)S(1)}, u32[]{:S(2)}, u32[]{:S(2)}) collective-permute-start(bf16[16,924]{1,0:T(8,128)(2,1)S(1)} %bitcast.54), channel_id=1, source_target_pairs={{0,16},{8,24},{16,0},{24,8},{1,17},{9,25},{17,1},{25,9},{2,18},{10... | collective-permute-start | bytes 88712 | tf_op jit(solution)/shard_map/ppermute | solution.py:19
  104.5 6.6 %collective-permute-start.31 = (bf16[4,16,924]{2,1,0:T(8,128)(2,1)}, bf16[4,16,924]{2,1,0:T(8,128)(2,1)S(1)}, u32[]{:S(2)}, u32[]{:S(2)}) collective-permute-start(bf16[4,16,924]{2,1,0:T(8,128)(2,1)} %pad_maximum_fusion.5), channel_id=1, source_target_pairs={{0,2},{2,4},{4,6},{6,0},{1,3},{3,5},{5,7},{7,1},{8,10},{10,12},{12... | collective-permute-start | bytes 354824 | tf_op jit(solution)/shard_map/ppermute | solution.py:19
  104.5 6.6 %collective-permute-start.30 = (bf16[4,16,924]{2,1,0:T(8,128)(2,1)}, bf16[4,16,924]{2,1,0:T(8,128)(2,1)S(1)}, u32[]{:S(2)}, u32[]{:S(2)}) collective-permute-start(bf16[4,16,924]{2,1,0:T(8,128)(2,1)} %pad_maximum_fusion.5), channel_id=1, source_target_pairs={{0,4},{2,6},{4,0},{6,2},{1,5},{3,7},{5,1},{7,3},{8,12},{10,14},{12... | collective-permute-start | bytes 354824 | tf_op jit(solution)/shard_map/ppermute | solution.py:19
  106.3 5.6 %collective-permute-start.29 = (bf16[4,16,924]{2,1,0:T(8,128)(2,1)}, bf16[4,16,924]{2,1,0:T(8,128)(2,1)}, u32[]{:S(2)}, u32[]{:S(2)}) collective-permute-start(bf16[4,16,924]{2,1,0:T(8,128)(2,1)} %pad_maximum_fusion.5), channel_id=1, source_target_pairs={{0,6},{2,0},{4,2},{6,4},{1,7},{3,1},{5,3},{7,5},{8,14},{10,8},{12,... | collective-permute-start | bytes 354824 | tf_op jit(solution)/shard_map/ppermute | solution.py:19
  112.9 16.9 %collective-permute-start.32 = (bf16[4,16,924]{2,1,0:T(8,128)(2,1)S(1)}, bf16[4,16,924]{2,1,0:T(8,128)(2,1)S(1)}, u32[]{:S(2)}, u32[]{:S(2)}) collective-permute-start(bf16[4,16,924]{2,1,0:T(8,128)(2,1)S(1)} %get-tuple-element.46), channel_id=1, source_target_pairs={{1,32},{3,34},{5,36},{7,38},{9,40},{11,42},{13,44},{15,46},{17,48}... | collective-permute-start | bytes 354824 | tf_op jit(solution)/shard_map/ppermute | solution.py:161
  124.9 10.6 %collective-permute-start.33 = (bf16[4,16,924]{2,1,0:T(8,128)(2,1)S(1)}, bf16[4,16,924]{2,1,0:T(8,128)(2,1)S(1)}, u32[]{:S(2)}, u32[]{:S(2)}) collective-permute-start(bf16[4,16,924]{2,1,0:T(8,128)(2,1)S(1)} %get-tuple-element.48), channel_id=1, source_target_pairs={{0,64},{2,66},{4,68},{6,70},{8,72},{10,74},{12,76},{14,78},{16,80}... | collective-permute-start | bytes 354824 | tf_op jit(solution)/shard_map/ppermute | solution.py:161
  125.0 10.7 %collective-permute-start.34 = (bf16[4,16,924]{2,1,0:T(8,128)(2,1)S(1)}, bf16[4,16,924]{2,1,0:T(8,128)(2,1)S(1)}, u32[]{:S(2)}, u32[]{:S(2)}) collective-permute-start(bf16[4,16,924]{2,1,0:T(8,128)(2,1)S(1)} %get-tuple-element.49), channel_id=1, source_target_pairs={{0,128},{2,130},{4,132},{6,134},{8,136},{10,138},{12,140},{14,142}... | collective-permute-start | bytes 354824 | tf_op jit(solution)/shard_map/ppermute | solution.py:161
  129.7 7.5 %collective-permute-start.35 = (bf16[4,16,924]{2,1,0:T(8,128)(2,1)S(1)}, bf16[4,16,924]{2,1,0:T(8,128)(2,1)S(1)}, u32[]{:S(2)}, u32[]{:S(2)}) collective-permute-start(bf16[4,16,924]{2,1,0:T(8,128)(2,1)S(1)} %get-tuple-element.47), channel_id=1, source_target_pairs={{0,192},{2,194},{4,196},{6,198},{8,200},{10,202},{12,204},{14,206}... | collective-permute-start | bytes 354824 | tf_op jit(solution)/shard_map/ppermute | solution.py:161
  137.3 2.0 %collective-permute-start.36 = (bf16[4,4,16,924]{3,2,1,0:T(8,128)(2,1)S(1)}, bf16[4,4,16,924]{3,2,1,0:T(8,128)(2,1)S(1)}, u32[]{:S(2)}, u32[]{:S(2)}) collective-permute-start(bf16[4,4,16,924]{3,2,1,0:T(8,128)(2,1)S(1)} %pad_maximum_fusion.1), channel_id=1, source_target_pairs={{0,1},{1,0},{2,3},{3,2},{4,5},{5,4},{6,7},{7,6},{8,9},{9,8},{10,11... | collective-permute-start | bytes 1419272 | tf_op jit(solution)/shard_map/ppermute | solution.py:19
  (7 other events, 21.5 us)

commit v6 on v5

--- a/solution.py
+++ b/solution.py
@@ -1,5 +1,3 @@
-import functools
-
 import numpy as np
 import jax
 import jax.numpy as jnp
@@ -20,13 +18,15 @@
 
 
 EVEN, ODD = (0, 2, 4, 6), (1, 3, 5, 7)
-Y_FIRST = [[(dy, dz) for dz in half] for dy in (2, 1, 3, 0) for half in (EVEN, ODD)]
-Z_FIRST = [[(dy, dz) for dy in range(Y)] for dz in (4, 5, 3, 6, 2, 7, 1, 0)]
-
-
-def grad_kernel(units, here, mine_ref, other_ref, cot_ref, *rest):
+UNITS = [[(dy, dz, 0) for dz in half] for dy in (2, 1, 3, 0) for half in (EVEN, ODD)]
+UNITS += [[(dy, dz, 1) for dy in range(Y)] for dz in (4, 5, 3, 6, 2, 7, 1, 0)]
+ROUNDED = (0, 1, 3, 4, 8, 9)
+
+
+def grad_kernel(here, mine_ref, other_ref, cot_ref, *rest):
     outs, held = rest[:-1], rest[-1]
     rows = held.shape[0] // (Z * Y)
+    part = rows // 2
     z_odd = lax.rem(here[0], 2) == 1
 
     @pl.when(pl.program_id(0) == 0)
@@ -40,37 +40,44 @@
                 held[pl.ds((dy * Z + dz) * rows, rows), :] = jnp.where(lax.div(oz, X) == c, block_here, block_there)
 
     g = lax.dot_general(held[...], cot_ref[...], (((1,), (1,)), ((), ())), preferred_element_type=f32)
-    place = lambda dy, dz: g[(dy * Z + dz % Z) * rows :][:rows]
-    for out, places in zip(outs, units):
-        turn = units is Y_FIRST and places[0][1] in ODD
-        for i, (dy, dz) in enumerate(places):
-            piece = jnp.where(z_odd, place(dy, dz - 2), place(dy, dz)) if turn else place(dy, dz)
-            out[i * rows : (i + 1) * rows, :] = piece.astype(out.dtype)
-
-
-def gradient(units, mine, other, cotangent, here, tile, start, stop):
+
+    def place(dy, dz, s):
+        block = lambda dz: g[(dy * Z + dz % Z) * rows + s * part :][:part]
+        return jnp.where(z_odd, block(dz - 2), block(dz)) if s == 0 and dz in ODD else block(dz)
+
+    for out, places in zip(outs, UNITS):
+        pieces = [place(*at) for at in places]
+        if out.dtype == f32:
+            for i, piece in enumerate(pieces):
+                out[i * part : (i + 1) * part, :] = piece
+        else:
+            out[...] = jnp.concatenate(pieces, 0).astype(out.dtype)
+
+
+def gradient(mine, other, cotangent, here):
     half, tokens = mine.shape
-    ff = min(stop * tile, cotangent.shape[1]) - start * tile
-    rows = 2 * half // (Z * Y)
+    ff = cotangent.shape[1]
+    part, tile = half // (Z * Y), min(1280, ff)
     whole = lambda i: (0, 0)
-    shapes = [(len(places) * rows, f32 if k > 1 else bf16) for k, places in enumerate(units)]
+    shapes = [(len(places) * part, bf16 if k in ROUNDED else f32) for k, places in enumerate(UNITS)]
+    held_in = pltpu.with_memory_space_constraint
     return pl.pallas_call(
-        functools.partial(grad_kernel, units),
-        grid=(stop - start,),
+        grad_kernel,
+        grid=(pl.cdiv(ff, tile),),
         in_specs=[
             pl.BlockSpec(memory_space=pltpu.SMEM),
-            pl.BlockSpec((half, tokens), whole),
-            pl.BlockSpec((half, tokens), whole),
-            pl.BlockSpec((tile, tokens), lambda i: (start + i, 0)),
+            pl.BlockSpec(memory_space=pltpu.VMEM),
+            pl.BlockSpec(memory_space=pltpu.VMEM),
+            pl.BlockSpec((tile, tokens), lambda i: (i, 0)),
         ],
         out_specs=[pl.BlockSpec((n, tile), lambda i: (0, i)) for n, _ in shapes],
         out_shape=[pltpu.HBM((n, ff), t) for n, t in shapes],
         scratch_shapes=[pltpu.VMEM((2 * half, tokens), bf16)],
-        compiler_params=pltpu.CompilerParams(vmem_limit_bytes=20 * 2**20),
+        compiler_params=pltpu.CompilerParams(vmem_limit_bytes=24 * 2**20),
         cost_estimate=pl.CostEstimate(
             flops=4 * half * tokens * ff, bytes_accessed=2 * tokens * ff + 14 * half * ff // 2, transcendentals=0
         ),
-    )(here, *(pltpu.with_memory_space_constraint(v, pltpu.HBM) for v in (mine, other, cotangent.T)))
+    )(here, held_in(mine, pltpu.VMEM), held_in(other, pltpu.VMEM), held_in(cotangent.T, pltpu.HBM))
 
 
 def near_order(rank):
@@ -99,15 +106,15 @@
     return mine, moved(mine, "c", 1), beside
 
 
-def scatter(ring, relay):
-    four, five, k3, k6, k2, k7, k1, k0 = ring()
+def scatter(*units):
+    two_low, two_high, one_low, one_high, three_low, three_high, low, high = units[:8]
+    four, five, k3, k6, k2, k7, k1, k0 = units[8:]
     up, down = moved(four, "z", 1), moved(five, "z", -1)
-    two_low, two_high, one_low, one_high, three_low, three_high, low, high = relay()
     high_y, low_y = moved(two_low, "y", 1), moved(two_high, "y", -1)
     up = moved((k3 + up.astype(f32)).astype(bf16), "z", 1)
     down = moved((k6 + down.astype(f32)).astype(bf16), "z", -1)
-    one = jnp.concatenate([(one_low + high_y.astype(f32)).astype(bf16), one_high.astype(bf16)], 0)
-    three = jnp.concatenate([three_low.astype(bf16), (three_high + low_y.astype(f32)).astype(bf16)], 0)
+    one = jnp.concatenate([(one_low + high_y.astype(f32)).astype(bf16), one_high], 0)
+    three = jnp.concatenate([three_low, (three_high + low_y.astype(f32)).astype(bf16)], 0)
     across = [moved(one, "y", 1), moved(three, "y", -1)]
     up, down = (k2 + up.astype(f32)).astype(bf16), (k7 + down.astype(f32)).astype(bf16)
     up, down = moved(up, "z", 1), moved(down, "z", -1)
@@ -127,7 +134,7 @@
     second, rounded = second[:rows], second.astype(bf16)
     for k in (2, 1, 3):
         second = second + moved(rounded[k * rows : (k + 1) * rows], "y", k).astype(f32)
-    return jnp.concatenate([first, second], 1)
+    return jnp.concatenate([first, second], 0)
 
 
 def picked(choices, index):
@@ -180,13 +187,7 @@
     here = jnp.stack([lax.axis_index(axis) for axis in ("z", "y", "x", "c")]).astype(jnp.int32)
     ordered = jnp.dot(basis, spread_order(rank), preferred_element_type=f32).astype(bf16)
     mine, other, ordered = project(tokens, basis, ordered)
-    lanes = 128
-    tile = pl.cdiv(pl.cdiv(ff, lanes), 6) * lanes
-    tiles = pl.cdiv(ff, tile)
-    made = functools.partial(gradient, mine=mine, other=other, cotangent=cotangent, here=here, tile=tile)
-    total = scatter(
-        lambda: made(Z_FIRST, start=tiles // 2, stop=tiles), lambda: made(Y_FIRST, start=0, stop=tiles // 2)
-    )
+    total = scatter(*gradient(mine, other, cotangent, here))
     total_tokens = cotangent.shape[0] * Z * Y
     grad_low = total * (1.0 / total_tokens)
     first = 0.9 * exp_avg + 0.1 * grad_low

time: 142 us -> 146 us (1.028)
  waiting for transfers between devices: 48.3 us -> 54.9 us
  Pallas kernels: 12.9 us -> 8.75 us
  starting transfers between devices: 58.3 us -> 60.8 us
    ppermute x4, starting transfers between devices: 15.9 us -> 21 us  [spread(): moved_in = lax.ppermute(sent, ('z', 'y', 'x', 'c'), pairs)]
    pallas_call x2 -> x1, Pallas kernels: 12.9 us -> 8.75 us  [gradient(): pl.pallas_call(grad_kernel, grid=(pl.cdiv(ff, tile),), in_specs=[pl.Block...]
    ppermute x32, waiting for transfers between devices: 39.9 us -> 43.9 us  [moved(): return lax.ppermute(value, axis, [(i, (i + by) % n) for i in range(n)])]
    ppermute x32, starting transfers between devices: 42.3 us -> 39.7 us  [moved(): return lax.ppermute(value, axis, [(i, (i + by) % n) for i in range(n)])]
    ppermute x1, waiting for transfers between devices: 0.97 us -> 3.36 us  [scatter(): pair = lax.ppermute(high.astype(bf16), 'z', [(z, z ^ 1) for z in range(Z)])]
    convert_element_type x2 -> x0, other arithmetic: 2.25 us -> none  [the longest x1 1.14 us: scatter(): one_high.astype(bf16)]
  transfers between devices with their start and end apart: 37 -> 37, of which waited for: 25 -> 25; matrix products, arithmetic and copies ran while one was open for 6% -> 5% of each run, Pallas kernels for 5% -> 0%
where the time goes in v6:
time: 146 us; the launch traced here: 145 us
  starting transfers between devices  60.8 us (42%)
  waiting for transfers between devices  54.9 us (38%)
  matrix products  9.14 us (6%)
  Pallas kernels  8.75 us (6%)
  other arithmetic  8.73 us (6%)
  local copies, waits for them, and re-layouts  1.88 us (1%)
    ppermute x32, waiting for transfers between devices, moved(): return lax.ppermute(value, axis, [(i, (i + by) % n) for i in range(n)])  43.9 us
    ppermute x32, starting transfers between devices, moved(): return lax.ppermute(value, axis, [(i, (i + by) % n) for i in range(n)])  39.7 us
    ppermute x4, starting transfers between devices, spread(): moved_in = lax.ppermute(sent, ('z', 'y', 'x', 'c'), pairs)  21 us
    pallas_call x1, Pallas kernels, gradient(): pl.pallas_call(grad_kernel, grid=(pl.cdiv(ff, tile),), in_specs=[pl.Block...  8.75 us
    ppermute x4, waiting for transfers between devices, spread(): moved_in = lax.ppermute(sent, ('z', 'y', 'x', 'c'), pairs)  7.65 us
    ppermute x1, waiting for transfers between devices, scatter(): pair = lax.ppermute(high.astype(bf16), 'z', [(z, z ^ 1) for z in range(Z)])  3.36 us
  transfers between devices with their start and end apart: 37, of which 25 were waited for; matrix products, arithmetic and copies ran while one was open for 5% of the time, Pallas kernels for 0%

profile of v6, /device:TPU:1, one launch (start us, length us, event | category | flops | bytes accessed | tf_op | source)
XLA Modules:
  0.0 145.3 jit_solution(11536252808513744824)
XLA Ops:
  1.2 2.9 %convolution_convert_fusion = bf16[512,1024]{1,0:T(8,128)(2,1)S(1)} fusion(bf16[1024,512]{1,0:T(8,128)(2,1)} %param.6, s32[512]{0:T(512)S(1)} %get-tuple-element.67, s32[512]{0:T(512)S(1)} %get-tuple-element.68, s32[512]{0:T(512)S(1)} %get-tuple-element.66, s32[512]{0:T(512)S(1)} %get-tuple-element.71, s32[]{:T(128)} %axis_index.29, ...), kind=kOutput, calls=%fused_computation.31 | convolution fusion | flops 548667392 | bytes 2110984 | tf_op jit(solution)/shard_map/dot_general | solution.py:96
  4.9 3.3 %collective-permute-start = (f32[256,1024]{1,0:T(8,128)S(1)}, f32[256,1024]{1,0:T(8,128)S(1)}, u32[]{:S(2)}, u32[]{:S(2)}) collective-permute-start(f32[256,1024]{1,0:T(8,128)S(1)} %fusion.36), channel_id=1, source_target_pairs={{0,1},{1,0},{2,3},{3,2},{4,5},{5,4},{6,7},{7,6},{8,9},{9,8},{10,11... | collective-permute-start | bytes 3145736 | tf_op jit(solution)/shard_map/ppermute | solution.py:17
  8.8 1.7 %collective-permute-done = f32[256,1024]{1,0:T(8,128)S(1)} collective-permute-done((f32[256,1024]{1,0:T(8,128)S(1)}, f32[256,1024]{1,0:T(8,128)S(1)}, u32[]{:S(2)}, u32[]{:S(2)}) %collective-permute-start) | collective-permute-done | bytes 1048608 | tf_op jit(solution)/shard_map/ppermute | solution.py:17
  12.0 1.0 collective-permute-start.3
  15.1 3.4 %collective-permute-done.3 = bf16[64,1024]{1,0:T(8,128)(2,1)S(1)} collective-permute-done((bf16[64,1024]{1,0:T(8,128)(2,1)}, bf16[64,1024]{1,0:T(8,128)(2,1)S(1)}, u32[]{:S(2)}, u32[]{:S(2)}) %collective-permute-start.3) | collective-permute-done | bytes 131104 | tf_op jit(solution)/shard_map/ppermute | solution.py:17
  18.4 1.3 collective-permute-done.2
  19.7 2.0 %collective-permute-done.1 = bf16[64,1024]{1,0:T(8,128)(2,1)} collective-permute-done((bf16[64,1024]{1,0:T(8,128)(2,1)S(1)}, bf16[64,1024]{1,0:T(8,128)(2,1)}, u32[]{:S(2)}, u32[]{:S(2)}) %collective-permute-start.1) | collective-permute-done | bytes 131104 | tf_op jit(solution)/shard_map/ppermute | solution.py:17
  21.7 1.0 fusion.84
  22.7 1.1 collective-permute-start.6
  25.0 2.0 %fusion = bf16[1024,512]{0,1:T(8,128)(2,1)S(1)} fusion(bf16[1024,512]{1,0:T(8,128)(2,1)} %param.6, s32[512]{0:T(512)} %get-tuple-element.74, s32[512]{0:T(512)S(1)} %get-tuple-element.75, s32[512]{0:T(512)} %get-tuple-element.73, s32[512]{0:T(512)S(1)} %get-tuple-element.76, s32[]{:T(128)S(6)} %add.289, s32[512]{0:T(512)S(1)} %get-tuple-element.65, ...), kind=kOutput, calls=%fused_computation.33 | convolution fusion | flops 555745280 | bytes 2115596 | tf_op jit(solution)/shard_map/dot_general | solution.py:188
  27.0 2.5 %collective-permute-done.5 = bf16[64,1024]{1,0:T(8,128)(2,1)S(1)} collective-permute-done((bf16[64,1024]{1,0:T(8,128)(2,1)S(1)}, bf16[64,1024]{1,0:T(8,128)(2,1)S(1)}, u32[]{:S(2)}, u32[]{:S(2)}) %collective-permute-start.5) | collective-permute-done | bytes 131104 | tf_op jit(solution)/shard_map/ppermute | solution.py:17
  29.5 3.9 %collective-permute-done.4 = bf16[64,1024]{1,0:T(8,128)(2,1)S(1)} collective-permute-done((bf16[64,1024]{1,0:T(8,128)(2,1)S(1)}, bf16[64,1024]{1,0:T(8,128)(2,1)S(1)}, u32[]{:S(2)}, u32[]{:S(2)}) %collective-permute-start.4) | collective-permute-done | bytes 131104 | tf_op jit(solution)/shard_map/ppermute | solution.py:17
  34.2 1.5 %collective-permute-done.7.other_ref = bf16[256,1024]{1,0:T(8,128)(2,1)S(1)} collective-permute-done((bf16[256,1024]{1,0:T(8,128)(2,1)S(1)}, bf16[256,1024]{1,0:T(8,128)(2,1)S(1)}, u32[]{:S(2)}, u32[]{:S(2)}) %collective-permute-start.7) | collective-permute-done | bytes 524320 | tf_op jit(solution)/shard_map/ppermute | solution.py:17
  35.6 8.8 %shard_map.76 = (bf16[32,3696]{1,0:T(8,128)(2,1)}, bf16[32,3696]{1,0:T(8,128)(2,1)}, f32[32,3696]{1,0:T(8,128)}, bf16[32,3696]{1,0:T(8,128)(2,1)}, bf16[32,3696]...) custom-call(s32[4]{0:T(128)S(1)} %pad_add_fusion.here, ...), custom_call_target="tpu_custom_call" | custom-call | flops 3875536896 | bytes 14192640 | tf_op jit(solution)/shard_map/pallas_call | solution.py:64
  44.4 5.6 %collective-permute-start.20 = (bf16[32,3696]{1,0:T(8,128)(2,1)}, bf16[32,3696]{1,0:T(8,128)(2,1)}, u32[]{:S(2)}, u32[]{:S(2)}) collective-permute-start(bf16[32,3696]{1,0:T(8,128)(2,1)} %get-tuple-element.38), channel_id=1, source_target_pairs={{0,224},{32,0},{64,32},{96,64},{128,96},{160,128},{192,160},{224,1... | collective-permute-start | bytes 709640 | tf_op jit(solution)/shard_map/ppermute | solution.py:17
  50.1 2.7 %collective-permute-start.10 = (bf16[32,3696]{1,0:T(8,128)(2,1)}, bf16[32,3696]{1,0:T(8,128)(2,1)S(1)}, u32[]{:S(2)}, u32[]{:S(2)}) collective-permute-start(bf16[32,3696]{1,0:T(8,128)(2,1)} %get-tuple-element.30), channel_id=1, source_target_pairs={{0,24},{8,0},{16,8},{24,16},{1,25},{9,1},{17,9},{25,17},{2,26},{10... | collective-permute-start | bytes 709640 | tf_op jit(solution)/shard_map/ppermute | solution.py:17
  52.8 2.3 %collective-permute-done.20 = bf16[32,3696]{1,0:T(8,128)(2,1)} collective-permute-done((bf16[32,3696]{1,0:T(8,128)(2,1)}, bf16[32,3696]{1,0:T(8,128)(2,1)}, u32[]{:S(2)}, u32[]{:S(2)}) %collective-permute-start.20) | collective-permute-done | bytes 236576 | tf_op jit(solution)/shard_map/ppermute | solution.py:17
  55.1 1.1 add_convert_fusion.2
  56.3 3.5 %collective-permute-start.21 = (bf16[32,3696]{1,0:T(8,128)(2,1)S(1)}, bf16[32,3696]{1,0:T(8,128)(2,1)S(1)}, u32[]{:S(2)}, u32[]{:S(2)}) collective-permute-start(bf16[32,3696]{1,0:T(8,128)(2,1)S(1)} %add_convert_fusion.2), channel_id=1, source_target_pairs={{0,224},{32,0},{64,32},{96,64},{128,96},{160,128},{192,160},{224,1... | collective-permute-start | bytes 709640 | tf_op jit(solution)/shard_map/ppermute | solution.py:17
  59.8 1.1 add_convert_fusion.5
  61.1 2.8 %collective-permute-start.11 = (bf16[64,3696]{1,0:T(8,128)(2,1)S(1)}, bf16[64,3696]{1,0:T(8,128)(2,1)S(1)}, u32[]{:S(2)}, u32[]{:S(2)}) collective-permute-start(bf16[64,3696]{1,0:T(8,128)(2,1)S(1)} %pad_maximum_fusion.3), channel_id=1, source_target_pairs={{0,24},{8,0},{16,8},{24,16},{1,25},{9,1},{17,9},{25,17},{2,26},{10... | collective-permute-start | bytes 1419272 | tf_op jit(solution)/shard_map/ppermute | solution.py:17
  64.2 3.0 %collective-permute-start.22 = (bf16[32,3696]{1,0:T(8,128)(2,1)S(1)}, bf16[32,3696]{1,0:T(8,128)(2,1)S(1)}, u32[]{:S(2)}, u32[]{:S(2)}) collective-permute-start(bf16[32,3696]{1,0:T(8,128)(2,1)S(1)} %add_convert_fusion.1), channel_id=1, source_target_pairs={{0,224},{32,0},{64,32},{96,64},{128,96},{160,128},{192,160},{224,1... | collective-permute-start | bytes 709640 | tf_op jit(solution)/shard_map/ppermute | solution.py:17
  68.0 4.5 %collective-permute-done.11 = bf16[64,3696]{1,0:T(8,128)(2,1)S(1)} collective-permute-done((bf16[64,3696]{1,0:T(8,128)(2,1)S(1)}, bf16[64,3696]{1,0:T(8,128)(2,1)S(1)}, u32[]{:S(2)}, u32[]{:S(2)}) %collective-permute-start.11) | collective-permute-done | bytes 473120 | tf_op jit(solution)/shard_map/ppermute | solution.py:17
  72.6 3.3 %collective-permute-done.9 = bf16[64,3696]{1,0:T(8,128)(2,1)S(1)} collective-permute-done((bf16[64,3696]{1,0:T(8,128)(2,1)S(1)}, bf16[64,3696]{1,0:T(8,128)(2,1)S(1)}, u32[]{:S(2)}, u32[]{:S(2)}) %collective-permute-start.9) | collective-permute-done | bytes 473120 | tf_op jit(solution)/shard_map/ppermute | solution.py:17
  76.2 1.5 %collective-permute-start.19 = (bf16[32,3696]{1,0:T(8,128)(2,1)S(1)}, bf16[32,3696]{1,0:T(8,128)(2,1)S(1)}, u32[]{:S(2)}, u32[]{:S(2)}) collective-permute-start(bf16[32,3696]{1,0:T(8,128)(2,1)S(1)} %add_convert_fusion.3), channel_id=1, source_target_pairs={{0,32},{32,64},{64,96},{96,128},{128,160},{160,192},{192,224},{224... | collective-permute-start | bytes 709640 | tf_op jit(solution)/shard_map/ppermute | solution.py:17
  77.7 3.4 %collective-permute-done.12 = bf16[32,3696]{1,0:T(8,128)(2,1)S(1)} collective-permute-done((bf16[32,3696]{1,0:T(8,128)(2,1)S(1)}, bf16[32,3696]{1,0:T(8,128)(2,1)S(1)}, u32[]{:S(2)}, u32[]{:S(2)}) %collective-permute-start.12) | collective-permute-done | bytes 236576 | tf_op jit(solution)/shard_map/ppermute | solution.py:125
  81.2 2.2 %collective-permute-start.15 = (bf16[8,3696]{1,0:T(8,128)(2,1)S(1)}, bf16[8,3696]{1,0:T(8,128)(2,1)S(1)}, u32[]{:S(2)}, u32[]{:S(2)}) collective-permute-start(bf16[8,3696]{1,0:T(8,128)(2,1)S(1)} %get-tuple-element.54), channel_id=1, source_target_pairs={{0,192},{32,224},{64,0},{96,32},{128,64},{160,96},{192,128},{224,1... | collective-permute-start | bytes 177416 | tf_op jit(solution)/shard_map/ppermute | solution.py:17
  83.6 1.9 %collective-permute-start.13 = (bf16[8,3696]{1,0:T(8,128)(2,1)S(1)}, bf16[8,3696]{1,0:T(8,128)(2,1)S(1)}, u32[]{:S(2)}, u32[]{:S(2)}) collective-permute-start(bf16[8,3696]{1,0:T(8,128)(2,1)S(1)} %get-tuple-element.53), channel_id=1, source_target_pairs={{0,128},{32,160},{64,192},{96,224},{128,0},{160,32},{192,64},{224,... | collective-permute-start | bytes 177416 | tf_op jit(solution)/shard_map/ppermute | solution.py:17
  85.8 1.4 collective-permute-start.24
  87.2 2.4 %collective-permute-done.14 = bf16[8,3696]{1,0:T(8,128)(2,1)S(1)} collective-permute-done((bf16[8,3696]{1,0:T(8,128)(2,1)S(1)}, bf16[8,3696]{1,0:T(8,128)(2,1)S(1)}, u32[]{:S(2)}, u32[]{:S(2)}) %collective-permute-start.14) | collective-permute-done | bytes 59168 | tf_op jit(solution)/shard_map/ppermute | solution.py:17
  89.6 1.7 %collective-permute-done.13 = bf16[8,3696]{1,0:T(8,128)(2,1)S(1)} collective-permute-done((bf16[8,3696]{1,0:T(8,128)(2,1)S(1)}, bf16[8,3696]{1,0:T(8,128)(2,1)S(1)}, u32[]{:S(2)}, u32[]{:S(2)}) %collective-permute-start.13) | collective-permute-done | bytes 59168 | tf_op jit(solution)/shard_map/ppermute | solution.py:17
  93.3 1.4 collective-permute-start.28
  95.5 1.2 collective-permute-done.28
  96.7 2.7 %collective-permute-done.27 = bf16[16,924]{1,0:T(8,128)(2,1)S(1)} collective-permute-done((bf16[16,924]{1,0:T(8,128)(2,1)S(1)}, bf16[16,924]{1,0:T(8,128)(2,1)S(1)}, u32[]{:S(2)}, u32[]{:S(2)}) %collective-permute-start.27) | collective-permute-done | bytes 29600 | tf_op jit(solution)/shard_map/ppermute | solution.py:17
  102.3 2.5 %collective-permute-done.29 = bf16[4,16,924]{2,1,0:T(8,128)(2,1)S(1)} collective-permute-done((bf16[4,16,924]{2,1,0:T(8,128)(2,1)}, bf16[4,16,924]{2,1,0:T(8,128)(2,1)S(1)}, u32[]{:S(2)}, u32[]{:S(2)}) %collective-permute-start.29) | collective-permute-done | bytes 118304 | tf_op jit(solution)/shard_map/ppermute | solution.py:17
  104.8 1.9 %collective-permute-done.30 = bf16[4,16,924]{2,1,0:T(8,128)(2,1)S(1)} collective-permute-done((bf16[4,16,924]{2,1,0:T(8,128)(2,1)}, bf16[4,16,924]{2,1,0:T(8,128)(2,1)S(1)}, u32[]{:S(2)}, u32[]{:S(2)}) %collective-permute-start.30) | collective-permute-done | bytes 118304 | tf_op jit(solution)/shard_map/ppermute | solution.py:17
  106.7 1.6 %collective-permute-done.31 = bf16[4,16,924]{2,1,0:T(8,128)(2,1)} collective-permute-done((bf16[4,16,924]{2,1,0:T(8,128)(2,1)}, bf16[4,16,924]{2,1,0:T(8,128)(2,1)}, u32[]{:S(2)}, u32[]{:S(2)}) %collective-permute-start.31) | collective-permute-done | bytes 118304 | tf_op jit(solution)/shard_map/ppermute | solution.py:17
  109.3 14.5 %collective-permute-start.35 = (bf16[4,16,924]{2,1,0:T(8,128)(2,1)S(1)}, bf16[4,16,924]{2,1,0:T(8,128)(2,1)S(1)}, u32[]{:S(2)}, u32[]{:S(2)}) collective-permute-start(bf16[4,16,924]{2,1,0:T(8,128)(2,1)S(1)} %get-tuple-element.47), channel_id=1, source_target_pairs={{0,192},{2,194},{4,196},{6,198},{8,200},{10,202},{12,204},{14,206}... | collective-permute-start | bytes 354824 | tf_op jit(solution)/shard_map/ppermute | solution.py:168
  123.8 1.9 %collective-permute-start.32 = (bf16[4,16,924]{2,1,0:T(8,128)(2,1)S(1)}, bf16[4,16,924]{2,1,0:T(8,128)(2,1)S(1)}, u32[]{:S(2)}, u32[]{:S(2)}) collective-permute-start(bf16[4,16,924]{2,1,0:T(8,128)(2,1)S(1)} %get-tuple-element.46), channel_id=1, source_target_pairs={{1,32},{3,34},{5,36},{7,38},{9,40},{11,42},{13,44},{15,46},{17,48}... | collective-permute-start | bytes 354824 | tf_op jit(solution)/shard_map/ppermute | solution.py:168
  125.7 1.0 select_select_fusion.5
  126.7 1.9 %collective-permute-start.34 = (bf16[4,16,924]{2,1,0:T(8,128)(2,1)S(1)}, bf16[4,16,924]{2,1,0:T(8,128)(2,1)S(1)}, u32[]{:S(2)}, u32[]{:S(2)}) collective-permute-start(bf16[4,16,924]{2,1,0:T(8,128)(2,1)S(1)} %get-tuple-element.49), channel_id=1, source_target_pairs={{0,128},{2,130},{4,132},{6,134},{8,136},{10,138},{12,140},{14,142}... | collective-permute-start | bytes 354824 | tf_op jit(solution)/shard_map/ppermute | solution.py:168
  128.6 2.8 %collective-permute-start.33 = (bf16[4,16,924]{2,1,0:T(8,128)(2,1)S(1)}, bf16[4,16,924]{2,1,0:T(8,128)(2,1)S(1)}, u32[]{:S(2)}, u32[]{:S(2)}) collective-permute-start(bf16[4,16,924]{2,1,0:T(8,128)(2,1)S(1)} %get-tuple-element.48), channel_id=1, source_target_pairs={{0,64},{2,66},{4,68},{6,70},{8,72},{10,74},{12,76},{14,78},{16,80}... | collective-permute-start | bytes 354824 | tf_op jit(solution)/shard_map/ppermute | solution.py:168
  131.3 2.6 %collective-permute-done.32 = bf16[4,16,924]{2,1,0:T(8,128)(2,1)S(1)} collective-permute-done((bf16[4,16,924]{2,1,0:T(8,128)(2,1)S(1)}, bf16[4,16,924]{2,1,0:T(8,128)(2,1)S(1)}, u32[]{:S(2)}, u32[]{:S(2)}) %collective-permute-start.32) | collective-permute-done | bytes 118304 | tf_op jit(solution)/shard_map/ppermute | solution.py:168
  133.9 2.2 %collective-permute-done.34 = bf16[4,16,924]{2,1,0:T(8,128)(2,1)S(1)} collective-permute-done((bf16[4,16,924]{2,1,0:T(8,128)(2,1)S(1)}, bf16[4,16,924]{2,1,0:T(8,128)(2,1)S(1)}, u32[]{:S(2)}, u32[]{:S(2)}) %collective-permute-start.34) | collective-permute-done | bytes 118304 | tf_op jit(solution)/shard_map/ppermute | solution.py:168
  136.2 2.8 %collective-permute-done.33 = bf16[4,16,924]{2,1,0:T(8,128)(2,1)S(1)} collective-permute-done((bf16[4,16,924]{2,1,0:T(8,128)(2,1)S(1)}, bf16[4,16,924]{2,1,0:T(8,128)(2,1)S(1)}, u32[]{:S(2)}, u32[]{:S(2)}) %collective-permute-start.33) | collective-permute-done | bytes 118304 | tf_op jit(solution)/shard_map/ppermute | solution.py:168
  139.1 2.0 %collective-permute-start.36 = (bf16[4,4,16,924]{3,2,1,0:T(8,128)(2,1)S(1)}, bf16[4,4,16,924]{3,2,1,0:T(8,128)(2,1)S(1)}, u32[]{:S(2)}, u32[]{:S(2)}) collective-permute-start(bf16[4,4,16,924]{3,2,1,0:T(8,128)(2,1)S(1)} %pad_maximum_fusion.1), channel_id=1, source_target_pairs={{0,1},{1,0},{2,3},{3,2},{4,5},{5,4},{6,7},{7,6},{8,9},{9,8},{10,11... | collective-permute-start | bytes 1419272 | tf_op jit(solution)/shard_map/ppermute | solution.py:17
  141.0 1.5 %collective-permute-done.36 = bf16[4,4,16,924]{3,2,1,0:T(8,128)(2,1)S(1)} collective-permute-done((bf16[4,4,16,924]{3,2,1,0:T(8,128)(2,1)S(1)}, bf16[4,4,16,924]{3,2,1,0:T(8,128)(2,1)S(1)}, u32[]{:S(2)}, u32[]{:S(2)}) %collective-permute-start.36) | collective-permute-done | bytes 473120 | tf_op jit(solution)/shard_map/ppermute | solution.py:17
  143.3 2.0 %add_convert_fusion = bf16[1024,924]{0,1:T(8,128)(2,1)} fusion(f32[1024,924]{0,1:T(8,128)S(1)} %fusion.39, bf16[256,924]{1,0:T(8,128)(2,1)S(1)} %bitcast.35, bf16[1024,512]{0,1:T(8,128)(2,1)S(1)} %fusion), kind=kOutput, calls=%fused_computation | convolution fusion | flops 486334464 | bytes 6742016 | tf_op jit(solution)/shard_map/dot_general | solution.py:197
  (103 shorter events, 17.0 us)
Async XLA Ops:
  4.9 5.6 %collective-permute-start = (f32[256,1024]{1,0:T(8,128)S(1)}, f32[256,1024]{1,0:T(8,128)S(1)}, u32[]{:S(2)}, u32[]{:S(2)}) collective-permute-start(f32[256,1024]{1,0:T(8,128)S(1)} %fusion.36), channel_id=1, source_target_pairs={{0,1},{1,0},{2,3},{3,2},{4,5},{5,4},{6,7},{7,6},{8,9},{9,8},{10,11... | collective-permute-start | bytes 3145736 | tf_op jit(solution)/shard_map/ppermute | solution.py:17
  12.0 6.4 %collective-permute-start.3 = (bf16[64,1024]{1,0:T(8,128)(2,1)}, bf16[64,1024]{1,0:T(8,128)(2,1)S(1)}, u32[]{:S(2)}, u32[]{:S(2)}) collective-permute-start(bf16[64,1024]{1,0:T(8,128)(2,1)} %get-tuple-element.51), channel_id=1, source_target_pairs={{0,4},{2,6},{4,0},{6,2},{1,5},{3,7},{5,1},{7,3},{8,12},{10,14},{12... | collective-permute-start | bytes 393224 | tf_op jit(solution)/shard_map/ppermute | solution.py:17
  13.0 6.7 %collective-permute-start.2 = (bf16[64,1024]{1,0:T(8,128)(2,1)}, bf16[64,1024]{1,0:T(8,128)(2,1)S(1)}, u32[]{:S(2)}, u32[]{:S(2)}) collective-permute-start(bf16[64,1024]{1,0:T(8,128)(2,1)} %get-tuple-element.52), channel_id=1, source_target_pairs={{0,6},{2,0},{4,2},{6,4},{1,7},{3,1},{5,3},{7,5},{8,14},{10,8},{12,... | collective-permute-start | bytes 393224 | tf_op jit(solution)/shard_map/ppermute | solution.py:17
  13.9 7.8 %collective-permute-start.1 = (bf16[64,1024]{1,0:T(8,128)(2,1)S(1)}, bf16[64,1024]{1,0:T(8,128)(2,1)}, u32[]{:S(2)}, u32[]{:S(2)}) collective-permute-start(bf16[64,1024]{1,0:T(8,128)(2,1)S(1)} %get-tuple-element.50), channel_id=1, source_target_pairs={{0,2},{2,4},{4,6},{6,0},{1,3},{3,5},{5,7},{7,1},{8,10},{10,12},{12... | collective-permute-start | bytes 393224 | tf_op jit(solution)/shard_map/ppermute | solution.py:17
  22.7 4.3 %collective-permute-start.6 = (bf16[64,1024]{1,0:T(8,128)(2,1)S(1)}, bf16[64,1024]{1,0:T(8,128)(2,1)S(1)}, u32[]{:S(2)}, u32[]{:S(2)}) collective-permute-start(bf16[64,1024]{1,0:T(8,128)(2,1)S(1)} %fusion.84), channel_id=1, source_target_pairs={{0,6},{2,0},{4,2},{6,4},{1,7},{3,1},{5,3},{7,5},{8,14},{10,8},{12,... | collective-permute-start | bytes 393224 | tf_op jit(solution)/shard_map/ppermute | solution.py:17
  23.7 5.8 %collective-permute-start.5 = (bf16[64,1024]{1,0:T(8,128)(2,1)S(1)}, bf16[64,1024]{1,0:T(8,128)(2,1)S(1)}, u32[]{:S(2)}, u32[]{:S(2)}) collective-permute-start(bf16[64,1024]{1,0:T(8,128)(2,1)S(1)} %fusion.84), channel_id=1, source_target_pairs={{0,4},{2,6},{4,0},{6,2},{1,5},{3,7},{5,1},{7,3},{8,12},{10,14},{12... | collective-permute-start | bytes 393224 | tf_op jit(solution)/shard_map/ppermute | solution.py:17
  24.4 9.0 %collective-permute-start.4 = (bf16[64,1024]{1,0:T(8,128)(2,1)S(1)}, bf16[64,1024]{1,0:T(8,128)(2,1)S(1)}, u32[]{:S(2)}, u32[]{:S(2)}) collective-permute-start(bf16[64,1024]{1,0:T(8,128)(2,1)S(1)} %fusion.84), channel_id=1, source_target_pairs={{0,2},{2,4},{4,6},{6,0},{1,3},{3,5},{5,7},{7,1},{8,10},{10,12},{12... | collective-permute-start | bytes 393224 | tf_op jit(solution)/shard_map/ppermute | solution.py:17
  33.4 2.2 %collective-permute-start.7 = (bf16[256,1024]{1,0:T(8,128)(2,1)S(1)}, bf16[256,1024]{1,0:T(8,128)(2,1)S(1)}, u32[]{:S(2)}, u32[]{:S(2)}) collective-permute-start(bf16[256,1024]{1,0:T(8,128)(2,1)S(1)} %pad_maximum_fusion.mine_ref), channel_id=1, source_target_pairs={{0,1},{1,0},{2,3},{3,2},{4,5},{5,4},{6,7},{7,6},{8,9},{9,8},{10,11... | collective-permute-start | bytes 1572872 | tf_op jit(solution)/shard_map/ppermute | solution.py:17
  44.4 16.6 %copy-start.12 = (bf16[32,3696]{1,0:T(8,128)(2,1)S(1)}, bf16[32,3696]{1,0:T(8,128)(2,1)}, u32[]{:S(2)}) copy-start(bf16[32,3696]{1,0:T(8,128)(2,1)} %get-tuple-element.28) | copy-start | bytes 709636
  44.4 10.7 %collective-permute-start.20 = (bf16[32,3696]{1,0:T(8,128)(2,1)}, bf16[32,3696]{1,0:T(8,128)(2,1)}, u32[]{:S(2)}, u32[]{:S(2)}) collective-permute-start(bf16[32,3696]{1,0:T(8,128)(2,1)} %get-tuple-element.38), channel_id=1, source_target_pairs={{0,224},{32,0},{64,32},{96,64},{128,96},{160,128},{192,160},{224,1... | collective-permute-start | bytes 709640 | tf_op jit(solution)/shard_map/ppermute | solution.py:17
  50.1 10.9 %copy-start.7 = (f32[32,3696]{1,0:T(8,128)S(1)}, f32[32,3696]{1,0:T(8,128)}, u32[]{:S(2)}) copy-start(f32[32,3696]{1,0:T(8,128)} %get-tuple-element.29) | copy-start | bytes 1419268
  50.1 13.9 %copy-start.6 = (f32[32,3696]{1,0:T(8,128)S(1)}, f32[32,3696]{1,0:T(8,128)}, u32[]{:S(2)}) copy-start(f32[32,3696]{1,0:T(8,128)} %get-tuple-element.25) | copy-start | bytes 1419268
  50.1 9.7 %collective-permute-start.16 = (bf16[32,3696]{1,0:T(8,128)(2,1)}, bf16[32,3696]{1,0:T(8,128)(2,1)S(1)}, u32[]{:S(2)}, u32[]{:S(2)}) collective-permute-start(bf16[32,3696]{1,0:T(8,128)(2,1)} %get-tuple-element.35), channel_id=1, source_target_pairs={{0,32},{32,64},{64,96},{96,128},{128,160},{160,192},{192,224},{224... | collective-permute-start | bytes 709640 | tf_op jit(solution)/shard_map/ppermute | solution.py:17
  50.1 10.9 %collective-permute-start.10 = (bf16[32,3696]{1,0:T(8,128)(2,1)}, bf16[32,3696]{1,0:T(8,128)(2,1)S(1)}, u32[]{:S(2)}, u32[]{:S(2)}) collective-permute-start(bf16[32,3696]{1,0:T(8,128)(2,1)} %get-tuple-element.30), channel_id=1, source_target_pairs={{0,24},{8,0},{16,8},{24,16},{1,25},{9,1},{17,9},{25,17},{2,26},{10... | collective-permute-start | bytes 709640 | tf_op jit(solution)/shard_map/ppermute | solution.py:17
  52.8 11.1 %collective-permute-start.8 = (bf16[32,3696]{1,0:T(8,128)(2,1)}, bf16[32,3696]{1,0:T(8,128)(2,1)S(1)}, u32[]{:S(2)}, u32[]{:S(2)}) collective-permute-start(bf16[32,3696]{1,0:T(8,128)(2,1)} %get-tuple-element.26), channel_id=1, source_target_pairs={{0,8},{8,16},{16,24},{24,0},{1,9},{9,17},{17,25},{25,1},{2,10},{10... | collective-permute-start | bytes 709640 | tf_op jit(solution)/shard_map/ppermute | solution.py:17
  56.3 7.7 %copy-start.11 = (bf16[32,3696]{1,0:T(8,128)(2,1)S(1)}, bf16[32,3696]{1,0:T(8,128)(2,1)}, u32[]{:S(2)}) copy-start(bf16[32,3696]{1,0:T(8,128)(2,1)} %get-tuple-element.27) | copy-start | bytes 709636
  56.3 7.8 %collective-permute-start.21 = (bf16[32,3696]{1,0:T(8,128)(2,1)S(1)}, bf16[32,3696]{1,0:T(8,128)(2,1)S(1)}, u32[]{:S(2)}, u32[]{:S(2)}) collective-permute-start(bf16[32,3696]{1,0:T(8,128)(2,1)S(1)} %add_convert_fusion.2), channel_id=1, source_target_pairs={{0,224},{32,0},{64,32},{96,64},{128,96},{160,128},{192,160},{224,1... | collective-permute-start | bytes 709640 | tf_op jit(solution)/shard_map/ppermute | solution.py:17
  60.9 7.1 %collective-permute-start.17 = (bf16[32,3696]{1,0:T(8,128)(2,1)S(1)}, bf16[32,3696]{1,0:T(8,128)(2,1)S(1)}, u32[]{:S(2)}, u32[]{:S(2)}) collective-permute-start(bf16[32,3696]{1,0:T(8,128)(2,1)S(1)} %add_convert_fusion.5), channel_id=1, source_target_pairs={{0,32},{32,64},{64,96},{96,128},{128,160},{160,192},{192,224},{224... | collective-permute-start | bytes 709640 | tf_op jit(solution)/shard_map/ppermute | solution.py:17
  61.0 6.9 %copy-start.4 = (f32[32,3696]{1,0:T(8,128)S(1)}, f32[32,3696]{1,0:T(8,128)}, u32[]{:S(2)}) copy-start(f32[32,3696]{1,0:T(8,128)} %get-tuple-element.33) | copy-start | bytes 1419268
  61.1 14.8 %copy-start.2 = (f32[32,3696]{1,0:T(8,128)S(1)}, f32[32,3696]{1,0:T(8,128)}, u32[]{:S(2)}) copy-start(f32[32,3696]{1,0:T(8,128)} %get-tuple-element.24) | copy-start | bytes 1419268
  61.1 11.5 %collective-permute-start.11 = (bf16[64,3696]{1,0:T(8,128)(2,1)S(1)}, bf16[64,3696]{1,0:T(8,128)(2,1)S(1)}, u32[]{:S(2)}, u32[]{:S(2)}) collective-permute-start(bf16[64,3696]{1,0:T(8,128)(2,1)S(1)} %pad_maximum_fusion.3), channel_id=1, source_target_pairs={{0,24},{8,0},{16,8},{24,16},{1,25},{9,1},{17,9},{25,17},{2,26},{10... | collective-permute-start | bytes 1419272 | tf_op jit(solution)/shard_map/ppermute | solution.py:17
  64.0 12.1 %copy-start.3 = (f32[32,3696]{1,0:T(8,128)S(1)}, f32[32,3696]{1,0:T(8,128)}, u32[]{:S(2)}) copy-start(f32[32,3696]{1,0:T(8,128)} %get-tuple-element.32) | copy-start | bytes 1419268
  64.0 17.0 %copy-start.8 = (f32[32,3696]{1,0:T(8,128)S(1)}, f32[32,3696]{1,0:T(8,128)}, u32[]{:S(2)}) copy-start(f32[32,3696]{1,0:T(8,128)} %get-tuple-element.23) | copy-start | bytes 1419268
  64.0 11.9 %collective-permute-start.9 = (bf16[64,3696]{1,0:T(8,128)(2,1)S(1)}, bf16[64,3696]{1,0:T(8,128)(2,1)S(1)}, u32[]{:S(2)}, u32[]{:S(2)}) collective-permute-start(bf16[64,3696]{1,0:T(8,128)(2,1)S(1)} %pad_maximum_fusion.2), channel_id=1, source_target_pairs={{0,8},{8,16},{16,24},{24,0},{1,9},{9,17},{17,25},{25,1},{2,10},{10... | collective-permute-start | bytes 1419272 | tf_op jit(solution)/shard_map/ppermute | solution.py:17
  64.2 21.3 %collective-permute-start.22 = (bf16[32,3696]{1,0:T(8,128)(2,1)S(1)}, bf16[32,3696]{1,0:T(8,128)(2,1)S(1)}, u32[]{:S(2)}, u32[]{:S(2)}) collective-permute-start(bf16[32,3696]{1,0:T(8,128)(2,1)S(1)} %add_convert_fusion.1), channel_id=1, source_target_pairs={{0,224},{32,0},{64,32},{96,64},{128,96},{160,128},{192,160},{224,1... | collective-permute-start | bytes 709640 | tf_op jit(solution)/shard_map/ppermute | solution.py:17
  68.0 8.1 %collective-permute-start.18 = (bf16[32,3696]{1,0:T(8,128)(2,1)S(1)}, bf16[32,3696]{1,0:T(8,128)(2,1)S(1)}, u32[]{:S(2)}, u32[]{:S(2)}) collective-permute-start(bf16[32,3696]{1,0:T(8,128)(2,1)S(1)} %add_convert_fusion.4), channel_id=1, source_target_pairs={{0,32},{32,64},{64,96},{96,128},{128,160},{160,192},{192,224},{224... | collective-permute-start | bytes 709640 | tf_op jit(solution)/shard_map/ppermute | solution.py:17
  75.9 9.6 %copy-start.1 = (f32[32,3696]{1,0:T(8,128)S(1)}, f32[32,3696]{1,0:T(8,128)}, u32[]{:S(2)}) copy-start(f32[32,3696]{1,0:T(8,128)} %get-tuple-element.31) | copy-start | bytes 1419268
  76.0 5.0 %collective-permute-start.12 = (bf16[32,3696]{1,0:T(8,128)(2,1)S(1)}, bf16[32,3696]{1,0:T(8,128)(2,1)S(1)}, u32[]{:S(2)}, u32[]{:S(2)}) collective-permute-start(bf16[32,3696]{1,0:T(8,128)(2,1)S(1)} %add_convert_fusion.6), channel_id=1, source_target_pairs={{0,32},{32,0},{64,96},{96,64},{128,160},{160,128},{192,224},{224,1... | collective-permute-start | bytes 709640 | tf_op jit(solution)/shard_map/ppermute | solution.py:125
  76.2 9.4 %collective-permute-start.19 = (bf16[32,3696]{1,0:T(8,128)(2,1)S(1)}, bf16[32,3696]{1,0:T(8,128)(2,1)S(1)}, u32[]{:S(2)}, u32[]{:S(2)}) collective-permute-start(bf16[32,3696]{1,0:T(8,128)(2,1)S(1)} %add_convert_fusion.3), channel_id=1, source_target_pairs={{0,32},{32,64},{64,96},{96,128},{128,160},{160,192},{192,224},{224... | collective-permute-start | bytes 709640 | tf_op jit(solution)/shard_map/ppermute | solution.py:17
  81.0 10.7 %copy-start.9 = (f32[16,3696]{1,0:T(8,128)S(1)}, f32[16,3696]{1,0:T(8,128)}, u32[]{:S(2)}) copy-start(f32[16,3696]{1,0:T(8,128)} %param.8) | copy-start | bytes 709636
  81.0 10.8 %copy-start.10 = (f32[16,3696]{1,0:T(8,128)S(1)}, f32[16,3696]{1,0:T(8,128)}, u32[]{:S(2)}) copy-start(f32[16,3696]{1,0:T(8,128)} %param.9) | copy-start | bytes 709636
  81.2 6.0 %collective-permute-start.15 = (bf16[8,3696]{1,0:T(8,128)(2,1)S(1)}, bf16[8,3696]{1,0:T(8,128)(2,1)S(1)}, u32[]{:S(2)}, u32[]{:S(2)}) collective-permute-start(bf16[8,3696]{1,0:T(8,128)(2,1)S(1)} %get-tuple-element.54), channel_id=1, source_target_pairs={{0,192},{32,224},{64,0},{96,32},{128,64},{160,96},{192,128},{224,1... | collective-permute-start | bytes 177416 | tf_op jit(solution)/shard_map/ppermute | solution.py:17
  83.4 6.2 %collective-permute-start.14 = (bf16[8,3696]{1,0:T(8,128)(2,1)S(1)}, bf16[8,3696]{1,0:T(8,128)(2,1)S(1)}, u32[]{:S(2)}, u32[]{:S(2)}) collective-permute-start(bf16[8,3696]{1,0:T(8,128)(2,1)S(1)} %get-tuple-element.55), channel_id=1, source_target_pairs={{0,64},{32,96},{64,128},{96,160},{128,192},{160,224},{192,0},{224,... | collective-permute-start | bytes 177416 | tf_op jit(solution)/shard_map/ppermute | solution.py:17
  83.6 7.7 %collective-permute-start.13 = (bf16[8,3696]{1,0:T(8,128)(2,1)S(1)}, bf16[8,3696]{1,0:T(8,128)(2,1)S(1)}, u32[]{:S(2)}, u32[]{:S(2)}) collective-permute-start(bf16[8,3696]{1,0:T(8,128)(2,1)S(1)} %get-tuple-element.53), channel_id=1, source_target_pairs={{0,128},{32,160},{64,192},{96,224},{128,0},{160,32},{192,64},{224,... | collective-permute-start | bytes 177416 | tf_op jit(solution)/shard_map/ppermute | solution.py:17
  85.6 5.7 %collective-permute-start.25 = (bf16[8,3696]{1,0:T(8,128)(2,1)S(1)}, bf16[8,3696]{1,0:T(8,128)(2,1)S(1)}, u32[]{:S(2)}, u32[]{:S(2)}) collective-permute-start(bf16[8,3696]{1,0:T(8,128)(2,1)S(1)} %get-tuple-element.57), channel_id=1, source_target_pairs={{0,24},{8,0},{16,8},{24,16},{1,25},{9,1},{17,9},{25,17},{2,26},{10... | collective-permute-start | bytes 177416 | tf_op jit(solution)/shard_map/ppermute | solution.py:17
  85.8 5.5 %collective-permute-start.24 = (bf16[8,3696]{1,0:T(8,128)(2,1)S(1)}, bf16[8,3696]{1,0:T(8,128)(2,1)S(1)}, u32[]{:S(2)}, u32[]{:S(2)}) collective-permute-start(bf16[8,3696]{1,0:T(8,128)(2,1)S(1)} %get-tuple-element.58), channel_id=1, source_target_pairs={{0,8},{8,16},{16,24},{24,0},{1,9},{9,17},{17,25},{25,1},{2,10},{10... | collective-permute-start | bytes 177416 | tf_op jit(solution)/shard_map/ppermute | solution.py:17
  87.2 4.6 %collective-permute-start.23 = (bf16[8,3696]{1,0:T(8,128)(2,1)S(1)}, bf16[8,3696]{1,0:T(8,128)(2,1)S(1)}, u32[]{:S(2)}, u32[]{:S(2)}) collective-permute-start(bf16[8,3696]{1,0:T(8,128)(2,1)S(1)} %get-tuple-element.56), channel_id=1, source_target_pairs={{0,16},{8,24},{16,0},{24,8},{1,17},{9,25},{17,1},{25,9},{2,18},{10... | collective-permute-start | bytes 177416 | tf_op jit(solution)/shard_map/ppermute | solution.py:17
  93.3 3.4 %collective-permute-start.28 = (bf16[16,924]{1,0:T(8,128)(2,1)S(1)}, bf16[16,924]{1,0:T(8,128)(2,1)S(1)}, u32[]{:S(2)}, u32[]{:S(2)}) collective-permute-start(bf16[16,924]{1,0:T(8,128)(2,1)S(1)} %bitcast.52), channel_id=1, source_target_pairs={{0,24},{8,0},{16,8},{24,16},{1,25},{9,1},{17,9},{25,17},{2,26},{10... | collective-permute-start | bytes 88712 | tf_op jit(solution)/shard_map/ppermute | solution.py:17
  94.7 4.7 %collective-permute-start.27 = (bf16[16,924]{1,0:T(8,128)(2,1)S(1)}, bf16[16,924]{1,0:T(8,128)(2,1)S(1)}, u32[]{:S(2)}, u32[]{:S(2)}) collective-permute-start(bf16[16,924]{1,0:T(8,128)(2,1)S(1)} %bitcast.53), channel_id=1, source_target_pairs={{0,16},{8,24},{16,0},{24,8},{1,17},{9,25},{17,1},{25,9},{2,18},{10... | collective-permute-start | bytes 88712 | tf_op jit(solution)/shard_map/ppermute | solution.py:17
  95.2 4.9 %collective-permute-start.26 = (bf16[16,924]{1,0:T(8,128)(2,1)S(1)}, bf16[16,924]{1,0:T(8,128)(2,1)S(1)}, u32[]{:S(2)}, u32[]{:S(2)}) collective-permute-start(bf16[16,924]{1,0:T(8,128)(2,1)S(1)} %bitcast.54), channel_id=1, source_target_pairs={{0,8},{8,16},{16,24},{24,0},{1,9},{9,17},{17,25},{25,1},{2,10},{10... | collective-permute-start | bytes 88712 | tf_op jit(solution)/shard_map/ppermute | solution.py:17
  100.8 4.0 %collective-permute-start.29 = (bf16[4,16,924]{2,1,0:T(8,128)(2,1)}, bf16[4,16,924]{2,1,0:T(8,128)(2,1)S(1)}, u32[]{:S(2)}, u32[]{:S(2)}) collective-permute-start(bf16[4,16,924]{2,1,0:T(8,128)(2,1)} %pad_maximum_fusion.5), channel_id=1, source_target_pairs={{0,6},{2,0},{4,2},{6,4},{1,7},{3,1},{5,3},{7,5},{8,14},{10,8},{12,... | collective-permute-start | bytes 354824 | tf_op jit(solution)/shard_map/ppermute | solution.py:17
  101.1 5.6 %collective-permute-start.30 = (bf16[4,16,924]{2,1,0:T(8,128)(2,1)}, bf16[4,16,924]{2,1,0:T(8,128)(2,1)S(1)}, u32[]{:S(2)}, u32[]{:S(2)}) collective-permute-start(bf16[4,16,924]{2,1,0:T(8,128)(2,1)} %pad_maximum_fusion.5), channel_id=1, source_target_pairs={{0,4},{2,6},{4,0},{6,2},{1,5},{3,7},{5,1},{7,3},{8,12},{10,14},{12... | collective-permute-start | bytes 354824 | tf_op jit(solution)/shard_map/ppermute | solution.py:17
  101.8 6.6 %collective-permute-start.31 = (bf16[4,16,924]{2,1,0:T(8,128)(2,1)}, bf16[4,16,924]{2,1,0:T(8,128)(2,1)}, u32[]{:S(2)}, u32[]{:S(2)}) collective-permute-start(bf16[4,16,924]{2,1,0:T(8,128)(2,1)} %pad_maximum_fusion.5), channel_id=1, source_target_pairs={{0,2},{2,4},{4,6},{6,0},{1,3},{3,5},{5,7},{7,1},{8,10},{10,12},{12... | collective-permute-start | bytes 354824 | tf_op jit(solution)/shard_map/ppermute | solution.py:17
  109.3 24.6 %collective-permute-start.35 = (bf16[4,16,924]{2,1,0:T(8,128)(2,1)S(1)}, bf16[4,16,924]{2,1,0:T(8,128)(2,1)S(1)}, u32[]{:S(2)}, u32[]{:S(2)}) collective-permute-start(bf16[4,16,924]{2,1,0:T(8,128)(2,1)S(1)} %get-tuple-element.47), channel_id=1, source_target_pairs={{0,192},{2,194},{4,196},{6,198},{8,200},{10,202},{12,204},{14,206}... | collective-permute-start | bytes 354824 | tf_op jit(solution)/shard_map/ppermute | solution.py:168
  123.8 10.1 %collective-permute-start.32 = (bf16[4,16,924]{2,1,0:T(8,128)(2,1)S(1)}, bf16[4,16,924]{2,1,0:T(8,128)(2,1)S(1)}, u32[]{:S(2)}, u32[]{:S(2)}) collective-permute-start(bf16[4,16,924]{2,1,0:T(8,128)(2,1)S(1)} %get-tuple-element.46), channel_id=1, source_target_pairs={{1,32},{3,34},{5,36},{7,38},{9,40},{11,42},{13,44},{15,46},{17,48}... | collective-permute-start | bytes 354824 | tf_op jit(solution)/shard_map/ppermute | solution.py:168
  126.7 9.5 %collective-permute-start.34 = (bf16[4,16,924]{2,1,0:T(8,128)(2,1)S(1)}, bf16[4,16,924]{2,1,0:T(8,128)(2,1)S(1)}, u32[]{:S(2)}, u32[]{:S(2)}) collective-permute-start(bf16[4,16,924]{2,1,0:T(8,128)(2,1)S(1)} %get-tuple-element.49), channel_id=1, source_target_pairs={{0,128},{2,130},{4,132},{6,134},{8,136},{10,138},{12,140},{14,142}... | collective-permute-start | bytes 354824 | tf_op jit(solution)/shard_map/ppermute | solution.py:168
  128.6 10.4 %collective-permute-start.33 = (bf16[4,16,924]{2,1,0:T(8,128)(2,1)S(1)}, bf16[4,16,924]{2,1,0:T(8,128)(2,1)S(1)}, u32[]{:S(2)}, u32[]{:S(2)}) collective-permute-start(bf16[4,16,924]{2,1,0:T(8,128)(2,1)S(1)} %get-tuple-element.48), channel_id=1, source_target_pairs={{0,64},{2,66},{4,68},{6,70},{8,72},{10,74},{12,76},{14,78},{16,80}... | collective-permute-start | bytes 354824 | tf_op jit(solution)/shard_map/ppermute | solution.py:168
  139.1 3.5 %collective-permute-start.36 = (bf16[4,4,16,924]{3,2,1,0:T(8,128)(2,1)S(1)}, bf16[4,4,16,924]{3,2,1,0:T(8,128)(2,1)S(1)}, u32[]{:S(2)}, u32[]{:S(2)}) collective-permute-start(bf16[4,4,16,924]{3,2,1,0:T(8,128)(2,1)S(1)} %pad_maximum_fusion.1), channel_id=1, source_target_pairs={{0,1},{1,0},{2,3},{3,2},{4,5},{5,4},{6,7},{7,6},{8,9},{9,8},{10,11... | collective-permute-start | bytes 1419272 | tf_op jit(solution)/shard_map/ppermute | solution.py:17
  (4 other events, 7.9 us)

commit v7 on v5

--- a/solution.py
+++ b/solution.py
@@ -22,6 +22,7 @@
 EVEN, ODD = (0, 2, 4, 6), (1, 3, 5, 7)
 Y_FIRST = [[(dy, dz) for dz in half] for dy in (2, 1, 3, 0) for half in (EVEN, ODD)]
 Z_FIRST = [[(dy, dz) for dy in range(Y)] for dz in (4, 5, 3, 6, 2, 7, 1, 0)]
+Y_ROUNDED, Z_ROUNDED = (0, 1, 3, 4), (0, 1)
 
 
 def grad_kernel(units, here, mine_ref, other_ref, cot_ref, *rest):
@@ -52,15 +53,15 @@
     half, tokens = mine.shape
     ff = min(stop * tile, cotangent.shape[1]) - start * tile
     rows = 2 * half // (Z * Y)
-    whole = lambda i: (0, 0)
-    shapes = [(len(places) * rows, f32 if k > 1 else bf16) for k, places in enumerate(units)]
+    shapes = [(len(places) * rows, bf16 if k in (Y_ROUNDED if units is Y_FIRST else Z_ROUNDED) else f32) for k, places in enumerate(units)]
+    held_in = pltpu.with_memory_space_constraint
     return pl.pallas_call(
         functools.partial(grad_kernel, units),
         grid=(stop - start,),
         in_specs=[
             pl.BlockSpec(memory_space=pltpu.SMEM),
-            pl.BlockSpec((half, tokens), whole),
-            pl.BlockSpec((half, tokens), whole),
+            pl.BlockSpec(memory_space=pltpu.VMEM),
+            pl.BlockSpec(memory_space=pltpu.VMEM),
             pl.BlockSpec((tile, tokens), lambda i: (start + i, 0)),
         ],
         out_specs=[pl.BlockSpec((n, tile), lambda i: (0, i)) for n, _ in shapes],
@@ -70,7 +71,7 @@
         cost_estimate=pl.CostEstimate(
             flops=4 * half * tokens * ff, bytes_accessed=2 * tokens * ff + 14 * half * ff // 2, transcendentals=0
         ),
-    )(here, *(pltpu.with_memory_space_constraint(v, pltpu.HBM) for v in (mine, other, cotangent.T)))
+    )(here, held_in(mine, pltpu.VMEM), held_in(other, pltpu.VMEM), held_in(cotangent.T, pltpu.HBM))
 
 
 def near_order(rank):
@@ -106,8 +107,8 @@
     high_y, low_y = moved(two_low, "y", 1), moved(two_high, "y", -1)
     up = moved((k3 + up.astype(f32)).astype(bf16), "z", 1)
     down = moved((k6 + down.astype(f32)).astype(bf16), "z", -1)
-    one = jnp.concatenate([(one_low + high_y.astype(f32)).astype(bf16), one_high.astype(bf16)], 0)
-    three = jnp.concatenate([three_low.astype(bf16), (three_high + low_y.astype(f32)).astype(bf16)], 0)
+    one = jnp.concatenate([(one_low + high_y.astype(f32)).astype(bf16), one_high], 0)
+    three = jnp.concatenate([three_low, (three_high + low_y.astype(f32)).astype(bf16)], 0)
     across = [moved(one, "y", 1), moved(three, "y", -1)]
     up, down = (k2 + up.astype(f32)).astype(bf16), (k7 + down.astype(f32)).astype(bf16)
     up, down = moved(up, "z", 1), moved(down, "z", -1)
@@ -137,7 +138,7 @@
     return out
 
 
-def spread(normed):
+def spread(normed, beside):
     z, y, x, c = (lax.axis_index(axis) for axis in ("z", "y", "x", "c"))
     rows, ff = normed.shape
     cut = normed.reshape(rows, Y, ff // Y).transpose(1, 0, 2)
@@ -160,8 +161,8 @@
                         pairs.append(((pz * Y * X + r) * C + pc, (((pz + 2 * k + po) % Z) * Y * X + r) * C + (pc ^ po)))
         moved_in = lax.ppermute(sent, ("z", "y", "x", "c"), pairs)
         half.append(moved_in if k else jnp.where(odd == 0, sent, moved_in))
-    half = jnp.stack(half)
-    return half, moved(half, "c", 1)
+    half, beside = lax.optimization_barrier((jnp.stack(half), beside))
+    return beside, half, moved(half, "c", 1)
 
 
 def spread_order(rank):
@@ -184,15 +185,15 @@
     tile = pl.cdiv(pl.cdiv(ff, lanes), 6) * lanes
     tiles = pl.cdiv(ff, tile)
     made = functools.partial(gradient, mine=mine, other=other, cotangent=cotangent, here=here, tile=tile)
-    total = scatter(
-        lambda: made(Z_FIRST, start=tiles // 2, stop=tiles), lambda: made(Y_FIRST, start=0, stop=tiles // 2)
-    )
+    relay = functools.partial(made, Y_FIRST, start=0, stop=tiles // 2)
+    total = scatter(functools.partial(made, Z_FIRST, start=tiles // 2, stop=tiles), relay)
     total_tokens = cotangent.shape[0] * Z * Y
     grad_low = total * (1.0 / total_tokens)
     first = 0.9 * exp_avg + 0.1 * grad_low
     second = 0.999 * exp_avg_sq + 0.001 * grad_low * grad_low
     normed = (first / bias_first / (jnp.sqrt(second / bias_second) + 1e-08)).astype(bf16)
-    mine, other = (part.reshape(rank // 2, ff // Y) for part in spread(normed))
+    ordered, *parts = spread(normed, ordered)
+    mine, other = (part.reshape(rank // 2, ff // Y) for part in parts)
     update = jnp.dot(ordered[:, : rank // 2], mine, preferred_element_type=f32)
     update = (update + jnp.dot(ordered[:, rank // 2 :], other, preferred_element_type=f32)).astype(bf16)
     return (update, first, second)

time: 142 us -> 138 us (0.972)
  waiting for transfers between devices: 48.3 us -> 45.4 us
  starting transfers between devices: 58.3 us -> 60.7 us
  other arithmetic: 8.85 us -> 6.56 us
    ppermute x32, waiting for transfers between devices: 39.9 us -> 37.6 us  [moved(): return lax.ppermute(value, axis, [(i, (i + by) % n) for i in range(n)])]
    convert_element_type x2 -> x0, other arithmetic: 2.25 us -> none  [the longest x1 1.14 us: scatter(): one_high.astype(bf16)]
    ppermute x4, starting transfers between devices: 15.9 us -> 18 us  [spread(): moved_in = lax.ppermute(sent, ('z', 'y', 'x', 'c'), pairs)]
  transfers between devices with their start and end apart: 37 -> 37, of which waited for: 25 -> 26; matrix products, arithmetic and copies ran while one was open for 6% -> 5% of each run, Pallas kernels for 5% -> 5%
where the time goes in v7:
time: 138 us
  starting transfers between devices  60.7 us (44%)
  waiting for transfers between devices  45.4 us (33%)
  Pallas kernels  12.3 us (9%)
  matrix products  10.2 us (7%)
  other arithmetic  6.56 us (5%)
  local copies, waits for them, and re-layouts  1.4 us (1%)
    ppermute x32, starting transfers between devices, moved(): return lax.ppermute(value, axis, [(i, (i + by) % n) for i in range(n)])  42.6 us
    ppermute x32, waiting for transfers between devices, moved(): return lax.ppermute(value, axis, [(i, (i + by) % n) for i in range(n)])  37.6 us
    ppermute x4, starting transfers between devices, spread(): moved_in = lax.ppermute(sent, ('z', 'y', 'x', 'c'), pairs)  18 us
    pallas_call x2, Pallas kernels, gradient(): pl.pallas_call(functools.partial(grad_kernel, units), grid=(stop - start,...  12.3 us
    ppermute x4, waiting for transfers between devices, spread(): moved_in = lax.ppermute(sent, ('z', 'y', 'x', 'c'), pairs)  6.9 us
    dot_general x1, matrix products, project(): lax.dot_general(near_order(rank), basis, lanes, preferred_element_type=f32)  3.02 us
    dot_general x1, matrix products, shards(): jnp.dot(basis, spread_order(rank), preferred_element_type=f32).astype(bf16)  3.01 us
  transfers between devices with their start and end apart: 37, of which 26 were waited for; matrix products, arithmetic and copies ran while one was open for 5% of the time, Pallas kernels for 5%

profile of v7, /device:TPU:1, one launch (start us, length us, event | category | flops | bytes accessed | tf_op | source)
XLA Modules:
  0.0 137.8 jit_solution(949767005858978187)
XLA Ops:
  0.7 3.0 %convolution_convert_fusion = bf16[512,1024]{1,0:T(8,128)(2,1)S(1)} fusion(bf16[1024,512]{1,0:T(8,128)(2,1)} %param.6, s32[512]{0:T(512)S(1)} %get-tuple-element.71, s32[512]{0:T(512)S(1)} %get-tuple-element.72, s32[512]{0:T(512)S(1)} %get-tuple-element.70, s32[512]{0:T(512)S(1)} %get-tuple-element.75, s32[]{:T(128)} %axis_index.32, ...), kind=kOutput, calls=%fused_computation.31 | convolution fusion | flops 548667392 | bytes 2110984 | tf_op jit(solution)/shard_map/dot_general | solution.py:90
  4.5 3.3 %collective-permute-start = (f32[256,1024]{1,0:T(8,128)S(1)}, f32[256,1024]{1,0:T(8,128)S(1)}, u32[]{:S(2)}, u32[]{:S(2)}) collective-permute-start(f32[256,1024]{1,0:T(8,128)S(1)} %fusion.36), channel_id=1, source_target_pairs={{0,1},{1,0},{2,3},{3,2},{4,5},{5,4},{6,7},{7,6},{8,9},{9,8},{10,11... | collective-permute-start | bytes 3145736 | tf_op jit(solution)/shard_map/ppermute | solution.py:19
  8.5 1.7 %collective-permute-done = f32[256,1024]{1,0:T(8,128)S(1)} collective-permute-done((f32[256,1024]{1,0:T(8,128)S(1)}, f32[256,1024]{1,0:T(8,128)S(1)}, u32[]{:S(2)}, u32[]{:S(2)}) %collective-permute-start) | collective-permute-done | bytes 1048608 | tf_op jit(solution)/shard_map/ppermute | solution.py:19
  11.6 1.9 %collective-permute-start.3 = (bf16[64,1024]{1,0:T(8,128)(2,1)}, bf16[64,1024]{1,0:T(8,128)(2,1)S(1)}, u32[]{:S(2)}, u32[]{:S(2)}) collective-permute-start(bf16[64,1024]{1,0:T(8,128)(2,1)} %get-tuple-element.55), channel_id=1, source_target_pairs={{0,4},{2,6},{4,0},{6,2},{1,5},{3,7},{5,1},{7,3},{8,12},{10,14},{12... | collective-permute-start | bytes 393224 | tf_op jit(solution)/shard_map/ppermute | solution.py:19
  13.6 1.2 collective-permute-start.2
  15.3 3.2 %collective-permute-done.1 = bf16[64,1024]{1,0:T(8,128)(2,1)S(1)} collective-permute-done((bf16[64,1024]{1,0:T(8,128)(2,1)}, bf16[64,1024]{1,0:T(8,128)(2,1)S(1)}, u32[]{:S(2)}, u32[]{:S(2)}) %collective-permute-start.1) | collective-permute-done | bytes 131104 | tf_op jit(solution)/shard_map/ppermute | solution.py:19
  18.5 1.4 collective-permute-done.3
  19.9 1.2 collective-permute-done.2
  21.0 1.0 fusion.84
  22.0 3.2 %collective-permute-start.6 = (bf16[64,1024]{1,0:T(8,128)(2,1)S(1)}, bf16[64,1024]{1,0:T(8,128)(2,1)S(1)}, u32[]{:S(2)}, u32[]{:S(2)}) collective-permute-start(bf16[64,1024]{1,0:T(8,128)(2,1)S(1)} %fusion.84), channel_id=1, source_target_pairs={{0,6},{2,0},{4,2},{6,4},{1,7},{3,1},{5,3},{7,5},{8,14},{10,8},{12,... | collective-permute-start | bytes 393224 | tf_op jit(solution)/shard_map/ppermute | solution.py:19
  25.9 3.0 %fusion = bf16[1024,512]{0,1:T(8,128)(2,1)} fusion(bf16[1024,512]{1,0:T(8,128)(2,1)} %param.6, s32[512]{0:T(512)S(1)} %get-tuple-element.78, s32[512]{0:T(512)} %get-tuple-element.79, s32[512]{0:T(512)S(1)} %get-tuple-element.77, s32[512]{0:T(512)} %get-tuple-element.80, s32[]{:T(128)S(6)} %add.293, s32[512]{0:T(512)S(1)} %get-tuple-element.69, ...), kind=kOutput, calls=%fused_computation.33 | convolution fusion | flops 555745280 | bytes 2115596 | tf_op jit(solution)/shard_map/dot_general | solution.py:182
  28.9 1.6 %collective-permute-done.6 = bf16[64,1024]{1,0:T(8,128)(2,1)S(1)} collective-permute-done((bf16[64,1024]{1,0:T(8,128)(2,1)S(1)}, bf16[64,1024]{1,0:T(8,128)(2,1)S(1)}, u32[]{:S(2)}, u32[]{:S(2)}) %collective-permute-start.6) | collective-permute-done | bytes 131104 | tf_op jit(solution)/shard_map/ppermute | solution.py:19
  31.0 3.4 %collective-permute-done.4 = bf16[64,1024]{1,0:T(8,128)(2,1)S(1)} collective-permute-done((bf16[64,1024]{1,0:T(8,128)(2,1)S(1)}, bf16[64,1024]{1,0:T(8,128)(2,1)S(1)}, u32[]{:S(2)}, u32[]{:S(2)}) %collective-permute-start.4) | collective-permute-done | bytes 131104 | tf_op jit(solution)/shard_map/ppermute | solution.py:19
  34.3 0.9 collective-permute-start.7
  35.4 1.5 %collective-permute-done.7.other_ref = bf16[256,1024]{1,0:T(8,128)(2,1)S(1)} collective-permute-done((bf16[256,1024]{1,0:T(8,128)(2,1)S(1)}, bf16[256,1024]{1,0:T(8,128)(2,1)S(1)}, u32[]{:S(2)}, u32[]{:S(2)}) %collective-permute-start.7) | collective-permute-done | bytes 524320 | tf_op jit(solution)/shard_map/ppermute | solution.py:19
  36.8 6.1 %shard_map.77 = (bf16[64,1776]{1,0:T(8,128)(2,1)}, bf16[64,1776]{1,0:T(8,128)(2,1)}, f32[64,1776]{1,0:T(8,128)}, f32[64,1776]{1,0:T(8,128)}, f32[64,1776]{1,0:T(...) custom-call(s32[4]{0:T(128)S(1)} %pad_add_fusion.here, ...), custom_call_target="tpu_custom_call" | custom-call | flops 1862270976 | bytes 6819840 | tf_op jit(solution)/shard_map/pallas_call | solution.py:58
  43.1 6.2 %shard_map.76 = (bf16[64,1920]{1,0:T(8,128)(2,1)}, bf16[64,1920]{1,0:T(8,128)(2,1)}, f32[64,1920]{1,0:T(8,128)}, bf16[64,1920]{1,0:T(8,128)(2,1)}, bf16[64,1920]...) custom-call(s32[4]{0:T(128)S(1)} %pad_add_fusion.here, ...), custom_call_target="tpu_custom_call" | custom-call | flops 2013265920 | bytes 7372800 | tf_op jit(solution)/shard_map/pallas_call | solution.py:58
  50.2 1.9 %collective-permute-start.10 = (bf16[64,1920]{1,0:T(8,128)(2,1)}, bf16[64,1920]{1,0:T(8,128)(2,1)S(1)}, u32[]{:S(2)}, u32[]{:S(2)}) collective-permute-start(bf16[64,1920]{1,0:T(8,128)(2,1)} %get-tuple-element.31), channel_id=1, source_target_pairs={{0,24},{8,0},{16,8},{24,16},{1,25},{9,1},{17,9},{25,17},{2,26},{10... | collective-permute-start | bytes 737288 | tf_op jit(solution)/shard_map/ppermute | solution.py:19
  52.1 3.9 %collective-permute-start.20 = (bf16[64,1776]{1,0:T(8,128)(2,1)S(1)}, bf16[64,1776]{1,0:T(8,128)(2,1)S(1)}, u32[]{:S(2)}, u32[]{:S(2)}) collective-permute-start(bf16[64,1776]{1,0:T(8,128)(2,1)S(1)} %copy-done.16), channel_id=1, source_target_pairs={{0,224},{32,0},{64,32},{96,64},{128,96},{160,128},{192,160},{224,1... | collective-permute-start | bytes 681992 | tf_op jit(solution)/shard_map/ppermute | solution.py:19
  56.1 4.1 %collective-permute-done.20 = bf16[64,1776]{1,0:T(8,128)(2,1)S(1)} collective-permute-done((bf16[64,1776]{1,0:T(8,128)(2,1)S(1)}, bf16[64,1776]{1,0:T(8,128)(2,1)S(1)}, u32[]{:S(2)}, u32[]{:S(2)}) %collective-permute-start.20) | collective-permute-done | bytes 227360 | tf_op jit(solution)/shard_map/ppermute | solution.py:19
  60.3 3.5 %collective-permute-start.21 = (bf16[64,1776]{1,0:T(8,128)(2,1)S(1)}, bf16[64,1776]{1,0:T(8,128)(2,1)S(1)}, u32[]{:S(2)}, u32[]{:S(2)}) collective-permute-start(bf16[64,1776]{1,0:T(8,128)(2,1)S(1)} %add_convert_fusion.5), channel_id=1, source_target_pairs={{0,224},{32,0},{64,32},{96,64},{128,96},{160,128},{192,160},{224,1... | collective-permute-start | bytes 681992 | tf_op jit(solution)/shard_map/ppermute | solution.py:19
  63.9 1.0 collective-permute-start.11
  65.8 1.4 collective-permute-done.21
  67.2 3.5 %collective-permute-start.22 = (bf16[64,1776]{1,0:T(8,128)(2,1)S(1)}, bf16[64,1776]{1,0:T(8,128)(2,1)S(1)}, u32[]{:S(2)}, u32[]{:S(2)}) collective-permute-start(bf16[64,1776]{1,0:T(8,128)(2,1)S(1)} %add_convert_fusion.4), channel_id=1, source_target_pairs={{0,224},{32,0},{64,32},{96,64},{128,96},{160,128},{192,160},{224,1... | collective-permute-start | bytes 681992 | tf_op jit(solution)/shard_map/ppermute | solution.py:19
  70.7 1.5 %collective-permute-done.18 = bf16[64,1776]{1,0:T(8,128)(2,1)S(1)} collective-permute-done((bf16[64,1776]{1,0:T(8,128)(2,1)S(1)}, bf16[64,1776]{1,0:T(8,128)(2,1)S(1)}, u32[]{:S(2)}, u32[]{:S(2)}) %collective-permute-start.18) | collective-permute-done | bytes 227360 | tf_op jit(solution)/shard_map/ppermute | solution.py:19
  72.3 2.6 %collective-permute-done.11 = bf16[128,1920]{1,0:T(8,128)(2,1)S(1)} collective-permute-done((bf16[128,1920]{1,0:T(8,128)(2,1)S(1)}, bf16[128,1920]{1,0:T(8,128)(2,1)S(1)}, u32[]{:S(2)}, u32[]{:S(2)}) %collective-permute-start.11) | collective-permute-done | bytes 491552 | tf_op jit(solution)/shard_map/ppermute | solution.py:19
  74.9 1.7 %collective-permute-done.9 = bf16[128,1920]{1,0:T(8,128)(2,1)S(1)} collective-permute-done((bf16[128,1920]{1,0:T(8,128)(2,1)S(1)}, bf16[128,1920]{1,0:T(8,128)(2,1)S(1)}, u32[]{:S(2)}, u32[]{:S(2)}) %collective-permute-start.9) | collective-permute-done | bytes 491552 | tf_op jit(solution)/shard_map/ppermute | solution.py:19
  76.8 1.9 %collective-permute-done.19 = bf16[64,1776]{1,0:T(8,128)(2,1)S(1)} collective-permute-done((bf16[64,1776]{1,0:T(8,128)(2,1)S(1)}, bf16[64,1776]{1,0:T(8,128)(2,1)S(1)}, u32[]{:S(2)}, u32[]{:S(2)}) %collective-permute-start.19) | collective-permute-done | bytes 227360 | tf_op jit(solution)/shard_map/ppermute | solution.py:19
  79.4 1.4 %collective-permute-start.25 = (bf16[16,1776]{1,0:T(8,128)(2,1)S(1)}, bf16[16,1776]{1,0:T(8,128)(2,1)S(1)}, u32[]{:S(2)}, u32[]{:S(2)}) collective-permute-start(bf16[16,1776]{1,0:T(8,128)(2,1)S(1)} %get-tuple-element.61), channel_id=1, source_target_pairs={{0,24},{8,0},{16,8},{24,16},{1,25},{9,1},{17,9},{25,17},{2,26},{10... | collective-permute-start | bytes 170504 | tf_op jit(solution)/shard_map/ppermute | solution.py:19
  82.3 3.7 %collective-permute-start.13 = (bf16[16,1920]{1,0:T(8,128)(2,1)S(1)}, bf16[16,1920]{1,0:T(8,128)(2,1)S(1)}, u32[]{:S(2)}, u32[]{:S(2)}) collective-permute-start(bf16[16,1920]{1,0:T(8,128)(2,1)S(1)} %get-tuple-element.57), channel_id=1, source_target_pairs={{0,128},{32,160},{64,192},{96,224},{128,0},{160,32},{192,64},{224,... | collective-permute-start | bytes 184328 | tf_op jit(solution)/shard_map/ppermute | solution.py:19
  86.2 2.2 %collective-permute-start.14 = (bf16[16,1920]{1,0:T(8,128)(2,1)S(1)}, bf16[16,1920]{1,0:T(8,128)(2,1)S(1)}, u32[]{:S(2)}, u32[]{:S(2)}) collective-permute-start(bf16[16,1920]{1,0:T(8,128)(2,1)S(1)} %get-tuple-element.59), channel_id=1, source_target_pairs={{0,64},{32,96},{64,128},{96,160},{128,192},{160,224},{192,0},{224,... | collective-permute-start | bytes 184328 | tf_op jit(solution)/shard_map/ppermute | solution.py:19
  88.4 1.6 %collective-permute-done.13 = bf16[16,1920]{1,0:T(8,128)(2,1)S(1)} collective-permute-done((bf16[16,1920]{1,0:T(8,128)(2,1)S(1)}, bf16[16,1920]{1,0:T(8,128)(2,1)S(1)}, u32[]{:S(2)}, u32[]{:S(2)}) %collective-permute-start.13) | collective-permute-done | bytes 61472 | tf_op jit(solution)/shard_map/ppermute | solution.py:19
  90.3 1.1 collective-permute-done.14
  91.4 0.9 divide_convert_fusion
  92.9 1.5 %collective-permute-start.28 = (bf16[16,924]{1,0:T(8,128)(2,1)S(1)}, bf16[16,924]{1,0:T(8,128)(2,1)S(1)}, u32[]{:S(2)}, u32[]{:S(2)}) collective-permute-start(bf16[16,924]{1,0:T(8,128)(2,1)S(1)} %bitcast.56), channel_id=1, source_target_pairs={{0,24},{8,0},{16,8},{24,16},{1,25},{9,1},{17,9},{25,17},{2,26},{10... | collective-permute-start | bytes 88712 | tf_op jit(solution)/shard_map/ppermute | solution.py:19
  94.5 2.6 %collective-permute-start.27 = (bf16[16,924]{1,0:T(8,128)(2,1)S(1)}, bf16[16,924]{1,0:T(8,128)(2,1)S(1)}, u32[]{:S(2)}, u32[]{:S(2)}) collective-permute-start(bf16[16,924]{1,0:T(8,128)(2,1)S(1)} %bitcast.54), channel_id=1, source_target_pairs={{0,16},{8,24},{16,0},{24,8},{1,17},{9,25},{17,1},{25,9},{2,18},{10... | collective-permute-start | bytes 88712 | tf_op jit(solution)/shard_map/ppermute | solution.py:19
  97.1 1.4 collective-permute-done.26
  99.5 1.7 %collective-permute-start.30 = (bf16[4,16,924]{2,1,0:T(8,128)(2,1)}, bf16[4,16,924]{2,1,0:T(8,128)(2,1)S(1)}, u32[]{:S(2)}, u32[]{:S(2)}) collective-permute-start(bf16[4,16,924]{2,1,0:T(8,128)(2,1)} %pad_maximum_fusion.5), channel_id=1, source_target_pairs={{0,4},{2,6},{4,0},{6,2},{1,5},{3,7},{5,1},{7,3},{8,12},{10,14},{12... | collective-permute-start | bytes 354824 | tf_op jit(solution)/shard_map/ppermute | solution.py:19
  101.1 1.0 collective-permute-start.29
  102.1 4.3 %collective-permute-done.31 = bf16[4,16,924]{2,1,0:T(8,128)(2,1)S(1)} collective-permute-done((bf16[4,16,924]{2,1,0:T(8,128)(2,1)}, bf16[4,16,924]{2,1,0:T(8,128)(2,1)S(1)}, u32[]{:S(2)}, u32[]{:S(2)}) %collective-permute-start.31) | collective-permute-done | bytes 118304 | tf_op jit(solution)/shard_map/ppermute | solution.py:19
  106.8 1.0 select_select_fusion.6
  107.8 13.1 %collective-permute-start.32 = (bf16[4,16,924]{2,1,0:T(8,128)(2,1)S(1)}, bf16[4,16,924]{2,1,0:T(8,128)(2,1)S(1)}, u32[]{:S(2)}, u32[]{:S(2)}) collective-permute-start(bf16[4,16,924]{2,1,0:T(8,128)(2,1)S(1)} %get-tuple-element.50), channel_id=1, source_target_pairs={{1,32},{3,34},{5,36},{7,38},{9,40},{11,42},{13,44},{15,46},{17,48}... | collective-permute-start | bytes 354824 | tf_op jit(solution)/shard_map/ppermute | solution.py:162
  120.9 1.0 select_select_fusion.5
  122.0 4.7 %collective-permute-start.34 = (bf16[4,16,924]{2,1,0:T(8,128)(2,1)S(1)}, bf16[4,16,924]{2,1,0:T(8,128)(2,1)S(1)}, u32[]{:S(2)}, u32[]{:S(2)}) collective-permute-start(bf16[4,16,924]{2,1,0:T(8,128)(2,1)S(1)} %get-tuple-element.53), channel_id=1, source_target_pairs={{0,128},{2,130},{4,132},{6,134},{8,136},{10,138},{12,140},{14,142}... | collective-permute-start | bytes 354824 | tf_op jit(solution)/shard_map/ppermute | solution.py:162
  126.8 3.4 %collective-permute-done.33 = bf16[4,16,924]{2,1,0:T(8,128)(2,1)S(1)} collective-permute-done((bf16[4,16,924]{2,1,0:T(8,128)(2,1)S(1)}, bf16[4,16,924]{2,1,0:T(8,128)(2,1)S(1)}, u32[]{:S(2)}, u32[]{:S(2)}) %collective-permute-start.33) | collective-permute-done | bytes 118304 | tf_op jit(solution)/shard_map/ppermute | solution.py:162
  130.2 1.9 %collective-permute-done.34 = bf16[4,16,924]{2,1,0:T(8,128)(2,1)S(1)} collective-permute-done((bf16[4,16,924]{2,1,0:T(8,128)(2,1)S(1)}, bf16[4,16,924]{2,1,0:T(8,128)(2,1)S(1)}, u32[]{:S(2)}, u32[]{:S(2)}) %collective-permute-start.34) | collective-permute-done | bytes 118304 | tf_op jit(solution)/shard_map/ppermute | solution.py:162
  132.1 1.6 %collective-permute-done.35 = bf16[4,16,924]{2,1,0:T(8,128)(2,1)S(1)} collective-permute-done((bf16[4,16,924]{2,1,0:T(8,128)(2,1)S(1)}, bf16[4,16,924]{2,1,0:T(8,128)(2,1)S(1)}, u32[]{:S(2)}, u32[]{:S(2)}) %collective-permute-start.35) | collective-permute-done | bytes 118304 | tf_op jit(solution)/shard_map/ppermute | solution.py:162
  135.8 2.0 %add_convert_fusion = bf16[1024,924]{0,1:T(8,128)(2,1)} fusion(f32[1024,924]{0,1:T(8,128)S(1)} %fusion.40, bf16[256,924]{1,0:T(8,128)(2,1)S(1)} %bitcast.38, bf16[1024,512]{0,1:T(8,128)(2,1)S(1)} %copy-done.1), kind=kOutput, calls=%fused_computation | convolution fusion | flops 486334464 | bytes 6742016 | tf_op jit(solution)/shard_map/dot_general | solution.py:198
  (112 shorter events, 14.0 us)
Async XLA Ops:
  4.5 5.6 %collective-permute-start = (f32[256,1024]{1,0:T(8,128)S(1)}, f32[256,1024]{1,0:T(8,128)S(1)}, u32[]{:S(2)}, u32[]{:S(2)}) collective-permute-start(f32[256,1024]{1,0:T(8,128)S(1)} %fusion.36), channel_id=1, source_target_pairs={{0,1},{1,0},{2,3},{3,2},{4,5},{5,4},{6,7},{7,6},{8,9},{9,8},{10,11... | collective-permute-start | bytes 3145736 | tf_op jit(solution)/shard_map/ppermute | solution.py:19
  11.6 6.9 %collective-permute-start.1 = (bf16[64,1024]{1,0:T(8,128)(2,1)}, bf16[64,1024]{1,0:T(8,128)(2,1)S(1)}, u32[]{:S(2)}, u32[]{:S(2)}) collective-permute-start(bf16[64,1024]{1,0:T(8,128)(2,1)} %get-tuple-element.54), channel_id=1, source_target_pairs={{0,2},{2,4},{4,6},{6,0},{1,3},{3,5},{5,7},{7,1},{8,10},{10,12},{12... | collective-permute-start | bytes 393224 | tf_op jit(solution)/shard_map/ppermute | solution.py:19
  11.6 8.2 %collective-permute-start.3 = (bf16[64,1024]{1,0:T(8,128)(2,1)}, bf16[64,1024]{1,0:T(8,128)(2,1)S(1)}, u32[]{:S(2)}, u32[]{:S(2)}) collective-permute-start(bf16[64,1024]{1,0:T(8,128)(2,1)} %get-tuple-element.55), channel_id=1, source_target_pairs={{0,4},{2,6},{4,0},{6,2},{1,5},{3,7},{5,1},{7,3},{8,12},{10,14},{12... | collective-permute-start | bytes 393224 | tf_op jit(solution)/shard_map/ppermute | solution.py:19
  13.6 7.5 %collective-permute-start.2 = (bf16[64,1024]{1,0:T(8,128)(2,1)S(1)}, bf16[64,1024]{1,0:T(8,128)(2,1)}, u32[]{:S(2)}, u32[]{:S(2)}) collective-permute-start(bf16[64,1024]{1,0:T(8,128)(2,1)S(1)} %get-tuple-element.56), channel_id=1, source_target_pairs={{0,6},{2,0},{4,2},{6,4},{1,7},{3,1},{5,3},{7,5},{8,14},{10,8},{12,... | collective-permute-start | bytes 393224 | tf_op jit(solution)/shard_map/ppermute | solution.py:19
  22.0 8.5 %collective-permute-start.6 = (bf16[64,1024]{1,0:T(8,128)(2,1)S(1)}, bf16[64,1024]{1,0:T(8,128)(2,1)S(1)}, u32[]{:S(2)}, u32[]{:S(2)}) collective-permute-start(bf16[64,1024]{1,0:T(8,128)(2,1)S(1)} %fusion.84), channel_id=1, source_target_pairs={{0,6},{2,0},{4,2},{6,4},{1,7},{3,1},{5,3},{7,5},{8,14},{10,8},{12,... | collective-permute-start | bytes 393224 | tf_op jit(solution)/shard_map/ppermute | solution.py:19
  25.2 5.7 %collective-permute-start.5 = (bf16[64,1024]{1,0:T(8,128)(2,1)S(1)}, bf16[64,1024]{1,0:T(8,128)(2,1)S(1)}, u32[]{:S(2)}, u32[]{:S(2)}) collective-permute-start(bf16[64,1024]{1,0:T(8,128)(2,1)S(1)} %fusion.84), channel_id=1, source_target_pairs={{0,4},{2,6},{4,0},{6,2},{1,5},{3,7},{5,1},{7,3},{8,12},{10,14},{12... | collective-permute-start | bytes 393224 | tf_op jit(solution)/shard_map/ppermute | solution.py:19
  25.2 9.1 %collective-permute-start.4 = (bf16[64,1024]{1,0:T(8,128)(2,1)S(1)}, bf16[64,1024]{1,0:T(8,128)(2,1)S(1)}, u32[]{:S(2)}, u32[]{:S(2)}) collective-permute-start(bf16[64,1024]{1,0:T(8,128)(2,1)S(1)} %fusion.84), channel_id=1, source_target_pairs={{0,2},{2,4},{4,6},{6,0},{1,3},{3,5},{5,7},{7,1},{8,10},{10,12},{12... | collective-permute-start | bytes 393224 | tf_op jit(solution)/shard_map/ppermute | solution.py:19
  34.3 2.5 %collective-permute-start.7 = (bf16[256,1024]{1,0:T(8,128)(2,1)S(1)}, bf16[256,1024]{1,0:T(8,128)(2,1)S(1)}, u32[]{:S(2)}, u32[]{:S(2)}) collective-permute-start(bf16[256,1024]{1,0:T(8,128)(2,1)S(1)} %pad_maximum_fusion.mine_ref), channel_id=1, source_target_pairs={{0,1},{1,0},{2,3},{3,2},{4,5},{5,4},{6,7},{7,6},{8,9},{9,8},{10,11... | collective-permute-start | bytes 1572872 | tf_op jit(solution)/shard_map/ppermute | solution.py:19
  42.9 13.0 %collective-permute-start.16 = (bf16[64,1776]{1,0:T(8,128)(2,1)}, bf16[64,1776]{1,0:T(8,128)(2,1)S(1)}, u32[]{:S(2)}, u32[]{:S(2)}) collective-permute-start(bf16[64,1776]{1,0:T(8,128)(2,1)} %get-tuple-element.36), channel_id=1, source_target_pairs={{0,32},{32,64},{64,96},{96,128},{128,160},{160,192},{192,224},{224... | collective-permute-start | bytes 681992 | tf_op jit(solution)/shard_map/ppermute | solution.py:19
  43.0 12.9 %copy-start.10 = (f32[64,1776]{1,0:T(8,128)S(1)}, f32[64,1776]{1,0:T(8,128)}, u32[]{:S(2)}) copy-start(f32[64,1776]{1,0:T(8,128)} %get-tuple-element.35) | copy-start | bytes 1363972
  43.0 17.2 %copy-start.9 = (f32[64,1776]{1,0:T(8,128)S(1)}, f32[64,1776]{1,0:T(8,128)}, u32[]{:S(2)}) copy-start(f32[64,1776]{1,0:T(8,128)} %get-tuple-element.38) | copy-start | bytes 1363972
  49.3 14.5 %copy-start.4 = (f32[64,1920]{1,0:T(8,128)S(1)}, f32[64,1920]{1,0:T(8,128)}, u32[]{:S(2)}) copy-start(f32[64,1920]{1,0:T(8,128)} %get-tuple-element.30) | copy-start | bytes 1474564
  49.3 14.6 %copy-start.13 = (bf16[64,1920]{1,0:T(8,128)(2,1)S(1)}, bf16[64,1920]{1,0:T(8,128)(2,1)}, u32[]{:S(2)}) copy-start(bf16[64,1920]{1,0:T(8,128)(2,1)} %get-tuple-element.29) | copy-start | bytes 737284
  49.3 15.6 %copy-start.3 = (f32[64,1920]{1,0:T(8,128)S(1)}, f32[64,1920]{1,0:T(8,128)}, u32[]{:S(2)}) copy-start(f32[64,1920]{1,0:T(8,128)} %get-tuple-element.26) | copy-start | bytes 1474564
  49.3 15.6 %collective-permute-start.8 = (bf16[64,1920]{1,0:T(8,128)(2,1)}, bf16[64,1920]{1,0:T(8,128)(2,1)S(1)}, u32[]{:S(2)}, u32[]{:S(2)}) collective-permute-start(bf16[64,1920]{1,0:T(8,128)(2,1)} %get-tuple-element.27), channel_id=1, source_target_pairs={{0,8},{8,16},{16,24},{24,0},{1,9},{9,17},{17,25},{25,1},{2,10},{10... | collective-permute-start | bytes 737288 | tf_op jit(solution)/shard_map/ppermute | solution.py:19
  50.2 13.6 %collective-permute-start.10 = (bf16[64,1920]{1,0:T(8,128)(2,1)}, bf16[64,1920]{1,0:T(8,128)(2,1)S(1)}, u32[]{:S(2)}, u32[]{:S(2)}) collective-permute-start(bf16[64,1920]{1,0:T(8,128)(2,1)} %get-tuple-element.31), channel_id=1, source_target_pairs={{0,24},{8,0},{16,8},{24,16},{1,25},{9,1},{17,9},{25,17},{2,26},{10... | collective-permute-start | bytes 737288 | tf_op jit(solution)/shard_map/ppermute | solution.py:19
  52.1 8.2 %collective-permute-start.20 = (bf16[64,1776]{1,0:T(8,128)(2,1)S(1)}, bf16[64,1776]{1,0:T(8,128)(2,1)S(1)}, u32[]{:S(2)}, u32[]{:S(2)}) collective-permute-start(bf16[64,1776]{1,0:T(8,128)(2,1)S(1)} %copy-done.16), channel_id=1, source_target_pairs={{0,224},{32,0},{64,32},{96,64},{128,96},{160,128},{192,160},{224,1... | collective-permute-start | bytes 681992 | tf_op jit(solution)/shard_map/ppermute | solution.py:19
  56.0 9.7 %collective-permute-start.17 = (bf16[64,1776]{1,0:T(8,128)(2,1)S(1)}, bf16[64,1776]{1,0:T(8,128)(2,1)S(1)}, u32[]{:S(2)}, u32[]{:S(2)}) collective-permute-start(bf16[64,1776]{1,0:T(8,128)(2,1)S(1)} %add_convert_fusion.8), channel_id=1, source_target_pairs={{0,32},{32,64},{64,96},{96,128},{128,160},{160,192},{192,224},{224... | collective-permute-start | bytes 681992 | tf_op jit(solution)/shard_map/ppermute | solution.py:19
  60.3 6.9 %collective-permute-start.21 = (bf16[64,1776]{1,0:T(8,128)(2,1)S(1)}, bf16[64,1776]{1,0:T(8,128)(2,1)S(1)}, u32[]{:S(2)}, u32[]{:S(2)}) collective-permute-start(bf16[64,1776]{1,0:T(8,128)(2,1)S(1)} %add_convert_fusion.5), channel_id=1, source_target_pairs={{0,224},{32,0},{64,32},{96,64},{128,96},{160,128},{192,160},{224,1... | collective-permute-start | bytes 681992 | tf_op jit(solution)/shard_map/ppermute | solution.py:19
  63.9 11.0 %collective-permute-start.11 = (bf16[128,1920]{1,0:T(8,128)(2,1)S(1)}, bf16[128,1920]{1,0:T(8,128)(2,1)S(1)}, u32[]{:S(2)}, u32[]{:S(2)}) collective-permute-start(bf16[128,1920]{1,0:T(8,128)(2,1)S(1)} %pad_maximum_fusion.3), channel_id=1, source_target_pairs={{0,24},{8,0},{16,8},{24,16},{1,25},{9,1},{17,9},{25,17},{2,26},{10... | collective-permute-start | bytes 1474568 | tf_op jit(solution)/shard_map/ppermute | solution.py:19
  64.9 11.7 %copy-start.2 = (f32[64,1920]{1,0:T(8,128)S(1)}, f32[64,1920]{1,0:T(8,128)}, u32[]{:S(2)}) copy-start(f32[64,1920]{1,0:T(8,128)} %get-tuple-element.25) | copy-start | bytes 1474564
  65.0 13.7 %copy-start.11 = (f32[64,1776]{1,0:T(8,128)S(1)}, f32[64,1776]{1,0:T(8,128)}, u32[]{:S(2)}) copy-start(f32[64,1776]{1,0:T(8,128)} %get-tuple-element.32) | copy-start | bytes 1363972
  65.0 11.6 %collective-permute-start.9 = (bf16[128,1920]{1,0:T(8,128)(2,1)S(1)}, bf16[128,1920]{1,0:T(8,128)(2,1)S(1)}, u32[]{:S(2)}, u32[]{:S(2)}) collective-permute-start(bf16[128,1920]{1,0:T(8,128)(2,1)S(1)} %pad_maximum_fusion.2), channel_id=1, source_target_pairs={{0,8},{8,16},{16,24},{24,0},{1,9},{9,17},{17,25},{25,1},{2,10},{10... | collective-permute-start | bytes 1474568 | tf_op jit(solution)/shard_map/ppermute | solution.py:19
  65.7 6.5 %collective-permute-start.18 = (bf16[64,1776]{1,0:T(8,128)(2,1)S(1)}, bf16[64,1776]{1,0:T(8,128)(2,1)S(1)}, u32[]{:S(2)}, u32[]{:S(2)}) collective-permute-start(bf16[64,1776]{1,0:T(8,128)(2,1)S(1)} %add_convert_fusion.7), channel_id=1, source_target_pairs={{0,32},{32,64},{64,96},{96,128},{128,160},{160,192},{192,224},{224... | collective-permute-start | bytes 681992 | tf_op jit(solution)/shard_map/ppermute | solution.py:19
  67.2 14.9 %copy-start.5 = (f32[64,1920]{1,0:T(8,128)S(1)}, f32[64,1920]{1,0:T(8,128)}, u32[]{:S(2)}) copy-start(f32[64,1920]{1,0:T(8,128)} %get-tuple-element.24) | copy-start | bytes 1474564
  67.2 9.6 %collective-permute-start.22 = (bf16[64,1776]{1,0:T(8,128)(2,1)S(1)}, bf16[64,1776]{1,0:T(8,128)(2,1)S(1)}, u32[]{:S(2)}, u32[]{:S(2)}) collective-permute-start(bf16[64,1776]{1,0:T(8,128)(2,1)S(1)} %add_convert_fusion.4), channel_id=1, source_target_pairs={{0,224},{32,0},{64,32},{96,64},{128,96},{160,128},{192,160},{224,1... | collective-permute-start | bytes 681992 | tf_op jit(solution)/shard_map/ppermute | solution.py:19
  72.2 6.5 %collective-permute-start.19 = (bf16[64,1776]{1,0:T(8,128)(2,1)S(1)}, bf16[64,1776]{1,0:T(8,128)(2,1)S(1)}, u32[]{:S(2)}, u32[]{:S(2)}) collective-permute-start(bf16[64,1776]{1,0:T(8,128)(2,1)S(1)} %add_convert_fusion.6), channel_id=1, source_target_pairs={{0,32},{32,64},{64,96},{96,128},{128,160},{160,192},{192,224},{224... | collective-permute-start | bytes 681992 | tf_op jit(solution)/shard_map/ppermute | solution.py:19
  76.7 5.4 %collective-permute-start.12 = (bf16[64,1920]{1,0:T(8,128)(2,1)S(1)}, bf16[64,1920]{1,0:T(8,128)(2,1)S(1)}, u32[]{:S(2)}, u32[]{:S(2)}) collective-permute-start(bf16[64,1920]{1,0:T(8,128)(2,1)S(1)} %add_convert_fusion.1), channel_id=1, source_target_pairs={{0,32},{32,0},{64,96},{96,64},{128,160},{160,128},{192,224},{224,1... | collective-permute-start | bytes 737288 | tf_op jit(solution)/shard_map/ppermute | solution.py:119
  78.8 12.6 %copy-start.14 = (f32[16,3696]{1,0:T(8,128)S(1)}, f32[16,3696]{1,0:T(8,128)}, u32[]{:S(2)}) copy-start(f32[16,3696]{1,0:T(8,128)} %param.8) | copy-start | bytes 709636
  78.8 12.6 %copy-start.15 = (f32[16,3696]{1,0:T(8,128)S(1)}, f32[16,3696]{1,0:T(8,128)}, u32[]{:S(2)}) copy-start(f32[16,3696]{1,0:T(8,128)} %param.9) | copy-start | bytes 709636
  78.8 7.4 %collective-permute-start.23 = (bf16[16,1776]{1,0:T(8,128)(2,1)S(1)}, bf16[16,1776]{1,0:T(8,128)(2,1)S(1)}, u32[]{:S(2)}, u32[]{:S(2)}) collective-permute-start(bf16[16,1776]{1,0:T(8,128)(2,1)S(1)} %get-tuple-element.60), channel_id=1, source_target_pairs={{0,16},{8,24},{16,0},{24,8},{1,17},{9,25},{17,1},{25,9},{2,18},{10... | collective-permute-start | bytes 170504 | tf_op jit(solution)/shard_map/ppermute | solution.py:19
  79.4 9.0 %collective-permute-start.25 = (bf16[16,1776]{1,0:T(8,128)(2,1)S(1)}, bf16[16,1776]{1,0:T(8,128)(2,1)S(1)}, u32[]{:S(2)}, u32[]{:S(2)}) collective-permute-start(bf16[16,1776]{1,0:T(8,128)(2,1)S(1)} %get-tuple-element.61), channel_id=1, source_target_pairs={{0,24},{8,0},{16,8},{24,16},{1,25},{9,1},{17,9},{25,17},{2,26},{10... | collective-permute-start | bytes 170504 | tf_op jit(solution)/shard_map/ppermute | solution.py:19
  80.8 7.6 %collective-permute-start.24 = (bf16[16,1776]{1,0:T(8,128)(2,1)S(1)}, bf16[16,1776]{1,0:T(8,128)(2,1)S(1)}, u32[]{:S(2)}, u32[]{:S(2)}) collective-permute-start(bf16[16,1776]{1,0:T(8,128)(2,1)S(1)} %get-tuple-element.62), channel_id=1, source_target_pairs={{0,8},{8,16},{16,24},{24,0},{1,9},{9,17},{17,25},{25,1},{2,10},{10... | collective-permute-start | bytes 170504 | tf_op jit(solution)/shard_map/ppermute | solution.py:19
  82.3 7.7 %collective-permute-start.13 = (bf16[16,1920]{1,0:T(8,128)(2,1)S(1)}, bf16[16,1920]{1,0:T(8,128)(2,1)S(1)}, u32[]{:S(2)}, u32[]{:S(2)}) collective-permute-start(bf16[16,1920]{1,0:T(8,128)(2,1)S(1)} %get-tuple-element.57), channel_id=1, source_target_pairs={{0,128},{32,160},{64,192},{96,224},{128,0},{160,32},{192,64},{224,... | collective-permute-start | bytes 184328 | tf_op jit(solution)/shard_map/ppermute | solution.py:19
  86.0 4.3 %collective-permute-start.15 = (bf16[16,1920]{1,0:T(8,128)(2,1)S(1)}, bf16[16,1920]{1,0:T(8,128)(2,1)S(1)}, u32[]{:S(2)}, u32[]{:S(2)}) collective-permute-start(bf16[16,1920]{1,0:T(8,128)(2,1)S(1)} %get-tuple-element.58), channel_id=1, source_target_pairs={{0,192},{32,224},{64,0},{96,32},{128,64},{160,96},{192,128},{224,1... | collective-permute-start | bytes 184328 | tf_op jit(solution)/shard_map/ppermute | solution.py:19
  86.2 5.2 %collective-permute-start.14 = (bf16[16,1920]{1,0:T(8,128)(2,1)S(1)}, bf16[16,1920]{1,0:T(8,128)(2,1)S(1)}, u32[]{:S(2)}, u32[]{:S(2)}) collective-permute-start(bf16[16,1920]{1,0:T(8,128)(2,1)S(1)} %get-tuple-element.59), channel_id=1, source_target_pairs={{0,64},{32,96},{64,128},{96,160},{128,192},{160,224},{192,0},{224,... | collective-permute-start | bytes 184328 | tf_op jit(solution)/shard_map/ppermute | solution.py:19
  92.8 41.4 %copy-start.1 = (bf16[1024,512]{0,1:T(8,128)(2,1)S(1)}, bf16[1024,512]{0,1:T(8,128)(2,1)}, u32[]{:S(2)}) copy-start(bf16[1024,512]{0,1:T(8,128)(2,1)} %fusion) | copy-start | bytes 3145732
  92.9 4.2 %collective-permute-start.28 = (bf16[16,924]{1,0:T(8,128)(2,1)S(1)}, bf16[16,924]{1,0:T(8,128)(2,1)S(1)}, u32[]{:S(2)}, u32[]{:S(2)}) collective-permute-start(bf16[16,924]{1,0:T(8,128)(2,1)S(1)} %bitcast.56), channel_id=1, source_target_pairs={{0,24},{8,0},{16,8},{24,16},{1,25},{9,1},{17,9},{25,17},{2,26},{10... | collective-permute-start | bytes 88712 | tf_op jit(solution)/shard_map/ppermute | solution.py:19
  94.5 4.0 %collective-permute-start.26 = (bf16[16,924]{1,0:T(8,128)(2,1)S(1)}, bf16[16,924]{1,0:T(8,128)(2,1)S(1)}, u32[]{:S(2)}, u32[]{:S(2)}) collective-permute-start(bf16[16,924]{1,0:T(8,128)(2,1)S(1)} %bitcast.55), channel_id=1, source_target_pairs={{0,8},{8,16},{16,24},{24,0},{1,9},{9,17},{17,25},{25,1},{2,10},{10... | collective-permute-start | bytes 88712 | tf_op jit(solution)/shard_map/ppermute | solution.py:19
  94.5 4.3 %collective-permute-start.27 = (bf16[16,924]{1,0:T(8,128)(2,1)S(1)}, bf16[16,924]{1,0:T(8,128)(2,1)S(1)}, u32[]{:S(2)}, u32[]{:S(2)}) collective-permute-start(bf16[16,924]{1,0:T(8,128)(2,1)S(1)} %bitcast.54), channel_id=1, source_target_pairs={{0,16},{8,24},{16,0},{24,8},{1,17},{9,25},{17,1},{25,9},{2,18},{10... | collective-permute-start | bytes 88712 | tf_op jit(solution)/shard_map/ppermute | solution.py:19
  99.5 6.9 %collective-permute-start.31 = (bf16[4,16,924]{2,1,0:T(8,128)(2,1)}, bf16[4,16,924]{2,1,0:T(8,128)(2,1)S(1)}, u32[]{:S(2)}, u32[]{:S(2)}) collective-permute-start(bf16[4,16,924]{2,1,0:T(8,128)(2,1)} %pad_maximum_fusion.5), channel_id=1, source_target_pairs={{0,2},{2,4},{4,6},{6,0},{1,3},{3,5},{5,7},{7,1},{8,10},{10,12},{12... | collective-permute-start | bytes 354824 | tf_op jit(solution)/shard_map/ppermute | solution.py:19
  99.5 6.9 %collective-permute-start.30 = (bf16[4,16,924]{2,1,0:T(8,128)(2,1)}, bf16[4,16,924]{2,1,0:T(8,128)(2,1)S(1)}, u32[]{:S(2)}, u32[]{:S(2)}) collective-permute-start(bf16[4,16,924]{2,1,0:T(8,128)(2,1)} %pad_maximum_fusion.5), channel_id=1, source_target_pairs={{0,4},{2,6},{4,0},{6,2},{1,5},{3,7},{5,1},{7,3},{8,12},{10,14},{12... | collective-permute-start | bytes 354824 | tf_op jit(solution)/shard_map/ppermute | solution.py:19
  101.1 5.7 %collective-permute-start.29 = (bf16[4,16,924]{2,1,0:T(8,128)(2,1)}, bf16[4,16,924]{2,1,0:T(8,128)(2,1)}, u32[]{:S(2)}, u32[]{:S(2)}) collective-permute-start(bf16[4,16,924]{2,1,0:T(8,128)(2,1)} %pad_maximum_fusion.5), channel_id=1, source_target_pairs={{0,6},{2,0},{4,2},{6,4},{1,7},{3,1},{5,3},{7,5},{8,14},{10,8},{12,... | collective-permute-start | bytes 354824 | tf_op jit(solution)/shard_map/ppermute | solution.py:19
  107.8 19.0 %collective-permute-start.32 = (bf16[4,16,924]{2,1,0:T(8,128)(2,1)S(1)}, bf16[4,16,924]{2,1,0:T(8,128)(2,1)S(1)}, u32[]{:S(2)}, u32[]{:S(2)}) collective-permute-start(bf16[4,16,924]{2,1,0:T(8,128)(2,1)S(1)} %get-tuple-element.50), channel_id=1, source_target_pairs={{1,32},{3,34},{5,36},{7,38},{9,40},{11,42},{13,44},{15,46},{17,48}... | collective-permute-start | bytes 354824 | tf_op jit(solution)/shard_map/ppermute | solution.py:162
  121.9 8.3 %collective-permute-start.33 = (bf16[4,16,924]{2,1,0:T(8,128)(2,1)S(1)}, bf16[4,16,924]{2,1,0:T(8,128)(2,1)S(1)}, u32[]{:S(2)}, u32[]{:S(2)}) collective-permute-start(bf16[4,16,924]{2,1,0:T(8,128)(2,1)S(1)} %get-tuple-element.52), channel_id=1, source_target_pairs={{0,64},{2,66},{4,68},{6,70},{8,72},{10,74},{12,76},{14,78},{16,80}... | collective-permute-start | bytes 354824 | tf_op jit(solution)/shard_map/ppermute | solution.py:162
  122.0 10.1 %collective-permute-start.34 = (bf16[4,16,924]{2,1,0:T(8,128)(2,1)S(1)}, bf16[4,16,924]{2,1,0:T(8,128)(2,1)S(1)}, u32[]{:S(2)}, u32[]{:S(2)}) collective-permute-start(bf16[4,16,924]{2,1,0:T(8,128)(2,1)S(1)} %get-tuple-element.53), channel_id=1, source_target_pairs={{0,128},{2,130},{4,132},{6,134},{8,136},{10,138},{12,140},{14,142}... | collective-permute-start | bytes 354824 | tf_op jit(solution)/shard_map/ppermute | solution.py:162
  126.7 6.9 %collective-permute-start.35 = (bf16[4,16,924]{2,1,0:T(8,128)(2,1)S(1)}, bf16[4,16,924]{2,1,0:T(8,128)(2,1)S(1)}, u32[]{:S(2)}, u32[]{:S(2)}) collective-permute-start(bf16[4,16,924]{2,1,0:T(8,128)(2,1)S(1)} %get-tuple-element.51), channel_id=1, source_target_pairs={{0,192},{2,194},{4,196},{6,198},{8,200},{10,202},{12,204},{14,206}... | collective-permute-start | bytes 354824 | tf_op jit(solution)/shard_map/ppermute | solution.py:162
  133.7 2.1 %collective-permute-start.36 = (bf16[4,4,16,924]{3,2,1,0:T(8,128)(2,1)S(1)}, bf16[4,4,16,924]{3,2,1,0:T(8,128)(2,1)S(1)}, u32[]{:S(2)}, u32[]{:S(2)}) collective-permute-start(bf16[4,4,16,924]{3,2,1,0:T(8,128)(2,1)S(1)} %pad_maximum_fusion.1), channel_id=1, source_target_pairs={{0,1},{1,0},{2,3},{3,2},{4,5},{5,4},{6,7},{7,6},{8,9},{9,8},{10,11... | collective-permute-start | bytes 1419272 | tf_op jit(solution)/shard_map/ppermute | solution.py:19
  (8 other events, 44.3 us)

commit v8 on v7

--- a/solution.py
+++ b/solution.py
@@ -65,7 +65,7 @@
             pl.BlockSpec((tile, tokens), lambda i: (start + i, 0)),
         ],
         out_specs=[pl.BlockSpec((n, tile), lambda i: (0, i)) for n, _ in shapes],
-        out_shape=[pltpu.HBM((n, ff), t) for n, t in shapes],
+        out_shape=[(pltpu.HBM if k > 1 else pltpu.VMEM)((n, ff), t) for k, (n, t) in enumerate(shapes)],
         scratch_shapes=[pltpu.VMEM((2 * half, tokens), bf16)],
         compiler_params=pltpu.CompilerParams(vmem_limit_bytes=20 * 2**20),
         cost_estimate=pl.CostEstimate(
@@ -131,13 +131,6 @@
     return jnp.concatenate([first, second], 1)
 
 
-def picked(choices, index):
-    out = choices[0]
-    for k in range(1, len(choices)):
-        out = jnp.where(index == k, choices[k], out)
-    return out
-
-
 def spread(normed, beside):
     z, y, x, c = (lax.axis_index(axis) for axis in ("z", "y", "x", "c"))
     rows, ff = normed.shape
@@ -146,12 +139,12 @@
     got = {d: moved(piece(d), "y", d) for d in (1, 3, 2)}
     tall = jnp.stack([piece(0), got[1], got[2], got[3]])
     got = {d: moved(tall, "x", d) for d in (1, 3, 2)}
-    wide = [tall, got[1], got[2], got[3]]
+    wide = jnp.stack([tall, got[1], got[2], got[3]])
     odd = (z + c) % 2
     half = []
     for k in range(Z // 2):
         to = (z + 2 * k + odd) % Z
-        sent = picked(wide, (x - to // 2) % X)
+        sent = lax.dynamic_index_in_dim(wide, (x - to // 2) % X, 0, keepdims=False)
         pairs = []
         for pz in range(Z):
             for pc in range(C):

time: 138 us -> 138 us (level)
  starting transfers between devices: 60.7 us -> 59.1 us
    ppermute x4, waiting for transfers between devices: 6.9 us -> 9.52 us  [spread(): moved_in = lax.ppermute(sent, ('z', 'y', 'x', 'c'), pairs)]
    select_n x2 -> x0, other arithmetic: 1.91 us -> none  [picked(): out = jnp.where(index == k, choices[k], out)]
    ppermute x4, starting transfers between devices: 18 us -> 16.4 us  [spread(): moved_in = lax.ppermute(sent, ('z', 'y', 'x', 'c'), pairs)]
where the time goes in v8:
time: 138 us
  starting transfers between devices  59.1 us (43%)
  waiting for transfers between devices  46.7 us (34%)
  Pallas kernels  12.4 us (9%)
  matrix products  10.2 us (7%)
  other arithmetic  5.98 us (4%)
  local copies, waits for them, and re-layouts  2.16 us (2%)
    ppermute x32, starting transfers between devices, moved(): return lax.ppermute(value, axis, [(i, (i + by) % n) for i in range(n)])  42.6 us
    ppermute x32, waiting for transfers between devices, moved(): return lax.ppermute(value, axis, [(i, (i + by) % n) for i in range(n)])  36.3 us
    ppermute x4, starting transfers between devices, spread(): moved_in = lax.ppermute(sent, ('z', 'y', 'x', 'c'), pairs)  16.4 us
    pallas_call x2, Pallas kernels, gradient(): pl.pallas_call(functools.partial(grad_kernel, units), grid=(stop - start,...  12.4 us
    ppermute x4, waiting for transfers between devices, spread(): moved_in = lax.ppermute(sent, ('z', 'y', 'x', 'c'), pairs)  9.52 us
    dot_general x1, matrix products, project(): lax.dot_general(near_order(rank), basis, lanes, preferred_element_type=f32)  3.02 us
    dot_general x1, matrix products, shards(): jnp.dot(basis, spread_order(rank), preferred_element_type=f32).astype(bf16)  3.01 us
  transfers between devices with their start and end apart: 37, of which 26 were waited for; matrix products, arithmetic and copies ran while one was open for 5% of the time, Pallas kernels for 5%

profile of v8, /device:TPU:1, one launch (start us, length us, event | category | flops | bytes accessed | tf_op | source)
XLA Modules:
  0.0 137.7 jit_solution(14234617677905952176)
XLA Ops:
  0.7 3.0 %convolution_convert_fusion = bf16[512,1024]{1,0:T(8,128)(2,1)S(1)} fusion(bf16[1024,512]{1,0:T(8,128)(2,1)} %param.6, s32[512]{0:T(512)S(1)} %get-tuple-element.77, s32[512]{0:T(512)S(1)} %get-tuple-element.78, s32[512]{0:T(512)S(1)} %get-tuple-element.76, s32[512]{0:T(512)S(1)} %get-tuple-element.79, s32[]{:T(128)} %axis_index.35, ...), kind=kOutput, calls=%fused_computation.31 | convolution fusion | flops 548667392 | bytes 2110984 | tf_op jit(solution)/shard_map/dot_general | solution.py:90
  4.5 3.3 %collective-permute-start = (f32[256,1024]{1,0:T(8,128)S(1)}, f32[256,1024]{1,0:T(8,128)S(1)}, u32[]{:S(2)}, u32[]{:S(2)}) collective-permute-start(f32[256,1024]{1,0:T(8,128)S(1)} %fusion.36), channel_id=1, source_target_pairs={{0,1},{1,0},{2,3},{3,2},{4,5},{5,4},{6,7},{7,6},{8,9},{9,8},{10,11... | collective-permute-start | bytes 3145736 | tf_op jit(solution)/shard_map/ppermute | solution.py:19
  8.5 1.7 %collective-permute-done = f32[256,1024]{1,0:T(8,128)S(1)} collective-permute-done((f32[256,1024]{1,0:T(8,128)S(1)}, f32[256,1024]{1,0:T(8,128)S(1)}, u32[]{:S(2)}, u32[]{:S(2)}) %collective-permute-start) | collective-permute-done | bytes 1048608 | tf_op jit(solution)/shard_map/ppermute | solution.py:19
  11.6 1.9 %collective-permute-start.3 = (bf16[64,1024]{1,0:T(8,128)(2,1)}, bf16[64,1024]{1,0:T(8,128)(2,1)S(1)}, u32[]{:S(2)}, u32[]{:S(2)}) collective-permute-start(bf16[64,1024]{1,0:T(8,128)(2,1)} %get-tuple-element.55), channel_id=1, source_target_pairs={{0,4},{2,6},{4,0},{6,2},{1,5},{3,7},{5,1},{7,3},{8,12},{10,14},{12... | collective-permute-start | bytes 393224 | tf_op jit(solution)/shard_map/ppermute | solution.py:19
  13.6 1.2 collective-permute-start.2
  15.3 3.2 %collective-permute-done.1 = bf16[64,1024]{1,0:T(8,128)(2,1)S(1)} collective-permute-done((bf16[64,1024]{1,0:T(8,128)(2,1)}, bf16[64,1024]{1,0:T(8,128)(2,1)S(1)}, u32[]{:S(2)}, u32[]{:S(2)}) %collective-permute-start.1) | collective-permute-done | bytes 131104 | tf_op jit(solution)/shard_map/ppermute | solution.py:19
  18.5 1.4 collective-permute-done.3
  19.9 1.2 collective-permute-done.2
  21.0 1.0 fusion.84
  22.0 3.2 %collective-permute-start.6 = (bf16[64,1024]{1,0:T(8,128)(2,1)S(1)}, bf16[64,1024]{1,0:T(8,128)(2,1)S(1)}, u32[]{:S(2)}, u32[]{:S(2)}) collective-permute-start(bf16[64,1024]{1,0:T(8,128)(2,1)S(1)} %fusion.84), channel_id=1, source_target_pairs={{0,6},{2,0},{4,2},{6,4},{1,7},{3,1},{5,3},{7,5},{8,14},{10,8},{12,... | collective-permute-start | bytes 393224 | tf_op jit(solution)/shard_map/ppermute | solution.py:19
  25.9 3.0 %fusion = bf16[1024,512]{0,1:T(8,128)(2,1)} fusion(bf16[1024,512]{1,0:T(8,128)(2,1)} %param.6, s32[512]{0:T(512)S(1)} %get-tuple-element.82, s32[512]{0:T(512)} %get-tuple-element.83, s32[512]{0:T(512)S(1)} %get-tuple-element.81, s32[512]{0:T(512)} %get-tuple-element.84, s32[]{:T(128)S(6)} %add.303, s32[512]{0:T(512)S(1)} %get-tuple-element.75, ...), kind=kOutput, calls=%fused_computation.33 | convolution fusion | flops 555745280 | bytes 2115596 | tf_op jit(solution)/shard_map/dot_general | solution.py:175
  28.9 1.6 %collective-permute-done.6 = bf16[64,1024]{1,0:T(8,128)(2,1)S(1)} collective-permute-done((bf16[64,1024]{1,0:T(8,128)(2,1)S(1)}, bf16[64,1024]{1,0:T(8,128)(2,1)S(1)}, u32[]{:S(2)}, u32[]{:S(2)}) %collective-permute-start.6) | collective-permute-done | bytes 131104 | tf_op jit(solution)/shard_map/ppermute | solution.py:19
  31.0 3.4 %collective-permute-done.4 = bf16[64,1024]{1,0:T(8,128)(2,1)S(1)} collective-permute-done((bf16[64,1024]{1,0:T(8,128)(2,1)S(1)}, bf16[64,1024]{1,0:T(8,128)(2,1)S(1)}, u32[]{:S(2)}, u32[]{:S(2)}) %collective-permute-start.4) | collective-permute-done | bytes 131104 | tf_op jit(solution)/shard_map/ppermute | solution.py:19
  34.3 0.9 collective-permute-start.7
  35.4 1.5 %collective-permute-done.7.other_ref = bf16[256,1024]{1,0:T(8,128)(2,1)S(1)} collective-permute-done((bf16[256,1024]{1,0:T(8,128)(2,1)S(1)}, bf16[256,1024]{1,0:T(8,128)(2,1)S(1)}, u32[]{:S(2)}, u32[]{:S(2)}) %collective-permute-start.7) | collective-permute-done | bytes 524320 | tf_op jit(solution)/shard_map/ppermute | solution.py:19
  36.8 6.1 %shard_map.77 = (bf16[64,1776]{1,0:T(8,128)(2,1)}, bf16[64,1776]{1,0:T(8,128)(2,1)S(1)}, f32[64,1776]{1,0:T(8,128)}, f32[64,1776]{1,0:T(8,128)}, f32[64,1776]{1,...) custom-call(s32[4]{0:T(128)S(1)} %pad_add_fusion.here, ...), custom_call_target="tpu_custom_call" | custom-call | flops 1862270976 | bytes 6819840 | tf_op jit(solution)/shard_map/pallas_call | solution.py:58
  43.0 6.3 %shard_map.76 = (bf16[64,1920]{1,0:T(8,128)(2,1)S(1)}, bf16[64,1920]{1,0:T(8,128)(2,1)S(1)}, f32[64,1920]{1,0:T(8,128)}, bf16[64,1920]{1,0:T(8,128)(2,1)}, bf16[...) custom-call(s32[4]{0:T(128)S(1)} %pad_add_fusion.here, ...), custom_call_target="tpu_custom_call" | custom-call | flops 2013265920 | bytes 7372800 | tf_op jit(solution)/shard_map/pallas_call | solution.py:58
  50.2 1.9 %collective-permute-start.10 = (bf16[64,1920]{1,0:T(8,128)(2,1)S(1)}, bf16[64,1920]{1,0:T(8,128)(2,1)S(1)}, u32[]{:S(2)}, u32[]{:S(2)}) collective-permute-start(bf16[64,1920]{1,0:T(8,128)(2,1)S(1)} %get-tuple-element.31), channel_id=1, source_target_pairs={{0,24},{8,0},{16,8},{24,16},{1,25},{9,1},{17,9},{25,17},{2,26},{10... | collective-permute-start | bytes 737288 | tf_op jit(solution)/shard_map/ppermute | solution.py:19
  52.1 3.9 %collective-permute-start.20 = (bf16[64,1776]{1,0:T(8,128)(2,1)S(1)}, bf16[64,1776]{1,0:T(8,128)(2,1)S(1)}, u32[]{:S(2)}, u32[]{:S(2)}) collective-permute-start(bf16[64,1776]{1,0:T(8,128)(2,1)S(1)} %get-tuple-element.39), channel_id=1, source_target_pairs={{0,224},{32,0},{64,32},{96,64},{128,96},{160,128},{192,160},{224,1... | collective-permute-start | bytes 681992 | tf_op jit(solution)/shard_map/ppermute | solution.py:19
  55.9 1.0 add_convert_fusion.8
  57.0 3.2 %collective-permute-done.20 = bf16[64,1776]{1,0:T(8,128)(2,1)S(1)} collective-permute-done((bf16[64,1776]{1,0:T(8,128)(2,1)S(1)}, bf16[64,1776]{1,0:T(8,128)(2,1)S(1)}, u32[]{:S(2)}, u32[]{:S(2)}) %collective-permute-start.20) | collective-permute-done | bytes 227360 | tf_op jit(solution)/shard_map/ppermute | solution.py:19
  60.3 3.5 %collective-permute-start.21 = (bf16[64,1776]{1,0:T(8,128)(2,1)S(1)}, bf16[64,1776]{1,0:T(8,128)(2,1)S(1)}, u32[]{:S(2)}, u32[]{:S(2)}) collective-permute-start(bf16[64,1776]{1,0:T(8,128)(2,1)S(1)} %add_convert_fusion.5), channel_id=1, source_target_pairs={{0,224},{32,0},{64,32},{96,64},{128,96},{160,128},{192,160},{224,1... | collective-permute-start | bytes 681992 | tf_op jit(solution)/shard_map/ppermute | solution.py:19
  63.9 1.0 collective-permute-start.11
  65.8 1.4 collective-permute-done.21
  67.2 3.5 %collective-permute-start.22 = (bf16[64,1776]{1,0:T(8,128)(2,1)S(1)}, bf16[64,1776]{1,0:T(8,128)(2,1)S(1)}, u32[]{:S(2)}, u32[]{:S(2)}) collective-permute-start(bf16[64,1776]{1,0:T(8,128)(2,1)S(1)} %add_convert_fusion.4), channel_id=1, source_target_pairs={{0,224},{32,0},{64,32},{96,64},{128,96},{160,128},{192,160},{224,1... | collective-permute-start | bytes 681992 | tf_op jit(solution)/shard_map/ppermute | solution.py:19
  70.7 1.5 %collective-permute-done.18 = bf16[64,1776]{1,0:T(8,128)(2,1)S(1)} collective-permute-done((bf16[64,1776]{1,0:T(8,128)(2,1)S(1)}, bf16[64,1776]{1,0:T(8,128)(2,1)S(1)}, u32[]{:S(2)}, u32[]{:S(2)}) %collective-permute-start.18) | collective-permute-done | bytes 227360 | tf_op jit(solution)/shard_map/ppermute | solution.py:19
  72.3 2.6 %collective-permute-done.11 = bf16[128,1920]{1,0:T(8,128)(2,1)S(1)} collective-permute-done((bf16[128,1920]{1,0:T(8,128)(2,1)S(1)}, bf16[128,1920]{1,0:T(8,128)(2,1)S(1)}, u32[]{:S(2)}, u32[]{:S(2)}) %collective-permute-start.11) | collective-permute-done | bytes 491552 | tf_op jit(solution)/shard_map/ppermute | solution.py:19
  74.9 1.7 %collective-permute-done.9 = bf16[128,1920]{1,0:T(8,128)(2,1)S(1)} collective-permute-done((bf16[128,1920]{1,0:T(8,128)(2,1)S(1)}, bf16[128,1920]{1,0:T(8,128)(2,1)S(1)}, u32[]{:S(2)}, u32[]{:S(2)}) %collective-permute-start.9) | collective-permute-done | bytes 491552 | tf_op jit(solution)/shard_map/ppermute | solution.py:19
  76.8 1.9 %collective-permute-done.19 = bf16[64,1776]{1,0:T(8,128)(2,1)S(1)} collective-permute-done((bf16[64,1776]{1,0:T(8,128)(2,1)S(1)}, bf16[64,1776]{1,0:T(8,128)(2,1)S(1)}, u32[]{:S(2)}, u32[]{:S(2)}) %collective-permute-start.19) | collective-permute-done | bytes 227360 | tf_op jit(solution)/shard_map/ppermute | solution.py:19
  79.4 1.4 %collective-permute-start.25 = (bf16[16,1776]{1,0:T(8,128)(2,1)S(1)}, bf16[16,1776]{1,0:T(8,128)(2,1)S(1)}, u32[]{:S(2)}, u32[]{:S(2)}) collective-permute-start(bf16[16,1776]{1,0:T(8,128)(2,1)S(1)} %get-tuple-element.61), channel_id=1, source_target_pairs={{0,24},{8,0},{16,8},{24,16},{1,25},{9,1},{17,9},{25,17},{2,26},{10... | collective-permute-start | bytes 170504 | tf_op jit(solution)/shard_map/ppermute | solution.py:19
  82.3 3.8 %collective-permute-start.13 = (bf16[16,1920]{1,0:T(8,128)(2,1)S(1)}, bf16[16,1920]{1,0:T(8,128)(2,1)S(1)}, u32[]{:S(2)}, u32[]{:S(2)}) collective-permute-start(bf16[16,1920]{1,0:T(8,128)(2,1)S(1)} %get-tuple-element.57), channel_id=1, source_target_pairs={{0,128},{32,160},{64,192},{96,224},{128,0},{160,32},{192,64},{224,... | collective-permute-start | bytes 184328 | tf_op jit(solution)/shard_map/ppermute | solution.py:19
  86.2 2.2 %collective-permute-start.14 = (bf16[16,1920]{1,0:T(8,128)(2,1)S(1)}, bf16[16,1920]{1,0:T(8,128)(2,1)S(1)}, u32[]{:S(2)}, u32[]{:S(2)}) collective-permute-start(bf16[16,1920]{1,0:T(8,128)(2,1)S(1)} %get-tuple-element.59), channel_id=1, source_target_pairs={{0,64},{32,96},{64,128},{96,160},{128,192},{160,224},{192,0},{224,... | collective-permute-start | bytes 184328 | tf_op jit(solution)/shard_map/ppermute | solution.py:19
  88.4 1.4 %collective-permute-done.13 = bf16[16,1920]{1,0:T(8,128)(2,1)S(1)} collective-permute-done((bf16[16,1920]{1,0:T(8,128)(2,1)S(1)}, bf16[16,1920]{1,0:T(8,128)(2,1)S(1)}, u32[]{:S(2)}, u32[]{:S(2)}) %collective-permute-start.13) | collective-permute-done | bytes 61472 | tf_op jit(solution)/shard_map/ppermute | solution.py:19
  90.3 1.1 collective-permute-done.14
  92.9 1.5 %collective-permute-start.28 = (bf16[16,924]{1,0:T(8,128)(2,1)S(1)}, bf16[16,924]{1,0:T(8,128)(2,1)S(1)}, u32[]{:S(2)}, u32[]{:S(2)}) collective-permute-start(bf16[16,924]{1,0:T(8,128)(2,1)S(1)} %bitcast.62), channel_id=1, source_target_pairs={{0,24},{8,0},{16,8},{24,16},{1,25},{9,1},{17,9},{25,17},{2,26},{10... | collective-permute-start | bytes 88712 | tf_op jit(solution)/shard_map/ppermute | solution.py:19
  94.5 2.6 %collective-permute-start.27 = (bf16[16,924]{1,0:T(8,128)(2,1)S(1)}, bf16[16,924]{1,0:T(8,128)(2,1)S(1)}, u32[]{:S(2)}, u32[]{:S(2)}) collective-permute-start(bf16[16,924]{1,0:T(8,128)(2,1)S(1)} %bitcast.57), channel_id=1, source_target_pairs={{0,16},{8,24},{16,0},{24,8},{1,17},{9,25},{17,1},{25,9},{2,18},{10... | collective-permute-start | bytes 88712 | tf_op jit(solution)/shard_map/ppermute | solution.py:19
  97.1 1.3 collective-permute-done.26
  100.0 1.9 %collective-permute-start.31 = (bf16[4,16,924]{2,1,0:T(8,128)(2,1)S(1)}, bf16[4,16,924]{2,1,0:T(8,128)(2,1)}, u32[]{:S(2)}, u32[]{:S(2)}) collective-permute-start(bf16[4,16,924]{2,1,0:T(8,128)(2,1)S(1)} %get-tuple-element.64), channel_id=1, source_target_pairs={{0,6},{2,0},{4,2},{6,4},{1,7},{3,1},{5,3},{7,5},{8,14},{10,8},{12,... | collective-permute-start | bytes 354824 | tf_op jit(solution)/shard_map/ppermute | solution.py:19
  101.8 2.5 %collective-permute-done.30 = bf16[4,16,924]{2,1,0:T(8,128)(2,1)S(1)} collective-permute-done((bf16[4,16,924]{2,1,0:T(8,128)(2,1)S(1)}, bf16[4,16,924]{2,1,0:T(8,128)(2,1)S(1)}, u32[]{:S(2)}, u32[]{:S(2)}) %collective-permute-start.30) | collective-permute-done | bytes 118304 | tf_op jit(solution)/shard_map/ppermute | solution.py:19
  104.3 1.6 %collective-permute-done.29 = bf16[4,16,924]{2,1,0:T(8,128)(2,1)} collective-permute-done((bf16[4,16,924]{2,1,0:T(8,128)(2,1)S(1)}, bf16[4,16,924]{2,1,0:T(8,128)(2,1)}, u32[]{:S(2)}, u32[]{:S(2)}) %collective-permute-start.29) | collective-permute-done | bytes 118304 | tf_op jit(solution)/shard_map/ppermute | solution.py:19
  105.9 1.0 pad_maximum_fusion.1
  107.7 12.7 %collective-permute-start.32 = (bf16[4,16,924]{2,1,0:T(8,128)(2,1)S(1)}, bf16[4,16,924]{2,1,0:T(8,128)(2,1)S(1)}, u32[]{:S(2)}, u32[]{:S(2)}) collective-permute-start(bf16[4,16,924]{2,1,0:T(8,128)(2,1)S(1)} %get-tuple-element.50), channel_id=1, source_target_pairs={{1,32},{3,34},{5,36},{7,38},{9,40},{11,42},{13,44},{15,46},{17,48}... | collective-permute-start | bytes 354824 | tf_op jit(solution)/shard_map/ppermute | solution.py:155
  120.5 2.7 %collective-permute-start.34 = (bf16[4,16,924]{2,1,0:T(8,128)(2,1)}, bf16[4,16,924]{2,1,0:T(8,128)(2,1)S(1)}, u32[]{:S(2)}, u32[]{:S(2)}) collective-permute-start(bf16[4,16,924]{2,1,0:T(8,128)(2,1)} %get-tuple-element.52), channel_id=1, source_target_pairs={{0,128},{2,130},{4,132},{6,134},{8,136},{10,138},{12,140},{14,142}... | collective-permute-start | bytes 354824 | tf_op jit(solution)/shard_map/ppermute | solution.py:155
  124.1 2.6 %collective-permute-done.35 = bf16[4,16,924]{2,1,0:T(8,128)(2,1)S(1)} collective-permute-done((bf16[4,16,924]{2,1,0:T(8,128)(2,1)}, bf16[4,16,924]{2,1,0:T(8,128)(2,1)S(1)}, u32[]{:S(2)}, u32[]{:S(2)}) %collective-permute-start.35) | collective-permute-done | bytes 118304 | tf_op jit(solution)/shard_map/ppermute | solution.py:155
  126.8 3.8 %collective-permute-done.34 = bf16[4,16,924]{2,1,0:T(8,128)(2,1)S(1)} collective-permute-done((bf16[4,16,924]{2,1,0:T(8,128)(2,1)}, bf16[4,16,924]{2,1,0:T(8,128)(2,1)S(1)}, u32[]{:S(2)}, u32[]{:S(2)}) %collective-permute-start.34) | collective-permute-done | bytes 118304 | tf_op jit(solution)/shard_map/ppermute | solution.py:155
  130.6 3.1 %collective-permute-done.33 = bf16[4,16,924]{2,1,0:T(8,128)(2,1)S(1)} collective-permute-done((bf16[4,16,924]{2,1,0:T(8,128)(2,1)S(1)}, bf16[4,16,924]{2,1,0:T(8,128)(2,1)S(1)}, u32[]{:S(2)}, u32[]{:S(2)}) %collective-permute-start.33) | collective-permute-done | bytes 118304 | tf_op jit(solution)/shard_map/ppermute | solution.py:155
  134.6 1.2 collective-permute-done.36
  135.7 2.0 %add_convert_fusion = bf16[1024,924]{0,1:T(8,128)(2,1)} fusion(f32[1024,924]{0,1:T(8,128)S(1)} %fusion.40, bf16[256,924]{1,0:T(8,128)(2,1)S(1)} %bitcast.51, bf16[1024,512]{0,1:T(8,128)(2,1)S(1)} %copy-done.1), kind=kOutput, calls=%fused_computation | convolution fusion | flops 486334464 | bytes 6742016 | tf_op jit(solution)/shard_map/dot_general | solution.py:191
  (110 shorter events, 15.6 us)
Async XLA Ops:
  4.5 5.6 %collective-permute-start = (f32[256,1024]{1,0:T(8,128)S(1)}, f32[256,1024]{1,0:T(8,128)S(1)}, u32[]{:S(2)}, u32[]{:S(2)}) collective-permute-start(f32[256,1024]{1,0:T(8,128)S(1)} %fusion.36), channel_id=1, source_target_pairs={{0,1},{1,0},{2,3},{3,2},{4,5},{5,4},{6,7},{7,6},{8,9},{9,8},{10,11... | collective-permute-start | bytes 3145736 | tf_op jit(solution)/shard_map/ppermute | solution.py:19
  11.6 6.9 %collective-permute-start.1 = (bf16[64,1024]{1,0:T(8,128)(2,1)}, bf16[64,1024]{1,0:T(8,128)(2,1)S(1)}, u32[]{:S(2)}, u32[]{:S(2)}) collective-permute-start(bf16[64,1024]{1,0:T(8,128)(2,1)} %get-tuple-element.54), channel_id=1, source_target_pairs={{0,2},{2,4},{4,6},{6,0},{1,3},{3,5},{5,7},{7,1},{8,10},{10,12},{12... | collective-permute-start | bytes 393224 | tf_op jit(solution)/shard_map/ppermute | solution.py:19
  11.6 8.2 %collective-permute-start.3 = (bf16[64,1024]{1,0:T(8,128)(2,1)}, bf16[64,1024]{1,0:T(8,128)(2,1)S(1)}, u32[]{:S(2)}, u32[]{:S(2)}) collective-permute-start(bf16[64,1024]{1,0:T(8,128)(2,1)} %get-tuple-element.55), channel_id=1, source_target_pairs={{0,4},{2,6},{4,0},{6,2},{1,5},{3,7},{5,1},{7,3},{8,12},{10,14},{12... | collective-permute-start | bytes 393224 | tf_op jit(solution)/shard_map/ppermute | solution.py:19
  13.6 7.5 %collective-permute-start.2 = (bf16[64,1024]{1,0:T(8,128)(2,1)S(1)}, bf16[64,1024]{1,0:T(8,128)(2,1)}, u32[]{:S(2)}, u32[]{:S(2)}) collective-permute-start(bf16[64,1024]{1,0:T(8,128)(2,1)S(1)} %get-tuple-element.56), channel_id=1, source_target_pairs={{0,6},{2,0},{4,2},{6,4},{1,7},{3,1},{5,3},{7,5},{8,14},{10,8},{12,... | collective-permute-start | bytes 393224 | tf_op jit(solution)/shard_map/ppermute | solution.py:19
  22.0 8.5 %collective-permute-start.6 = (bf16[64,1024]{1,0:T(8,128)(2,1)S(1)}, bf16[64,1024]{1,0:T(8,128)(2,1)S(1)}, u32[]{:S(2)}, u32[]{:S(2)}) collective-permute-start(bf16[64,1024]{1,0:T(8,128)(2,1)S(1)} %fusion.84), channel_id=1, source_target_pairs={{0,6},{2,0},{4,2},{6,4},{1,7},{3,1},{5,3},{7,5},{8,14},{10,8},{12,... | collective-permute-start | bytes 393224 | tf_op jit(solution)/shard_map/ppermute | solution.py:19
  25.2 5.7 %collective-permute-start.5 = (bf16[64,1024]{1,0:T(8,128)(2,1)S(1)}, bf16[64,1024]{1,0:T(8,128)(2,1)S(1)}, u32[]{:S(2)}, u32[]{:S(2)}) collective-permute-start(bf16[64,1024]{1,0:T(8,128)(2,1)S(1)} %fusion.84), channel_id=1, source_target_pairs={{0,4},{2,6},{4,0},{6,2},{1,5},{3,7},{5,1},{7,3},{8,12},{10,14},{12... | collective-permute-start | bytes 393224 | tf_op jit(solution)/shard_map/ppermute | solution.py:19
  25.2 9.1 %collective-permute-start.4 = (bf16[64,1024]{1,0:T(8,128)(2,1)S(1)}, bf16[64,1024]{1,0:T(8,128)(2,1)S(1)}, u32[]{:S(2)}, u32[]{:S(2)}) collective-permute-start(bf16[64,1024]{1,0:T(8,128)(2,1)S(1)} %fusion.84), channel_id=1, source_target_pairs={{0,2},{2,4},{4,6},{6,0},{1,3},{3,5},{5,7},{7,1},{8,10},{10,12},{12... | collective-permute-start | bytes 393224 | tf_op jit(solution)/shard_map/ppermute | solution.py:19
  34.3 2.5 %collective-permute-start.7 = (bf16[256,1024]{1,0:T(8,128)(2,1)S(1)}, bf16[256,1024]{1,0:T(8,128)(2,1)S(1)}, u32[]{:S(2)}, u32[]{:S(2)}) collective-permute-start(bf16[256,1024]{1,0:T(8,128)(2,1)S(1)} %pad_maximum_fusion.mine_ref), channel_id=1, source_target_pairs={{0,1},{1,0},{2,3},{3,2},{4,5},{5,4},{6,7},{7,6},{8,9},{9,8},{10,11... | collective-permute-start | bytes 1572872 | tf_op jit(solution)/shard_map/ppermute | solution.py:19
  42.9 13.0 %collective-permute-start.16 = (bf16[64,1776]{1,0:T(8,128)(2,1)}, bf16[64,1776]{1,0:T(8,128)(2,1)}, u32[]{:S(2)}, u32[]{:S(2)}) collective-permute-start(bf16[64,1776]{1,0:T(8,128)(2,1)} %get-tuple-element.36), channel_id=1, source_target_pairs={{0,32},{32,64},{64,96},{96,128},{128,160},{160,192},{192,224},{224... | collective-permute-start | bytes 681992 | tf_op jit(solution)/shard_map/ppermute | solution.py:19
  43.0 12.9 %copy-start.10 = (f32[64,1776]{1,0:T(8,128)S(1)}, f32[64,1776]{1,0:T(8,128)}, u32[]{:S(2)}) copy-start(f32[64,1776]{1,0:T(8,128)} %get-tuple-element.35) | copy-start | bytes 1363972
  43.0 17.2 %copy-start.9 = (f32[64,1776]{1,0:T(8,128)S(1)}, f32[64,1776]{1,0:T(8,128)}, u32[]{:S(2)}) copy-start(f32[64,1776]{1,0:T(8,128)} %get-tuple-element.38) | copy-start | bytes 1363972
  49.3 14.5 %copy-start.4 = (f32[64,1920]{1,0:T(8,128)S(1)}, f32[64,1920]{1,0:T(8,128)}, u32[]{:S(2)}) copy-start(f32[64,1920]{1,0:T(8,128)} %get-tuple-element.30) | copy-start | bytes 1474564
  49.3 14.6 %copy-start.13 = (bf16[64,1920]{1,0:T(8,128)(2,1)S(1)}, bf16[64,1920]{1,0:T(8,128)(2,1)}, u32[]{:S(2)}) copy-start(bf16[64,1920]{1,0:T(8,128)(2,1)} %get-tuple-element.29) | copy-start | bytes 737284
  49.3 15.6 %copy-start.3 = (f32[64,1920]{1,0:T(8,128)S(1)}, f32[64,1920]{1,0:T(8,128)}, u32[]{:S(2)}) copy-start(f32[64,1920]{1,0:T(8,128)} %get-tuple-element.26) | copy-start | bytes 1474564
  49.3 15.6 %collective-permute-start.8 = (bf16[64,1920]{1,0:T(8,128)(2,1)S(1)}, bf16[64,1920]{1,0:T(8,128)(2,1)S(1)}, u32[]{:S(2)}, u32[]{:S(2)}) collective-permute-start(bf16[64,1920]{1,0:T(8,128)(2,1)S(1)} %get-tuple-element.27), channel_id=1, source_target_pairs={{0,8},{8,16},{16,24},{24,0},{1,9},{9,17},{17,25},{25,1},{2,10},{10... | collective-permute-start | bytes 737288 | tf_op jit(solution)/shard_map/ppermute | solution.py:19
  50.2 13.6 %collective-permute-start.10 = (bf16[64,1920]{1,0:T(8,128)(2,1)S(1)}, bf16[64,1920]{1,0:T(8,128)(2,1)S(1)}, u32[]{:S(2)}, u32[]{:S(2)}) collective-permute-start(bf16[64,1920]{1,0:T(8,128)(2,1)S(1)} %get-tuple-element.31), channel_id=1, source_target_pairs={{0,24},{8,0},{16,8},{24,16},{1,25},{9,1},{17,9},{25,17},{2,26},{10... | collective-permute-start | bytes 737288 | tf_op jit(solution)/shard_map/ppermute | solution.py:19
  52.1 8.2 %collective-permute-start.20 = (bf16[64,1776]{1,0:T(8,128)(2,1)S(1)}, bf16[64,1776]{1,0:T(8,128)(2,1)S(1)}, u32[]{:S(2)}, u32[]{:S(2)}) collective-permute-start(bf16[64,1776]{1,0:T(8,128)(2,1)S(1)} %get-tuple-element.39), channel_id=1, source_target_pairs={{0,224},{32,0},{64,32},{96,64},{128,96},{160,128},{192,160},{224,1... | collective-permute-start | bytes 681992 | tf_op jit(solution)/shard_map/ppermute | solution.py:19
  56.9 8.7 %collective-permute-start.17 = (bf16[64,1776]{1,0:T(8,128)(2,1)S(1)}, bf16[64,1776]{1,0:T(8,128)(2,1)S(1)}, u32[]{:S(2)}, u32[]{:S(2)}) collective-permute-start(bf16[64,1776]{1,0:T(8,128)(2,1)S(1)} %add_convert_fusion.8), channel_id=1, source_target_pairs={{0,32},{32,64},{64,96},{96,128},{128,160},{160,192},{192,224},{224... | collective-permute-start | bytes 681992 | tf_op jit(solution)/shard_map/ppermute | solution.py:19
  60.3 6.9 %collective-permute-start.21 = (bf16[64,1776]{1,0:T(8,128)(2,1)S(1)}, bf16[64,1776]{1,0:T(8,128)(2,1)S(1)}, u32[]{:S(2)}, u32[]{:S(2)}) collective-permute-start(bf16[64,1776]{1,0:T(8,128)(2,1)S(1)} %add_convert_fusion.5), channel_id=1, source_target_pairs={{0,224},{32,0},{64,32},{96,64},{128,96},{160,128},{192,160},{224,1... | collective-permute-start | bytes 681992 | tf_op jit(solution)/shard_map/ppermute | solution.py:19
  63.9 11.0 %collective-permute-start.11 = (bf16[128,1920]{1,0:T(8,128)(2,1)S(1)}, bf16[128,1920]{1,0:T(8,128)(2,1)S(1)}, u32[]{:S(2)}, u32[]{:S(2)}) collective-permute-start(bf16[128,1920]{1,0:T(8,128)(2,1)S(1)} %pad_maximum_fusion.4), channel_id=1, source_target_pairs={{0,24},{8,0},{16,8},{24,16},{1,25},{9,1},{17,9},{25,17},{2,26},{10... | collective-permute-start | bytes 1474568 | tf_op jit(solution)/shard_map/ppermute | solution.py:19
  64.9 11.7 %copy-start.2 = (f32[64,1920]{1,0:T(8,128)S(1)}, f32[64,1920]{1,0:T(8,128)}, u32[]{:S(2)}) copy-start(f32[64,1920]{1,0:T(8,128)} %get-tuple-element.25) | copy-start | bytes 1474564
  65.0 13.7 %copy-start.11 = (f32[64,1776]{1,0:T(8,128)S(1)}, f32[64,1776]{1,0:T(8,128)}, u32[]{:S(2)}) copy-start(f32[64,1776]{1,0:T(8,128)} %get-tuple-element.32) | copy-start | bytes 1363972
  65.0 11.6 %collective-permute-start.9 = (bf16[128,1920]{1,0:T(8,128)(2,1)S(1)}, bf16[128,1920]{1,0:T(8,128)(2,1)S(1)}, u32[]{:S(2)}, u32[]{:S(2)}) collective-permute-start(bf16[128,1920]{1,0:T(8,128)(2,1)S(1)} %pad_maximum_fusion.3), channel_id=1, source_target_pairs={{0,8},{8,16},{16,24},{24,0},{1,9},{9,17},{17,25},{25,1},{2,10},{10... | collective-permute-start | bytes 1474568 | tf_op jit(solution)/shard_map/ppermute | solution.py:19
  65.7 6.5 %collective-permute-start.18 = (bf16[64,1776]{1,0:T(8,128)(2,1)S(1)}, bf16[64,1776]{1,0:T(8,128)(2,1)S(1)}, u32[]{:S(2)}, u32[]{:S(2)}) collective-permute-start(bf16[64,1776]{1,0:T(8,128)(2,1)S(1)} %add_convert_fusion.7), channel_id=1, source_target_pairs={{0,32},{32,64},{64,96},{96,128},{128,160},{160,192},{192,224},{224... | collective-permute-start | bytes 681992 | tf_op jit(solution)/shard_map/ppermute | solution.py:19
  67.2 14.9 %copy-start.5 = (f32[64,1920]{1,0:T(8,128)S(1)}, f32[64,1920]{1,0:T(8,128)}, u32[]{:S(2)}) copy-start(f32[64,1920]{1,0:T(8,128)} %get-tuple-element.24) | copy-start | bytes 1474564
  67.2 9.6 %collective-permute-start.22 = (bf16[64,1776]{1,0:T(8,128)(2,1)S(1)}, bf16[64,1776]{1,0:T(8,128)(2,1)S(1)}, u32[]{:S(2)}, u32[]{:S(2)}) collective-permute-start(bf16[64,1776]{1,0:T(8,128)(2,1)S(1)} %add_convert_fusion.4), channel_id=1, source_target_pairs={{0,224},{32,0},{64,32},{96,64},{128,96},{160,128},{192,160},{224,1... | collective-permute-start | bytes 681992 | tf_op jit(solution)/shard_map/ppermute | solution.py:19
  72.2 6.5 %collective-permute-start.19 = (bf16[64,1776]{1,0:T(8,128)(2,1)S(1)}, bf16[64,1776]{1,0:T(8,128)(2,1)S(1)}, u32[]{:S(2)}, u32[]{:S(2)}) collective-permute-start(bf16[64,1776]{1,0:T(8,128)(2,1)S(1)} %add_convert_fusion.6), channel_id=1, source_target_pairs={{0,32},{32,64},{64,96},{96,128},{128,160},{160,192},{192,224},{224... | collective-permute-start | bytes 681992 | tf_op jit(solution)/shard_map/ppermute | solution.py:19
  76.7 5.4 %collective-permute-start.12 = (bf16[64,1920]{1,0:T(8,128)(2,1)S(1)}, bf16[64,1920]{1,0:T(8,128)(2,1)S(1)}, u32[]{:S(2)}, u32[]{:S(2)}) collective-permute-start(bf16[64,1920]{1,0:T(8,128)(2,1)S(1)} %add_convert_fusion.1), channel_id=1, source_target_pairs={{0,32},{32,0},{64,96},{96,64},{128,160},{160,128},{192,224},{224,1... | collective-permute-start | bytes 737288 | tf_op jit(solution)/shard_map/ppermute | solution.py:119
  78.8 12.6 %copy-start.14 = (f32[16,3696]{1,0:T(8,128)S(1)}, f32[16,3696]{1,0:T(8,128)}, u32[]{:S(2)}) copy-start(f32[16,3696]{1,0:T(8,128)} %param.8) | copy-start | bytes 709636
  78.8 12.6 %copy-start.15 = (f32[16,3696]{1,0:T(8,128)S(1)}, f32[16,3696]{1,0:T(8,128)}, u32[]{:S(2)}) copy-start(f32[16,3696]{1,0:T(8,128)} %param.9) | copy-start | bytes 709636
  78.8 7.4 %collective-permute-start.23 = (bf16[16,1776]{1,0:T(8,128)(2,1)S(1)}, bf16[16,1776]{1,0:T(8,128)(2,1)S(1)}, u32[]{:S(2)}, u32[]{:S(2)}) collective-permute-start(bf16[16,1776]{1,0:T(8,128)(2,1)S(1)} %get-tuple-element.60), channel_id=1, source_target_pairs={{0,16},{8,24},{16,0},{24,8},{1,17},{9,25},{17,1},{25,9},{2,18},{10... | collective-permute-start | bytes 170504 | tf_op jit(solution)/shard_map/ppermute | solution.py:19
  79.4 9.0 %collective-permute-start.25 = (bf16[16,1776]{1,0:T(8,128)(2,1)S(1)}, bf16[16,1776]{1,0:T(8,128)(2,1)S(1)}, u32[]{:S(2)}, u32[]{:S(2)}) collective-permute-start(bf16[16,1776]{1,0:T(8,128)(2,1)S(1)} %get-tuple-element.61), channel_id=1, source_target_pairs={{0,24},{8,0},{16,8},{24,16},{1,25},{9,1},{17,9},{25,17},{2,26},{10... | collective-permute-start | bytes 170504 | tf_op jit(solution)/shard_map/ppermute | solution.py:19
  80.8 7.6 %collective-permute-start.24 = (bf16[16,1776]{1,0:T(8,128)(2,1)S(1)}, bf16[16,1776]{1,0:T(8,128)(2,1)S(1)}, u32[]{:S(2)}, u32[]{:S(2)}) collective-permute-start(bf16[16,1776]{1,0:T(8,128)(2,1)S(1)} %get-tuple-element.62), channel_id=1, source_target_pairs={{0,8},{8,16},{16,24},{24,0},{1,9},{9,17},{17,25},{25,1},{2,10},{10... | collective-permute-start | bytes 170504 | tf_op jit(solution)/shard_map/ppermute | solution.py:19
  82.3 7.6 %collective-permute-start.13 = (bf16[16,1920]{1,0:T(8,128)(2,1)S(1)}, bf16[16,1920]{1,0:T(8,128)(2,1)S(1)}, u32[]{:S(2)}, u32[]{:S(2)}) collective-permute-start(bf16[16,1920]{1,0:T(8,128)(2,1)S(1)} %get-tuple-element.57), channel_id=1, source_target_pairs={{0,128},{32,160},{64,192},{96,224},{128,0},{160,32},{192,64},{224,... | collective-permute-start | bytes 184328 | tf_op jit(solution)/shard_map/ppermute | solution.py:19
  86.0 4.3 %collective-permute-start.15 = (bf16[16,1920]{1,0:T(8,128)(2,1)S(1)}, bf16[16,1920]{1,0:T(8,128)(2,1)S(1)}, u32[]{:S(2)}, u32[]{:S(2)}) collective-permute-start(bf16[16,1920]{1,0:T(8,128)(2,1)S(1)} %get-tuple-element.58), channel_id=1, source_target_pairs={{0,192},{32,224},{64,0},{96,32},{128,64},{160,96},{192,128},{224,1... | collective-permute-start | bytes 184328 | tf_op jit(solution)/shard_map/ppermute | solution.py:19
  86.2 5.2 %collective-permute-start.14 = (bf16[16,1920]{1,0:T(8,128)(2,1)S(1)}, bf16[16,1920]{1,0:T(8,128)(2,1)S(1)}, u32[]{:S(2)}, u32[]{:S(2)}) collective-permute-start(bf16[16,1920]{1,0:T(8,128)(2,1)S(1)} %get-tuple-element.59), channel_id=1, source_target_pairs={{0,64},{32,96},{64,128},{96,160},{128,192},{160,224},{192,0},{224,... | collective-permute-start | bytes 184328 | tf_op jit(solution)/shard_map/ppermute | solution.py:19
  92.9 4.2 %collective-permute-start.28 = (bf16[16,924]{1,0:T(8,128)(2,1)S(1)}, bf16[16,924]{1,0:T(8,128)(2,1)S(1)}, u32[]{:S(2)}, u32[]{:S(2)}) collective-permute-start(bf16[16,924]{1,0:T(8,128)(2,1)S(1)} %bitcast.62), channel_id=1, source_target_pairs={{0,24},{8,0},{16,8},{24,16},{1,25},{9,1},{17,9},{25,17},{2,26},{10... | collective-permute-start | bytes 88712 | tf_op jit(solution)/shard_map/ppermute | solution.py:19
  94.4 4.0 %collective-permute-start.26 = (bf16[16,924]{1,0:T(8,128)(2,1)S(1)}, bf16[16,924]{1,0:T(8,128)(2,1)S(1)}, u32[]{:S(2)}, u32[]{:S(2)}) collective-permute-start(bf16[16,924]{1,0:T(8,128)(2,1)S(1)} %bitcast.60), channel_id=1, source_target_pairs={{0,8},{8,16},{16,24},{24,0},{1,9},{9,17},{17,25},{25,1},{2,10},{10... | collective-permute-start | bytes 88712 | tf_op jit(solution)/shard_map/ppermute | solution.py:19
  94.5 4.3 %collective-permute-start.27 = (bf16[16,924]{1,0:T(8,128)(2,1)S(1)}, bf16[16,924]{1,0:T(8,128)(2,1)S(1)}, u32[]{:S(2)}, u32[]{:S(2)}) collective-permute-start(bf16[16,924]{1,0:T(8,128)(2,1)S(1)} %bitcast.57), channel_id=1, source_target_pairs={{0,16},{8,24},{16,0},{24,8},{1,17},{9,25},{17,1},{25,9},{2,18},{10... | collective-permute-start | bytes 88712 | tf_op jit(solution)/shard_map/ppermute | solution.py:19
  98.8 35.1 %copy-start.1 = (bf16[1024,512]{0,1:T(8,128)(2,1)S(1)}, bf16[1024,512]{0,1:T(8,128)(2,1)}, u32[]{:S(2)}) copy-start(bf16[1024,512]{0,1:T(8,128)(2,1)} %fusion) | copy-start | bytes 3145732
  98.8 5.5 %collective-permute-start.30 = (bf16[4,16,924]{2,1,0:T(8,128)(2,1)S(1)}, bf16[4,16,924]{2,1,0:T(8,128)(2,1)S(1)}, u32[]{:S(2)}, u32[]{:S(2)}) collective-permute-start(bf16[4,16,924]{2,1,0:T(8,128)(2,1)S(1)} %get-tuple-element.64), channel_id=1, source_target_pairs={{0,4},{2,6},{4,0},{6,2},{1,5},{3,7},{5,1},{7,3},{8,12},{10,14},{12... | collective-permute-start | bytes 354824 | tf_op jit(solution)/shard_map/ppermute | solution.py:19
  99.2 6.7 %collective-permute-start.29 = (bf16[4,16,924]{2,1,0:T(8,128)(2,1)S(1)}, bf16[4,16,924]{2,1,0:T(8,128)(2,1)}, u32[]{:S(2)}, u32[]{:S(2)}) collective-permute-start(bf16[4,16,924]{2,1,0:T(8,128)(2,1)S(1)} %get-tuple-element.64), channel_id=1, source_target_pairs={{0,2},{2,4},{4,6},{6,0},{1,3},{3,5},{5,7},{7,1},{8,10},{10,12},{12... | collective-permute-start | bytes 354824 | tf_op jit(solution)/shard_map/ppermute | solution.py:19
  100.0 5.9 %collective-permute-start.31 = (bf16[4,16,924]{2,1,0:T(8,128)(2,1)S(1)}, bf16[4,16,924]{2,1,0:T(8,128)(2,1)}, u32[]{:S(2)}, u32[]{:S(2)}) collective-permute-start(bf16[4,16,924]{2,1,0:T(8,128)(2,1)S(1)} %get-tuple-element.64), channel_id=1, source_target_pairs={{0,6},{2,0},{4,2},{6,4},{1,7},{3,1},{5,3},{7,5},{8,14},{10,8},{12,... | collective-permute-start | bytes 354824 | tf_op jit(solution)/shard_map/ppermute | solution.py:19
  107.7 16.4 %collective-permute-start.32 = (bf16[4,16,924]{2,1,0:T(8,128)(2,1)S(1)}, bf16[4,16,924]{2,1,0:T(8,128)(2,1)S(1)}, u32[]{:S(2)}, u32[]{:S(2)}) collective-permute-start(bf16[4,16,924]{2,1,0:T(8,128)(2,1)S(1)} %get-tuple-element.50), channel_id=1, source_target_pairs={{1,32},{3,34},{5,36},{7,38},{9,40},{11,42},{13,44},{15,46},{17,48}... | collective-permute-start | bytes 354824 | tf_op jit(solution)/shard_map/ppermute | solution.py:155
  120.4 6.4 %collective-permute-start.35 = (bf16[4,16,924]{2,1,0:T(8,128)(2,1)}, bf16[4,16,924]{2,1,0:T(8,128)(2,1)S(1)}, u32[]{:S(2)}, u32[]{:S(2)}) collective-permute-start(bf16[4,16,924]{2,1,0:T(8,128)(2,1)} %get-tuple-element.51), channel_id=1, source_target_pairs={{0,192},{2,194},{4,196},{6,198},{8,200},{10,202},{12,204},{14,206}... | collective-permute-start | bytes 354824 | tf_op jit(solution)/shard_map/ppermute | solution.py:155
  120.5 10.1 %collective-permute-start.34 = (bf16[4,16,924]{2,1,0:T(8,128)(2,1)}, bf16[4,16,924]{2,1,0:T(8,128)(2,1)S(1)}, u32[]{:S(2)}, u32[]{:S(2)}) collective-permute-start(bf16[4,16,924]{2,1,0:T(8,128)(2,1)} %get-tuple-element.52), channel_id=1, source_target_pairs={{0,128},{2,130},{4,132},{6,134},{8,136},{10,138},{12,140},{14,142}... | collective-permute-start | bytes 354824 | tf_op jit(solution)/shard_map/ppermute | solution.py:155
  123.2 10.4 %collective-permute-start.33 = (bf16[4,16,924]{2,1,0:T(8,128)(2,1)S(1)}, bf16[4,16,924]{2,1,0:T(8,128)(2,1)S(1)}, u32[]{:S(2)}, u32[]{:S(2)}) collective-permute-start(bf16[4,16,924]{2,1,0:T(8,128)(2,1)S(1)} %get-tuple-element.53), channel_id=1, source_target_pairs={{0,64},{2,66},{4,68},{6,70},{8,72},{10,74},{12,76},{14,78},{16,80}... | collective-permute-start | bytes 354824 | tf_op jit(solution)/shard_map/ppermute | solution.py:155
  133.7 2.0 %collective-permute-start.36 = (bf16[4,4,16,924]{3,2,1,0:T(8,128)(2,1)S(1)}, bf16[4,4,16,924]{3,2,1,0:T(8,128)(2,1)S(1)}, u32[]{:S(2)}, u32[]{:S(2)}) collective-permute-start(bf16[4,4,16,924]{3,2,1,0:T(8,128)(2,1)S(1)} %pad_maximum_fusion.2), channel_id=1, source_target_pairs={{0,1},{1,0},{2,3},{3,2},{4,5},{5,4},{6,7},{7,6},{8,9},{9,8},{10,11... | collective-permute-start | bytes 1419272 | tf_op jit(solution)/shard_map/ppermute | solution.py:19
  (7 other events, 34.3 us)

commit v9 on v8

--- a/solution.py
+++ b/solution.py
@@ -83,7 +83,7 @@
     return (r == chunk * part + n % part).astype(bf16)
 
 
-def project(tokens, basis, beside):
+def project(tokens, basis):
     rank = basis.shape[1]
     half, part = rank // C, rank // (X * C)
     lanes = (((1,), (1,)), ((), ()))
@@ -96,8 +96,8 @@
         total = total + got.astype(f32)
     mine = total.astype(bf16)
     got = {d: moved(mine, "x", d) for d in (1, 3, 2)}
-    mine, beside = lax.optimization_barrier((jnp.concatenate([mine, got[1], got[2], got[3]], 0), beside))
-    return mine, moved(mine, "c", 1), beside
+    mine = jnp.concatenate([mine, got[1], got[2], got[3]], 0)
+    return mine, moved(mine, "c", 1)
 
 
 def scatter(ring, relay):
@@ -131,7 +131,7 @@
     return jnp.concatenate([first, second], 1)
 
 
-def spread(normed, beside):
+def spread(normed, basis):
     z, y, x, c = (lax.axis_index(axis) for axis in ("z", "y", "x", "c"))
     rows, ff = normed.shape
     cut = normed.reshape(rows, Y, ff // Y).transpose(1, 0, 2)
@@ -139,7 +139,8 @@
     got = {d: moved(piece(d), "y", d) for d in (1, 3, 2)}
     tall = jnp.stack([piece(0), got[1], got[2], got[3]])
     got = {d: moved(tall, "x", d) for d in (1, 3, 2)}
-    wide = jnp.stack([tall, got[1], got[2], got[3]])
+    wide, basis = lax.optimization_barrier((jnp.stack([tall, got[1], got[2], got[3]]), basis))
+    ordered = jnp.dot(basis, spread_order(basis.shape[1]), preferred_element_type=f32).astype(bf16)
     odd = (z + c) % 2
     half = []
     for k in range(Z // 2):
@@ -154,8 +155,8 @@
                         pairs.append(((pz * Y * X + r) * C + pc, (((pz + 2 * k + po) % Z) * Y * X + r) * C + (pc ^ po)))
         moved_in = lax.ppermute(sent, ("z", "y", "x", "c"), pairs)
         half.append(moved_in if k else jnp.where(odd == 0, sent, moved_in))
-    half, beside = lax.optimization_barrier((jnp.stack(half), beside))
-    return beside, half, moved(half, "c", 1)
+    half, ordered = lax.optimization_barrier((jnp.stack(half), ordered))
+    return ordered, half, moved(half, "c", 1)
 
 
 def spread_order(rank):
@@ -172,8 +173,7 @@
 def shards(tokens, basis, cotangent, exp_avg, exp_avg_sq):
     rank, ff = basis.shape[1], cotangent.shape[1]
     here = jnp.stack([lax.axis_index(axis) for axis in ("z", "y", "x", "c")]).astype(jnp.int32)
-    ordered = jnp.dot(basis, spread_order(rank), preferred_element_type=f32).astype(bf16)
-    mine, other, ordered = project(tokens, basis, ordered)
+    mine, other = project(tokens, basis)
     lanes = 128
     tile = pl.cdiv(pl.cdiv(ff, lanes), 6) * lanes
     tiles = pl.cdiv(ff, tile)
@@ -185,7 +185,7 @@
     first = 0.9 * exp_avg + 0.1 * grad_low
     second = 0.999 * exp_avg_sq + 0.001 * grad_low * grad_low
     normed = (first / bias_first / (jnp.sqrt(second / bias_second) + 1e-08)).astype(bf16)
-    ordered, *parts = spread(normed, ordered)
+    ordered, *parts = spread(normed, basis)
     mine, other = (part.reshape(rank // 2, ff // Y) for part in parts)
     update = jnp.dot(ordered[:, : rank // 2], mine, preferred_element_type=f32)
     update = (update + jnp.dot(ordered[:, rank // 2 :], other, preferred_element_type=f32)).astype(bf16)

time: 138 us -> 136 us (0.986)
  starting transfers between devices: 59.1 us -> 62.9 us
  other arithmetic: 5.98 us -> 2.96 us
  matrix products: 10.2 us -> 8.02 us
  local copies, waits for them, and re-layouts: 2.16 us -> 0.74 us
    ppermute x32, waiting for transfers between devices: 36.3 us -> 39.7 us  [moved(): return lax.ppermute(value, axis, [(i, (i + by) % n) for i in range(n)])]
    ppermute x4, waiting for transfers between devices: 9.52 us -> 6.86 us  [spread(): moved_in = lax.ppermute(sent, ('z', 'y', 'x', 'c'), pairs)]
    dot_general x1, matrix products: 3.01 us -> 0.81 us  [spread(): jnp.dot(basis, spread_order(basis.shape[1]), preferred_element_type=f32)]
    ppermute x32, starting transfers between devices: 42.6 us -> 44.8 us  [moved(): return lax.ppermute(value, axis, [(i, (i + by) % n) for i in range(n)])]
    ppermute x4, starting transfers between devices: 16.4 us -> 18 us  [spread(): moved_in = lax.ppermute(sent, ('z', 'y', 'x', 'c'), pairs)]
  transfers between devices with their start and end apart: 37 -> 37, of which waited for: 26 -> 24; matrix products, arithmetic and copies ran while one was open for 5% -> 2% of each run, Pallas kernels for 5% -> 5%
where the time goes in v9:
time: 136 us; the launch traced here: 135 us
  starting transfers between devices  62.9 us (46%)
  waiting for transfers between devices  47.4 us (35%)
  Pallas kernels  12.3 us (9%)
  matrix products  8.02 us (6%)
  other arithmetic  2.96 us (2%)
    ppermute x32, starting transfers between devices, moved(): return lax.ppermute(value, axis, [(i, (i + by) % n) for i in range(n)])  44.8 us
    ppermute x32, waiting for transfers between devices, moved(): return lax.ppermute(value, axis, [(i, (i + by) % n) for i in range(n)])  39.7 us
    ppermute x4, starting transfers between devices, spread(): moved_in = lax.ppermute(sent, ('z', 'y', 'x', 'c'), pairs)  18 us
    pallas_call x2, Pallas kernels, gradient(): pl.pallas_call(functools.partial(grad_kernel, units), grid=(stop - start,...  12.3 us
    ppermute x4, waiting for transfers between devices, spread(): moved_in = lax.ppermute(sent, ('z', 'y', 'x', 'c'), pairs)  6.86 us
    dot_general x1, matrix products, project(): lax.dot_general(near_order(rank), basis, lanes, preferred_element_type=f32)  3.03 us
  transfers between devices with their start and end apart: 37, of which 24 were waited for; matrix products, arithmetic and copies ran while one was open for 2% of the time, Pallas kernels for 5%

profile of v9, /device:TPU:1, one launch (start us, length us, event | category | flops | bytes accessed | tf_op | source)
XLA Modules:
  0.0 135.5 jit_solution(10910430604204643904)
XLA Ops:
  0.7 3.0 %convolution_convert_fusion.1 = bf16[512,1024]{1,0:T(8,128)(2,1)S(1)} fusion(bf16[1024,512]{1,0:T(8,128)(2,1)} %param.6, s32[512]{0:T(512)S(1)} %get-tuple-element.77, s32[512]{0:T(512)S(1)} %get-tuple-element.78, s32[512]{0:T(512)S(1)} %get-tuple-element.76, s32[512]{0:T(512)S(1)} %get-tuple-element.79, s32[]{:T(128)} %axis_index.35, ...), kind=kOutput, calls=%fused_computation.32 | convolution fusion | flops 548667392 | bytes 2110984 | tf_op jit(solution)/shard_map/dot_general | solution.py:90
  4.5 3.3 %collective-permute-start = (f32[256,1024]{1,0:T(8,128)S(1)}, f32[256,1024]{1,0:T(8,128)S(1)}, u32[]{:S(2)}, u32[]{:S(2)}) collective-permute-start(f32[256,1024]{1,0:T(8,128)S(1)} %fusion.49), channel_id=1, source_target_pairs={{0,1},{1,0},{2,3},{3,2},{4,5},{5,4},{6,7},{7,6},{8,9},{9,8},{10,11... | collective-permute-start | bytes 3145736 | tf_op jit(solution)/shard_map/ppermute | solution.py:19
  7.8 2.3 %collective-permute-done = f32[256,1024]{1,0:T(8,128)S(1)} collective-permute-done((f32[256,1024]{1,0:T(8,128)S(1)}, f32[256,1024]{1,0:T(8,128)S(1)}, u32[]{:S(2)}, u32[]{:S(2)}) %collective-permute-start) | collective-permute-done | bytes 1048608 | tf_op jit(solution)/shard_map/ppermute | solution.py:19
  11.0 1.9 %collective-permute-start.3 = (bf16[64,1024]{1,0:T(8,128)(2,1)S(1)}, bf16[64,1024]{1,0:T(8,128)(2,1)S(1)}, u32[]{:S(2)}, u32[]{:S(2)}) collective-permute-start(bf16[64,1024]{1,0:T(8,128)(2,1)S(1)} %get-tuple-element.55), channel_id=1, source_target_pairs={{0,4},{2,6},{4,0},{6,2},{1,5},{3,7},{5,1},{7,3},{8,12},{10,14},{12... | collective-permute-start | bytes 393224 | tf_op jit(solution)/shard_map/ppermute | solution.py:19
  12.9 1.2 collective-permute-start.2
  14.1 3.6 %collective-permute-done.1 = bf16[64,1024]{1,0:T(8,128)(2,1)S(1)} collective-permute-done((bf16[64,1024]{1,0:T(8,128)(2,1)S(1)}, bf16[64,1024]{1,0:T(8,128)(2,1)S(1)}, u32[]{:S(2)}, u32[]{:S(2)}) %collective-permute-start.1) | collective-permute-done | bytes 131104 | tf_op jit(solution)/shard_map/ppermute | solution.py:19
  17.7 1.4 %collective-permute-done.3 = bf16[64,1024]{1,0:T(8,128)(2,1)S(1)} collective-permute-done((bf16[64,1024]{1,0:T(8,128)(2,1)S(1)}, bf16[64,1024]{1,0:T(8,128)(2,1)S(1)}, u32[]{:S(2)}, u32[]{:S(2)}) %collective-permute-start.3) | collective-permute-done | bytes 131104 | tf_op jit(solution)/shard_map/ppermute | solution.py:19
  19.0 1.0 collective-permute-done.2
  20.1 3.5 %collective-permute-start.6 = (bf16[64,1024]{1,0:T(8,128)(2,1)S(1)}, bf16[64,1024]{1,0:T(8,128)(2,1)S(1)}, u32[]{:S(2)}, u32[]{:S(2)}) collective-permute-start(bf16[64,1024]{1,0:T(8,128)(2,1)S(1)} %fusion.97), channel_id=1, source_target_pairs={{0,6},{2,0},{4,2},{6,4},{1,7},{3,1},{5,3},{7,5},{8,14},{10,8},{12,... | collective-permute-start | bytes 393224 | tf_op jit(solution)/shard_map/ppermute | solution.py:19
  24.2 4.7 %collective-permute-done.6 = bf16[64,1024]{1,0:T(8,128)(2,1)S(1)} collective-permute-done((bf16[64,1024]{1,0:T(8,128)(2,1)S(1)}, bf16[64,1024]{1,0:T(8,128)(2,1)S(1)}, u32[]{:S(2)}, u32[]{:S(2)}) %collective-permute-start.6) | collective-permute-done | bytes 131104 | tf_op jit(solution)/shard_map/ppermute | solution.py:19
  29.4 3.3 %collective-permute-done.4 = bf16[64,1024]{1,0:T(8,128)(2,1)S(1)} collective-permute-done((bf16[64,1024]{1,0:T(8,128)(2,1)S(1)}, bf16[64,1024]{1,0:T(8,128)(2,1)S(1)}, u32[]{:S(2)}, u32[]{:S(2)}) %collective-permute-start.4) | collective-permute-done | bytes 131104 | tf_op jit(solution)/shard_map/ppermute | solution.py:19
  32.7 0.9 collective-permute-start.7
  33.7 1.5 %collective-permute-done.7.other_ref = bf16[256,1024]{1,0:T(8,128)(2,1)S(1)} collective-permute-done((bf16[256,1024]{1,0:T(8,128)(2,1)S(1)}, bf16[256,1024]{1,0:T(8,128)(2,1)S(1)}, u32[]{:S(2)}, u32[]{:S(2)}) %collective-permute-start.7) | collective-permute-done | bytes 524320 | tf_op jit(solution)/shard_map/ppermute | solution.py:19
  35.2 6.1 %shard_map.77 = (bf16[64,1776]{1,0:T(8,128)(2,1)}, bf16[64,1776]{1,0:T(8,128)(2,1)S(1)}, f32[64,1776]{1,0:T(8,128)}, f32[64,1776]{1,0:T(8,128)}, f32[64,1776]{1,...) custom-call(s32[4]{0:T(128)S(1)} %pad_add_fusion.here, ...), custom_call_target="tpu_custom_call" | custom-call | flops 1862270976 | bytes 6819840 | tf_op jit(solution)/shard_map/pallas_call | solution.py:58
  41.4 6.2 %shard_map.76 = (bf16[64,1920]{1,0:T(8,128)(2,1)S(1)}, bf16[64,1920]{1,0:T(8,128)(2,1)S(1)}, f32[64,1920]{1,0:T(8,128)}, bf16[64,1920]{1,0:T(8,128)(2,1)}, bf16[...) custom-call(s32[4]{0:T(128)S(1)} %pad_add_fusion.here, ...), custom_call_target="tpu_custom_call" | custom-call | flops 2013265920 | bytes 7372800 | tf_op jit(solution)/shard_map/pallas_call | solution.py:58
  48.4 2.0 %collective-permute-start.10 = (bf16[64,1920]{1,0:T(8,128)(2,1)S(1)}, bf16[64,1920]{1,0:T(8,128)(2,1)S(1)}, u32[]{:S(2)}, u32[]{:S(2)}) collective-permute-start(bf16[64,1920]{1,0:T(8,128)(2,1)S(1)} %get-tuple-element.30), channel_id=1, source_target_pairs={{0,24},{8,0},{16,8},{24,16},{1,25},{9,1},{17,9},{25,17},{2,26},{10... | collective-permute-start | bytes 737288 | tf_op jit(solution)/shard_map/ppermute | solution.py:19
  50.3 3.6 %collective-permute-start.20 = (bf16[64,1776]{1,0:T(8,128)(2,1)S(1)}, bf16[64,1776]{1,0:T(8,128)(2,1)S(1)}, u32[]{:S(2)}, u32[]{:S(2)}) collective-permute-start(bf16[64,1776]{1,0:T(8,128)(2,1)S(1)} %get-tuple-element.38), channel_id=1, source_target_pairs={{0,224},{32,0},{64,32},{96,64},{128,96},{160,128},{192,160},{224,1... | collective-permute-start | bytes 681992 | tf_op jit(solution)/shard_map/ppermute | solution.py:19
  53.9 1.0 add_convert_fusion.8
  55.0 3.1 %collective-permute-done.20 = bf16[64,1776]{1,0:T(8,128)(2,1)S(1)} collective-permute-done((bf16[64,1776]{1,0:T(8,128)(2,1)S(1)}, bf16[64,1776]{1,0:T(8,128)(2,1)S(1)}, u32[]{:S(2)}, u32[]{:S(2)}) %collective-permute-start.20) | collective-permute-done | bytes 227360 | tf_op jit(solution)/shard_map/ppermute | solution.py:19
  58.1 3.5 %collective-permute-start.21 = (bf16[64,1776]{1,0:T(8,128)(2,1)S(1)}, bf16[64,1776]{1,0:T(8,128)(2,1)S(1)}, u32[]{:S(2)}, u32[]{:S(2)}) collective-permute-start(bf16[64,1776]{1,0:T(8,128)(2,1)S(1)} %add_convert_fusion.5), channel_id=1, source_target_pairs={{0,224},{32,0},{64,32},{96,64},{128,96},{160,128},{192,160},{224,1... | collective-permute-start | bytes 681992 | tf_op jit(solution)/shard_map/ppermute | solution.py:19
  61.8 1.3 collective-permute-start.11
  63.7 1.2 collective-permute-done.21
  64.9 3.5 %collective-permute-start.22 = (bf16[64,1776]{1,0:T(8,128)(2,1)S(1)}, bf16[64,1776]{1,0:T(8,128)(2,1)S(1)}, u32[]{:S(2)}, u32[]{:S(2)}) collective-permute-start(bf16[64,1776]{1,0:T(8,128)(2,1)S(1)} %add_convert_fusion.4), channel_id=1, source_target_pairs={{0,224},{32,0},{64,32},{96,64},{128,96},{160,128},{192,160},{224,1... | collective-permute-start | bytes 681992 | tf_op jit(solution)/shard_map/ppermute | solution.py:19
  68.4 1.3 collective-permute-done.18
  69.9 2.7 %collective-permute-done.11 = bf16[128,1920]{1,0:T(8,128)(2,1)S(1)} collective-permute-done((bf16[128,1920]{1,0:T(8,128)(2,1)S(1)}, bf16[128,1920]{1,0:T(8,128)(2,1)S(1)}, u32[]{:S(2)}, u32[]{:S(2)}) %collective-permute-start.11) | collective-permute-done | bytes 491552 | tf_op jit(solution)/shard_map/ppermute | solution.py:19
  72.6 2.2 %collective-permute-done.9 = bf16[128,1920]{1,0:T(8,128)(2,1)S(1)} collective-permute-done((bf16[128,1920]{1,0:T(8,128)(2,1)S(1)}, bf16[128,1920]{1,0:T(8,128)(2,1)S(1)}, u32[]{:S(2)}, u32[]{:S(2)}) %collective-permute-start.9) | collective-permute-done | bytes 491552 | tf_op jit(solution)/shard_map/ppermute | solution.py:19
  75.0 1.2 collective-permute-done.19
  76.3 1.2 collective-permute-start.23
  77.5 1.4 %collective-permute-start.25 = (bf16[16,1776]{1,0:T(8,128)(2,1)S(1)}, bf16[16,1776]{1,0:T(8,128)(2,1)S(1)}, u32[]{:S(2)}, u32[]{:S(2)}) collective-permute-start(bf16[16,1776]{1,0:T(8,128)(2,1)S(1)} %get-tuple-element.61), channel_id=1, source_target_pairs={{0,24},{8,0},{16,8},{24,16},{1,25},{9,1},{17,9},{25,17},{2,26},{10... | collective-permute-start | bytes 170504 | tf_op jit(solution)/shard_map/ppermute | solution.py:19
  79.4 0.9 collective-permute-done.12
  80.4 3.6 %collective-permute-start.13 = (bf16[16,1920]{1,0:T(8,128)(2,1)S(1)}, bf16[16,1920]{1,0:T(8,128)(2,1)S(1)}, u32[]{:S(2)}, u32[]{:S(2)}) collective-permute-start(bf16[16,1920]{1,0:T(8,128)(2,1)S(1)} %get-tuple-element.57), channel_id=1, source_target_pairs={{0,128},{32,160},{64,192},{96,224},{128,0},{160,32},{192,64},{224,... | collective-permute-start | bytes 184328 | tf_op jit(solution)/shard_map/ppermute | solution.py:19
  84.2 2.2 %collective-permute-start.14 = (bf16[16,1920]{1,0:T(8,128)(2,1)S(1)}, bf16[16,1920]{1,0:T(8,128)(2,1)S(1)}, u32[]{:S(2)}, u32[]{:S(2)}) collective-permute-start(bf16[16,1920]{1,0:T(8,128)(2,1)S(1)} %get-tuple-element.59), channel_id=1, source_target_pairs={{0,64},{32,96},{64,128},{96,160},{128,192},{160,224},{192,0},{224,... | collective-permute-start | bytes 184328 | tf_op jit(solution)/shard_map/ppermute | solution.py:19
  86.4 1.5 %collective-permute-done.13 = bf16[16,1920]{1,0:T(8,128)(2,1)S(1)} collective-permute-done((bf16[16,1920]{1,0:T(8,128)(2,1)S(1)}, bf16[16,1920]{1,0:T(8,128)(2,1)S(1)}, u32[]{:S(2)}, u32[]{:S(2)}) %collective-permute-start.13) | collective-permute-done | bytes 61472 | tf_op jit(solution)/shard_map/ppermute | solution.py:19
  88.1 1.3 collective-permute-done.14
  89.4 0.9 divide_convert_fusion
  90.9 1.9 %collective-permute-start.28 = (bf16[16,924]{1,0:T(8,128)(2,1)S(1)}, bf16[16,924]{1,0:T(8,128)(2,1)S(1)}, u32[]{:S(2)}, u32[]{:S(2)}) collective-permute-start(bf16[16,924]{1,0:T(8,128)(2,1)S(1)} %bitcast.62), channel_id=1, source_target_pairs={{0,24},{8,0},{16,8},{24,16},{1,25},{9,1},{17,9},{25,17},{2,26},{10... | collective-permute-start | bytes 88712 | tf_op jit(solution)/shard_map/ppermute | solution.py:19
  92.8 1.5 %collective-permute-start.27 = (bf16[16,924]{1,0:T(8,128)(2,1)S(1)}, bf16[16,924]{1,0:T(8,128)(2,1)S(1)}, u32[]{:S(2)}, u32[]{:S(2)}) collective-permute-start(bf16[16,924]{1,0:T(8,128)(2,1)S(1)} %bitcast.57), channel_id=1, source_target_pairs={{0,16},{8,24},{16,0},{24,8},{1,17},{9,25},{17,1},{25,9},{2,18},{10... | collective-permute-start | bytes 88712 | tf_op jit(solution)/shard_map/ppermute | solution.py:19
  94.4 2.4 %collective-permute-done.26 = bf16[16,924]{1,0:T(8,128)(2,1)S(1)} collective-permute-done((bf16[16,924]{1,0:T(8,128)(2,1)S(1)}, bf16[16,924]{1,0:T(8,128)(2,1)S(1)}, u32[]{:S(2)}, u32[]{:S(2)}) %collective-permute-start.26) | collective-permute-done | bytes 29600 | tf_op jit(solution)/shard_map/ppermute | solution.py:19
  97.2 0.9 collective-permute-start.30
  98.1 2.6 %collective-permute-start.31 = (bf16[4,16,924]{2,1,0:T(8,128)(2,1)S(1)}, bf16[4,16,924]{2,1,0:T(8,128)(2,1)S(1)}, u32[]{:S(2)}, u32[]{:S(2)}) collective-permute-start(bf16[4,16,924]{2,1,0:T(8,128)(2,1)S(1)} %get-tuple-element.64), channel_id=1, source_target_pairs={{0,6},{2,0},{4,2},{6,4},{1,7},{3,1},{5,3},{7,5},{8,14},{10,8},{12,... | collective-permute-start | bytes 354824 | tf_op jit(solution)/shard_map/ppermute | solution.py:19
  100.7 2.0 %collective-permute-done.30 = bf16[4,16,924]{2,1,0:T(8,128)(2,1)S(1)} collective-permute-done((bf16[4,16,924]{2,1,0:T(8,128)(2,1)S(1)}, bf16[4,16,924]{2,1,0:T(8,128)(2,1)S(1)}, u32[]{:S(2)}, u32[]{:S(2)}) %collective-permute-start.30) | collective-permute-done | bytes 118304 | tf_op jit(solution)/shard_map/ppermute | solution.py:19
  102.7 1.3 collective-permute-done.29
  104.1 9.4 %collective-permute-start.35 = (bf16[4,16,924]{2,1,0:T(8,128)(2,1)S(1)}, bf16[4,16,924]{2,1,0:T(8,128)(2,1)S(1)}, u32[]{:S(2)}, u32[]{:S(2)}) collective-permute-start(bf16[4,16,924]{2,1,0:T(8,128)(2,1)S(1)} %get-tuple-element.51), channel_id=1, source_target_pairs={{0,192},{2,194},{4,196},{6,198},{8,200},{10,202},{12,204},{14,206}... | collective-permute-start | bytes 354824 | tf_op jit(solution)/shard_map/ppermute | solution.py:156
  113.5 2.7 %collective-permute-start.34 = (bf16[4,16,924]{2,1,0:T(8,128)(2,1)S(1)}, bf16[4,16,924]{2,1,0:T(8,128)(2,1)S(1)}, u32[]{:S(2)}, u32[]{:S(2)}) collective-permute-start(bf16[4,16,924]{2,1,0:T(8,128)(2,1)S(1)} %get-tuple-element.52), channel_id=1, source_target_pairs={{0,128},{2,130},{4,132},{6,134},{8,136},{10,138},{12,140},{14,142}... | collective-permute-start | bytes 354824 | tf_op jit(solution)/shard_map/ppermute | solution.py:156
  117.1 5.1 %collective-permute-start.32 = (bf16[4,16,924]{2,1,0:T(8,128)(2,1)S(1)}, bf16[4,16,924]{2,1,0:T(8,128)(2,1)S(1)}, u32[]{:S(2)}, u32[]{:S(2)}) collective-permute-start(bf16[4,16,924]{2,1,0:T(8,128)(2,1)S(1)} %get-tuple-element.50), channel_id=1, source_target_pairs={{1,32},{3,34},{5,36},{7,38},{9,40},{11,42},{13,44},{15,46},{17,48}... | collective-permute-start | bytes 354824 | tf_op jit(solution)/shard_map/ppermute | solution.py:156
  123.0 6.9 %collective-permute-done.32 = bf16[4,16,924]{2,1,0:T(8,128)(2,1)S(1)} collective-permute-done((bf16[4,16,924]{2,1,0:T(8,128)(2,1)S(1)}, bf16[4,16,924]{2,1,0:T(8,128)(2,1)S(1)}, u32[]{:S(2)}, u32[]{:S(2)}) %collective-permute-start.32) | collective-permute-done | bytes 118304 | tf_op jit(solution)/shard_map/ppermute | solution.py:156
  130.0 2.0 %collective-permute-start.36 = (bf16[4,4,16,924]{3,2,1,0:T(8,128)(2,1)S(1)}, bf16[4,4,16,924]{3,2,1,0:T(8,128)(2,1)S(1)}, u32[]{:S(2)}, u32[]{:S(2)}) collective-permute-start(bf16[4,4,16,924]{3,2,1,0:T(8,128)(2,1)S(1)} %pad_maximum_fusion.2), channel_id=1, source_target_pairs={{0,1},{1,0},{2,3},{3,2},{4,5},{5,4},{6,7},{7,6},{8,9},{9,8},{10,11... | collective-permute-start | bytes 1419272 | tf_op jit(solution)/shard_map/ppermute | solution.py:19
  133.5 2.0 %add_convert_fusion = bf16[1024,924]{0,1:T(8,128)(2,1)} fusion(f32[1024,924]{0,1:T(8,128)S(1)} %fusion.53, bf16[256,924]{1,0:T(8,128)(2,1)S(1)} %bitcast.49, bf16[1024,512]{1,0:T(8,128)(2,1)S(1)} %convolution_convert_fusion), kind=kOutput, calls=%fused_computation | convolution fusion | flops 486334464 | bytes 6742016 | tf_op jit(solution)/shard_map/dot_general | solution.py:191
  (106 shorter events, 10.4 us)
Async XLA Ops:
  4.5 5.6 %collective-permute-start = (f32[256,1024]{1,0:T(8,128)S(1)}, f32[256,1024]{1,0:T(8,128)S(1)}, u32[]{:S(2)}, u32[]{:S(2)}) collective-permute-start(f32[256,1024]{1,0:T(8,128)S(1)} %fusion.49), channel_id=1, source_target_pairs={{0,1},{1,0},{2,3},{3,2},{4,5},{5,4},{6,7},{7,6},{8,9},{9,8},{10,11... | collective-permute-start | bytes 3145736 | tf_op jit(solution)/shard_map/ppermute | solution.py:19
  10.9 6.7 %collective-permute-start.1 = (bf16[64,1024]{1,0:T(8,128)(2,1)S(1)}, bf16[64,1024]{1,0:T(8,128)(2,1)S(1)}, u32[]{:S(2)}, u32[]{:S(2)}) collective-permute-start(bf16[64,1024]{1,0:T(8,128)(2,1)S(1)} %get-tuple-element.54), channel_id=1, source_target_pairs={{0,2},{2,4},{4,6},{6,0},{1,3},{3,5},{5,7},{7,1},{8,10},{10,12},{12... | collective-permute-start | bytes 393224 | tf_op jit(solution)/shard_map/ppermute | solution.py:19
  11.0 8.0 %collective-permute-start.3 = (bf16[64,1024]{1,0:T(8,128)(2,1)S(1)}, bf16[64,1024]{1,0:T(8,128)(2,1)S(1)}, u32[]{:S(2)}, u32[]{:S(2)}) collective-permute-start(bf16[64,1024]{1,0:T(8,128)(2,1)S(1)} %get-tuple-element.55), channel_id=1, source_target_pairs={{0,4},{2,6},{4,0},{6,2},{1,5},{3,7},{5,1},{7,3},{8,12},{10,14},{12... | collective-permute-start | bytes 393224 | tf_op jit(solution)/shard_map/ppermute | solution.py:19
  12.9 7.1 %collective-permute-start.2 = (bf16[64,1024]{1,0:T(8,128)(2,1)S(1)}, bf16[64,1024]{1,0:T(8,128)(2,1)S(1)}, u32[]{:S(2)}, u32[]{:S(2)}) collective-permute-start(bf16[64,1024]{1,0:T(8,128)(2,1)S(1)} %get-tuple-element.56), channel_id=1, source_target_pairs={{0,6},{2,0},{4,2},{6,4},{1,7},{3,1},{5,3},{7,5},{8,14},{10,8},{12,... | collective-permute-start | bytes 393224 | tf_op jit(solution)/shard_map/ppermute | solution.py:19
  20.1 8.8 %collective-permute-start.6 = (bf16[64,1024]{1,0:T(8,128)(2,1)S(1)}, bf16[64,1024]{1,0:T(8,128)(2,1)S(1)}, u32[]{:S(2)}, u32[]{:S(2)}) collective-permute-start(bf16[64,1024]{1,0:T(8,128)(2,1)S(1)} %fusion.97), channel_id=1, source_target_pairs={{0,6},{2,0},{4,2},{6,4},{1,7},{3,1},{5,3},{7,5},{8,14},{10,8},{12,... | collective-permute-start | bytes 393224 | tf_op jit(solution)/shard_map/ppermute | solution.py:19
  23.6 5.8 %collective-permute-start.5 = (bf16[64,1024]{1,0:T(8,128)(2,1)S(1)}, bf16[64,1024]{1,0:T(8,128)(2,1)S(1)}, u32[]{:S(2)}, u32[]{:S(2)}) collective-permute-start(bf16[64,1024]{1,0:T(8,128)(2,1)S(1)} %fusion.97), channel_id=1, source_target_pairs={{0,4},{2,6},{4,0},{6,2},{1,5},{3,7},{5,1},{7,3},{8,12},{10,14},{12... | collective-permute-start | bytes 393224 | tf_op jit(solution)/shard_map/ppermute | solution.py:19
  23.6 9.1 %collective-permute-start.4 = (bf16[64,1024]{1,0:T(8,128)(2,1)S(1)}, bf16[64,1024]{1,0:T(8,128)(2,1)S(1)}, u32[]{:S(2)}, u32[]{:S(2)}) collective-permute-start(bf16[64,1024]{1,0:T(8,128)(2,1)S(1)} %fusion.97), channel_id=1, source_target_pairs={{0,2},{2,4},{4,6},{6,0},{1,3},{3,5},{5,7},{7,1},{8,10},{10,12},{12... | collective-permute-start | bytes 393224 | tf_op jit(solution)/shard_map/ppermute | solution.py:19
  32.7 2.4 %collective-permute-start.7 = (bf16[256,1024]{1,0:T(8,128)(2,1)S(1)}, bf16[256,1024]{1,0:T(8,128)(2,1)S(1)}, u32[]{:S(2)}, u32[]{:S(2)}) collective-permute-start(bf16[256,1024]{1,0:T(8,128)(2,1)S(1)} %pad_maximum_fusion.mine_ref), channel_id=1, source_target_pairs={{0,1},{1,0},{2,3},{3,2},{4,5},{5,4},{6,7},{7,6},{8,9},{9,8},{10,11... | collective-permute-start | bytes 1572872 | tf_op jit(solution)/shard_map/ppermute | solution.py:19
  41.3 12.7 %collective-permute-start.16 = (bf16[64,1776]{1,0:T(8,128)(2,1)}, bf16[64,1776]{1,0:T(8,128)(2,1)}, u32[]{:S(2)}, u32[]{:S(2)}) collective-permute-start(bf16[64,1776]{1,0:T(8,128)(2,1)} %get-tuple-element.35), channel_id=1, source_target_pairs={{0,32},{32,64},{64,96},{96,128},{128,160},{160,192},{192,224},{224... | collective-permute-start | bytes 681992 | tf_op jit(solution)/shard_map/ppermute | solution.py:19
  41.3 12.6 %copy-start.9 = (f32[64,1776]{1,0:T(8,128)S(1)}, f32[64,1776]{1,0:T(8,128)}, u32[]{:S(2)}) copy-start(f32[64,1776]{1,0:T(8,128)} %get-tuple-element.34) | copy-start | bytes 1363972
  41.4 16.7 %copy-start.8 = (f32[64,1776]{1,0:T(8,128)S(1)}, f32[64,1776]{1,0:T(8,128)}, u32[]{:S(2)}) copy-start(f32[64,1776]{1,0:T(8,128)} %get-tuple-element.37) | copy-start | bytes 1363972
  47.6 14.1 %copy-start.3 = (f32[64,1920]{1,0:T(8,128)S(1)}, f32[64,1920]{1,0:T(8,128)}, u32[]{:S(2)}) copy-start(f32[64,1920]{1,0:T(8,128)} %get-tuple-element.29) | copy-start | bytes 1474564
  47.6 14.1 %copy-start.12 = (bf16[64,1920]{1,0:T(8,128)(2,1)S(1)}, bf16[64,1920]{1,0:T(8,128)(2,1)}, u32[]{:S(2)}) copy-start(bf16[64,1920]{1,0:T(8,128)(2,1)} %get-tuple-element.28) | copy-start | bytes 737284
  47.6 15.5 %copy-start.2 = (f32[64,1920]{1,0:T(8,128)S(1)}, f32[64,1920]{1,0:T(8,128)}, u32[]{:S(2)}) copy-start(f32[64,1920]{1,0:T(8,128)} %get-tuple-element.25) | copy-start | bytes 1474564
  47.6 15.5 %collective-permute-start.8 = (bf16[64,1920]{1,0:T(8,128)(2,1)S(1)}, bf16[64,1920]{1,0:T(8,128)(2,1)S(1)}, u32[]{:S(2)}, u32[]{:S(2)}) collective-permute-start(bf16[64,1920]{1,0:T(8,128)(2,1)S(1)} %get-tuple-element.26), channel_id=1, source_target_pairs={{0,8},{8,16},{16,24},{24,0},{1,9},{9,17},{17,25},{25,1},{2,10},{10... | collective-permute-start | bytes 737288 | tf_op jit(solution)/shard_map/ppermute | solution.py:19
  48.4 13.3 %collective-permute-start.10 = (bf16[64,1920]{1,0:T(8,128)(2,1)S(1)}, bf16[64,1920]{1,0:T(8,128)(2,1)S(1)}, u32[]{:S(2)}, u32[]{:S(2)}) collective-permute-start(bf16[64,1920]{1,0:T(8,128)(2,1)S(1)} %get-tuple-element.30), channel_id=1, source_target_pairs={{0,24},{8,0},{16,8},{24,16},{1,25},{9,1},{17,9},{25,17},{2,26},{10... | collective-permute-start | bytes 737288 | tf_op jit(solution)/shard_map/ppermute | solution.py:19
  50.3 7.7 %collective-permute-start.20 = (bf16[64,1776]{1,0:T(8,128)(2,1)S(1)}, bf16[64,1776]{1,0:T(8,128)(2,1)S(1)}, u32[]{:S(2)}, u32[]{:S(2)}) collective-permute-start(bf16[64,1776]{1,0:T(8,128)(2,1)S(1)} %get-tuple-element.38), channel_id=1, source_target_pairs={{0,224},{32,0},{64,32},{96,64},{128,96},{160,128},{192,160},{224,1... | collective-permute-start | bytes 681992 | tf_op jit(solution)/shard_map/ppermute | solution.py:19
  54.9 8.6 %collective-permute-start.17 = (bf16[64,1776]{1,0:T(8,128)(2,1)S(1)}, bf16[64,1776]{1,0:T(8,128)(2,1)S(1)}, u32[]{:S(2)}, u32[]{:S(2)}) collective-permute-start(bf16[64,1776]{1,0:T(8,128)(2,1)S(1)} %add_convert_fusion.8), channel_id=1, source_target_pairs={{0,32},{32,64},{64,96},{96,128},{128,160},{160,192},{192,224},{224... | collective-permute-start | bytes 681992 | tf_op jit(solution)/shard_map/ppermute | solution.py:19
  58.1 6.7 %collective-permute-start.21 = (bf16[64,1776]{1,0:T(8,128)(2,1)S(1)}, bf16[64,1776]{1,0:T(8,128)(2,1)S(1)}, u32[]{:S(2)}, u32[]{:S(2)}) collective-permute-start(bf16[64,1776]{1,0:T(8,128)(2,1)S(1)} %add_convert_fusion.5), channel_id=1, source_target_pairs={{0,224},{32,0},{64,32},{96,64},{128,96},{160,128},{192,160},{224,1... | collective-permute-start | bytes 681992 | tf_op jit(solution)/shard_map/ppermute | solution.py:19
  61.8 10.8 %collective-permute-start.11 = (bf16[128,1920]{1,0:T(8,128)(2,1)S(1)}, bf16[128,1920]{1,0:T(8,128)(2,1)S(1)}, u32[]{:S(2)}, u32[]{:S(2)}) collective-permute-start(bf16[128,1920]{1,0:T(8,128)(2,1)S(1)} %pad_maximum_fusion.4), channel_id=1, source_target_pairs={{0,24},{8,0},{16,8},{24,16},{1,25},{9,1},{17,9},{25,17},{2,26},{10... | collective-permute-start | bytes 1474568 | tf_op jit(solution)/shard_map/ppermute | solution.py:19
  63.1 11.7 %copy-start.1 = (f32[64,1920]{1,0:T(8,128)S(1)}, f32[64,1920]{1,0:T(8,128)}, u32[]{:S(2)}) copy-start(f32[64,1920]{1,0:T(8,128)} %get-tuple-element.24) | copy-start | bytes 1474564
  63.2 13.1 %copy-start.10 = (f32[64,1776]{1,0:T(8,128)S(1)}, f32[64,1776]{1,0:T(8,128)}, u32[]{:S(2)}) copy-start(f32[64,1776]{1,0:T(8,128)} %get-tuple-element.31) | copy-start | bytes 1363972
  63.2 11.6 %collective-permute-start.9 = (bf16[128,1920]{1,0:T(8,128)(2,1)S(1)}, bf16[128,1920]{1,0:T(8,128)(2,1)S(1)}, u32[]{:S(2)}, u32[]{:S(2)}) collective-permute-start(bf16[128,1920]{1,0:T(8,128)(2,1)S(1)} %pad_maximum_fusion.3), channel_id=1, source_target_pairs={{0,8},{8,16},{16,24},{24,0},{1,9},{9,17},{17,25},{25,1},{2,10},{10... | collective-permute-start | bytes 1474568 | tf_op jit(solution)/shard_map/ppermute | solution.py:19
  63.6 6.2 %collective-permute-start.18 = (bf16[64,1776]{1,0:T(8,128)(2,1)S(1)}, bf16[64,1776]{1,0:T(8,128)(2,1)S(1)}, u32[]{:S(2)}, u32[]{:S(2)}) collective-permute-start(bf16[64,1776]{1,0:T(8,128)(2,1)S(1)} %add_convert_fusion.7), channel_id=1, source_target_pairs={{0,32},{32,64},{64,96},{96,128},{128,160},{160,192},{192,224},{224... | collective-permute-start | bytes 681992 | tf_op jit(solution)/shard_map/ppermute | solution.py:19
  64.9 15.4 %copy-start.4 = (f32[64,1920]{1,0:T(8,128)S(1)}, f32[64,1920]{1,0:T(8,128)}, u32[]{:S(2)}) copy-start(f32[64,1920]{1,0:T(8,128)} %get-tuple-element.23) | copy-start | bytes 1474564
  64.9 10.1 %collective-permute-start.22 = (bf16[64,1776]{1,0:T(8,128)(2,1)S(1)}, bf16[64,1776]{1,0:T(8,128)(2,1)S(1)}, u32[]{:S(2)}, u32[]{:S(2)}) collective-permute-start(bf16[64,1776]{1,0:T(8,128)(2,1)S(1)} %add_convert_fusion.4), channel_id=1, source_target_pairs={{0,224},{32,0},{64,32},{96,64},{128,96},{160,128},{192,160},{224,1... | collective-permute-start | bytes 681992 | tf_op jit(solution)/shard_map/ppermute | solution.py:19
  69.8 6.5 %collective-permute-start.19 = (bf16[64,1776]{1,0:T(8,128)(2,1)S(1)}, bf16[64,1776]{1,0:T(8,128)(2,1)S(1)}, u32[]{:S(2)}, u32[]{:S(2)}) collective-permute-start(bf16[64,1776]{1,0:T(8,128)(2,1)S(1)} %add_convert_fusion.6), channel_id=1, source_target_pairs={{0,32},{32,64},{64,96},{96,128},{128,160},{160,192},{192,224},{224... | collective-permute-start | bytes 681992 | tf_op jit(solution)/shard_map/ppermute | solution.py:19
  74.9 5.4 %collective-permute-start.12 = (bf16[64,1920]{1,0:T(8,128)(2,1)S(1)}, bf16[64,1920]{1,0:T(8,128)(2,1)S(1)}, u32[]{:S(2)}, u32[]{:S(2)}) collective-permute-start(bf16[64,1920]{1,0:T(8,128)(2,1)S(1)} %add_convert_fusion.1), channel_id=1, source_target_pairs={{0,32},{32,0},{64,96},{96,64},{128,160},{160,128},{192,224},{224,1... | collective-permute-start | bytes 737288 | tf_op jit(solution)/shard_map/ppermute | solution.py:119
  76.3 13.1 %copy-start.13 = (f32[16,3696]{1,0:T(8,128)S(1)}, f32[16,3696]{1,0:T(8,128)}, u32[]{:S(2)}) copy-start(f32[16,3696]{1,0:T(8,128)} %param.8) | copy-start | bytes 709636
  76.3 13.1 %copy-start.14 = (f32[16,3696]{1,0:T(8,128)S(1)}, f32[16,3696]{1,0:T(8,128)}, u32[]{:S(2)}) copy-start(f32[16,3696]{1,0:T(8,128)} %param.9) | copy-start | bytes 709636
  76.3 7.8 %collective-permute-start.23 = (bf16[16,1776]{1,0:T(8,128)(2,1)S(1)}, bf16[16,1776]{1,0:T(8,128)(2,1)S(1)}, u32[]{:S(2)}, u32[]{:S(2)}) collective-permute-start(bf16[16,1776]{1,0:T(8,128)(2,1)S(1)} %get-tuple-element.60), channel_id=1, source_target_pairs={{0,16},{8,24},{16,0},{24,8},{1,17},{9,25},{17,1},{25,9},{2,18},{10... | collective-permute-start | bytes 170504 | tf_op jit(solution)/shard_map/ppermute | solution.py:19
  77.5 8.9 %collective-permute-start.25 = (bf16[16,1776]{1,0:T(8,128)(2,1)S(1)}, bf16[16,1776]{1,0:T(8,128)(2,1)S(1)}, u32[]{:S(2)}, u32[]{:S(2)}) collective-permute-start(bf16[16,1776]{1,0:T(8,128)(2,1)S(1)} %get-tuple-element.61), channel_id=1, source_target_pairs={{0,24},{8,0},{16,8},{24,16},{1,25},{9,1},{17,9},{25,17},{2,26},{10... | collective-permute-start | bytes 170504 | tf_op jit(solution)/shard_map/ppermute | solution.py:19
  78.9 7.4 %collective-permute-start.24 = (bf16[16,1776]{1,0:T(8,128)(2,1)S(1)}, bf16[16,1776]{1,0:T(8,128)(2,1)S(1)}, u32[]{:S(2)}, u32[]{:S(2)}) collective-permute-start(bf16[16,1776]{1,0:T(8,128)(2,1)S(1)} %get-tuple-element.62), channel_id=1, source_target_pairs={{0,8},{8,16},{16,24},{24,0},{1,9},{9,17},{17,25},{25,1},{2,10},{10... | collective-permute-start | bytes 170504 | tf_op jit(solution)/shard_map/ppermute | solution.py:19
  80.4 7.5 %collective-permute-start.13 = (bf16[16,1920]{1,0:T(8,128)(2,1)S(1)}, bf16[16,1920]{1,0:T(8,128)(2,1)S(1)}, u32[]{:S(2)}, u32[]{:S(2)}) collective-permute-start(bf16[16,1920]{1,0:T(8,128)(2,1)S(1)} %get-tuple-element.57), channel_id=1, source_target_pairs={{0,128},{32,160},{64,192},{96,224},{128,0},{160,32},{192,64},{224,... | collective-permute-start | bytes 184328 | tf_op jit(solution)/shard_map/ppermute | solution.py:19
  84.0 4.1 %collective-permute-start.15 = (bf16[16,1920]{1,0:T(8,128)(2,1)S(1)}, bf16[16,1920]{1,0:T(8,128)(2,1)S(1)}, u32[]{:S(2)}, u32[]{:S(2)}) collective-permute-start(bf16[16,1920]{1,0:T(8,128)(2,1)S(1)} %get-tuple-element.58), channel_id=1, source_target_pairs={{0,192},{32,224},{64,0},{96,32},{128,64},{160,96},{192,128},{224,1... | collective-permute-start | bytes 184328 | tf_op jit(solution)/shard_map/ppermute | solution.py:19
  84.2 5.2 %collective-permute-start.14 = (bf16[16,1920]{1,0:T(8,128)(2,1)S(1)}, bf16[16,1920]{1,0:T(8,128)(2,1)S(1)}, u32[]{:S(2)}, u32[]{:S(2)}) collective-permute-start(bf16[16,1920]{1,0:T(8,128)(2,1)S(1)} %get-tuple-element.59), channel_id=1, source_target_pairs={{0,64},{32,96},{64,128},{96,160},{128,192},{160,224},{192,0},{224,... | collective-permute-start | bytes 184328 | tf_op jit(solution)/shard_map/ppermute | solution.py:19
  90.9 3.4 %collective-permute-start.28 = (bf16[16,924]{1,0:T(8,128)(2,1)S(1)}, bf16[16,924]{1,0:T(8,128)(2,1)S(1)}, u32[]{:S(2)}, u32[]{:S(2)}) collective-permute-start(bf16[16,924]{1,0:T(8,128)(2,1)S(1)} %bitcast.62), channel_id=1, source_target_pairs={{0,24},{8,0},{16,8},{24,16},{1,25},{9,1},{17,9},{25,17},{2,26},{10... | collective-permute-start | bytes 88712 | tf_op jit(solution)/shard_map/ppermute | solution.py:19
  92.8 4.0 %collective-permute-start.26 = (bf16[16,924]{1,0:T(8,128)(2,1)S(1)}, bf16[16,924]{1,0:T(8,128)(2,1)S(1)}, u32[]{:S(2)}, u32[]{:S(2)}) collective-permute-start(bf16[16,924]{1,0:T(8,128)(2,1)S(1)} %bitcast.60), channel_id=1, source_target_pairs={{0,8},{8,16},{16,24},{24,0},{1,9},{9,17},{17,25},{25,1},{2,10},{10... | collective-permute-start | bytes 88712 | tf_op jit(solution)/shard_map/ppermute | solution.py:19
  92.8 4.3 %collective-permute-start.27 = (bf16[16,924]{1,0:T(8,128)(2,1)S(1)}, bf16[16,924]{1,0:T(8,128)(2,1)S(1)}, u32[]{:S(2)}, u32[]{:S(2)}) collective-permute-start(bf16[16,924]{1,0:T(8,128)(2,1)S(1)} %bitcast.57), channel_id=1, source_target_pairs={{0,16},{8,24},{16,0},{24,8},{1,17},{9,25},{17,1},{25,9},{2,18},{10... | collective-permute-start | bytes 88712 | tf_op jit(solution)/shard_map/ppermute | solution.py:19
  97.2 5.5 %collective-permute-start.30 = (bf16[4,16,924]{2,1,0:T(8,128)(2,1)S(1)}, bf16[4,16,924]{2,1,0:T(8,128)(2,1)S(1)}, u32[]{:S(2)}, u32[]{:S(2)}) collective-permute-start(bf16[4,16,924]{2,1,0:T(8,128)(2,1)S(1)} %get-tuple-element.64), channel_id=1, source_target_pairs={{0,4},{2,6},{4,0},{6,2},{1,5},{3,7},{5,1},{7,3},{8,12},{10,14},{12... | collective-permute-start | bytes 354824 | tf_op jit(solution)/shard_map/ppermute | solution.py:19
  98.0 6.0 %collective-permute-start.29 = (bf16[4,16,924]{2,1,0:T(8,128)(2,1)S(1)}, bf16[4,16,924]{2,1,0:T(8,128)(2,1)S(1)}, u32[]{:S(2)}, u32[]{:S(2)}) collective-permute-start(bf16[4,16,924]{2,1,0:T(8,128)(2,1)S(1)} %get-tuple-element.64), channel_id=1, source_target_pairs={{0,2},{2,4},{4,6},{6,0},{1,3},{3,5},{5,7},{7,1},{8,10},{10,12},{12... | collective-permute-start | bytes 354824 | tf_op jit(solution)/shard_map/ppermute | solution.py:19
  98.1 5.9 %collective-permute-start.31 = (bf16[4,16,924]{2,1,0:T(8,128)(2,1)S(1)}, bf16[4,16,924]{2,1,0:T(8,128)(2,1)S(1)}, u32[]{:S(2)}, u32[]{:S(2)}) collective-permute-start(bf16[4,16,924]{2,1,0:T(8,128)(2,1)S(1)} %get-tuple-element.64), channel_id=1, source_target_pairs={{0,6},{2,0},{4,2},{6,4},{1,7},{3,1},{5,3},{7,5},{8,14},{10,8},{12,... | collective-permute-start | bytes 354824 | tf_op jit(solution)/shard_map/ppermute | solution.py:19
  100.7 21.4 %copy-start.15 = (bf16[1024,512]{1,0:T(8,128)(2,1)S(1)}, bf16[1024,512]{1,0:T(8,128)(2,1)}, u32[]{:S(2)}) copy-start(bf16[1024,512]{1,0:T(8,128)(2,1)} %param.6) | copy-start | bytes 3145732
  104.1 25.7 %collective-permute-start.35 = (bf16[4,16,924]{2,1,0:T(8,128)(2,1)S(1)}, bf16[4,16,924]{2,1,0:T(8,128)(2,1)S(1)}, u32[]{:S(2)}, u32[]{:S(2)}) collective-permute-start(bf16[4,16,924]{2,1,0:T(8,128)(2,1)S(1)} %get-tuple-element.51), channel_id=1, source_target_pairs={{0,192},{2,194},{4,196},{6,198},{8,200},{10,202},{12,204},{14,206}... | collective-permute-start | bytes 354824 | tf_op jit(solution)/shard_map/ppermute | solution.py:156
  113.5 16.3 %collective-permute-start.34 = (bf16[4,16,924]{2,1,0:T(8,128)(2,1)S(1)}, bf16[4,16,924]{2,1,0:T(8,128)(2,1)S(1)}, u32[]{:S(2)}, u32[]{:S(2)}) collective-permute-start(bf16[4,16,924]{2,1,0:T(8,128)(2,1)S(1)} %get-tuple-element.52), channel_id=1, source_target_pairs={{0,128},{2,130},{4,132},{6,134},{8,136},{10,138},{12,140},{14,142}... | collective-permute-start | bytes 354824 | tf_op jit(solution)/shard_map/ppermute | solution.py:156
  116.3 13.6 %collective-permute-start.33 = (bf16[4,16,924]{2,1,0:T(8,128)(2,1)S(1)}, bf16[4,16,924]{2,1,0:T(8,128)(2,1)S(1)}, u32[]{:S(2)}, u32[]{:S(2)}) collective-permute-start(bf16[4,16,924]{2,1,0:T(8,128)(2,1)S(1)} %get-tuple-element.53), channel_id=1, source_target_pairs={{0,64},{2,66},{4,68},{6,70},{8,72},{10,74},{12,76},{14,78},{16,80}... | collective-permute-start | bytes 354824 | tf_op jit(solution)/shard_map/ppermute | solution.py:156
  117.1 12.8 %collective-permute-start.32 = (bf16[4,16,924]{2,1,0:T(8,128)(2,1)S(1)}, bf16[4,16,924]{2,1,0:T(8,128)(2,1)S(1)}, u32[]{:S(2)}, u32[]{:S(2)}) collective-permute-start(bf16[4,16,924]{2,1,0:T(8,128)(2,1)S(1)} %get-tuple-element.50), channel_id=1, source_target_pairs={{1,32},{3,34},{5,36},{7,38},{9,40},{11,42},{13,44},{15,46},{17,48}... | collective-permute-start | bytes 354824 | tf_op jit(solution)/shard_map/ppermute | solution.py:156
  130.0 3.6 %collective-permute-start.36 = (bf16[4,4,16,924]{3,2,1,0:T(8,128)(2,1)S(1)}, bf16[4,4,16,924]{3,2,1,0:T(8,128)(2,1)S(1)}, u32[]{:S(2)}, u32[]{:S(2)}) collective-permute-start(bf16[4,4,16,924]{3,2,1,0:T(8,128)(2,1)S(1)} %pad_maximum_fusion.2), channel_id=1, source_target_pairs={{0,1},{1,0},{2,3},{3,2},{4,5},{5,4},{6,7},{7,6},{8,9},{9,8},{10,11... | collective-permute-start | bytes 1419272 | tf_op jit(solution)/shard_map/ppermute | solution.py:19
  (5 other events, 27.8 us)
